TPU v7x, 32 devices: a whole 2x2x4 slice. The times are simulated.
32 devices in a mesh: row: 8 (over y, x, core), col: 4 (over z).
Axes of the slice: x: 2, y: 2, z: 4, core: 2. Of those that a mesh axis runs over, the one named last changes fastest.
Arguments:
- atom_types: int32 [32, 256], P(('row', 'col')), may hold values from 0 to 3
- neighbor_ids: int32 [32, 32, 256], P(('row', 'col')), may hold values from 0 to 255
- switching: float32 [32, 32, 256], P(('row', 'col')), may hold values from 0.1 to 1
- environment: float32 [32, 256, 64], P(('row', 'col')), may hold values from -6 to 6
- force_weights: float32 [32, 256], P(('row', 'col')), may hold values from -1 to 1
- targets: float32 [32], P(('row', 'col')), may hold values from -6 to 6
- type_embed: float32 [4, 64], replicated, may hold values from -8 to 8, as said below
- layer_weight: float32 [64, 128], replicated, may hold values from -1 to 1
- out_weight: float32 [128], replicated, may hold values from -0.5 to 0.5
- covariance: float32 [8192, 8192], P('row', 'col'), as said below
Outputs:
- new_weight: float32 [8192], P(('row', 'col'))
- new_cov: float32 [8192, 8192], P('row', 'col')
Inputs may be any that keep to these rules, and one draw needn't show every extreme that they name: `neighbor_ids`: indices of atoms of the same configuration. `covariance`: symmetric positive definite. `type_embed`: each feature sums to zero over the 4 types.
All inputs are finite; a program needn't handle non-finite values. Where the computation divides by a largest or mean magnitude, that divisor is 1e-20 or more.
Results may differ from a plain program's by a relative error of at most 0.0003.
Values sent between devices are 32-bit elements; how exact they have to be, the bound alone decides.
No kernel may reach another device: no remote copies, remote signals or barrier semaphores. Data moves between devices by JAX's collectives and lax.ppermute only.
A program may use at most 64 MiB of HBM per device.

v0:
```python
import math

import jax
import jax.numpy as jnp
from jax import lax
from jax.sharding import PartitionSpec as P

NEWTON = 4


forget = 0.98
highest = lax.Precision.HIGHEST


def network(
    atom_types,
    neighbor_ids,
    switching,
    environment,
    force_weights,
    type_embed,
    layer_weight,
    out_weight,
):
    type_ids = jnp.arange(type_embed.shape[0], dtype=jnp.int32)
    onehot = (atom_types[:, None] == type_ids[None, :]).astype(jnp.float32)
    mixed = environment + jnp.dot(onehot, type_embed, precision=highest)
    nearby = jnp.take(mixed, neighbor_ids, axis=0)
    descriptor = jnp.sum(switching[:, :, None] * nearby, axis=0) / math.sqrt(neighbor_ids.shape[0])
    hidden = jnp.tanh(descriptor)
    activity = jnp.tanh(jnp.dot(hidden, layer_weight, precision=highest))
    energy = jnp.dot(activity, out_weight, precision=highest)
    atom_scale = 1.0 / math.sqrt(energy.shape[0])
    predicted = jnp.sum(force_weights * energy) * atom_scale
    slopes = out_weight[None, :] * (1.0 - activity * activity)
    jacobian = jnp.dot((force_weights[:, None] * hidden).T, slopes, precision=highest) * atom_scale
    return (predicted, jacobian.reshape(-1))


def contract_rows(left, right):
    return lax.dot_general(left, right, (((1,), (1,)), ((), ())), precision=highest)


def contract_first(left, right):
    return lax.dot_general(left, right, (((0,), (1,)), ((), ())), precision=highest)


def newton_rows(inverse, innovation, groups, position):
    height = inverse.shape[0] // groups
    window = lax.dynamic_slice_in_dim(inverse, position * height, height, 0)
    return 2.0 * window - jnp.dot(
        jnp.dot(window, innovation, precision=highest), inverse, precision=highest
    )


def on_device(
    atom_types,
    neighbor_ids,
    switching,
    environment,
    force_weights,
    targets,
    type_embed,
    layer_weight,
    out_weight,
    covariance,
):
    rows_n = lax.axis_size("row")
    cols_n = lax.axis_size("col")
    row_at = lax.axis_index("row")
    col_at = lax.axis_index("col")
    predicted, jacobian = jax.vmap(network, in_axes=(0, 0, 0, 0, 0, None, None, None))(
        atom_types,
        neighbor_ids,
        switching,
        environment,
        force_weights,
        type_embed,
        layer_weight,
        out_weight,
    )
    errors = targets - predicted
    per_dev = jacobian.shape[0]
    params = jacobian.shape[1]
    streams = per_dev * rows_n * cols_n
    slab_rows = params // (rows_n * cols_n)
    tile_rows = covariance.shape[0]
    blocks = jacobian.reshape(1, 1, per_dev, cols_n, rows_n, slab_rows)
    spread = jnp.broadcast_to(errors.reshape(1, 1, per_dev, 1, 1), (1, 1, per_dev, cols_n, rows_n))
    own_cols, all_errors = (
        lax.all_to_all(
            lax.all_to_all(blocks, "row", split_axis=4, concat_axis=0, tiled=True),
            "col",
            split_axis=3,
            concat_axis=1,
            tiled=True,
        ),
        lax.all_to_all(
            lax.all_to_all(spread, "row", split_axis=4, concat_axis=0, tiled=True),
            "col",
            split_axis=3,
            concat_axis=1,
            tiled=True,
        ),
    )
    own_cols = own_cols.reshape(streams, slab_rows)
    all_errors = all_errors.reshape(streams)
    row_pieces = jacobian.reshape(1, 1, per_dev, rows_n, tile_rows)
    row_pieces = lax.all_to_all(row_pieces, "row", split_axis=3, concat_axis=0, tiled=True)
    row_jac = lax.all_gather(row_pieces, "col", axis=1, tiled=True).reshape(streams, tile_rows)
    window = covariance
    rows_term = contract_rows(window, lax.all_gather(own_cols, "row", axis=1, tiled=True))
    window = covariance
    cross_own = lax.psum_scatter(
        contract_first(window, row_jac), "row", scatter_dimension=0, tiled=True
    )
    identity = jnp.eye(streams, dtype=jnp.float32)
    innovation = (
        lax.psum(jnp.dot(own_cols, cross_own, precision=highest), ("row", "col"))
        + forget * identity
    )
    row_bound = jnp.max(jnp.sum(jnp.abs(innovation), axis=1))
    inverse = identity * (2.0 / row_bound) - innovation / (row_bound * row_bound)
    for repeat in range(NEWTON - 1):
        inverse = lax.all_gather(
            newton_rows(inverse, innovation, rows_n, row_at), "row", axis=0, tiled=True
        )
    cross_rows = lax.psum(rows_term, "col")
    gain_rows = jnp.dot(cross_rows, inverse, precision=highest)
    gain_own = lax.dynamic_slice_in_dim(gain_rows, col_at * slab_rows, slab_rows, 0)
    flat_weight = layer_weight.reshape(-1)
    own_weight = lax.dynamic_slice_in_dim(
        flat_weight, (row_at * cols_n + col_at) * slab_rows, slab_rows, 0
    )
    new_weight = own_weight + jnp.dot(gain_own, all_errors, precision=highest)
    update = contract_rows(gain_rows, lax.all_gather(cross_own, "row", axis=0, tiled=True))
    new_cov = (covariance - update) / forget
    return (new_weight, new_cov)


def solution(mesh):
    in_specs = (
        P(("row", "col"), None),
        P(("row", "col"), None, None),
        P(("row", "col"), None, None),
        P(("row", "col"), None, None),
        P(("row", "col"), None),
        P(("row", "col")),
        P(),
        P(),
        P(),
        P("row", "col"),
    )
    out_specs = (P(("row", "col")), P("row", "col"))
    return jax.shard_map(
        on_device, mesh=mesh, in_specs=in_specs, out_specs=out_specs, check_vma=False
    )
```

profile of v0, /device:TPU:0, one launch (start us, length us, event | category | flops | bytes accessed | tf_op | source)
XLA Modules:
  0.0 288.6 jit_solution(2580422493975503229)
XLA Ops:
  8.0 0.8 and_bitcast_fusion
  8.8 0.8 fusion.21
  10.3 1.1 fusion
  11.4 0.1 copy.17
  11.5 73.9 %gather_fusion = f32[8192,64]{1,0:T(8,128)} fusion(f32[1,256,64]{2,1,0:T(8,128)S(1)} %copy.17, s32[8192]{0:T(1024)S(1)} %bitcast.78), kind=kCustom, calls=%fused_computation | custom fusion | bytes 4259840 | tf_op jit(solution)/shard_map/vmap(jit(_take))/gather | solution.py:28
  85.4 6.1 %multiply_reduce_fusion = f32[256,64]{1,0:T(8,128)S(1)} fusion(f32[1,32,256,64]{3,2,1,0:T(8,128)} %bitcast.79, f32[32,256]{1,0:T(8,128)S(1)} %bitcast.87, pred[32,256]{1,0:T(8,128)(4,1)S(1)} %and_bitcast_fusion), kind=kLoop, calls=%fused_computation.2 | loop fusion | flops 1556480 | bytes 2203648 | tf_op jit(solution)/shard_map/vmap()/reduce_sum | solution.py:29
  91.5 0.3 convolution_tanh_fusion
  91.8 0.8 fusion.4
  93.3 9.6 %all_to_all.66 = f32[1,1,1,4,8]{3,2,1,0,4:T(1,128)S(1)} all-to-all(f32[1,1,1,4,8]{3,2,1,0,4:T(1,128)S(1)} %broadcast_in_dim.28), channel_id=1, replica_groups=mesh['row'=8,'col'=4] {'row'}, dimensions={4} | all-to-all | bytes 256 | tf_op jit(solution)/shard_map/all_to_all | solution.py:99
  102.9 0.7 copy.22
  103.6 4.9 %all-to-all-start.4 = ((f32[8,1,1,4,1]{0,4,2,1,3:T(1,128)}), f32[8,1,1,4,1]{0,4,2,1,3:T(1,128)S(1)}, u32[]{:S(2)}, u32[]{:S(2)}) async-start(f32[8,1,1,4,1]{0,4,2,1,3:T(1,128)} %bitcast.28), calls=%async_computation.5 | async-start | bytes 4096 | tf_op jit(solution)/shard_map/all_to_all | solution.py:98
  108.5 1.1 convolution_multiply_fusion
  109.6 0.8 reshape.133
  110.4 3.5 %all-to-all-done.4 = f32[8,1,1,4,1]{0,4,2,1,3:T(1,128)S(1)} async-done(((f32[8,1,1,4,1]{0,4,2,1,3:T(1,128)}), f32[8,1,1,4,1]{0,4,2,1,3:T(1,128)S(1)}, u32[]{:S(2)}, u32[]{:S(2)}) %all-to-all-start.4) | async-done | bytes 160 | tf_op jit(solution)/shard_map/all_to_all | solution.py:98
  113.9 7.2 %all_to_all.67 = f32[1,1,1,4,8,256]{5,3,2,1,0,4:T(4,128)S(1)} all-to-all(f32[1,1,1,4,8,256]{5,3,2,1,0,4:T(4,128)S(1)} %copy.18), channel_id=1, replica_groups=mesh['row'=8,'col'=4] {'row'}, dimensions={4} | all-to-all | bytes 65536 | tf_op jit(solution)/shard_map/all_to_all | solution.py:92
  121.1 3.3 %all-to-all-start.2 = ((f32[1,1,1,8,1024]{4,2,1,0,3:T(1,128)}), f32[1,1,1,8,1024]{4,2,1,0,3:T(1,128)S(1)}, u32[]{:S(2)}, u32[]{:S(2)}) async-start(f32[1,1,1,8,1024]{4,2,1,0,3:T(1,128)} %bitcast.13), calls=%async_computation.2 | async-start | bytes 65536 | tf_op jit(solution)/shard_map/all_to_all | solution.py:109
  124.4 0.1 copy.24
  124.5 0.1 reshape.157
  124.6 0.6 copy.19
  125.2 4.0 %all-to-all-done.2 = f32[1,1,1,8,1024]{4,2,1,0,3:T(1,128)S(1)} async-done(((f32[1,1,1,8,1024]{4,2,1,0,3:T(1,128)}), f32[1,1,1,8,1024]{4,2,1,0,3:T(1,128)S(1)}, u32[]{:S(2)}, u32[]{:S(2)}) %all-to-all-start.2) | async-done | bytes 32800 | tf_op jit(solution)/shard_map/all_to_all | solution.py:109
  129.2 3.3 %all-to-all-start.1 = ((f32[8,1,1,4,1,256]{5,0,4,2,1,3:T(8,128)}), f32[8,1,1,4,1,256]{5,0,4,2,1,3:T(8,128)S(1)}, u32[]{:S(2)}, u32[]{:S(2)}) async-start(f32[8,1,1,4,1,256]{5,0,4,2,1,3:T(8,128)} %copy.19), calls=%async_computation.1 | async-start | bytes 65536 | tf_op jit(solution)/shard_map/all_to_all | solution.py:91
  132.5 0.0 reduce-scatter.2.cloned.1.call-start
  132.5 13.9 %all-gather = f32[1,1,1,8,4096]{4,2,1,0,3:T(1,128)S(1)} all-gather(f32[1,1,1,8,1024]{4,2,1,0,3:T(1,128)S(1)} %all-to-all-done.2), channel_id=2, replica_groups=mesh['row'=8,'col'=4] {'col'}, dimensions={4}, use_global_device_ids=true | all-gather | bytes 163840 | tf_op jit(solution)/shard_map/all_gather | solution.py:110
  146.5 0.3 reduce.2
  146.8 7.9 %convolution_bitcast_fusion = f32[2048,32]{0,1:T(8,128)} fusion(f32[32,1024]{1,0:T(8,128)S(1)} %reshape.136, f32[1024,2048]{1,0:T(8,128)} %param.19), kind=kOutput, calls=%fused_computation.3 | convolution fusion | flops 805306368 | bytes 8781824 | tf_op jit(solution)/shard_map/dot_general | solution.py:45
  154.7 0.0 all-reduce.2.cloned.1.call-start
  154.8 8.2 %all_gather.18 = f32[32,2048]{1,0:T(8,128)S(1)} all-gather(f32[32,256]{1,0:T(8,128)S(1)} %reshape.134), channel_id=1, replica_groups=mesh['row'=8,'col'=4] {'row'}, dimensions={1}, use_global_device_ids=true | all-gather | bytes 294912 | tf_op jit(solution)/shard_map/all_gather | solution.py:112
  163.0 10.6 %convolution_bitcast_fusion.1 = f32[1024,32]{0,1:T(8,128)} fusion(f32[32,2048]{1,0:T(8,128)S(1)} %all_gather.18, f32[1024,2048]{1,0:T(8,128)} %param.19), kind=kOutput, calls=%fused_computation.4 | convolution fusion | flops 805306368 | bytes 8781824 | tf_op jit(solution)/shard_map/dot_general | solution.py:41
  173.6 0.0 all-reduce.2.cloned.1.call-update
  173.7 14.1 %reduce-scatter.2.cloned.1.call-done = f32[256,32]{0,1:T(8,128)} async-done(((f32[2048,32]{0,1:T(8,128)}), f32[256,32]{0,1:T(8,128)}) %reduce-scatter.2.cloned.1.call-update) | async-done | bytes 32784 | tf_op jit(solution)/shard_map/reduce_scatter | solution.py:114
  187.8 0.9 fusion.42
  188.7 39.5 %psum.15 = f32[32,32]{1,0:T(8,128)S(1)} all-reduce(f32[32,32]{1,0:T(8,128)S(1)} %fusion.42), channel_id=1, replica_groups=mesh['row'=8,'col'=4] {'row','col'}, use_global_device_ids=true, to_apply=%region_3.4 | all-reduce | flops 1024 | bytes 8192 | tf_op jit(solution)/shard_map/psum | solution.py:119
  228.2 0.1 abs_reduce_fusion
  228.3 0.6 reduce_max.9
  230.9 0.1 fusion.24
  231.0 0.1 fusion.3
  231.2 9.7 %all-gather.1 = f32[8,4,32]{2,1,0:T(4,128)S(1)} all-gather(f32[1,4,32]{2,1,0:T(4,128)S(1)} %fusion.3), channel_id=1, replica_groups=mesh['row'=8,'col'=4] {'row'}, dimensions={0}, use_global_device_ids=true | all-gather | bytes 4608 | tf_op jit(solution)/shard_map/all_gather | solution.py:125
  240.8 0.1 fusion.23
  241.0 0.1 fusion.2
  241.1 8.8 %all-gather.2 = f32[8,4,32]{2,1,0:T(4,128)S(1)} all-gather(f32[1,4,32]{2,1,0:T(4,128)S(1)} %fusion.2), channel_id=1, replica_groups=mesh['row'=8,'col'=4] {'row'}, dimensions={0}, use_global_device_ids=true | all-gather | bytes 4608 | tf_op jit(solution)/shard_map/all_gather | solution.py:125
  249.9 0.1 fusion.22
  250.1 0.1 fusion.1
  250.2 8.0 %all-gather.3 = f32[8,4,32]{2,1,0:T(4,128)S(1)} all-gather(f32[1,4,32]{2,1,0:T(4,128)S(1)} %fusion.1), channel_id=1, replica_groups=mesh['row'=8,'col'=4] {'row'}, dimensions={0}, use_global_device_ids=true | all-gather | bytes 4608 | tf_op jit(solution)/shard_map/all_gather | solution.py:125
  258.2 9.4 %all_gather.23 = f32[2048,32]{0,1:T(8,128)S(1)} all-gather(f32[256,32]{0,1:T(8,128)} %reduce-scatter.2.cloned.1.call-done), channel_id=1, replica_groups=mesh['row'=8,'col'=4] {'row'}, dimensions={0}, use_global_device_ids=true | all-gather | bytes 294912 | tf_op jit(solution)/shard_map/all_gather | solution.py:136
  267.6 1.2 fusion.43
  268.8 11.5 %subtract_multiply_fusion = f32[1024,2048]{1,0:T(8,128)} fusion(f32[1024,2048]{1,0:T(8,128)} %param.19, f32[1024,32]{0,1:T(8,128)S(1)} %fusion.43, f32[2048,32]{0,1:T(8,128)S(1)} %all_gather.23), kind=kOutput, calls=%fused_computation.1 | convolution fusion | flops 809500672 | bytes 17170432 | tf_op jit(solution)/shard_map/dot_general | solution.py:41
  280.3 0.1 fusion.19
  280.5 0.6 dynamic-slice_add_fusion
  (22 shorter events, 0.2 us)
Async XLA Ops:
  8.0 2.3 copy-start
  11.5 73.9 %copy-start.2 = (f32[1,32,256]{2,1,0:T(8,128)S(1)}, f32[1,32,256]{2,1,0:T(8,128)}, u32[]{:S(2)}) copy-start(f32[1,32,256]{2,1,0:T(8,128)} %param.12) | copy-start | bytes 98308
  85.4 6.1 %copy-start.1 = (f32[64,128]{1,0:T(8,128)S(1)}, f32[64,128]{1,0:T(8,128)}, u32[]{:S(2)}) copy-start(f32[64,128]{1,0:T(8,128)} %param.17) | copy-start | bytes 98308
  85.4 6.4 %copy-start.3 = (f32[1,256]{1,0:T(1,128)S(1)}, f32[1,256]{1,0:T(1,128)}, u32[]{:S(2)}) copy-start(f32[1,256]{1,0:T(1,128)} %param.14) | copy-start | bytes 3076
  85.4 6.4 %copy-start.4 = (f32[128]{0:T(128)S(1)}, f32[128]{0:T(128)}, u32[]{:S(2)}) copy-start(f32[128]{0:T(128)} %param.18) | copy-start | bytes 1540
  103.6 10.3 %all-to-all-start.4 = ((f32[8,1,1,4,1]{0,4,2,1,3:T(1,128)}), f32[8,1,1,4,1]{0,4,2,1,3:T(1,128)S(1)}, u32[]{:S(2)}, u32[]{:S(2)}) async-start(f32[8,1,1,4,1]{0,4,2,1,3:T(1,128)} %bitcast.28), calls=%async_computation.5 | async-start | bytes 4096 | tf_op jit(solution)/shard_map/all_to_all | solution.py:98
  121.1 8.1 %all-to-all-start.2 = ((f32[1,1,1,8,1024]{4,2,1,0,3:T(1,128)}), f32[1,1,1,8,1024]{4,2,1,0,3:T(1,128)S(1)}, u32[]{:S(2)}, u32[]{:S(2)}) async-start(f32[1,1,1,8,1024]{4,2,1,0,3:T(1,128)} %bitcast.13), calls=%async_computation.2 | async-start | bytes 65536 | tf_op jit(solution)/shard_map/all_to_all | solution.py:109
  129.2 25.6 %all-to-all-start.1 = ((f32[8,1,1,4,1,256]{5,0,4,2,1,3:T(8,128)}), f32[8,1,1,4,1,256]{5,0,4,2,1,3:T(8,128)S(1)}, u32[]{:S(2)}, u32[]{:S(2)}) async-start(f32[8,1,1,4,1,256]{5,0,4,2,1,3:T(8,128)} %copy.19), calls=%async_computation.1 | async-start | bytes 65536 | tf_op jit(solution)/shard_map/all_to_all | solution.py:91
  132.5 55.3 %reduce-scatter.2.cloned.1.call-start = ((), (), s32[]{:S(2)}) async-start(), calls=%async_computation.7 | async-start | bytes 294912 | tf_op jit(solution)/shard_map/reduce_scatter | solution.py:114
  154.7 112.8 %all-reduce.2.cloned.1.call-start = ((), (), s32[]{:S(2)}) async-start(), calls=%async_computation.6 | async-start | bytes 262144 | tf_op jit(solution)/shard_map/psum | solution.py:128
Sparse Core Ops, SparseCore 0:
  154.8 32.8 reduce-scatter.1
Sparse Core Ops, SparseCore 1:
  173.8 34.5 all-reduce.1
where the time goes:
time: 290 us; the launch traced here: 289 us
  blocking collectives  114 us (39%)
  local copies, waits for them, and re-layouts  76.3 us (26%)
  matrix products  36.4 us (13%)
  waiting for transfers between devices  21.6 us (7%)
  between operations  19 us (7%)
  starting transfers between devices  11.6 us (4%)
  other arithmetic  9.34 us (3%)
    gather x2, local copies, waits for them, and re-layouts, network(): nearby = jnp.take(mixed, neighbor_ids, axis=0)  73.9 us
    psum x1, blocking collectives, on_device(): lax.psum(jnp.dot(own_cols, cross_own, precision=highest), ('row', 'col'))  39.5 us
    all_gather x3, blocking collectives, on_device(): lax.all_gather(newton_rows(inverse, innovation, rows_n, row_at), 'row', a...  26.5 us
    dot_general x2, matrix products, contract_rows(): lax.dot_general(left, right, (((1,), (1,)), ((), ())), precision=highest)  22.1 us
    reduce_scatter x1, waiting for transfers between devices, on_device(): lax.psum_scatter(contract_first(window, row_jac), 'row', scatter_dimensio...  14.1 us
    all_gather x1, blocking collectives, on_device(): lax.all_gather(row_pieces, 'col', axis=1, tiled=True)  13.9 us
    all_to_all x1, blocking collectives, on_device(): lax.all_to_all(spread, 'row', split_axis=4, concat_axis=0, tiled=True)  9.63 us
    all_gather x1, blocking collectives, on_device(): lax.all_gather(cross_own, 'row', axis=0, tiled=True)  9.38 us
  transfers between devices with their start and end apart: 5, of which 3 were waited for; matrix products, arithmetic and copies ran while one was open for 8% of the time, Pallas kernels for 0%

commit v1 on v0

v1 whole, which is shorter than its diff:
```python
import functools
import math

import jax
import jax.numpy as jnp
from jax import lax
from jax.experimental import pallas as pl
from jax.experimental.pallas import tpu as pltpu
from jax.sharding import PartitionSpec as P

NEWTON = 4
LANES = 128
SUBLANES = 8


forget = 0.98
highest = lax.Precision.HIGHEST
f32 = jnp.float32
bf16 = jnp.bfloat16


def dot(left, right, contract, precision=None):
    return lax.dot_general(
        left, right, (contract, ((), ())), precision=precision, preferred_element_type=f32
    )


def split3(x):
    hi = x.astype(bf16)
    rest = x - hi.astype(f32)
    mid = rest.astype(bf16)
    lo = (rest - mid.astype(f32)).astype(bf16)
    return hi, mid, lo


def split2(x):
    hi = x.astype(bf16)
    return hi, (x - hi.astype(f32)).astype(bf16)


def network_kernel(
    types_ref,
    ids_ref,
    switch_ref,
    env_ref,
    force_ref,
    target_ref,
    embed_ref,
    weight_ref,
    out_weight_ref,
    payload_ref,
    mix_ref,
):
    neighbours, atoms = ids_ref.shape
    hin, _ = weight_ref.shape
    n_types = embed_ref.shape[0]
    height = min(64, atoms)
    for start in range(0, atoms, height):
        atom_at = lax.broadcasted_iota(jnp.int32, (height, atoms), 0) + start
        total = jnp.zeros((height, atoms), f32)
        for k in range(neighbours):
            total = total + jnp.where(ids_ref[k : k + 1, :] == atom_at, switch_ref[k : k + 1, :], 0.0)
        mix_ref[start : start + height, :] = total
    mix = mix_ref[...]
    type_at = lax.broadcasted_iota(jnp.int32, (n_types, atoms), 0)
    onehot = (types_ref[...] == type_at).astype(f32)
    mixed = env_ref[...] + dot(onehot, embed_ref[...], ((0,), (0,)), highest)
    descriptor = dot(mixed, mix, ((0,), (0,)), highest) * (1.0 / math.sqrt(neighbours))
    hidden = jnp.tanh(descriptor)
    activity = jnp.tanh(dot(hidden, weight_ref[...], ((0,), (0,)), highest))
    out_weight = out_weight_ref[...]
    scale = 1.0 / math.sqrt(atoms)
    force = force_ref[...]
    weighted = dot(force, activity, ((1,), (0,)), highest)
    predicted = jnp.sum(weighted * out_weight, axis=1, keepdims=True) * scale
    slopes = out_weight * (1.0 - activity * activity)
    jacobian = dot(hidden * force, slopes, ((1,), (0,)), highest) * scale
    payload_ref[0:hin, :] = jacobian
    error = target_ref[...] - predicted
    payload_ref[hin:, :] = jnp.broadcast_to(error, (SUBLANES, jacobian.shape[1]))


def network(atom_types, neighbor_ids, switching, environment, force_weights, targets, type_embed, layer_weight, out_weight):
    per_dev, neighbours, atoms = neighbor_ids.shape
    hin, width = layer_weight.shape

    def per_stream(*shape):
        return pl.BlockSpec((None,) + shape, lambda s: (s,) + (0,) * len(shape))

    def shared(shape):
        return pl.BlockSpec(shape, lambda s: (0,) * len(shape))

    return pl.pallas_call(
        network_kernel,
        grid=(per_dev,),
        in_specs=[
            per_stream(1, atoms),
            per_stream(neighbours, atoms),
            per_stream(neighbours, atoms),
            per_stream(atoms, hin),
            per_stream(1, atoms),
            per_stream(1, 1),
            shared(type_embed.shape),
            shared(layer_weight.shape),
            shared((1, width)),
        ],
        out_specs=per_stream(hin + SUBLANES, width),
        out_shape=jax.ShapeDtypeStruct((per_dev, hin + SUBLANES, width), f32),
        scratch_shapes=[pltpu.VMEM((atoms, atoms), f32)],
        name="network",
    )(
        atom_types.reshape(per_dev, 1, atoms),
        neighbor_ids,
        switching,
        environment,
        force_weights.reshape(per_dev, 1, atoms),
        targets.reshape(per_dev, 1, 1),
        type_embed,
        layer_weight,
        out_weight.reshape(1, width),
    )


def cross_kernel(at_ref, jac_ref, cov_ref, cross_ref, parts_ref):
    streams, rows, lanes = jac_ref.shape

    @pl.when(pl.program_id(0) == 0)
    def _():
        flat = jac_ref.reshape(streams * rows, lanes)
        for i in range(rows):
            parts = split3(flat[pl.ds(i, streams, stride=rows), :])
            for n, part in enumerate(parts):
                parts_ref[n * streams : (n + 1) * streams, i * lanes : (i + 1) * lanes] = part

    hi, lo = split2(cov_ref[...])
    by_hi = dot(parts_ref[...], hi, ((1,), (1,)))
    by_lo = dot(parts_ref[0 : 2 * streams, :], lo, ((1,), (1,)))
    cross_ref[...] = by_hi[0:streams] + (
        by_hi[streams : 2 * streams]
        + by_lo[0:streams]
        + (by_hi[2 * streams :] + by_lo[streams:])
    )


def cross_partial(at, jac_all, covariance, slab):
    streams = jac_all.shape[0]
    tile_rows, tile_cols = covariance.shape
    jac_rows = tile_cols // LANES
    slabs = tile_rows // slab
    return pl.pallas_call(
        cross_kernel,
        grid_spec=pltpu.PrefetchScalarGridSpec(
            num_scalar_prefetch=1,
            grid=(slabs,),
            in_specs=[
                pl.BlockSpec((streams, jac_rows, LANES), lambda n, at: (0, at[1], 0)),
                pl.BlockSpec((slab, tile_cols), lambda n, at: (n, 0)),
            ],
            out_specs=pl.BlockSpec((None, streams, slab), lambda n, at: (n, 0, 0)),
            scratch_shapes=[pltpu.VMEM((3 * streams, tile_cols), bf16)],
        ),
        out_shape=jax.ShapeDtypeStruct((slabs, streams, slab), f32),
        compiler_params=pltpu.CompilerParams(vmem_limit_bytes=40 << 20),
        name="cross",
    )(at, jac_all, covariance)


def slab_kernel(at_ref, pieces_ref, jac_ref, out_ref, *, cols_n):
    pieces, streams, slab = pieces_ref.shape
    _, group, lanes = jac_ref.shape
    cross = pieces_ref[0]
    for n in range(1, pieces):
        cross = cross + pieces_ref[n]
    out_ref[:, 0:slab] = cross
    rows = slab // lanes
    first = ((at_ref[0] * cols_n + at_ref[1]) * rows) % group
    flat = jac_ref.reshape(streams * group, lanes)
    term = jnp.zeros((streams, streams), f32)
    for i in range(rows):
        own = flat[pl.ds(first + i, streams, stride=group), :]
        term = term + dot(own, cross[:, i * lanes : (i + 1) * lanes], ((1,), (1,)), highest)
    out_ref[:, slab:] = jnp.concatenate(
        [term, jnp.zeros((streams, out_ref.shape[1] - slab - streams), f32)], axis=1
    )


def slab_sum(at, pieces, jac_all, cols_n):
    count, streams, slab = pieces.shape
    rows = slab // LANES
    group = SUBLANES
    padded = slab + pl.cdiv(streams, LANES) * LANES
    return pl.pallas_call(
        functools.partial(slab_kernel, cols_n=cols_n),
        grid_spec=pltpu.PrefetchScalarGridSpec(
            num_scalar_prefetch=1,
            grid=(1,),
            in_specs=[
                pl.BlockSpec(pieces.shape, lambda n, at: (0, 0, 0)),
                pl.BlockSpec(
                    (streams, group, LANES),
                    lambda n, at: (0, (at[0] * cols_n + at[1]) * rows // group, 0),
                ),
            ],
            out_specs=pl.BlockSpec((streams, padded), lambda n, at: (0, 0)),
        ),
        out_shape=jax.ShapeDtypeStruct((streams, padded), f32),
        name="slab",
    )(at, pieces, jac_all)


def invert(innovation):
    streams = innovation.shape[0]
    row = lax.broadcasted_iota(jnp.int32, (streams, streams), 0)
    col = lax.broadcasted_iota(jnp.int32, (streams, streams), 1)
    identity = (row == col).astype(f32)
    innovation = innovation + forget * identity
    sums = jnp.sum(jnp.abs(innovation), axis=1, keepdims=True)
    bound = jnp.max(sums, axis=0, keepdims=True)
    inverse = identity * (2.0 / bound) - innovation / (bound * bound)
    for repeat in range(NEWTON - 1):
        step = dot(inverse, innovation, ((1,), (0,)), highest)
        inverse = 2.0 * inverse - dot(step, inverse, ((1,), (0,)), highest)
    return inverse


def update_kernel(
    at_ref, terms_ref, rows_ref, cols_ref, error_ref, weight_ref, cov_ref, new_weight_ref, new_cov_ref, gain_ref, right_ref
):
    devices, streams, _ = terms_ref.shape
    slabs, _, _ = rows_ref.shape
    slab = cov_ref.shape[0]
    step = pl.program_id(0)

    @pl.when(step == 0)
    def _():
        innovation = terms_ref[0, :, 0:streams]
        for n in range(1, devices):
            innovation = innovation + terms_ref[n, :, 0:streams]
        inverse = invert(innovation)
        for n in range(slabs):
            gain_ref[n] = dot(inverse, rows_ref[n, :, 0:slab], ((0,), (0,)), highest)
        for n in range(cols_ref.shape[0]):
            hi, mid, lo = split3(cols_ref[n, :, 0:slab])
            for m, part in enumerate((hi, mid, lo, hi, mid, hi)):
                right_ref[m * streams : (m + 1) * streams, n * slab : (n + 1) * slab] = part

    gain = gain_ref[step]
    hi, mid, lo = split3(gain)
    left = jnp.concatenate([hi, hi, hi, mid, mid, lo], axis=0)
    update = dot(left, right_ref[...], ((0,), (0,)))
    new_cov_ref[...] = (cov_ref[...] - update) * (1.0 / forget)

    @pl.when(step == at_ref[1])
    def _():
        group = error_ref.shape[1]
        lanes = error_ref.shape[2]
        errors = error_ref.reshape(streams * group, lanes)[pl.ds(0, streams, stride=group), :]
        for i in range(slab // lanes):
            moved = jnp.sum(gain[:, i * lanes : (i + 1) * lanes] * errors, axis=0, keepdims=True)
            own = weight_ref[pl.ds((at_ref[0] * slabs + at_ref[1]) * (slab // lanes) + i, 1), :]
            new_weight_ref[i : i + 1, :] = own + moved


def update(at, gathered, jac_all, layer_weight, covariance, slab):
    devices, streams, padded = gathered.shape
    tile_rows, tile_cols = covariance.shape
    hin, width = layer_weight.shape
    slabs = tile_rows // slab
    return pl.pallas_call(
        update_kernel,
        grid_spec=pltpu.PrefetchScalarGridSpec(
            num_scalar_prefetch=1,
            grid=(slabs,),
            in_specs=[
                pl.BlockSpec((devices, streams, LANES), lambda n, at: (0, 0, slab // LANES)),
                pl.BlockSpec((slabs, streams, padded), lambda n, at: (at[0], 0, 0)),
                pl.BlockSpec((tile_cols // slab, streams, padded), lambda n, at: (at[1], 0, 0)),
                pl.BlockSpec((streams, SUBLANES, width), lambda n, at: (0, hin // SUBLANES, 0)),
                pl.BlockSpec((hin, width), lambda n, at: (0, 0)),
                pl.BlockSpec((slab, tile_cols), lambda n, at: (n, 0)),
            ],
            out_specs=[
                pl.BlockSpec((slab // width, width), lambda n, at: (0, 0)),
                pl.BlockSpec((slab, tile_cols), lambda n, at: (n, 0)),
            ],
            scratch_shapes=[
                pltpu.VMEM((slabs, streams, slab), f32),
                pltpu.VMEM((6 * streams, tile_cols), bf16),
            ],
        ),
        out_shape=[
            jax.ShapeDtypeStruct((slab // width, width), f32),
            jax.ShapeDtypeStruct((tile_rows, tile_cols), f32),
        ],
        compiler_params=pltpu.CompilerParams(vmem_limit_bytes=48 << 20),
        name="update",
    )(at, gathered, gathered, gathered, jac_all, layer_weight, covariance)


def plain_steps(at, jac_all, layer_weight, covariance, slab, cols_n):
    streams = jac_all.shape[0]
    hin, width = layer_weight.shape
    tile_rows, tile_cols = covariance.shape
    first = (at[0] * cols_n + at[1]) * slab
    jacobian = jac_all[:, 0:hin, :].reshape(streams, hin * width)
    errors = jac_all[:, hin, 0]
    jac_cols = lax.dynamic_slice_in_dim(jacobian, at[1] * tile_cols, tile_cols, 1)
    partial = dot(jac_cols, covariance, ((1,), (1,)), highest)
    cross_own = lax.psum_scatter(partial, "col", scatter_dimension=1, tiled=True)
    cross = lax.all_gather(cross_own, ("row", "col"), axis=1, tiled=True)
    inverse = invert(dot(jacobian, cross, ((1,), (1,)), highest))
    gain = dot(inverse, lax.dynamic_slice_in_dim(cross, at[0] * tile_rows, tile_rows, 1), ((0,), (0,)), highest)
    across = lax.dynamic_slice_in_dim(cross, at[1] * tile_cols, tile_cols, 1)
    new_cov = (covariance - dot(gain, across, ((0,), (0,)), highest)) / forget
    own_gain = lax.dynamic_slice_in_dim(gain, at[1] * slab, slab, 1)
    own_weight = lax.dynamic_slice_in_dim(layer_weight.reshape(-1), first, slab, 0)
    new_weight = own_weight + dot(errors, own_gain, ((0,), (0,)), highest)
    return new_weight, new_cov


def on_device(
    atom_types,
    neighbor_ids,
    switching,
    environment,
    force_weights,
    targets,
    type_embed,
    layer_weight,
    out_weight,
    covariance,
):
    rows_n = lax.axis_size("row")
    cols_n = lax.axis_size("col")
    at = jnp.stack([lax.axis_index("row"), lax.axis_index("col")]).astype(jnp.int32)
    tile_rows, tile_cols = covariance.shape
    slab = tile_rows // cols_n
    payload = network(
        atom_types,
        neighbor_ids,
        switching,
        environment,
        force_weights,
        targets,
        type_embed,
        layer_weight,
        out_weight,
    )
    jac_all = lax.all_gather(payload, ("row", "col"), axis=0, tiled=True)
    slab_rows = slab // LANES
    if slab % LANES or SUBLANES % slab_rows or layer_weight.shape[1] != LANES or tile_cols % (SUBLANES * LANES):
        return plain_steps(at, jac_all, layer_weight, covariance, slab, cols_n)
    partial = cross_partial(at, jac_all, covariance, slab)
    pieces = lax.all_to_all(partial, "col", split_axis=0, concat_axis=0, tiled=True)
    own = slab_sum(at, pieces, jac_all, cols_n)
    gathered = lax.all_gather(own, ("row", "col"), axis=0, tiled=False)
    new_weight, new_cov = update(at, gathered, jac_all, layer_weight, covariance, slab)
    return new_weight.reshape(-1), new_cov


def solution(mesh):
    in_specs = (
        P(("row", "col"), None),
        P(("row", "col"), None, None),
        P(("row", "col"), None, None),
        P(("row", "col"), None, None),
        P(("row", "col"), None),
        P(("row", "col")),
        P(),
        P(),
        P(),
        P("row", "col"),
    )
    out_specs = (P(("row", "col")), P("row", "col"))
    return jax.shard_map(
        on_device, mesh=mesh, in_specs=in_specs, out_specs=out_specs, check_vma=False
    )
```

time: 290 us -> 163 us (0.56)
  blocking collectives: 114 us -> 9.81 us
  waiting for transfers between devices: 21.6 us -> 110 us
  local copies, waits for them, and re-layouts: 76.3 us -> 8.32 us
  matrix products: 36.4 us -> 0 us
  Pallas kernels: 0 us -> 19.7 us
  starting transfers between devices: 11.6 us -> 0.08 us
  other arithmetic: 9.34 us -> 0.08 us
  between operations: 19 us -> 14.7 us
    all_gather x0 -> x2, waiting for transfers between devices: none -> 110 us  [the longest x1 56.8 us: on_device(): jac_all = lax.all_gather(payload, ('row', 'col'), axis=0, tiled=True)]
    gather x2 -> x0, local copies, waits for them, and re-layouts: 73.9 us -> none  [network(): nearby = jnp.take(mixed, neighbor_ids, axis=0)]
    all_gather x6 -> x0, blocking collectives: 58 us -> none  [the longest x3 26.5 us: on_device(): lax.all_gather(newton_rows(inverse, innovation, rows_n, row_at), 'row', a...]
    psum x1 -> x0, blocking collectives: 39.5 us -> none  [on_device(): lax.psum(jnp.dot(own_cols, cross_own, precision=highest), ('row', 'col'))]
    dot_general x16 -> x0, matrix products: 36.4 us -> none  [the longest x2 22.1 us: contract_rows(): lax.dot_general(left, right, (((1,), (1,)), ((), ())), precision=highest)]
    pallas_call x0 -> x4, Pallas kernels: none -> 19.7 us  [the longest x1 9.65 us: update(): pl.pallas_call(update_kernel, grid_spec=pltpu.PrefetchScalarGridSpec(num_...]
    reduce_scatter x1 -> x0, waiting for transfers between devices: 14.1 us -> none  [on_device(): lax.psum_scatter(contract_first(window, row_jac), 'row', scatter_dimensio...]
    all_to_all x3 -> x0, starting transfers between devices: 11.5 us -> none  [the longest x1 4.87 us: on_device(): lax.all_to_all(lax.all_to_all(spread, 'row', split_axis=4, concat_axis=0,...]
  transfers between devices with their start and end apart: 5 -> 2, of which waited for: 3 -> 2; matrix products, arithmetic and copies ran while one was open for 8% -> 0% of each run, Pallas kernels for 0% -> 0%
where the time goes in v1:
time: 163 us
  waiting for transfers between devices  110 us (67%)
  Pallas kernels  19.7 us (12%)
  between operations  14.7 us (9%)
  blocking collectives  9.81 us (6%)
  local copies, waits for them, and re-layouts  8.32 us (5%)
    all_gather x1, waiting for transfers between devices, on_device(): jac_all = lax.all_gather(payload, ('row', 'col'), axis=0, tiled=True)  56.8 us
    all_gather x1, waiting for transfers between devices, on_device(): gathered = lax.all_gather(own, ('row', 'col'), axis=0, tiled=False)  53.5 us
    all_to_all x1, blocking collectives, on_device(): lax.all_to_all(partial, 'col', split_axis=0, concat_axis=0, tiled=True)  9.81 us
    pallas_call x1, Pallas kernels, update(): pl.pallas_call(update_kernel, grid_spec=pltpu.PrefetchScalarGridSpec(num_...  9.65 us
    unnamed x15, local copies, waits for them, and re-layouts  8.32 us
    pallas_call x1, Pallas kernels, network(): pl.pallas_call(network_kernel, grid=(per_dev,), in_specs=[per_stream(1, a...  3.83 us
    pallas_call x1, Pallas kernels, cross_partial(): pl.pallas_call(cross_kernel, grid_spec=pltpu.PrefetchScalarGridSpec(num_s...  3.77 us
  transfers between devices with their start and end apart: 2, of which 2 were waited for; matrix products, arithmetic and copies ran while one was open for 0% of the time, Pallas kernels for 0%

profile of v1, /device:TPU:0, one launch (start us, length us, event | category | flops | bytes accessed | tf_op | source)
XLA Modules:
  0.0 163.0 jit_solution(14982733868470910690)
XLA Ops:
  7.2 0.0 copy-start.4
  7.2 0.0 all-gather.4.cloned.1.call-start
  7.9 1.6 copy.13.env_ref
  9.5 3.8 %network.1 = f32[1,72,128]{2,1,0:T(8,128)} custom-call(s32[1,1,256]{2,1,0:T(1,128)} %bitcast.12, s32[1,32,256]{2,1,0:T(8,128)} %ids_ref.1, f32[1,32,256]{2,1,0:T(8,128)} %switch_ref.1, f32[1,256,64]{2,1,0:T(8,128)} %copy.13.env_ref, f32[1,1,256]{2,1,0:T(1,128)} %bitcast.13, f32[1,1,1]{2,1,0:T(1,128)} %bitcast.8.target_ref, f32[4,64]{1,0:T(4,128)} %embed_ref.1, ...), custom_call_target="tpu_custom_call" | custom-call | tf_op jit(solution)/shard_map/network/pallas_call | solution.py:93
  13.3 0.0 all-gather.4.cloned.1.call-update
  13.3 0.0 all-gather.6.cloned.1.call-start
  13.4 0.1 pad_add_fusion.at_ref
  13.4 0.0 copy-start.5
  13.5 56.8 %all-gather.4.cloned.1.call-done.jac_ref.error_ref = f32[32,72,128]{2,1,0:T(8,128)} async-done(((f32[1,72,128]{2,1,0:T(8,128)}), f32[32,72,128]{2,1,0:T(8,128)}) %all-gather.4.cloned.1.call-update) | async-done | bytes 1179664 | tf_op jit(solution)/shard_map/all_gather | solution.py:349
  70.3 0.0 copy-start
  70.3 3.4 %copy-done = f32[1024,2048]{1,0:T(8,128)S(1)} copy-done((f32[1024,2048]{1,0:T(8,128)S(1)}, f32[1024,2048]{1,0:T(8,128)}, u32[]{:S(2)}) %copy-start) | copy-done | bytes 8388632
  73.6 0.0 copy-start.2
  73.6 1.3 copy-done.2
  74.9 0.0 copy-start.3
  74.9 3.8 %cross.1 = f32[4,32,256]{2,1,0:T(8,128)S(1)} custom-call(s32[2]{0:T(128)S(1)} %pad_add_fusion.at_ref, f32[32,72,128]{2,1,0:T(8,128)S(1)} %copy-done.2, f32[1024,2048]{1,0:T(8,128)S(1)} %copy-done), custom_call_target="tpu_custom_call" | custom-call | tf_op jit(solution)/shard_map/cross/pallas_call | solution.py:150
  78.7 9.8 %all_to_all.5.pieces_ref = f32[4,32,256]{2,1,0:T(8,128)} all-to-all(f32[4,32,256]{2,1,0:T(8,128)S(1)} %cross.1), channel_id=1, replica_groups=mesh['row'=8,'col'=4] {'col'}, dimensions={0} | all-to-all | bytes 262144 | tf_op jit(solution)/shard_map/all_to_all | solution.py:354
  88.5 0.0 copy-done.5
  88.5 2.4 %slab.1 = f32[32,384]{1,0:T(8,128)} custom-call(s32[2]{0:T(128)} %copy-done.5, f32[4,32,256]{2,1,0:T(8,128)} %all_to_all.5.pieces_ref, f32[32,72,128]{2,1,0:T(8,128)} %all-gather.4.cloned.1.call-done.jac_ref.error_ref), custom_call_target="tpu_custom_call" | custom-call | tf_op jit(solution)/shard_map/slab/pallas_call | solution.py:192
  90.9 0.0 all-gather.6.cloned.1.call-update
  91.0 53.5 %all-gather.6.cloned.1.call-done = f32[1024,384]{1,0:T(8,128)} async-done(((f32[32,384]{1,0:T(8,128)}), f32[1024,384]{1,0:T(8,128)}) %all-gather.6.cloned.1.call-update) | async-done | bytes 1572880 | tf_op jit(solution)/shard_map/all_gather | solution.py:356
  144.5 0.0 copy-done.4
  144.5 0.0 copy-done.3
  144.5 0.0 copy-start.1
  144.5 1.4 copy-done.1
  145.9 0.0 copy-start.6
  145.9 0.7 copy-done.6
  146.5 9.7 %update.1 = (f32[2,128]{1,0:T(2,128)}, f32[1024,2048]{1,0:T(8,128)}) custom-call(s32[2]{0:T(128)S(1)} %copy-done.6, f32[32,32,384]{2,1,0:T(8,128)S(1)} %bitcast.9, f32[32,32,384]{2,1,0:T(8,128)S(1)} %bitcast.10, f32[32,32,384]{2,1,0:T(8,128)S(1)} %bitcast.11, f32[32,72,128]{2,1,0:T(8,128)S(1)} %copy-done.3, f32[64,128]{1,0:T(8,128)S(1)} %copy-done.4, ...), custom_call_target="tpu_custom_call" | custom-call | tf_op jit(solution)/shard_map/update/pallas_call | solution.py:269
Async XLA Ops:
  7.2 137.3 %copy-start.4 = (f32[64,128]{1,0:T(8,128)S(1)}, f32[64,128]{1,0:T(8,128)}, u32[]{:S(2)}) copy-start(f32[64,128]{1,0:T(8,128)} %weight_ref.3) | copy-start | bytes 98308
  7.2 63.1 %all-gather.4.cloned.1.call-start = ((), (), s32[]{:S(2)}) async-start(), calls=%async_computation.1 | async-start | bytes 1216512 | tf_op jit(solution)/shard_map/all_gather | solution.py:349
  13.3 131.1 %all-gather.6.cloned.1.call-start = ((), (), s32[]{:S(2)}) async-start(), calls=%async_computation.2 | async-start | bytes 1622016 | tf_op jit(solution)/shard_map/all_gather | solution.py:356
  13.4 75.1 %copy-start.5 = (s32[2]{0:T(128)}, s32[2]{0:T(128)S(1)}, u32[]{:S(2)}) copy-start(s32[2]{0:T(128)S(1)} %pad_add_fusion.at_ref) | copy-start | bytes 28
  70.3 3.4 %copy-start = (f32[1024,2048]{1,0:T(8,128)S(1)}, f32[1024,2048]{1,0:T(8,128)}, u32[]{:S(2)}) copy-start(f32[1024,2048]{1,0:T(8,128)} %cov_ref.3) | copy-start | bytes 25165828
  73.6 1.3 copy-start.2
  74.9 69.5 %copy-start.3 = (f32[32,72,128]{2,1,0:T(8,128)S(1)}, f32[32,72,128]{2,1,0:T(8,128)}, u32[]{:S(2)}) copy-start(f32[32,72,128]{2,1,0:T(8,128)} %all-gather.4.cloned.1.call-done.jac_ref.error_ref) | copy-start | bytes 3538948
  144.5 1.4 copy-start.1
  145.9 0.7 copy-start.6
Sparse Core Ops, SparseCore 0:
  13.4 56.7 all-gather.3
  91.1 53.3 all-gather.5

commit v2 on v1

v2 whole, which is shorter than its diff:
```python
import functools
import math

import jax
import jax.numpy as jnp
from jax import lax
from jax.experimental import pallas as pl
from jax.experimental.pallas import tpu as pltpu
from jax.sharding import PartitionSpec as P

NEWTON = 4
LANES = 128
SUBLANES = 8


forget = 0.98
highest = lax.Precision.HIGHEST
f32 = jnp.float32
bf16 = jnp.bfloat16


def dot(left, right, contract, precision=None):
    return lax.dot_general(
        left, right, (contract, ((), ())), precision=precision, preferred_element_type=f32
    )


def split3(x):
    hi = x.astype(bf16)
    rest = x - hi.astype(f32)
    mid = rest.astype(bf16)
    lo = (rest - mid.astype(f32)).astype(bf16)
    return hi, mid, lo


def split2(x):
    hi = x.astype(bf16)
    return hi, (x - hi.astype(f32)).astype(bf16)


def network_kernel(
    types_ref,
    ids_ref,
    switch_ref,
    env_ref,
    force_ref,
    target_ref,
    embed_ref,
    weight_ref,
    out_weight_ref,
    payload_ref,
    mix_ref,
    *,
    plan,
):
    neighbours, atoms = ids_ref.shape
    n_types = embed_ref.shape[0]
    height = min(64, atoms)
    for start in range(0, atoms, height):
        atom_at = lax.broadcasted_iota(jnp.int32, (height, atoms), 0) + start
        total = jnp.zeros((height, atoms), f32)
        for k in range(neighbours):
            total = total + jnp.where(ids_ref[k : k + 1, :] == atom_at, switch_ref[k : k + 1, :], 0.0)
        mix_ref[start : start + height, :] = total
    mix = mix_ref[...]
    type_at = lax.broadcasted_iota(jnp.int32, (n_types, atoms), 0)
    onehot = (types_ref[...] == type_at).astype(f32)
    mixed = env_ref[...] + dot(embed_ref[...], onehot, ((0,), (0,)), highest)
    descriptor = dot(mixed, mix, ((1,), (0,)), highest) * (1.0 / math.sqrt(neighbours))
    hidden = jnp.tanh(descriptor)
    activity = jnp.tanh(dot(hidden, weight_ref[...], ((0,), (0,)), highest))
    out_weight = out_weight_ref[...]
    scale = 1.0 / math.sqrt(atoms)
    force = force_ref[...]
    weighted = dot(force, activity, ((1,), (0,)), highest)
    predicted = jnp.sum(weighted * out_weight, axis=1, keepdims=True) * scale
    slopes = out_weight * (1.0 - activity * activity)
    jacobian = dot(hidden * force, slopes, ((1,), (0,)), highest) * scale
    error = jnp.broadcast_to(target_ref[...] - predicted, (1, jacobian.shape[1]))
    for block, pieces in enumerate(plan):
        at = 0
        for start, size in pieces:
            payload_ref[block, at : at + size, :] = jacobian[start : start + size, :]
            at += size
        rest = payload_ref.shape[1] - at
        payload_ref[block, at:, :] = jnp.broadcast_to(error, (rest, jacobian.shape[1]))


def network(
    plan, atom_types, neighbor_ids, switching, environment, force_weights, targets, type_embed, layer_weight, out_weight
):
    per_dev, neighbours, atoms = neighbor_ids.shape
    hin, width = layer_weight.shape
    rows = pl.cdiv(sum(size for _, size in plan[0]) + 1, SUBLANES) * SUBLANES

    def per_stream(*shape):
        return pl.BlockSpec((None,) + shape, lambda s: (s,) + (0,) * len(shape))

    def shared(shape):
        return pl.BlockSpec(shape, lambda s: (0,) * len(shape))

    return pl.pallas_call(
        functools.partial(network_kernel, plan=plan),
        grid=(per_dev,),
        in_specs=[
            per_stream(1, atoms),
            per_stream(neighbours, atoms),
            per_stream(neighbours, atoms),
            per_stream(hin, atoms),
            per_stream(1, atoms),
            per_stream(1, 1),
            shared(type_embed.shape),
            shared(layer_weight.shape),
            shared((1, width)),
        ],
        out_specs=pl.BlockSpec((len(plan), None, rows, width), lambda s: (0, s, 0, 0)),
        out_shape=jax.ShapeDtypeStruct((len(plan), per_dev, rows, width), f32),
        scratch_shapes=[pltpu.VMEM((atoms, atoms), f32)],
        name="network",
    )(
        atom_types.reshape(per_dev, 1, atoms),
        neighbor_ids,
        switching,
        environment.swapaxes(1, 2),
        force_weights.reshape(per_dev, 1, atoms),
        targets.reshape(per_dev, 1, 1),
        type_embed,
        layer_weight,
        out_weight.reshape(1, width),
    )


def cross_kernel(at_ref, jac_ref, cov_ref, *refs, col_rows):
    outs, (parts_ref, term_ref) = refs[:-2], refs[-2:]
    streams, rows, lanes = jac_ref.shape
    slab = cov_ref.shape[0]
    step = pl.program_id(0)
    slabs = len(outs)
    flat = jac_ref.reshape(streams * rows, lanes)

    @pl.when(step == 0)
    def _():
        term_ref[...] = jnp.zeros_like(term_ref)
        for i in range(col_rows):
            parts = split3(flat[pl.ds(i, streams, stride=rows), :])
            for n, part in enumerate(parts):
                parts_ref[n * streams : (n + 1) * streams, i * lanes : (i + 1) * lanes] = part

    hi, lo = split2(cov_ref[...])
    by_hi = dot(parts_ref[...], hi, ((1,), (1,)))
    by_lo = dot(parts_ref[0 : 2 * streams, :], lo, ((1,), (1,)))
    cross = by_hi[0:streams] + (
        by_hi[streams : 2 * streams]
        + by_lo[0:streams]
        + (by_hi[2 * streams :] + by_lo[streams:])
    )
    first = col_rows + (at_ref[1] + step) % slabs * (slab // lanes)
    term = jnp.zeros((streams, streams), f32)
    for i in range(slab // lanes):
        own = flat[pl.ds(first + i, streams, stride=rows), :]
        term = term + dot(own, cross[:, i * lanes : (i + 1) * lanes], ((1,), (1,)), highest)
    term_ref[:, 0:streams] += term
    for n in range(slabs):

        @pl.when(step == n)
        def _():
            outs[n][:, 0:slab] = cross

    @pl.when(step == slabs - 1)
    def _():
        for n in range(slabs):
            outs[n][:, slab:] = term_ref[...]


def cross_partial(at, jac, covariance, slab):
    streams, rows, _ = jac.shape
    tile_rows, tile_cols = covariance.shape
    slabs = tile_rows // slab
    term_lanes = pl.cdiv(streams, LANES) * LANES
    out = jax.ShapeDtypeStruct((streams, slab + term_lanes), f32)
    return pl.pallas_call(
        functools.partial(cross_kernel, col_rows=tile_cols // LANES),
        grid_spec=pltpu.PrefetchScalarGridSpec(
            num_scalar_prefetch=1,
            grid=(slabs,),
            in_specs=[
                pl.BlockSpec(jac.shape, lambda n, at: (0, 0, 0)),
                pl.BlockSpec((slab, tile_cols), lambda n, at: ((at[1] + n) % slabs, 0)),
            ],
            out_specs=[pl.BlockSpec(out.shape, lambda n, at: (0, 0))] * slabs,
            scratch_shapes=[
                pltpu.VMEM((3 * streams, tile_cols), bf16),
                pltpu.VMEM((streams, term_lanes), f32),
            ],
        ),
        out_shape=[out] * slabs,
        compiler_params=pltpu.CompilerParams(vmem_limit_bytes=40 << 20),
        name="cross",
    )(at, jac, covariance)


def slab_kernel(*refs, count):
    row_ref, col_ref = refs[2 * count :]
    slab = row_ref.shape[1]
    row = refs[0][...]
    col = refs[count][:, 0:slab]
    for n in range(1, count):
        row = row + refs[n][...]
        col = col + refs[count + n][:, 0:slab]
    row_ref[...] = row[:, 0:slab]
    col_ref[:, 0:slab] = col
    col_ref[:, slab:] = row[:, slab:]


def slab_sums(for_row, for_col, slab):
    streams, padded = for_row[0].shape
    return pl.pallas_call(
        functools.partial(slab_kernel, count=len(for_row)),
        out_shape=[
            jax.ShapeDtypeStruct((streams, slab), f32),
            jax.ShapeDtypeStruct((streams, padded), f32),
        ],
        name="slab",
    )(*for_row, *for_col)


def invert(innovation):
    streams = innovation.shape[0]
    row = lax.broadcasted_iota(jnp.int32, (streams, streams), 0)
    col = lax.broadcasted_iota(jnp.int32, (streams, streams), 1)
    identity = (row == col).astype(f32)
    innovation = innovation + forget * identity
    sums = jnp.sum(jnp.abs(innovation), axis=1, keepdims=True)
    bound = jnp.max(sums, axis=0, keepdims=True)
    inverse = identity * (2.0 / bound) - innovation / (bound * bound)
    for repeat in range(NEWTON - 1):
        step = dot(inverse, innovation, ((1,), (0,)), highest)
        inverse = 2.0 * inverse - dot(step, inverse, ((1,), (0,)), highest)
    return inverse


def update_kernel(
    at_ref, rows_ref, cols_ref, error_ref, weight_ref, cov_ref, new_weight_ref, new_cov_ref, gain_ref, right_ref
):
    slabs, streams, slab = rows_ref.shape
    col_slabs = cols_ref.shape[0]
    step = pl.program_id(0)

    @pl.when(step == 0)
    def _():
        innovation = cols_ref[0, :, slab : slab + streams]
        for n in range(1, col_slabs):
            innovation = innovation + cols_ref[n, :, slab : slab + streams]
        inverse = invert(innovation)
        for n in range(slabs):
            gain_ref[n] = dot(inverse, rows_ref[n], ((0,), (0,)), highest)
        for n in range(col_slabs):
            hi, mid, lo = split3(cols_ref[n, :, 0:slab])
            for m, part in enumerate((hi, mid, lo, hi, mid, hi)):
                right_ref[m * streams : (m + 1) * streams, n * slab : (n + 1) * slab] = part

    gain = gain_ref[step]
    hi, mid, lo = split3(gain)
    left = jnp.concatenate([hi, hi, hi, mid, mid, lo], axis=0)
    update = dot(left, right_ref[...], ((0,), (0,)))
    new_cov_ref[...] = (cov_ref[...] - update) * (1.0 / forget)

    @pl.when(step == at_ref[1])
    def _():
        group = error_ref.shape[1]
        lanes = error_ref.shape[2]
        errors = error_ref.reshape(streams * group, lanes)[pl.ds(0, streams, stride=group), :]
        for i in range(slab // lanes):
            moved = jnp.sum(gain[:, i * lanes : (i + 1) * lanes] * errors, axis=0, keepdims=True)
            own = weight_ref[pl.ds((at_ref[0] * slabs + at_ref[1]) * (slab // lanes) + i, 1), :]
            new_weight_ref[i : i + 1, :] = own + moved


def update(at, row_slabs, col_slabs, jac, layer_weight, covariance):
    slabs, streams, slab = row_slabs.shape
    tile_rows, tile_cols = covariance.shape
    hin, width = layer_weight.shape
    return pl.pallas_call(
        update_kernel,
        grid_spec=pltpu.PrefetchScalarGridSpec(
            num_scalar_prefetch=1,
            grid=(slabs,),
            in_specs=[
                pl.BlockSpec(row_slabs.shape, lambda n, at: (0, 0, 0)),
                pl.BlockSpec(col_slabs.shape, lambda n, at: (0, 0, 0)),
                pl.BlockSpec(
                    (streams, SUBLANES, width), lambda n, at: (0, (tile_rows + tile_cols) // LANES // SUBLANES, 0)
                ),
                pl.BlockSpec((hin, width), lambda n, at: (0, 0)),
                pl.BlockSpec((slab, tile_cols), lambda n, at: (n, 0)),
            ],
            out_specs=[
                pl.BlockSpec((slab // width, width), lambda n, at: (0, 0)),
                pl.BlockSpec((slab, tile_cols), lambda n, at: (n, 0)),
            ],
            scratch_shapes=[
                pltpu.VMEM((slabs, streams, slab), f32),
                pltpu.VMEM((6 * streams, tile_cols), bf16),
            ],
        ),
        out_shape=[
            jax.ShapeDtypeStruct((slab // width, width), f32),
            jax.ShapeDtypeStruct((tile_rows, tile_cols), f32),
        ],
        compiler_params=pltpu.CompilerParams(vmem_limit_bytes=48 << 20),
        name="update",
    )(at, row_slabs, col_slabs, jac, layer_weight, covariance)


def plain_steps(at, jac_all, layer_weight, covariance, slab, cols_n):
    streams = jac_all.shape[0]
    hin, width = layer_weight.shape
    tile_rows, tile_cols = covariance.shape
    first = (at[0] * cols_n + at[1]) * slab
    jacobian = jac_all[:, 0:hin, :].reshape(streams, hin * width)
    errors = jac_all[:, hin, 0]
    jac_cols = lax.dynamic_slice_in_dim(jacobian, at[1] * tile_cols, tile_cols, 1)
    partial = dot(jac_cols, covariance, ((1,), (1,)), highest)
    cross_own = lax.psum_scatter(partial, "col", scatter_dimension=1, tiled=True)
    cross = lax.all_gather(cross_own, ("row", "col"), axis=1, tiled=True)
    inverse = invert(dot(jacobian, cross, ((1,), (1,)), highest))
    gain = dot(inverse, lax.dynamic_slice_in_dim(cross, at[0] * tile_rows, tile_rows, 1), ((0,), (0,)), highest)
    across = lax.dynamic_slice_in_dim(cross, at[1] * tile_cols, tile_cols, 1)
    new_cov = (covariance - dot(gain, across, ((0,), (0,)), highest)) / forget
    own_gain = lax.dynamic_slice_in_dim(gain, at[1] * slab, slab, 1)
    own_weight = lax.dynamic_slice_in_dim(layer_weight.reshape(-1), first, slab, 0)
    new_weight = own_weight + dot(errors, own_gain, ((0,), (0,)), highest)
    return new_weight, new_cov


def on_device(
    atom_types,
    neighbor_ids,
    switching,
    environment,
    force_weights,
    targets,
    type_embed,
    layer_weight,
    out_weight,
    covariance,
):
    rows_n = lax.axis_size("row")
    cols_n = lax.axis_size("col")
    at = jnp.stack([lax.axis_index("row"), lax.axis_index("col")]).astype(jnp.int32)
    tile_rows, tile_cols = covariance.shape
    slab = tile_rows // cols_n
    hin, width = layer_weight.shape
    run_network = functools.partial(
        network,
        atom_types=atom_types,
        neighbor_ids=neighbor_ids,
        switching=switching,
        environment=environment,
        force_weights=force_weights,
        targets=targets,
        type_embed=type_embed,
        layer_weight=layer_weight,
        out_weight=out_weight,
    )
    if slab % LANES or width != LANES or (tile_rows + tile_cols) % (SUBLANES * LANES):
        payload = run_network([[(0, hin)]])[0]
        jac_all = lax.all_gather(payload, ("row", "col"), axis=0, tiled=True)
        return plain_steps(at, jac_all, layer_weight, covariance, slab, cols_n)
    row_size, col_size = tile_rows // LANES, tile_cols // LANES
    plan = [[(c * col_size, col_size), (r * row_size, row_size)] for r in range(rows_n) for c in range(cols_n)]
    payload = run_network(plan)
    jac = lax.all_to_all(payload, ("row", "col"), split_axis=0, concat_axis=0, tiled=True)
    jac = jac.reshape(-1, *jac.shape[2:])
    partial = cross_partial(at, jac, covariance, slab)
    devices = [(r, c) for r in range(rows_n) for c in range(cols_n)]
    for_row, for_col = [partial[0]], []
    for k in range(cols_n):
        to_row, to_col = [], []
        for r, c in devices:
            d = r * cols_n + (c + k) % cols_n
            to_row.append((r * cols_n + c, d))
            to_col.append((r * cols_n + c, d % rows_n * cols_n + d // rows_n))
        if k:
            for_row.append(lax.ppermute(partial[k], ("row", "col"), to_row))
        for_col.append(lax.ppermute(partial[k], ("row", "col"), to_col))
    row_own, col_own = slab_sums(for_row, for_col, slab)
    row_slabs = lax.all_gather(row_own, "col", axis=0, tiled=False)
    col_slabs = lax.all_gather(col_own, "row", axis=0, tiled=False)
    new_weight, new_cov = update(at, row_slabs, col_slabs, jac, layer_weight, covariance)
    return new_weight.reshape(-1), new_cov


def solution(mesh):
    in_specs = (
        P(("row", "col"), None),
        P(("row", "col"), None, None),
        P(("row", "col"), None, None),
        P(("row", "col"), None, None),
        P(("row", "col"), None),
        P(("row", "col")),
        P(),
        P(),
        P(),
        P("row", "col"),
    )
    out_specs = (P(("row", "col")), P("row", "col"))
    return jax.shard_map(
        on_device, mesh=mesh, in_specs=in_specs, out_specs=out_specs, check_vma=False
    )
```

time: 163 us -> 94.5 us (0.58)
  waiting for transfers between devices: 110 us -> 18.9 us
  starting transfers between devices: 0.08 us -> 25.9 us
  blocking collectives: 9.81 us -> 23.6 us
  between operations: 14.7 us -> 1.44 us
  local copies, waits for them, and re-layouts: 8.32 us -> 4.02 us
    all_gather x2 -> x0, waiting for transfers between devices: 110 us -> none  [the longest x1 56.8 us: on_device(): jac_all = lax.all_gather(payload, ('row', 'col'), axis=0, tiled=True)]
    all_gather x0 -> x2, blocking collectives: none -> 23.6 us  [the longest x1 13.6 us: on_device(): row_slabs = lax.all_gather(row_own, 'col', axis=0, tiled=False)]
    ppermute x0 -> x7, starting transfers between devices: none -> 18.6 us  [the longest x3 11.3 us: on_device(): for_row.append(lax.ppermute(partial[k], ('row', 'col'), to_row))]
    all_to_all x0 -> x1, waiting for transfers between devices: none -> 14.3 us  [on_device(): lax.all_to_all(payload, ('row', 'col'), split_axis=0, concat_axis=0, tile...]
    all_to_all x1 -> x0, blocking collectives: 9.81 us -> none  [on_device(): lax.all_to_all(partial, 'col', split_axis=0, concat_axis=0, tiled=True)]
    all_to_all x0 -> x1, starting transfers between devices: none -> 7.3 us  [on_device(): lax.all_to_all(payload, ('row', 'col'), split_axis=0, concat_axis=0, tile...]
    ppermute x0 -> x7, waiting for transfers between devices: none -> 4.59 us  [the longest x4 3.53 us: on_device(): for_col.append(lax.ppermute(partial[k], ('row', 'col'), to_col))]
    unnamed x15 -> x20, local copies, waits for them, and re-layouts: 8.32 us -> 4.02 us
  transfers between devices with their start and end apart: 2 -> 8, of which waited for: 2 -> 3; matrix products, arithmetic and copies ran while one was open for 0% -> 0% of each run, Pallas kernels for 0% -> 0%
where the time goes in v2:
time: 94.5 us; the launch traced here: 93.9 us
  starting transfers between devices  25.9 us (27%)
  blocking collectives  23.6 us (25%)
  Pallas kernels  20 us (21%)
  waiting for transfers between devices  18.9 us (20%)
  local copies, waits for them, and re-layouts  4.02 us (4%)
  between operations  1.44 us (2%)
    all_to_all x1, waiting for transfers between devices, on_device(): lax.all_to_all(payload, ('row', 'col'), split_axis=0, concat_axis=0, tile...  14.3 us
    all_gather x1, blocking collectives, on_device(): row_slabs = lax.all_gather(row_own, 'col', axis=0, tiled=False)  13.6 us
    ppermute x3, starting transfers between devices, on_device(): for_row.append(lax.ppermute(partial[k], ('row', 'col'), to_row))  11.3 us
    all_gather x1, blocking collectives, on_device(): col_slabs = lax.all_gather(col_own, 'row', axis=0, tiled=False)  10 us
    pallas_call x1, Pallas kernels, update(): pl.pallas_call(update_kernel, grid_spec=pltpu.PrefetchScalarGridSpec(num_...  9.62 us
    ppermute x4, starting transfers between devices, on_device(): for_col.append(lax.ppermute(partial[k], ('row', 'col'), to_col))  7.34 us
    all_to_all x1, starting transfers between devices, on_device(): lax.all_to_all(payload, ('row', 'col'), split_axis=0, concat_axis=0, tile...  7.3 us
    pallas_call x1, Pallas kernels, cross_partial(): pl.pallas_call(functools.partial(cross_kernel, col_rows=tile_cols // LANE...  5.01 us
  transfers between devices with their start and end apart: 8, of which 3 were waited for; matrix products, arithmetic and copies ran while one was open for 0% of the time, Pallas kernels for 0%

profile of v2, /device:TPU:0, one launch (start us, length us, event | category | flops | bytes accessed | tf_op | source)
XLA Modules:
  0.0 93.9 jit_solution(7090562279314420803)
XLA Ops:
  0.6 0.0 copy-start.1
  1.3 3.8 %network.1 = f32[32,1,32,128]{3,2,1,0:T(8,128)} custom-call(s32[1,1,256]{2,1,0:T(1,128)} %bitcast.17, s32[1,32,256]{2,1,0:T(8,128)} %ids_ref.1, f32[1,32,256]{2,1,0:T(8,128)} %switch_ref.1, f32[1,64,256]{2,1,0:T(8,128)} %bitcast.16, f32[1,1,256]{2,1,0:T(1,128)} %bitcast.18, f32[1,1,1]{2,1,0:T(1,128)} %bitcast.11.target_ref, f32[4,64]{1,0:T(4,128)} %embed_ref.1, ...), custom_call_target="tpu_custom_call" | custom-call | tf_op jit(solution)/shard_map/network/pallas_call | solution.py:102
  5.1 7.3 %all-to-all-start = ((f32[32,1,32,128]{3,2,1,0:T(8,128)}), f32[32,1,32,128]{3,2,1,0:T(8,128)S(1)}, u32[]{:S(2)}, u32[]{:S(2)}) async-start(f32[32,1,32,128]{3,2,1,0:T(8,128)} %network.1), calls=%async_computation | async-start | bytes 1048576 | tf_op jit(solution)/shard_map/all_to_all | solution.py:373
  12.4 0.1 pad_add_fusion.at_ref
  12.4 14.3 %all-to-all-done = f32[32,1,32,128]{3,2,1,0:T(8,128)S(1)} async-done(((f32[32,1,32,128]{3,2,1,0:T(8,128)}), f32[32,1,32,128]{3,2,1,0:T(8,128)S(1)}, u32[]{:S(2)}, u32[]{:S(2)}) %all-to-all-start) | async-done | bytes 524320 | tf_op jit(solution)/shard_map/all_to_all | solution.py:373
  26.7 0.0 copy-start
  26.7 3.4 %copy-done = f32[1024,2048]{1,0:T(8,128)S(1)} copy-done((f32[1024,2048]{1,0:T(8,128)S(1)}, f32[1024,2048]{1,0:T(8,128)}, u32[]{:S(2)}) %copy-start) | copy-done | bytes 8388632
  30.1 5.0 %cross.1 = (f32[32,384]{1,0:T(8,128)S(1)}, f32[32,384]{1,0:T(8,128)S(1)}, f32[32,384]{1,0:T(8,128)S(1)}, f32[32,384]{1,0:T(8,128)S(1)}) custom-call(s32[2]{0:T(128)S(1)} %pad_add_fusion.at_ref, f32[32,32,128]{2,1,0:T(8,128)S(1)} %bitcast.12, f32[1024,2048]{1,0:T(8,128)S(1)} %copy-done), custom_call_target="tpu_custom_call" | custom-call | tf_op jit(solution)/shard_map/cross/pallas_call | solution.py:181
  35.1 0.0 copy-start.2
  35.2 0.7 collective-permute-start.3
  35.8 4.8 %collective-permute-start.4 = (f32[32,384]{1,0:T(8,128)S(1)}, f32[32,384]{1,0:T(8,128)S(1)}, u32[]{:S(2)}, u32[]{:S(2)}) collective-permute-start(f32[32,384]{1,0:T(8,128)S(1)} %get-tuple-element.11), channel_id=1, source_target_pairs={{0,4},{1,8},{2,12},{3,0},{4,20},{5,24},{6,28},{7,16},{8,5},{9,9},{... | collective-permute-start | bytes 147464 | tf_op jit(solution)/shard_map/ppermute | solution.py:386
  40.6 3.9 %collective-permute-start = (f32[32,384]{1,0:T(8,128)S(1)}, f32[32,384]{1,0:T(8,128)S(1)}, u32[]{:S(2)}, u32[]{:S(2)}) collective-permute-start(f32[32,384]{1,0:T(8,128)S(1)} %get-tuple-element.11), channel_id=1, source_target_pairs={{0,1},{1,2},{2,3},{3,0},{4,5},{5,6},{6,7},{7,4},{8,9},{9,10},{10,1... | collective-permute-start | bytes 147464 | tf_op jit(solution)/shard_map/ppermute | solution.py:385
  44.5 0.0 collective-permute-start.5
  44.5 2.9 %collective-permute-start.1 = (f32[32,384]{1,0:T(8,128)S(1)}, f32[32,384]{1,0:T(8,128)S(1)}, u32[]{:S(2)}, u32[]{:S(2)}) collective-permute-start(f32[32,384]{1,0:T(8,128)S(1)} %get-tuple-element.12), channel_id=1, source_target_pairs={{0,2},{1,3},{2,0},{3,1},{4,6},{5,7},{6,4},{7,5},{8,10},{9,11},{10,... | collective-permute-start | bytes 147464 | tf_op jit(solution)/shard_map/ppermute | solution.py:385
  47.4 0.0 collective-permute-done.3.refs_4_
  47.4 0.0 copy-start.3
  47.4 1.9 %collective-permute-start.6 = (f32[32,384]{1,0:T(8,128)S(1)}, f32[32,384]{1,0:T(8,128)S(1)}, u32[]{:S(2)}, u32[]{:S(2)}) collective-permute-start(f32[32,384]{1,0:T(8,128)S(1)} %get-tuple-element.13), channel_id=1, source_target_pairs={{0,12},{1,0},{2,4},{3,8},{4,28},{5,16},{6,20},{7,24},{8,13},{9,1},... | collective-permute-start | bytes 147464 | tf_op jit(solution)/shard_map/ppermute | solution.py:386
  49.4 0.0 collective-permute-done.4.refs_5_
  49.4 0.0 copy-start.4
  49.4 4.5 %collective-permute-start.2 = (f32[32,384]{1,0:T(8,128)S(1)}, f32[32,384]{1,0:T(8,128)S(1)}, u32[]{:S(2)}, u32[]{:S(2)}) collective-permute-start(f32[32,384]{1,0:T(8,128)S(1)} %get-tuple-element.13), channel_id=1, source_target_pairs={{0,3},{1,0},{2,1},{3,2},{4,7},{5,4},{6,5},{7,6},{8,11},{9,8},{10,9... | collective-permute-start | bytes 147464 | tf_op jit(solution)/shard_map/ppermute | solution.py:385
  53.8 0.0 collective-permute-done.refs_1_
  53.8 0.0 copy-start.5
  53.8 0.0 collective-permute-done.5.refs_6_
  53.8 0.0 copy-start.6
  53.9 0.0 collective-permute-done.1.refs_2_
  53.9 0.0 copy-start.7
  53.9 3.5 %collective-permute-done.6.refs_7_ = f32[32,384]{1,0:T(8,128)S(1)} collective-permute-done((f32[32,384]{1,0:T(8,128)S(1)}, f32[32,384]{1,0:T(8,128)S(1)}, u32[]{:S(2)}, u32[]{:S(2)}) %collective-permute-start.6) | collective-permute-done | bytes 49184 | tf_op jit(solution)/shard_map/ppermute | solution.py:386
  57.4 0.0 copy-start.8
  57.4 1.1 %collective-permute-done.2.refs_3_ = f32[32,384]{1,0:T(8,128)S(1)} collective-permute-done((f32[32,384]{1,0:T(8,128)S(1)}, f32[32,384]{1,0:T(8,128)S(1)}, u32[]{:S(2)}, u32[]{:S(2)}) %collective-permute-start.2) | collective-permute-done | bytes 49184 | tf_op jit(solution)/shard_map/ppermute | solution.py:385
  58.5 0.0 copy-done.2
  58.5 0.0 copy-done.3
  58.5 0.0 copy-done.4
  58.5 0.0 copy-done.5
  58.5 0.0 copy-done.6
  58.5 0.0 copy-done.7
  58.5 0.0 copy-done.8
  58.5 0.0 copy-start.9
  58.5 0.6 copy-done.9
  59.1 1.6 %slab.1 = (f32[32,256]{1,0:T(8,128)}, f32[32,384]{1,0:T(8,128)}) custom-call(f32[32,384]{1,0:T(8,128)} %copy-done.2, f32[32,384]{1,0:T(8,128)} %copy-done.5, f32[32,384]{1,0:T(8,128)} %copy-done.7, f32[32,384]{1,0:T(8,128)} %copy-done.9, f32[32,384]{1,0:T(8,128)} %copy-done.3, f32[32,384]{1,0:T(8,128)} %copy-done.4, f32[32,384]{1,0:T(8,128)} %copy-done.6, ...), custom_call_target="tpu_custom_call" | custom-call | tf_op jit(solution)/shard_map/slab/pallas_call | solution.py:217
  60.7 13.6 %all-gather = f32[128,256]{1,0:T(8,128)S(1)} all-gather(f32[32,256]{1,0:T(8,128)} %get-tuple-element.14), channel_id=2, replica_groups=mesh['row'=8,'col'=4] {'col'}, dimensions={0}, use_global_device_ids=true | all-gather | bytes 163840 | tf_op jit(solution)/shard_map/all_gather | solution.py:388
  74.3 10.0 %all-gather.1 = f32[256,384]{1,0:T(8,128)S(1)} all-gather(f32[32,384]{1,0:T(8,128)} %get-tuple-element.15), channel_id=3, replica_groups=mesh['row'=8,'col'=4] {'row'}, dimensions={0}, use_global_device_ids=true | all-gather | bytes 442368 | tf_op jit(solution)/shard_map/all_gather | solution.py:389
  84.3 0.0 copy-done.1
  84.3 9.6 %update.1 = (f32[2,128]{1,0:T(2,128)}, f32[1024,2048]{1,0:T(8,128)}) custom-call(s32[2]{0:T(128)S(1)} %pad_add_fusion.at_ref, f32[4,32,256]{2,1,0:T(8,128)S(1)} %bitcast.15, f32[8,32,384]{2,1,0:T(8,128)S(1)} %bitcast.14, f32[32,32,128]{2,1,0:T(8,128)S(1)} %bitcast.13, f32[64,128]{1,0:T(8,128)S(1)} %copy-done.1, f32[1024,2048]{1,0:T(8,128)} %cov_ref.3), custom_call_target="tpu_custom_call" | custom-call | tf_op jit(solution)/shard_map/update/pallas_call | solution.py:283
Async XLA Ops:
  0.6 83.6 %copy-start.1 = (f32[64,128]{1,0:T(8,128)S(1)}, f32[64,128]{1,0:T(8,128)}, u32[]{:S(2)}) copy-start(f32[64,128]{1,0:T(8,128)} %weight_ref.3) | copy-start | bytes 98308
  5.1 21.7 %all-to-all-start = ((f32[32,1,32,128]{3,2,1,0:T(8,128)}), f32[32,1,32,128]{3,2,1,0:T(8,128)S(1)}, u32[]{:S(2)}, u32[]{:S(2)}) async-start(f32[32,1,32,128]{3,2,1,0:T(8,128)} %network.1), calls=%async_computation | async-start | bytes 1048576 | tf_op jit(solution)/shard_map/all_to_all | solution.py:373
  26.7 3.4 %copy-start = (f32[1024,2048]{1,0:T(8,128)S(1)}, f32[1024,2048]{1,0:T(8,128)}, u32[]{:S(2)}) copy-start(f32[1024,2048]{1,0:T(8,128)} %cov_ref.3) | copy-start | bytes 25165828
  35.1 23.3 %copy-start.2 = (f32[32,384]{1,0:T(8,128)}, f32[32,384]{1,0:T(8,128)S(1)}, u32[]{:S(2)}) copy-start(f32[32,384]{1,0:T(8,128)S(1)} %get-tuple-element.10.refs_0_) | copy-start | bytes 147460
  35.2 12.3 %collective-permute-start.3 = (f32[32,384]{1,0:T(8,128)S(1)}, f32[32,384]{1,0:T(8,128)S(1)}, u32[]{:S(2)}, u32[]{:S(2)}) collective-permute-start(f32[32,384]{1,0:T(8,128)S(1)} %get-tuple-element.10.refs_0_), channel_id=1, source_target_pairs={{0,0},{1,4},{2,8},{3,12},{4,16},{5,20},{6,24},{7,28},{8,1},{9,5},{... | collective-permute-start | bytes 147464 | tf_op jit(solution)/shard_map/ppermute | solution.py:386
  35.8 13.5 %collective-permute-start.4 = (f32[32,384]{1,0:T(8,128)S(1)}, f32[32,384]{1,0:T(8,128)S(1)}, u32[]{:S(2)}, u32[]{:S(2)}) collective-permute-start(f32[32,384]{1,0:T(8,128)S(1)} %get-tuple-element.11), channel_id=1, source_target_pairs={{0,4},{1,8},{2,12},{3,0},{4,20},{5,24},{6,28},{7,16},{8,5},{9,9},{... | collective-permute-start | bytes 147464 | tf_op jit(solution)/shard_map/ppermute | solution.py:386
  40.6 13.2 %collective-permute-start = (f32[32,384]{1,0:T(8,128)S(1)}, f32[32,384]{1,0:T(8,128)S(1)}, u32[]{:S(2)}, u32[]{:S(2)}) collective-permute-start(f32[32,384]{1,0:T(8,128)S(1)} %get-tuple-element.11), channel_id=1, source_target_pairs={{0,1},{1,2},{2,3},{3,0},{4,5},{5,6},{6,7},{7,4},{8,9},{9,10},{10,1... | collective-permute-start | bytes 147464 | tf_op jit(solution)/shard_map/ppermute | solution.py:385
  44.5 9.3 %collective-permute-start.5 = (f32[32,384]{1,0:T(8,128)S(1)}, f32[32,384]{1,0:T(8,128)S(1)}, u32[]{:S(2)}, u32[]{:S(2)}) collective-permute-start(f32[32,384]{1,0:T(8,128)S(1)} %get-tuple-element.12), channel_id=1, source_target_pairs={{0,8},{1,12},{2,0},{3,4},{4,24},{5,28},{6,16},{7,20},{8,9},{9,13},... | collective-permute-start | bytes 147464 | tf_op jit(solution)/shard_map/ppermute | solution.py:386
  44.5 9.3 %collective-permute-start.1 = (f32[32,384]{1,0:T(8,128)S(1)}, f32[32,384]{1,0:T(8,128)S(1)}, u32[]{:S(2)}, u32[]{:S(2)}) collective-permute-start(f32[32,384]{1,0:T(8,128)S(1)} %get-tuple-element.12), channel_id=1, source_target_pairs={{0,2},{1,3},{2,0},{3,1},{4,6},{5,7},{6,4},{7,5},{8,10},{9,11},{10,... | collective-permute-start | bytes 147464 | tf_op jit(solution)/shard_map/ppermute | solution.py:385
  47.4 11.0 %copy-start.3 = (f32[32,384]{1,0:T(8,128)}, f32[32,384]{1,0:T(8,128)S(1)}, u32[]{:S(2)}) copy-start(f32[32,384]{1,0:T(8,128)S(1)} %collective-permute-done.3.refs_4_) | copy-start | bytes 147460
  47.4 10.0 %collective-permute-start.6 = (f32[32,384]{1,0:T(8,128)S(1)}, f32[32,384]{1,0:T(8,128)S(1)}, u32[]{:S(2)}, u32[]{:S(2)}) collective-permute-start(f32[32,384]{1,0:T(8,128)S(1)} %get-tuple-element.13), channel_id=1, source_target_pairs={{0,12},{1,0},{2,4},{3,8},{4,28},{5,16},{6,20},{7,24},{8,13},{9,1},... | collective-permute-start | bytes 147464 | tf_op jit(solution)/shard_map/ppermute | solution.py:386
  49.4 9.1 %copy-start.4 = (f32[32,384]{1,0:T(8,128)}, f32[32,384]{1,0:T(8,128)S(1)}, u32[]{:S(2)}) copy-start(f32[32,384]{1,0:T(8,128)S(1)} %collective-permute-done.4.refs_5_) | copy-start | bytes 147460
  49.4 9.1 %collective-permute-start.2 = (f32[32,384]{1,0:T(8,128)S(1)}, f32[32,384]{1,0:T(8,128)S(1)}, u32[]{:S(2)}, u32[]{:S(2)}) collective-permute-start(f32[32,384]{1,0:T(8,128)S(1)} %get-tuple-element.13), channel_id=1, source_target_pairs={{0,3},{1,0},{2,1},{3,2},{4,7},{5,4},{6,5},{7,6},{8,11},{9,8},{10,9... | collective-permute-start | bytes 147464 | tf_op jit(solution)/shard_map/ppermute | solution.py:385
  53.8 4.6 %copy-start.5 = (f32[32,384]{1,0:T(8,128)}, f32[32,384]{1,0:T(8,128)S(1)}, u32[]{:S(2)}) copy-start(f32[32,384]{1,0:T(8,128)S(1)} %collective-permute-done.refs_1_) | copy-start | bytes 147460
  53.8 4.6 %copy-start.6 = (f32[32,384]{1,0:T(8,128)}, f32[32,384]{1,0:T(8,128)S(1)}, u32[]{:S(2)}) copy-start(f32[32,384]{1,0:T(8,128)S(1)} %collective-permute-done.5.refs_6_) | copy-start | bytes 147460
  53.9 4.6 %copy-start.7 = (f32[32,384]{1,0:T(8,128)}, f32[32,384]{1,0:T(8,128)S(1)}, u32[]{:S(2)}) copy-start(f32[32,384]{1,0:T(8,128)S(1)} %collective-permute-done.1.refs_2_) | copy-start | bytes 147460
  57.4 1.1 %copy-start.8 = (f32[32,384]{1,0:T(8,128)}, f32[32,384]{1,0:T(8,128)S(1)}, u32[]{:S(2)}) copy-start(f32[32,384]{1,0:T(8,128)S(1)} %collective-permute-done.6.refs_7_) | copy-start | bytes 147460
  58.5 0.6 copy-start.9

commit v3 on v1

v3 whole, which is shorter than its diff:
```python
import functools
import math

import jax
import jax.numpy as jnp
from jax import lax
from jax.experimental import pallas as pl
from jax.experimental.pallas import tpu as pltpu
from jax.sharding import PartitionSpec as P

NEWTON = 4
LANES = 128
SUBLANES = 8


forget = 0.98
highest = lax.Precision.HIGHEST
f32 = jnp.float32
bf16 = jnp.bfloat16


def dot(left, right, contract, precision=None):
    return lax.dot_general(
        left, right, (contract, ((), ())), precision=precision, preferred_element_type=f32
    )


def split3(x):
    hi = x.astype(bf16)
    rest = x - hi.astype(f32)
    mid = rest.astype(bf16)
    lo = (rest - mid.astype(f32)).astype(bf16)
    return hi, mid, lo


def split2(x):
    hi = x.astype(bf16)
    return hi, (x - hi.astype(f32)).astype(bf16)


def network_kernel(
    types_ref,
    ids_ref,
    switch_ref,
    env_ref,
    force_ref,
    target_ref,
    embed_ref,
    weight_ref,
    out_weight_ref,
    payload_ref,
    error_ref,
    mix_ref,
):
    neighbours, atoms = ids_ref.shape
    n_types = embed_ref.shape[0]
    height = min(64, atoms)
    for start in range(0, atoms, height):
        atom_at = lax.broadcasted_iota(jnp.int32, (height, atoms), 0) + start
        total = jnp.zeros((height, atoms), f32)
        for k in range(neighbours):
            total = total + jnp.where(ids_ref[k : k + 1, :] == atom_at, switch_ref[k : k + 1, :], 0.0)
        mix_ref[start : start + height, :] = total
    mix = mix_ref[...]
    type_at = lax.broadcasted_iota(jnp.int32, (n_types, atoms), 0)
    onehot = (types_ref[...] == type_at).astype(f32)
    mixed = env_ref[...] + dot(embed_ref[...], onehot, ((0,), (0,)), highest)
    descriptor = dot(mixed, mix, ((1,), (0,)), highest) * (1.0 / math.sqrt(neighbours))
    hidden = jnp.tanh(descriptor)
    activity = jnp.tanh(dot(hidden, weight_ref[...], ((0,), (0,)), highest))
    out_weight = out_weight_ref[...]
    scale = 1.0 / math.sqrt(atoms)
    force = force_ref[...]
    weighted = dot(force, activity, ((1,), (0,)), highest)
    predicted = jnp.sum(weighted * out_weight, axis=1, keepdims=True) * scale
    slopes = out_weight * (1.0 - activity * activity)
    jacobian = dot(hidden * force, slopes, ((1,), (0,)), highest) * scale
    error_ref[...] = jnp.broadcast_to(target_ref[...] - predicted, error_ref.shape)
    blocks, rows, _ = payload_ref.shape
    for block in range(blocks):
        start = block * rows % jacobian.shape[0]
        payload_ref[block] = jacobian[start : start + rows, :]


def network(
    blocks, rows, atom_types, neighbor_ids, switching, environment, force_weights, targets, type_embed, layer_weight, out_weight
):
    per_dev, neighbours, atoms = neighbor_ids.shape
    hin, width = layer_weight.shape

    def per_stream(*shape):
        return pl.BlockSpec((None,) + shape, lambda s: (s,) + (0,) * len(shape))

    def shared(shape):
        return pl.BlockSpec(shape, lambda s: (0,) * len(shape))

    return pl.pallas_call(
        network_kernel,
        grid=(per_dev,),
        in_specs=[
            per_stream(1, atoms),
            per_stream(neighbours, atoms),
            per_stream(neighbours, atoms),
            per_stream(hin, atoms),
            per_stream(1, atoms),
            per_stream(1, 1),
            shared(type_embed.shape),
            shared(layer_weight.shape),
            shared((1, width)),
        ],
        out_specs=[
            pl.BlockSpec((blocks, None, rows, width), lambda s: (0, s, 0, 0)),
            per_stream(1, width),
        ],
        out_shape=[
            jax.ShapeDtypeStruct((blocks, per_dev, rows, width), f32),
            jax.ShapeDtypeStruct((per_dev, 1, width), f32),
        ],
        scratch_shapes=[pltpu.VMEM((atoms, atoms), f32)],
        name="network",
    )(
        atom_types.reshape(per_dev, 1, atoms),
        neighbor_ids,
        switching,
        environment.swapaxes(1, 2),
        force_weights.reshape(per_dev, 1, atoms),
        targets.reshape(per_dev, 1, 1),
        type_embed,
        layer_weight,
        out_weight.reshape(1, width),
    )


def stage_kernel(cov_ref, held_ref, hi_ref, lo_ref, sems):
    chunks = sems.shape[0]
    height = cov_ref.shape[0] // chunks
    copies = []
    for n in range(chunks):
        rows = pl.ds(n * height, height)
        copies.append(pltpu.make_async_copy(cov_ref.at[rows], held_ref.at[rows], sems.at[n]))
        copies[-1].start()
    for n in range(chunks):
        copies[n].wait()
        rows = pl.ds(n * height, height)
        hi, lo = split2(held_ref[rows, :])
        hi_ref[rows, :] = hi
        lo_ref[rows, :] = lo


def stage(covariance):
    shape = covariance.shape
    return pl.pallas_call(
        stage_kernel,
        in_specs=[pl.BlockSpec(memory_space=pl.ANY)],
        out_specs=[pl.BlockSpec(memory_space=pltpu.VMEM)] * 3,
        out_shape=[pltpu.VMEM(shape, f32), pltpu.VMEM(shape, bf16), pltpu.VMEM(shape, bf16)],
        scratch_shapes=[pltpu.SemaphoreType.DMA((8,))],
        compiler_params=pltpu.CompilerParams(vmem_limit_bytes=16 << 20),
        name="stage",
    )(covariance)


def cross_kernel(jac_ref, hi_ref, lo_ref, out_ref, parts_ref):
    streams, rows, lanes = jac_ref.shape
    slabs, _, slab = out_ref.shape
    flat = jac_ref.reshape(streams * rows, lanes)
    for i in range(rows):
        parts = split3(flat[pl.ds(i, streams, stride=rows), :])
        for n, part in enumerate(parts):
            parts_ref[n * streams : (n + 1) * streams, i * lanes : (i + 1) * lanes] = part
    for n in range(slabs):
        here = slice(n * slab, (n + 1) * slab)
        by_hi = dot(parts_ref[...], hi_ref[here, :], ((1,), (1,)))
        by_lo = dot(parts_ref[0 : 2 * streams, :], lo_ref[here, :], ((1,), (1,)))
        out_ref[n] = by_hi[0:streams] + (
            by_hi[streams : 2 * streams]
            + by_lo[0:streams]
            + (by_hi[2 * streams :] + by_lo[streams:])
        )


def cross_partial(jac, hi, lo, slab):
    streams = jac.shape[0]
    tile_rows, tile_cols = hi.shape
    whole = pl.BlockSpec(memory_space=pltpu.VMEM)
    return pl.pallas_call(
        cross_kernel,
        in_specs=[whole] * 3,
        out_specs=whole,
        out_shape=jax.ShapeDtypeStruct((tile_rows // slab, streams, slab), f32),
        scratch_shapes=[pltpu.VMEM((3 * streams, tile_cols), bf16)],
        compiler_params=pltpu.CompilerParams(vmem_limit_bytes=16 << 20),
        name="cross",
    )(jac, in_vmem(hi), in_vmem(lo))


def in_vmem(x):
    return pltpu.with_memory_space_constraint(x, pltpu.VMEM)


def slab_kernel(pieces_ref, error_ref, out_ref):
    pieces, streams, slab = pieces_ref.shape
    cross = pieces_ref[0]
    for n in range(1, pieces):
        cross = cross + pieces_ref[n]
    out_ref[0:streams, :] = cross
    out_ref[streams:, :] = jnp.broadcast_to(error_ref[0, :, 0:1], (SUBLANES, slab))


def slab_sum(pieces, error):
    _, streams, slab = pieces.shape
    return pl.pallas_call(
        slab_kernel,
        out_shape=jax.ShapeDtypeStruct((streams + SUBLANES, slab), f32),
        name="slab",
    )(pieces, error)


def term_kernel(own_ref, cols_ref, jac_ref, out_ref):
    streams, rows, lanes = jac_ref.shape
    count, _, slab = cols_ref.shape
    flat = jac_ref.reshape(streams * rows, lanes)
    term = jnp.zeros((streams, streams), f32)
    for i in range(rows):
        own = flat[pl.ds(i, streams, stride=rows), :]
        start = i * lanes % slab
        across = cols_ref[i * lanes // slab, 0:streams, start : start + lanes]
        term = term + dot(own, across, ((1,), (1,)), highest)
    out_ref[:, 0:slab] = own_ref[0:streams, :]
    out_ref[:, slab : slab + streams] = term
    first = lax.axis_index("col") * count
    stream_at = lax.broadcasted_iota(jnp.int32, (streams, lanes), 0)
    errors = jnp.zeros((streams, lanes), f32)
    for n in range(count):
        errors = jnp.where(stream_at == first + n, cols_ref[n, streams : streams + 1, 0:lanes], errors)
    out_ref[:, slab + streams :] = errors[:, streams:]


def with_terms(own, col_slabs, jac):
    streams = jac.shape[0]
    slab = own.shape[1]
    return pl.pallas_call(
        term_kernel,
        out_shape=jax.ShapeDtypeStruct((streams, slab + LANES), f32),
        name="term",
    )(own, col_slabs, jac)


def invert(innovation):
    streams = innovation.shape[0]
    row = lax.broadcasted_iota(jnp.int32, (streams, streams), 0)
    col = lax.broadcasted_iota(jnp.int32, (streams, streams), 1)
    identity = (row == col).astype(f32)
    innovation = innovation + forget * identity
    sums = jnp.sum(jnp.abs(innovation), axis=1, keepdims=True)
    bound = jnp.max(sums, axis=0, keepdims=True)
    power = identity - innovation / bound
    inverse = identity + power
    for repeat in range(NEWTON - 1):
        power = dot(power, power, ((1,), (0,)), highest)
        inverse = inverse + dot(inverse, power, ((1,), (0,)), highest)
    return inverse / bound


def update_kernel(
    rows_ref, cols_ref, weight_ref, cov_ref, new_weight_ref, new_cov_ref, right_ref, done_ref, sems
):
    slabs, streams, _ = rows_ref.shape
    col_slabs, _, slab = cols_ref.shape
    lanes = weight_ref.shape[1]
    beside = rows_ref[0, :, slab:]
    for n in range(1, slabs):
        beside = beside + rows_ref[n, :, slab:]
    inverse = invert(beside[:, 0:streams])
    errors = beside[:, streams : streams + 1]
    for n in range(col_slabs):
        hi, mid, lo = split3(cols_ref[n, 0:streams, :])
        for m, part in enumerate((hi, mid, lo, hi, mid, hi)):
            right_ref[m * streams : (m + 1) * streams, n * slab : (n + 1) * slab] = part
    col_at = lax.axis_index("col")
    own_at = (lax.axis_index("row") * slabs + col_at) * (slab // lanes)
    copies = []
    for n in range(slabs):
        gain = dot(inverse, rows_ref[n, :, 0:slab], ((0,), (0,)), highest)
        hi, mid, lo = split3(gain)
        left = jnp.concatenate([hi, hi, hi, mid, mid, lo], axis=0)
        update = dot(left, right_ref[...], ((0,), (0,)))
        here = slice(n * slab, (n + 1) * slab)
        done_ref[here, :] = (cov_ref[here, :] - update) * (1.0 / forget)
        copies.append(pltpu.make_async_copy(done_ref.at[here], new_cov_ref.at[here], sems.at[n]))
        copies[-1].start()

        @pl.when(col_at == n)
        def _():
            moved = jnp.sum(gain * errors, axis=0, keepdims=True)
            for i in range(slab // lanes):
                own = weight_ref[pl.ds(own_at + i, 1), :]
                new_weight_ref[i : i + 1, :] = own + moved[:, i * lanes : (i + 1) * lanes]

    for copy in copies:
        copy.wait()


def update(row_slabs, col_slabs, layer_weight, held):
    slabs, streams, _ = row_slabs.shape
    slab = col_slabs.shape[2]
    tile_rows, tile_cols = held.shape
    width = layer_weight.shape[1]
    whole = pl.BlockSpec(memory_space=pltpu.VMEM)
    return pl.pallas_call(
        update_kernel,
        in_specs=[whole] * 4,
        out_specs=[whole, pl.BlockSpec(memory_space=pl.ANY)],
        out_shape=[
            jax.ShapeDtypeStruct((slab // width, width), f32),
            jax.ShapeDtypeStruct((tile_rows, tile_cols), f32),
        ],
        scratch_shapes=[
            pltpu.VMEM((6 * streams, tile_cols), bf16),
            pltpu.VMEM((tile_rows, tile_cols), f32),
            pltpu.SemaphoreType.DMA((slabs,)),
        ],
        compiler_params=pltpu.CompilerParams(vmem_limit_bytes=24 << 20),
        name="update",
    )(row_slabs, col_slabs, layer_weight, in_vmem(held))


def plain_steps(at, jac_all, errors, layer_weight, covariance, slab, cols_n):
    streams = jac_all.shape[0]
    hin, width = layer_weight.shape
    tile_rows, tile_cols = covariance.shape
    first = (at[0] * cols_n + at[1]) * slab
    jacobian = jac_all[:, 0:hin, :].reshape(streams, hin * width)
    jac_cols = lax.dynamic_slice_in_dim(jacobian, at[1] * tile_cols, tile_cols, 1)
    partial = dot(jac_cols, covariance, ((1,), (1,)), highest)
    cross_own = lax.psum_scatter(partial, "col", scatter_dimension=1, tiled=True)
    cross = lax.all_gather(cross_own, ("row", "col"), axis=1, tiled=True)
    inverse = invert(dot(jacobian, cross, ((1,), (1,)), highest))
    gain = dot(inverse, lax.dynamic_slice_in_dim(cross, at[0] * tile_rows, tile_rows, 1), ((0,), (0,)), highest)
    across = lax.dynamic_slice_in_dim(cross, at[1] * tile_cols, tile_cols, 1)
    new_cov = (covariance - dot(gain, across, ((0,), (0,)), highest)) / forget
    own_gain = lax.dynamic_slice_in_dim(gain, at[1] * slab, slab, 1)
    own_weight = lax.dynamic_slice_in_dim(layer_weight.reshape(-1), first, slab, 0)
    new_weight = own_weight + dot(errors, own_gain, ((0,), (0,)), highest)
    return new_weight, new_cov


def on_device(
    atom_types,
    neighbor_ids,
    switching,
    environment,
    force_weights,
    targets,
    type_embed,
    layer_weight,
    out_weight,
    covariance,
):
    rows_n = lax.axis_size("row")
    cols_n = lax.axis_size("col")
    at = jnp.stack([lax.axis_index("row"), lax.axis_index("col")]).astype(jnp.int32)
    tile_rows, tile_cols = covariance.shape
    slab = tile_rows // cols_n
    hin, width = layer_weight.shape
    run_network = functools.partial(
        network,
        atom_types=atom_types,
        neighbor_ids=neighbor_ids,
        switching=switching,
        environment=environment,
        force_weights=force_weights,
        targets=targets,
        type_embed=type_embed,
        layer_weight=layer_weight,
        out_weight=out_weight,
    )
    streams = rows_n * cols_n * atom_types.shape[0]
    kernels = (
        atom_types.shape[0] == 1
        and width == LANES
        and slab % LANES == 0
        and tile_cols % (SUBLANES * LANES) == 0
        and rows_n * slab == tile_cols
        and streams < LANES
    )
    if not kernels:
        payload, error = run_network(1, hin)
        jac_all = lax.all_gather(payload[0], ("row", "col"), axis=0, tiled=True)
        errors = lax.all_gather(error[:, 0, 0], ("row", "col"), axis=0, tiled=True)
        return plain_steps(at, jac_all, errors, layer_weight, covariance, slab, cols_n)
    payload, error = run_network(rows_n * cols_n, tile_cols // LANES)
    jac = lax.all_to_all(payload, ("row", "col"), split_axis=0, concat_axis=0, tiled=True)
    jac = jac.reshape(-1, *jac.shape[2:])
    held, hi, lo = stage(covariance)
    partial = cross_partial(jac, hi, lo, slab)
    pieces = lax.all_to_all(partial, "col", split_axis=0, concat_axis=0, tiled=True)
    own = slab_sum(pieces, error)
    to_col = [(d, d % rows_n * cols_n + d // rows_n) for d in range(rows_n * cols_n)]
    col_slabs = lax.all_gather(lax.ppermute(own, ("row", "col"), to_col), "row", axis=0, tiled=False)
    row_slabs = lax.all_gather(with_terms(own, col_slabs, jac), "col", axis=0, tiled=False)
    new_weight, new_cov = update(row_slabs, col_slabs, layer_weight, held)
    return new_weight.reshape(-1), new_cov


def solution(mesh):
    in_specs = (
        P(("row", "col"), None),
        P(("row", "col"), None, None),
        P(("row", "col"), None, None),
        P(("row", "col"), None, None),
        P(("row", "col"), None),
        P(("row", "col")),
        P(),
        P(),
        P(),
        P("row", "col"),
    )
    out_specs = (P(("row", "col")), P("row", "col"))
    return jax.shard_map(
        on_device, mesh=mesh, in_specs=in_specs, out_specs=out_specs, check_vma=False
    )
```

time: 163 us -> 89.5 us (0.55)
  waiting for transfers between devices: 110 us -> 0.01 us
  blocking collectives: 9.81 us -> 42.2 us
  between operations: 14.7 us -> 1.32 us
  local copies, waits for them, and re-layouts: 8.32 us -> 19.5 us
  starting transfers between devices: 0.08 us -> 8.72 us
  Pallas kernels: 19.7 us -> 17.2 us
    all_gather x2 -> x0, waiting for transfers between devices: 110 us -> none  [the longest x1 56.8 us: on_device(): jac_all = lax.all_gather(payload, ('row', 'col'), axis=0, tiled=True)]
    all_gather x0 -> x2, blocking collectives: none -> 31.1 us  [the longest x1 17.3 us: on_device(): lax.all_gather(lax.ppermute(own, ('row', 'col'), to_col), 'row', axis=0,...]
    unnamed x15 -> x20, local copies, waits for them, and re-layouts: 8.32 us -> 19.5 us
    all_to_all x0 -> x1, starting transfers between devices: none -> 7.3 us  [on_device(): lax.all_to_all(payload, ('row', 'col'), split_axis=0, concat_axis=0, tile...]
    pallas_call x3 -> x5, Pallas kernels: 15.9 us -> 13.6 us  [the longest x1 5.39 us: update(): pl.pallas_call(update_kernel, in_specs=[whole] * 4, out_specs=[whole, pl....]
  transfers between devices with their start and end apart: 2 -> 2, of which waited for: 2 -> 0; matrix products, arithmetic and copies ran while one was open for 0% -> 0% of each run, Pallas kernels for 0% -> 2%
where the time goes in v3:
time: 89.5 us; the launch traced here: 88.9 us
  blocking collectives  42.2 us (47%)
  local copies, waits for them, and re-layouts  19.5 us (22%)
  Pallas kernels  17.2 us (19%)
  starting transfers between devices  8.72 us (10%)
  between operations  1.32 us (1%)
    unnamed x20, local copies, waits for them, and re-layouts  19.5 us
    all_gather x1, blocking collectives, on_device(): lax.all_gather(lax.ppermute(own, ('row', 'col'), to_col), 'row', axis=0,...  17.3 us
    all_gather x1, blocking collectives, on_device(): lax.all_gather(with_terms(own, col_slabs, jac), 'col', axis=0, tiled=False)  13.8 us
    all_to_all x1, blocking collectives, on_device(): lax.all_to_all(partial, 'col', split_axis=0, concat_axis=0, tiled=True)  11 us
    all_to_all x1, starting transfers between devices, on_device(): lax.all_to_all(payload, ('row', 'col'), split_axis=0, concat_axis=0, tile...  7.3 us
    pallas_call x1, Pallas kernels, update(): pl.pallas_call(update_kernel, in_specs=[whole] * 4, out_specs=[whole, pl....  5.39 us
    pallas_call x1, Pallas kernels, network(): pl.pallas_call(network_kernel, grid=(per_dev,), in_specs=[per_stream(1, a...  3.58 us
    pallas_call x1, Pallas kernels, cross_partial(): pl.pallas_call(cross_kernel, in_specs=[whole] * 3, out_specs=whole, out_s...  2.65 us
  transfers between devices with their start and end apart: 2, of which 0 were waited for; matrix products, arithmetic and copies ran while one was open for 0% of the time, Pallas kernels for 2%

profile of v3, /device:TPU:0, one launch (start us, length us, event | category | flops | bytes accessed | tf_op | source)
XLA Modules:
  0.0 88.9 jit_solution(18214835665812269834)
XLA Ops:
  1.3 3.6 %network.1 = (f32[32,1,16,128]{3,2,1,0:T(8,128)}, f32[1,1,128]{2,1,0:T(1,128)}) custom-call(s32[1,1,256]{2,1,0:T(1,128)} %bitcast.16, s32[1,32,256]{2,1,0:T(8,128)} %ids_ref.1, f32[1,32,256]{2,1,0:T(8,128)} %switch_ref.1, f32[1,64,256]{2,1,0:T(8,128)} %bitcast.15, f32[1,1,256]{2,1,0:T(1,128)} %bitcast.17, f32[1,1,1]{2,1,0:T(1,128)} %bitcast.9.target_ref, ...), custom_call_target="tpu_custom_call" | custom-call | tf_op jit(solution)/shard_map/network/pallas_call | solution.py:97
  4.9 7.3 %all-to-all-start = ((f32[32,1,16,128]{3,2,1,0:T(8,128)}), f32[32,1,16,128]{3,2,1,0:T(8,128)S(1)}, u32[]{:S(2)}, u32[]{:S(2)}) async-start(f32[32,1,16,128]{3,2,1,0:T(8,128)} %get-tuple-element.9), calls=%async_computation | async-start | bytes 524288 | tf_op jit(solution)/shard_map/all_to_all | solution.py:393
  12.2 0.0 copy-start
  12.2 3.4 %copy-done = f32[1024,2048]{1,0:T(8,128)S(1)} copy-done((f32[1024,2048]{1,0:T(8,128)S(1)}, f32[1024,2048]{1,0:T(8,128)}, u32[]{:S(2)}) %copy-start) | copy-done | bytes 8388632
  15.6 0.0 copy-start.9
  15.6 1.8 %stage.1 = (f32[1024,2048]{1,0:T(8,128)S(1)}, bf16[1024,2048]{1,0:T(8,128)(2,1)S(1)}, bf16[1024,2048]{1,0:T(8,128)(2,1)S(1)}) custom-call(f32[1024,2048]{1,0:T(8,128)S(1)} %copy-done), custom_call_target="tpu_custom_call" | custom-call | tf_op jit(solution)/shard_map/stage/pallas_call | solution.py:152
  17.3 0.0 copy-start.1
  17.3 3.4 %copy-done.1 = f32[1024,2048]{1,0:T(8,128)} copy-done((f32[1024,2048]{1,0:T(8,128)}, f32[1024,2048]{1,0:T(8,128)S(1)}, u32[]{:S(2)}) %copy-start.1) | copy-done | bytes 8388632
  20.7 0.0 copy-start.3
  20.7 2.0 %copy-done.3 = bf16[1024,2048]{1,0:T(8,128)(2,1)} copy-done((bf16[1024,2048]{1,0:T(8,128)(2,1)}, bf16[1024,2048]{1,0:T(8,128)(2,1)S(1)}, u32[]{:S(2)}) %copy-start.3) | copy-done | bytes 4194328
  22.7 0.0 copy-start.5
  22.7 2.0 %copy-done.5 = bf16[1024,2048]{1,0:T(8,128)(2,1)} copy-done((bf16[1024,2048]{1,0:T(8,128)(2,1)}, bf16[1024,2048]{1,0:T(8,128)(2,1)S(1)}, u32[]{:S(2)}) %copy-start.5) | copy-done | bytes 4194328
  24.7 0.0 all-to-all-done
  24.7 0.0 copy-start.8
  24.7 0.0 copy-start.4
  24.7 2.3 %copy-done.4 = bf16[1024,2048]{1,0:T(8,128)(2,1)S(1)} copy-done((bf16[1024,2048]{1,0:T(8,128)(2,1)S(1)}, bf16[1024,2048]{1,0:T(8,128)(2,1)}, u32[]{:S(2)}) %copy-start.4) | copy-done | bytes 4194328
  26.9 0.0 copy-start.6
  26.9 2.2 %copy-done.6 = bf16[1024,2048]{1,0:T(8,128)(2,1)S(1)} copy-done((bf16[1024,2048]{1,0:T(8,128)(2,1)S(1)}, bf16[1024,2048]{1,0:T(8,128)(2,1)}, u32[]{:S(2)}) %copy-start.6) | copy-done | bytes 4194328
  29.1 2.6 %cross.1 = f32[4,32,256]{2,1,0:T(8,128)S(1)} custom-call(f32[32,16,128]{2,1,0:T(8,128)S(1)} %bitcast.12, bf16[1024,2048]{1,0:T(8,128)(2,1)S(1)} %copy-done.4, bf16[1024,2048]{1,0:T(8,128)(2,1)S(1)} %copy-done.6), custom_call_target="tpu_custom_call" | custom-call | tf_op jit(solution)/shard_map/cross/pallas_call | solution.py:186
  31.8 11.0 %all_to_all.10.pieces_ref = f32[4,32,256]{2,1,0:T(8,128)} all-to-all(f32[4,32,256]{2,1,0:T(8,128)S(1)} %cross.1), channel_id=1, replica_groups=mesh['row'=8,'col'=4] {'col'}, dimensions={0} | all-to-all | bytes 262144 | tf_op jit(solution)/shard_map/all_to_all | solution.py:397
  42.8 1.6 %slab.1.own_ref = f32[40,256]{1,0:T(8,128)} custom-call(f32[4,32,256]{2,1,0:T(8,128)} %all_to_all.10.pieces_ref, f32[1,1,128]{2,1,0:T(1,128)} %get-tuple-element.12.error_ref), custom_call_target="tpu_custom_call" | custom-call | tf_op jit(solution)/shard_map/slab/pallas_call | solution.py:212
  44.4 1.4 %collective-permute-start = (f32[40,256]{1,0:T(8,128)}, f32[40,256]{1,0:T(8,128)S(1)}, u32[]{:S(2)}, u32[]{:S(2)}) collective-permute-start(f32[40,256]{1,0:T(8,128)} %slab.1.own_ref), channel_id=1, source_target_pairs={{0,0},{1,4},{2,8},{3,12},{4,16},{5,20},{6,24},{7,28},{8,1},{9,5},{... | collective-permute-start | bytes 122888 | tf_op jit(solution)/shard_map/ppermute | solution.py:400
  45.8 0.0 collective-permute-done
  45.8 17.3 %all-gather = f32[320,256]{1,0:T(8,128)} all-gather(f32[40,256]{1,0:T(8,128)S(1)} %collective-permute-done), channel_id=2, replica_groups=mesh['row'=8,'col'=4] {'row'}, dimensions={0}, use_global_device_ids=true | all-gather | bytes 368640 | tf_op jit(solution)/shard_map/all_gather | solution.py:400
  63.1 0.0 copy-done.8
  63.1 2.2 %term.1 = f32[32,384]{1,0:T(8,128)} custom-call(f32[40,256]{1,0:T(8,128)} %slab.1.own_ref, f32[8,40,256]{2,1,0:T(8,128)} %bitcast.10, f32[32,16,128]{2,1,0:T(8,128)} %bitcast.13), custom_call_target="tpu_custom_call" | custom-call | tf_op jit(solution)/shard_map/term/pallas_call | solution.py:242
  65.4 13.8 %all-gather.1 = f32[128,384]{1,0:T(8,128)S(1)} all-gather(f32[32,384]{1,0:T(8,128)} %term.1), channel_id=3, replica_groups=mesh['row'=8,'col'=4] {'col'}, dimensions={0}, use_global_device_ids=true | all-gather | bytes 245760 | tf_op jit(solution)/shard_map/all_gather | solution.py:401
  79.2 0.0 copy-done.9
  79.2 0.0 copy-start.2
  79.2 3.4 %copy-done.2 = f32[1024,2048]{1,0:T(8,128)S(1)} copy-done((f32[1024,2048]{1,0:T(8,128)S(1)}, f32[1024,2048]{1,0:T(8,128)}, u32[]{:S(2)}) %copy-start.2) | copy-done | bytes 8388632
  82.6 0.0 copy-start.7
  82.6 1.0 %copy-done.7 = f32[320,256]{1,0:T(8,128)S(1)} copy-done((f32[320,256]{1,0:T(8,128)S(1)}, f32[320,256]{1,0:T(8,128)}, u32[]{:S(2)}) %copy-start.7) | copy-done | bytes 327704
  83.5 5.4 %update.1 = (f32[2,128]{1,0:T(2,128)}, f32[1024,2048]{1,0:T(8,128)}) custom-call(f32[4,32,384]{2,1,0:T(8,128)S(1)} %bitcast.14, f32[8,40,256]{2,1,0:T(8,128)S(1)} %bitcast.11, f32[64,128]{1,0:T(8,128)S(1)} %copy-done.9, f32[1024,2048]{1,0:T(8,128)S(1)} %copy-done.2), custom_call_target="tpu_custom_call" | custom-call | tf_op jit(solution)/shard_map/update/pallas_call | solution.py:310
Async XLA Ops:
  4.9 19.8 %all-to-all-start = ((f32[32,1,16,128]{3,2,1,0:T(8,128)}), f32[32,1,16,128]{3,2,1,0:T(8,128)S(1)}, u32[]{:S(2)}, u32[]{:S(2)}) async-start(f32[32,1,16,128]{3,2,1,0:T(8,128)} %get-tuple-element.9), calls=%async_computation | async-start | bytes 524288 | tf_op jit(solution)/shard_map/all_to_all | solution.py:393
  12.2 3.4 %copy-start = (f32[1024,2048]{1,0:T(8,128)S(1)}, f32[1024,2048]{1,0:T(8,128)}, u32[]{:S(2)}) copy-start(f32[1024,2048]{1,0:T(8,128)} %cov_ref.1) | copy-start | bytes 25165828
  15.6 63.6 %copy-start.9 = (f32[64,128]{1,0:T(8,128)S(1)}, f32[64,128]{1,0:T(8,128)}, u32[]{:S(2)}) copy-start(f32[64,128]{1,0:T(8,128)} %weight_ref.3) | copy-start | bytes 98308
  17.3 3.4 %copy-start.1 = (f32[1024,2048]{1,0:T(8,128)}, f32[1024,2048]{1,0:T(8,128)S(1)}, u32[]{:S(2)}) copy-start(f32[1024,2048]{1,0:T(8,128)S(1)} %get-tuple-element.13.cov_ref) | copy-start | bytes 25165828
  20.7 2.0 %copy-start.3 = (bf16[1024,2048]{1,0:T(8,128)(2,1)}, bf16[1024,2048]{1,0:T(8,128)(2,1)S(1)}, u32[]{:S(2)}) copy-start(bf16[1024,2048]{1,0:T(8,128)(2,1)S(1)} %get-tuple-element.10.hi_ref) | copy-start | bytes 12582916
  22.7 2.0 %copy-start.5 = (bf16[1024,2048]{1,0:T(8,128)(2,1)}, bf16[1024,2048]{1,0:T(8,128)(2,1)S(1)}, u32[]{:S(2)}) copy-start(bf16[1024,2048]{1,0:T(8,128)(2,1)S(1)} %get-tuple-element.11.lo_ref) | copy-start | bytes 12582916
  24.7 38.5 %copy-start.8 = (f32[32,1,16,128]{3,2,1,0:T(8,128)}, f32[32,1,16,128]{3,2,1,0:T(8,128)S(1)}, u32[]{:S(2)}) copy-start(f32[32,1,16,128]{3,2,1,0:T(8,128)S(1)} %all-to-all-done) | copy-start | bytes 786436
  24.7 2.3 %copy-start.4 = (bf16[1024,2048]{1,0:T(8,128)(2,1)S(1)}, bf16[1024,2048]{1,0:T(8,128)(2,1)}, u32[]{:S(2)}) copy-start(bf16[1024,2048]{1,0:T(8,128)(2,1)} %copy-done.3) | copy-start | bytes 12582916
  26.9 2.2 %copy-start.6 = (bf16[1024,2048]{1,0:T(8,128)(2,1)S(1)}, bf16[1024,2048]{1,0:T(8,128)(2,1)}, u32[]{:S(2)}) copy-start(bf16[1024,2048]{1,0:T(8,128)(2,1)} %copy-done.5) | copy-start | bytes 12582916
  44.4 1.4 %collective-permute-start = (f32[40,256]{1,0:T(8,128)}, f32[40,256]{1,0:T(8,128)S(1)}, u32[]{:S(2)}, u32[]{:S(2)}) collective-permute-start(f32[40,256]{1,0:T(8,128)} %slab.1.own_ref), channel_id=1, source_target_pairs={{0,0},{1,4},{2,8},{3,12},{4,16},{5,20},{6,24},{7,28},{8,1},{9,5},{... | collective-permute-start | bytes 122888 | tf_op jit(solution)/shard_map/ppermute | solution.py:400
  79.2 3.4 %copy-start.2 = (f32[1024,2048]{1,0:T(8,128)S(1)}, f32[1024,2048]{1,0:T(8,128)}, u32[]{:S(2)}) copy-start(f32[1024,2048]{1,0:T(8,128)} %copy-done.1) | copy-start | bytes 25165828
  82.6 1.0 %copy-start.7 = (f32[320,256]{1,0:T(8,128)S(1)}, f32[320,256]{1,0:T(8,128)}, u32[]{:S(2)}) copy-start(f32[320,256]{1,0:T(8,128)} %all-gather) | copy-start | bytes 983044

commit v4 on v3

v4 whole, which is shorter than its diff:
```python
import functools
import math

import jax
import jax.numpy as jnp
from jax import lax
from jax.experimental import pallas as pl
from jax.experimental.pallas import tpu as pltpu
from jax.sharding import PartitionSpec as P

NEWTON = 4
LANES = 128
SUBLANES = 8


forget = 0.98
highest = lax.Precision.HIGHEST
f32 = jnp.float32
bf16 = jnp.bfloat16


def dot(left, right, contract, precision=None):
    return lax.dot_general(
        left, right, (contract, ((), ())), precision=precision, preferred_element_type=f32
    )


def split3(x):
    hi = x.astype(bf16)
    rest = x - hi.astype(f32)
    mid = rest.astype(bf16)
    lo = (rest - mid.astype(f32)).astype(bf16)
    return hi, mid, lo


def split2(x):
    hi = x.astype(bf16)
    return hi, (x - hi.astype(f32)).astype(bf16)


def network_kernel(
    types_ref,
    ids_ref,
    switch_ref,
    env_ref,
    force_ref,
    target_ref,
    embed_ref,
    weight_ref,
    out_weight_ref,
    payload_ref,
    error_ref,
    mix_ref,
    *,
    plan,
):
    neighbours, atoms = ids_ref.shape
    n_types = embed_ref.shape[0]
    height = min(64, atoms)
    for start in range(0, atoms, height):
        atom_at = lax.broadcasted_iota(jnp.int32, (height, atoms), 0) + start
        total = jnp.zeros((height, atoms), f32)
        for k in range(neighbours):
            total = total + jnp.where(ids_ref[k : k + 1, :] == atom_at, switch_ref[k : k + 1, :], 0.0)
        mix_ref[start : start + height, :] = total
    mix = mix_ref[...]
    type_at = lax.broadcasted_iota(jnp.int32, (n_types, atoms), 0)
    onehot = (types_ref[...] == type_at).astype(f32)
    mixed = env_ref[...] + dot(embed_ref[...], onehot, ((0,), (0,)), highest)
    descriptor = dot(mixed, mix, ((1,), (0,)), highest) * (1.0 / math.sqrt(neighbours))
    hidden = jnp.tanh(descriptor)
    activity = jnp.tanh(dot(hidden, weight_ref[...], ((0,), (0,)), highest))
    out_weight = out_weight_ref[...]
    scale = 1.0 / math.sqrt(atoms)
    force = force_ref[...]
    weighted = dot(force, activity, ((1,), (0,)), highest)
    predicted = jnp.sum(weighted * out_weight, axis=1, keepdims=True) * scale
    slopes = out_weight * (1.0 - activity * activity)
    jacobian = dot(hidden * force, slopes, ((1,), (0,)), highest) * scale
    error_ref[...] = jnp.broadcast_to(target_ref[...] - predicted, error_ref.shape)
    for block, pieces in enumerate(plan):
        at = 0
        for start, size in pieces:
            payload_ref[block, at : at + size, :] = jacobian[start : start + size, :]
            at += size


def network(
    plan, atom_types, neighbor_ids, switching, environment, force_weights, targets, type_embed, layer_weight, out_weight
):
    per_dev, neighbours, atoms = neighbor_ids.shape
    hin, width = layer_weight.shape
    blocks, rows = len(plan), sum(size for _, size in plan[0])

    def per_stream(*shape):
        return pl.BlockSpec((None,) + shape, lambda s: (s,) + (0,) * len(shape))

    def shared(shape):
        return pl.BlockSpec(shape, lambda s: (0,) * len(shape))

    return pl.pallas_call(
        functools.partial(network_kernel, plan=plan),
        grid=(per_dev,),
        in_specs=[
            per_stream(1, atoms),
            per_stream(neighbours, atoms),
            per_stream(neighbours, atoms),
            per_stream(hin, atoms),
            per_stream(1, atoms),
            per_stream(1, 1),
            shared(type_embed.shape),
            shared(layer_weight.shape),
            shared((1, width)),
        ],
        out_specs=[
            pl.BlockSpec((blocks, None, rows, width), lambda s: (0, s, 0, 0)),
            per_stream(1, width),
        ],
        out_shape=[
            jax.ShapeDtypeStruct((blocks, per_dev, rows, width), f32),
            jax.ShapeDtypeStruct((per_dev, 1, width), f32),
        ],
        scratch_shapes=[pltpu.VMEM((atoms, atoms), f32)],
        name="network",
    )(
        atom_types.reshape(per_dev, 1, atoms),
        neighbor_ids,
        switching,
        environment.swapaxes(1, 2),
        force_weights.reshape(per_dev, 1, atoms),
        targets.reshape(per_dev, 1, 1),
        type_embed,
        layer_weight,
        out_weight.reshape(1, width),
    )


def in_hbm(x):
    return pltpu.with_memory_space_constraint(x, pltpu.HBM)


def stage_kernel(cov_ref, hi_ref, lo_ref):
    hi_ref[...], lo_ref[...] = split2(cov_ref[...])


def stage(covariance):
    rows, cols = covariance.shape
    height = rows // 8
    block = pl.BlockSpec((height, cols), lambda n: (n, 0))
    return pl.pallas_call(
        stage_kernel,
        grid=(rows // height,),
        in_specs=[block],
        out_specs=[block] * 2,
        out_shape=[pltpu.HBM((rows, cols), bf16)] * 2,
        compiler_params=pltpu.CompilerParams(vmem_limit_bytes=16 << 20),
        name="stage",
    )(in_hbm(covariance))


def five_products(parts, hi, lo, contract):
    streams = parts.shape[0] // 3
    by_hi = dot(parts, hi, contract)
    by_lo = dot(parts[0 : 2 * streams], lo, contract)
    return by_hi[0:streams] + (
        by_hi[streams : 2 * streams] + by_lo[0:streams] + (by_hi[2 * streams :] + by_lo[streams:])
    )


def cross_kernel(jac_ref, error_ref, hi_ref, lo_ref, row_ref, col_ref, parts_ref, row_parts_ref, sum_ref, term_ref, *, col_rows):
    streams, rows, lanes = jac_ref.shape
    slab, tile_cols = hi_ref.shape
    slab_rows = slab // lanes
    step = pl.program_id(0)
    flat = jac_ref.reshape(streams * rows, lanes)

    @pl.when(step == 0)
    def _():
        term_ref[...] = jnp.zeros_like(term_ref)
        sum_ref[...] = jnp.zeros_like(sum_ref)
        for i in range(col_rows):
            parts = split3(flat[pl.ds(i, streams, stride=rows), :])
            for n, part in enumerate(parts):
                parts_ref[n * streams : (n + 1) * streams, i * lanes : (i + 1) * lanes] = part

    hi, lo = hi_ref[...], lo_ref[...]
    cross = five_products(parts_ref[...], hi, lo, ((1,), (1,)))
    row_ref[...] = cross
    term = jnp.zeros((streams, streams), f32)
    for i in range(slab_rows):
        own = flat[pl.ds(col_rows + step * slab_rows + i, streams, stride=rows), :]
        term = term + dot(own, cross[:, i * lanes : (i + 1) * lanes], ((1,), (1,)), highest)
        for n, part in enumerate(split3(own)):
            row_parts_ref[n * streams : (n + 1) * streams, i * lanes : (i + 1) * lanes] = part
    term_ref[:, 0:streams] += term
    sum_ref[...] += five_products(row_parts_ref[...], hi, lo, ((1,), (0,)))

    @pl.when(step == pl.num_programs(0) - 1)
    def _():
        own_at = lax.axis_index("row") * lax.axis_size("col") + lax.axis_index("col")
        stream_at = lax.broadcasted_iota(jnp.int32, (streams, lanes), 0)
        lane_at = lax.broadcasted_iota(jnp.int32, (streams, lanes), 1)
        error = jnp.where((stream_at == own_at) & (lane_at >= streams), error_ref[0], 0.0)
        beside = term_ref[...] + error
        for n in range(tile_cols // slab):
            col_ref[n, :, 0:slab] = sum_ref[:, n * slab : (n + 1) * slab]
            col_ref[n, :, slab:] = beside


def cross_partial(jac, error, hi, lo, slab):
    streams = jac.shape[0]
    tile_rows, tile_cols = hi.shape
    col_slabs = tile_cols // slab
    block = pl.BlockSpec((slab, tile_cols), lambda n: (n, 0))
    return pl.pallas_call(
        functools.partial(cross_kernel, col_rows=tile_cols // LANES),
        grid=(tile_rows // slab,),
        in_specs=[
            pl.BlockSpec(jac.shape, lambda n: (0, 0, 0)),
            pl.BlockSpec(error.shape, lambda n: (0, 0, 0)),
            block,
            block,
        ],
        out_specs=[
            pl.BlockSpec((None, streams, slab), lambda n: (n, 0, 0)),
            pl.BlockSpec((col_slabs, streams, slab + LANES), lambda n: (0, 0, 0)),
        ],
        out_shape=[
            jax.ShapeDtypeStruct((tile_rows // slab, streams, slab), f32),
            jax.ShapeDtypeStruct((col_slabs, streams, slab + LANES), f32),
        ],
        scratch_shapes=[
            pltpu.VMEM((3 * streams, tile_cols), bf16),
            pltpu.VMEM((3 * streams, slab), bf16),
            pltpu.VMEM((streams, tile_cols), f32),
            pltpu.VMEM((streams, LANES), f32),
        ],
        compiler_params=pltpu.CompilerParams(vmem_limit_bytes=32 << 20),
        name="cross",
    )(jac, error, in_hbm(hi), in_hbm(lo))


def slab_kernel(rows_ref, cols_ref, row_ref, col_ref):
    slab = rows_ref.shape[2]
    row = rows_ref[0]
    for n in range(1, rows_ref.shape[0]):
        row = row + rows_ref[n]
    col = cols_ref[0]
    for n in range(1, cols_ref.shape[0]):
        col = col + cols_ref[n]
    for n in range(row_ref.shape[0]):
        row_ref[n, :, 0:slab] = row
        row_ref[n, :, slab:] = col[:, slab:]
    for n in range(col_ref.shape[0]):
        col_ref[n] = col[:, 0:slab]


def slab_sums(row_pieces, col_pieces):
    rows_n, streams, slab = row_pieces.shape
    cols_n, _, padded = col_pieces.shape
    return pl.pallas_call(
        slab_kernel,
        out_shape=[
            jax.ShapeDtypeStruct((rows_n, streams, padded), f32),
            jax.ShapeDtypeStruct((cols_n, streams, slab), f32),
        ],
        name="slab",
    )(row_pieces, col_pieces)


def invert(innovation):
    streams = innovation.shape[0]
    row = lax.broadcasted_iota(jnp.int32, (streams, streams), 0)
    col = lax.broadcasted_iota(jnp.int32, (streams, streams), 1)
    identity = (row == col).astype(f32)
    innovation = innovation + forget * identity
    sums = jnp.sum(jnp.abs(innovation), axis=1, keepdims=True)
    bound = jnp.max(sums, axis=0, keepdims=True)
    power = identity - innovation / bound
    inverse = identity + power
    for repeat in range(NEWTON - 1):
        power = dot(power, power, ((1,), (0,)), highest)
        inverse = inverse + dot(inverse, power, ((1,), (0,)), highest)
    return inverse / bound


def update_kernel(
    rows_ref, cols_ref, weight_ref, cov_ref, new_weight_ref, new_cov_ref, right_ref, tile_ref, in_sems, out_sems
):
    slabs, streams, _ = rows_ref.shape
    col_slabs, _, slab = cols_ref.shape
    lanes = weight_ref.shape[1]
    reads = []
    for n in range(slabs):
        here = pl.ds(n * slab, slab)
        reads.append(pltpu.make_async_copy(cov_ref.at[here], tile_ref.at[here], in_sems.at[n]))
        reads[-1].start()
    beside = rows_ref[0, :, slab:]
    for n in range(1, slabs):
        beside = beside + rows_ref[n, :, slab:]
    inverse = invert(beside[:, 0:streams])
    errors = beside[:, streams : streams + 1]
    for n in range(col_slabs):
        hi, mid, lo = split3(cols_ref[n])
        for m, part in enumerate((hi, mid, lo, hi, mid, hi)):
            right_ref[m * streams : (m + 1) * streams, n * slab : (n + 1) * slab] = part
    col_at = lax.axis_index("col")
    own_at = (lax.axis_index("row") * slabs + col_at) * (slab // lanes)
    writes = []
    for n in range(slabs):
        gain = dot(inverse, rows_ref[n, :, 0:slab], ((0,), (0,)), highest)
        hi, mid, lo = split3(gain)
        left = jnp.concatenate([hi, hi, hi, mid, mid, lo], axis=0)
        update = dot(left, right_ref[...], ((0,), (0,)))
        here = pl.ds(n * slab, slab)
        reads[n].wait()
        tile_ref[here, :] = (tile_ref[here, :] - update) * (1.0 / forget)
        writes.append(pltpu.make_async_copy(tile_ref.at[here], new_cov_ref.at[here], out_sems.at[n]))
        writes[-1].start()

        @pl.when(col_at == n)
        def _():
            moved = jnp.sum(gain * errors, axis=0, keepdims=True)
            for i in range(slab // lanes):
                own = weight_ref[pl.ds(own_at + i, 1), :]
                new_weight_ref[i : i + 1, :] = own + moved[:, i * lanes : (i + 1) * lanes]

    for write in writes:
        write.wait()


def update(row_slabs, col_slabs, layer_weight, covariance):
    slabs, streams, _ = row_slabs.shape
    slab = col_slabs.shape[2]
    tile_rows, tile_cols = covariance.shape
    width = layer_weight.shape[1]
    whole = pl.BlockSpec(memory_space=pltpu.VMEM)
    beyond = pl.BlockSpec(memory_space=pl.ANY)
    return pl.pallas_call(
        update_kernel,
        in_specs=[whole, whole, whole, beyond],
        out_specs=[whole, beyond],
        out_shape=[
            jax.ShapeDtypeStruct((slab // width, width), f32),
            jax.ShapeDtypeStruct((tile_rows, tile_cols), f32),
        ],
        scratch_shapes=[
            pltpu.VMEM((6 * streams, tile_cols), bf16),
            pltpu.VMEM((tile_rows, tile_cols), f32),
            pltpu.SemaphoreType.DMA((slabs,)),
            pltpu.SemaphoreType.DMA((slabs,)),
        ],
        compiler_params=pltpu.CompilerParams(vmem_limit_bytes=32 << 20),
        name="update",
    )(row_slabs, col_slabs, layer_weight, in_hbm(covariance))


def plain_steps(at, jac_all, errors, layer_weight, covariance, slab, cols_n):
    streams = jac_all.shape[0]
    hin, width = layer_weight.shape
    tile_rows, tile_cols = covariance.shape
    first = (at[0] * cols_n + at[1]) * slab
    jacobian = jac_all[:, 0:hin, :].reshape(streams, hin * width)
    jac_cols = lax.dynamic_slice_in_dim(jacobian, at[1] * tile_cols, tile_cols, 1)
    partial = dot(jac_cols, covariance, ((1,), (1,)), highest)
    cross_own = lax.psum_scatter(partial, "col", scatter_dimension=1, tiled=True)
    cross = lax.all_gather(cross_own, ("row", "col"), axis=1, tiled=True)
    inverse = invert(dot(jacobian, cross, ((1,), (1,)), highest))
    gain = dot(inverse, lax.dynamic_slice_in_dim(cross, at[0] * tile_rows, tile_rows, 1), ((0,), (0,)), highest)
    across = lax.dynamic_slice_in_dim(cross, at[1] * tile_cols, tile_cols, 1)
    new_cov = (covariance - dot(gain, across, ((0,), (0,)), highest)) / forget
    own_gain = lax.dynamic_slice_in_dim(gain, at[1] * slab, slab, 1)
    own_weight = lax.dynamic_slice_in_dim(layer_weight.reshape(-1), first, slab, 0)
    new_weight = own_weight + dot(errors, own_gain, ((0,), (0,)), highest)
    return new_weight, new_cov


def exchange(x, axes):
    return lax.all_to_all(x, axes, split_axis=0, concat_axis=0, tiled=True)


def on_device(
    atom_types,
    neighbor_ids,
    switching,
    environment,
    force_weights,
    targets,
    type_embed,
    layer_weight,
    out_weight,
    covariance,
):
    rows_n = lax.axis_size("row")
    cols_n = lax.axis_size("col")
    at = jnp.stack([lax.axis_index("row"), lax.axis_index("col")]).astype(jnp.int32)
    tile_rows, tile_cols = covariance.shape
    slab = tile_rows // cols_n
    hin, width = layer_weight.shape
    run_network = functools.partial(
        network,
        atom_types=atom_types,
        neighbor_ids=neighbor_ids,
        switching=switching,
        environment=environment,
        force_weights=force_weights,
        targets=targets,
        type_embed=type_embed,
        layer_weight=layer_weight,
        out_weight=out_weight,
    )
    streams = rows_n * cols_n * atom_types.shape[0]
    kernels = (
        atom_types.shape[0] == 1
        and width == LANES
        and slab % LANES == 0
        and tile_rows % (SUBLANES * LANES) == 0
        and tile_cols % (SUBLANES * LANES) == 0
        and rows_n * slab == tile_cols
        and streams < LANES
    )
    if not kernels:
        payload, error = run_network([[(0, hin)]])
        jac_all = lax.all_gather(payload[0], ("row", "col"), axis=0, tiled=True)
        errors = lax.all_gather(error[:, 0, 0], ("row", "col"), axis=0, tiled=True)
        return plain_steps(at, jac_all, errors, layer_weight, covariance, slab, cols_n)
    row_size, col_size = tile_rows // LANES, tile_cols // LANES
    plan = [[(c * col_size, col_size), (r * row_size, row_size)] for r in range(rows_n) for c in range(cols_n)]
    payload, error = run_network(plan)
    jac = exchange(payload, ("row", "col"))
    jac = jac.reshape(-1, *jac.shape[2:])
    hi, lo = stage(covariance)
    row_part, col_part = cross_partial(jac, error, hi, lo, slab)
    row_own, col_own = slab_sums(exchange(row_part, "col"), exchange(col_part, "row"))
    row_slabs, col_slabs = exchange(row_own, "col"), exchange(col_own, "row")
    new_weight, new_cov = update(row_slabs, col_slabs, layer_weight, covariance)
    return new_weight.reshape(-1), new_cov


def solution(mesh):
    in_specs = (
        P(("row", "col"), None),
        P(("row", "col"), None, None),
        P(("row", "col"), None, None),
        P(("row", "col"), None, None),
        P(("row", "col"), None),
        P(("row", "col")),
        P(),
        P(),
        P(),
        P("row", "col"),
    )
    out_specs = (P(("row", "col")), P("row", "col"))
    return jax.shard_map(
        on_device, mesh=mesh, in_specs=in_specs, out_specs=out_specs, check_vma=False
    )
```

time: 89.5 us -> 86.6 us (0.968)
  local copies, waits for them, and re-layouts: 19.5 us -> 0.01 us
  Pallas kernels: 17.2 us -> 31.8 us
  waiting for transfers between devices: 0.01 us -> 2.86 us
  starting transfers between devices: 8.72 us -> 7.3 us
    all_to_all x1 -> x4, blocking collectives: 11 us -> 42.5 us  [exchange(): return lax.all_to_all(x, axes, split_axis=0, concat_axis=0, tiled=True)]
    all_gather x2 -> x0, blocking collectives: 31.1 us -> none  [the longest x1 17.3 us: on_device(): lax.all_gather(lax.ppermute(own, ('row', 'col'), to_col), 'row', axis=0,...]
    unnamed x20 -> x4, local copies, waits for them, and re-layouts: 19.5 us -> 0.01 us
    pallas_call x6 -> x5, Pallas kernels: 17.2 us -> 31.8 us  [the longest x1 9.05 us: cross_partial(): pl.pallas_call(functools.partial(cross_kernel, col_rows=tile_cols // LANE...]
    all_to_all x1, waiting for transfers between devices: 0.01 us -> 2.86 us  [exchange(): return lax.all_to_all(x, axes, split_axis=0, concat_axis=0, tiled=True)]
    ppermute x1 -> x0, starting transfers between devices: 1.42 us -> none  [on_device(): lax.ppermute(own, ('row', 'col'), to_col)]
  transfers between devices with their start and end apart: 2 -> 1, of which waited for: 0 -> 1; matrix products, arithmetic and copies ran while one was open for 0% -> 0% of each run, Pallas kernels for 2% -> 10%
where the time goes in v4:
time: 86.6 us; the launch traced here: 85.8 us
  blocking collectives  42.5 us (49%)
  Pallas kernels  31.8 us (37%)
  starting transfers between devices  7.3 us (8%)
  waiting for transfers between devices  2.86 us (3%)
  between operations  1.31 us (2%)
    all_to_all x4, blocking collectives, exchange(): return lax.all_to_all(x, axes, split_axis=0, concat_axis=0, tiled=True)  42.5 us
    pallas_call x1, Pallas kernels, cross_partial(): pl.pallas_call(functools.partial(cross_kernel, col_rows=tile_cols // LANE...  9.05 us
    pallas_call x1, Pallas kernels, stage(): pl.pallas_call(stage_kernel, grid=(rows // height,), in_specs=[block], ou...  8.95 us
    pallas_call x1, Pallas kernels, update(): pl.pallas_call(update_kernel, in_specs=[whole, whole, whole, beyond], out...  8.32 us
    all_to_all x1, starting transfers between devices, exchange(): return lax.all_to_all(x, axes, split_axis=0, concat_axis=0, tiled=True)  7.3 us
    pallas_call x1, Pallas kernels, network(): pl.pallas_call(functools.partial(network_kernel, plan=plan), grid=(per_de...  3.63 us
    all_to_all x1, waiting for transfers between devices, exchange(): return lax.all_to_all(x, axes, split_axis=0, concat_axis=0, tiled=True)  2.86 us
    pallas_call x1, Pallas kernels, slab_sums(): pl.pallas_call(slab_kernel, out_shape=[jax.ShapeDtypeStruct((rows_n, stre...  1.86 us
  transfers between devices with their start and end apart: 1, of which 1 were waited for; matrix products, arithmetic and copies ran while one was open for 0% of the time, Pallas kernels for 10%

profile of v4, /device:TPU:0, one launch (start us, length us, event | category | flops | bytes accessed | tf_op | source)
XLA Modules:
  0.0 85.8 jit_solution(11727676533134071513)
XLA Ops:
  1.3 3.6 %network.1 = (f32[32,1,24,128]{3,2,1,0:T(8,128)}, f32[1,1,128]{2,1,0:T(1,128)}) custom-call(s32[1,1,256]{2,1,0:T(1,128)} %bitcast.10, s32[1,32,256]{2,1,0:T(8,128)} %ids_ref.1, f32[1,32,256]{2,1,0:T(8,128)} %switch_ref.1, f32[1,64,256]{2,1,0:T(8,128)} %bitcast.9, f32[1,1,256]{2,1,0:T(1,128)} %bitcast.11, f32[1,1,1]{2,1,0:T(1,128)} %bitcast.7.target_ref, ...), custom_call_target="tpu_custom_call" | custom-call | tf_op jit(solution)/shard_map/network/pallas_call | solution.py:101
  4.9 0.0 copy-start.1
  4.9 7.3 %all-to-all-start = ((f32[32,1,24,128]{3,2,1,0:T(8,128)}), f32[32,1,24,128]{3,2,1,0:T(8,128)S(1)}, u32[]{:S(2)}, u32[]{:S(2)}) async-start(f32[32,1,24,128]{3,2,1,0:T(8,128)} %get-tuple-element.12), calls=%async_computation | async-start | bytes 786432 | tf_op jit(solution)/shard_map/all_to_all | solution.py:379
  12.2 0.0 copy-start
  12.2 9.0 %stage.1 = (bf16[1024,2048]{1,0:T(8,128)(2,1)}, bf16[1024,2048]{1,0:T(8,128)(2,1)}) custom-call(f32[1024,2048]{1,0:T(8,128)} %cov_ref.3), custom_call_target="tpu_custom_call" | custom-call | tf_op jit(solution)/shard_map/stage/pallas_call | solution.py:150
  21.2 2.9 %all-to-all-done = f32[32,1,24,128]{3,2,1,0:T(8,128)S(1)} async-done(((f32[32,1,24,128]{3,2,1,0:T(8,128)}), f32[32,1,24,128]{3,2,1,0:T(8,128)S(1)}, u32[]{:S(2)}, u32[]{:S(2)}) %all-to-all-start) | async-done | bytes 393248 | tf_op jit(solution)/shard_map/all_to_all | solution.py:379
  24.0 0.0 copy-done.1
  24.0 9.0 %cross.1 = (f32[4,32,256]{2,1,0:T(8,128)S(1)}, f32[8,32,384]{2,1,0:T(8,128)S(1)}) custom-call(f32[32,24,128]{2,1,0:T(8,128)S(1)} %bitcast.8, f32[1,1,128]{2,1,0:T(1,128)S(1)} %copy-done.1, bf16[1024,2048]{1,0:T(8,128)(2,1)} %get-tuple-element.14.hi_ref, bf16[1024,2048]{1,0:T(8,128)(2,1)} %get-tuple-element.15.lo_ref), custom_call_target="tpu_custom_call" | custom-call | tf_op jit(solution)/shard_map/cross/pallas_call | solution.py:215
  33.1 10.3 %all_to_all.25.rows_ref = f32[4,32,256]{2,1,0:T(8,128)} all-to-all(f32[4,32,256]{2,1,0:T(8,128)S(1)} %get-tuple-element.16), channel_id=1, replica_groups=mesh['row'=8,'col'=4] {'col'}, dimensions={0} | all-to-all | bytes 262144 | tf_op jit(solution)/shard_map/all_to_all | solution.py:379
  43.4 11.4 %all_to_all.26.cols_ref = f32[8,32,384]{2,1,0:T(8,128)} all-to-all(f32[8,32,384]{2,1,0:T(8,128)S(1)} %get-tuple-element.17), channel_id=1, replica_groups=mesh['row'=8,'col'=4] {'row'}, dimensions={0} | all-to-all | bytes 786432 | tf_op jit(solution)/shard_map/all_to_all | solution.py:379
  54.8 1.9 %slab.1 = (f32[4,32,384]{2,1,0:T(8,128)}, f32[8,32,256]{2,1,0:T(8,128)}) custom-call(f32[4,32,256]{2,1,0:T(8,128)} %all_to_all.25.rows_ref, f32[8,32,384]{2,1,0:T(8,128)} %all_to_all.26.cols_ref), custom_call_target="tpu_custom_call" | custom-call | tf_op jit(solution)/shard_map/slab/pallas_call | solution.py:261
  56.6 10.3 %all_to_all.27.cols_ref = f32[8,32,256]{2,1,0:T(8,128)S(1)} all-to-all(f32[8,32,256]{2,1,0:T(8,128)} %get-tuple-element.19), channel_id=1, replica_groups=mesh['row'=8,'col'=4] {'row'}, dimensions={0} | all-to-all | bytes 524288 | tf_op jit(solution)/shard_map/all_to_all | solution.py:379
  66.9 10.6 %all_to_all.28.rows_ref = f32[4,32,384]{2,1,0:T(8,128)S(1)} all-to-all(f32[4,32,384]{2,1,0:T(8,128)} %get-tuple-element.18), channel_id=1, replica_groups=mesh['row'=8,'col'=4] {'col'}, dimensions={0} | all-to-all | bytes 393216 | tf_op jit(solution)/shard_map/all_to_all | solution.py:379
  77.5 0.0 copy-done
  77.5 8.3 %update.1 = (f32[2,128]{1,0:T(2,128)}, f32[1024,2048]{1,0:T(8,128)}) custom-call(f32[4,32,384]{2,1,0:T(8,128)S(1)} %all_to_all.28.rows_ref, f32[8,32,256]{2,1,0:T(8,128)S(1)} %all_to_all.27.cols_ref, f32[64,128]{1,0:T(8,128)S(1)} %copy-done, f32[1024,2048]{1,0:T(8,128)} %cov_ref.3), custom_call_target="tpu_custom_call" | custom-call | tf_op jit(solution)/shard_map/update/pallas_call | solution.py:339
Async XLA Ops:
  4.9 19.1 %copy-start.1 = (f32[1,1,128]{2,1,0:T(1,128)S(1)}, f32[1,1,128]{2,1,0:T(1,128)}, u32[]{:S(2)}) copy-start(f32[1,1,128]{2,1,0:T(1,128)} %get-tuple-element.13.error_ref) | copy-start | bytes 1540
  4.9 19.1 %all-to-all-start = ((f32[32,1,24,128]{3,2,1,0:T(8,128)}), f32[32,1,24,128]{3,2,1,0:T(8,128)S(1)}, u32[]{:S(2)}, u32[]{:S(2)}) async-start(f32[32,1,24,128]{3,2,1,0:T(8,128)} %get-tuple-element.12), calls=%async_computation | async-start | bytes 786432 | tf_op jit(solution)/shard_map/all_to_all | solution.py:379
  12.2 65.3 %copy-start = (f32[64,128]{1,0:T(8,128)S(1)}, f32[64,128]{1,0:T(8,128)}, u32[]{:S(2)}) copy-start(f32[64,128]{1,0:T(8,128)} %weight_ref.3) | copy-start | bytes 98308

commit v5 on v4

--- a/solution.py
+++ b/solution.py
@@ -167,9 +167,9 @@
     )
 
 
-def cross_kernel(jac_ref, error_ref, hi_ref, lo_ref, row_ref, col_ref, parts_ref, row_parts_ref, sum_ref, term_ref, *, col_rows):
+def row_kernel(jac_ref, error_ref, hi_ref, lo_ref, cross_ref, beside_ref, parts_ref, term_ref, *, col_rows):
     streams, rows, lanes = jac_ref.shape
-    slab, tile_cols = hi_ref.shape
+    slab = hi_ref.shape[0]
     slab_rows = slab // lanes
     step = pl.program_id(0)
     flat = jac_ref.reshape(streams * rows, lanes)
@@ -177,23 +177,18 @@
     @pl.when(step == 0)
     def _():
         term_ref[...] = jnp.zeros_like(term_ref)
-        sum_ref[...] = jnp.zeros_like(sum_ref)
         for i in range(col_rows):
             parts = split3(flat[pl.ds(i, streams, stride=rows), :])
             for n, part in enumerate(parts):
                 parts_ref[n * streams : (n + 1) * streams, i * lanes : (i + 1) * lanes] = part
 
-    hi, lo = hi_ref[...], lo_ref[...]
-    cross = five_products(parts_ref[...], hi, lo, ((1,), (1,)))
-    row_ref[...] = cross
+    cross = five_products(parts_ref[...], hi_ref[...], lo_ref[...], ((1,), (1,)))
+    cross_ref[...] = cross
     term = jnp.zeros((streams, streams), f32)
     for i in range(slab_rows):
         own = flat[pl.ds(col_rows + step * slab_rows + i, streams, stride=rows), :]
         term = term + dot(own, cross[:, i * lanes : (i + 1) * lanes], ((1,), (1,)), highest)
-        for n, part in enumerate(split3(own)):
-            row_parts_ref[n * streams : (n + 1) * streams, i * lanes : (i + 1) * lanes] = part
     term_ref[:, 0:streams] += term
-    sum_ref[...] += five_products(row_parts_ref[...], hi, lo, ((1,), (0,)))
 
     @pl.when(step == pl.num_programs(0) - 1)
     def _():
@@ -202,18 +197,16 @@
         lane_at = lax.broadcasted_iota(jnp.int32, (streams, lanes), 1)
         error = jnp.where((stream_at == own_at) & (lane_at >= streams), error_ref[0], 0.0)
         beside = term_ref[...] + error
-        for n in range(tile_cols // slab):
-            col_ref[n, :, 0:slab] = sum_ref[:, n * slab : (n + 1) * slab]
-            col_ref[n, :, slab:] = beside
-
-
-def cross_partial(jac, error, hi, lo, slab):
+        for n in range(beside_ref.shape[0]):
+            beside_ref[n] = beside
+
+
+def row_partial(jac, error, hi, lo, slab, copies):
     streams = jac.shape[0]
     tile_rows, tile_cols = hi.shape
-    col_slabs = tile_cols // slab
     block = pl.BlockSpec((slab, tile_cols), lambda n: (n, 0))
     return pl.pallas_call(
-        functools.partial(cross_kernel, col_rows=tile_cols // LANES),
+        functools.partial(row_kernel, col_rows=tile_cols // LANES),
         grid=(tile_rows // slab,),
         in_specs=[
             pl.BlockSpec(jac.shape, lambda n: (0, 0, 0)),
@@ -222,50 +215,87 @@
             block,
         ],
         out_specs=[
-            pl.BlockSpec((None, streams, slab), lambda n: (n, 0, 0)),
-            pl.BlockSpec((col_slabs, streams, slab + LANES), lambda n: (0, 0, 0)),
+            pl.BlockSpec((streams, slab), lambda n: (0, n)),
+            pl.BlockSpec((copies, streams, LANES), lambda n: (0, 0, 0)),
         ],
         out_shape=[
-            jax.ShapeDtypeStruct((tile_rows // slab, streams, slab), f32),
-            jax.ShapeDtypeStruct((col_slabs, streams, slab + LANES), f32),
+            jax.ShapeDtypeStruct((streams, tile_rows), f32),
+            jax.ShapeDtypeStruct((copies, streams, LANES), f32),
         ],
         scratch_shapes=[
             pltpu.VMEM((3 * streams, tile_cols), bf16),
+            pltpu.VMEM((streams, LANES), f32),
+        ],
+        compiler_params=pltpu.CompilerParams(vmem_limit_bytes=16 << 20),
+        name="row_cross",
+    )(jac, error, in_hbm(hi), in_hbm(lo))
+
+
+def col_kernel(jac_ref, hi_ref, lo_ref, out_ref, parts_ref, sum_ref, *, col_rows):
+    streams, rows, lanes = jac_ref.shape
+    slab, tile_cols = hi_ref.shape
+    slab_rows = slab // lanes
+    step = pl.program_id(0)
+    flat = jac_ref.reshape(streams * rows, lanes)
+    for i in range(slab_rows):
+        parts = split3(flat[pl.ds(col_rows + step * slab_rows + i, streams, stride=rows), :])
+        for n, part in enumerate(parts):
+            parts_ref[n * streams : (n + 1) * streams, i * lanes : (i + 1) * lanes] = part
+    cross = five_products(parts_ref[...], hi_ref[...], lo_ref[...], ((1,), (0,)))
+
+    @pl.when(step == 0)
+    def _():
+        sum_ref[...] = cross
+
+    @pl.when(step > 0)
+    def _():
+        sum_ref[...] += cross
+
+    @pl.when(step == pl.num_programs(0) - 1)
+    def _():
+        for n in range(tile_cols // slab):
+            out_ref[n] = sum_ref[:, n * slab : (n + 1) * slab]
+
+
+def col_partial(jac, hi, lo, slab):
+    streams = jac.shape[0]
+    tile_rows, tile_cols = hi.shape
+    out_shape = (tile_cols // slab, streams, slab)
+    block = pl.BlockSpec((slab, tile_cols), lambda n: (n, 0))
+    return pl.pallas_call(
+        functools.partial(col_kernel, col_rows=tile_cols // LANES),
+        grid=(tile_rows // slab,),
+        in_specs=[pl.BlockSpec(jac.shape, lambda n: (0, 0, 0)), block, block],
+        out_specs=pl.BlockSpec(out_shape, lambda n: (0, 0, 0)),
+        out_shape=jax.ShapeDtypeStruct(out_shape, f32),
+        scratch_shapes=[
             pltpu.VMEM((3 * streams, slab), bf16),
             pltpu.VMEM((streams, tile_cols), f32),
-            pltpu.VMEM((streams, LANES), f32),
-        ],
-        compiler_params=pltpu.CompilerParams(vmem_limit_bytes=32 << 20),
-        name="cross",
-    )(jac, error, in_hbm(hi), in_hbm(lo))
-
-
-def slab_kernel(rows_ref, cols_ref, row_ref, col_ref):
-    slab = rows_ref.shape[2]
-    row = rows_ref[0]
-    for n in range(1, rows_ref.shape[0]):
-        row = row + rows_ref[n]
-    col = cols_ref[0]
-    for n in range(1, cols_ref.shape[0]):
-        col = col + cols_ref[n]
-    for n in range(row_ref.shape[0]):
-        row_ref[n, :, 0:slab] = row
-        row_ref[n, :, slab:] = col[:, slab:]
-    for n in range(col_ref.shape[0]):
-        col_ref[n] = col[:, 0:slab]
-
-
-def slab_sums(row_pieces, col_pieces):
-    rows_n, streams, slab = row_pieces.shape
-    cols_n, _, padded = col_pieces.shape
+        ],
+        compiler_params=pltpu.CompilerParams(vmem_limit_bytes=16 << 20),
+        name="col_cross",
+    )(jac, in_hbm(hi), in_hbm(lo))
+
+
+def slab_kernel(pieces_ref, beside_ref, out_ref):
+    slab = pieces_ref.shape[2]
+    cross = pieces_ref[0]
+    for n in range(1, pieces_ref.shape[0]):
+        cross = cross + pieces_ref[n]
+    beside = beside_ref[0]
+    for n in range(1, beside_ref.shape[0]):
+        beside = beside + beside_ref[n]
+    out_ref[:, 0:slab] = cross
+    out_ref[:, slab:] = beside
+
+
+def slab_sum(pieces, beside):
+    _, streams, slab = pieces.shape
     return pl.pallas_call(
         slab_kernel,
-        out_shape=[
-            jax.ShapeDtypeStruct((rows_n, streams, padded), f32),
-            jax.ShapeDtypeStruct((cols_n, streams, slab), f32),
-        ],
+        out_shape=jax.ShapeDtypeStruct((streams, slab + LANES), f32),
         name="slab",
-    )(row_pieces, col_pieces)
+    )(pieces, beside)
 
 
 def invert(innovation):
@@ -287,28 +317,30 @@
 def update_kernel(
     rows_ref, cols_ref, weight_ref, cov_ref, new_weight_ref, new_cov_ref, right_ref, tile_ref, in_sems, out_sems
 ):
-    slabs, streams, _ = rows_ref.shape
-    col_slabs, _, slab = cols_ref.shape
+    streams, tile_rows = rows_ref.shape
+    col_slabs, _, padded = cols_ref.shape
     lanes = weight_ref.shape[1]
+    slab = padded - lanes
+    slabs = tile_rows // slab
     reads = []
     for n in range(slabs):
         here = pl.ds(n * slab, slab)
         reads.append(pltpu.make_async_copy(cov_ref.at[here], tile_ref.at[here], in_sems.at[n]))
         reads[-1].start()
-    beside = rows_ref[0, :, slab:]
-    for n in range(1, slabs):
-        beside = beside + rows_ref[n, :, slab:]
+    beside = cols_ref[0, :, slab:]
+    for n in range(1, col_slabs):
+        beside = beside + cols_ref[n, :, slab:]
     inverse = invert(beside[:, 0:streams])
     errors = beside[:, streams : streams + 1]
     for n in range(col_slabs):
-        hi, mid, lo = split3(cols_ref[n])
+        hi, mid, lo = split3(cols_ref[n, :, 0:slab])
         for m, part in enumerate((hi, mid, lo, hi, mid, hi)):
             right_ref[m * streams : (m + 1) * streams, n * slab : (n + 1) * slab] = part
     col_at = lax.axis_index("col")
     own_at = (lax.axis_index("row") * slabs + col_at) * (slab // lanes)
     writes = []
     for n in range(slabs):
-        gain = dot(inverse, rows_ref[n, :, 0:slab], ((0,), (0,)), highest)
+        gain = dot(inverse, rows_ref[:, n * slab : (n + 1) * slab], ((0,), (0,)), highest)
         hi, mid, lo = split3(gain)
         left = jnp.concatenate([hi, hi, hi, mid, mid, lo], axis=0)
         update = dot(left, right_ref[...], ((0,), (0,)))
@@ -329,10 +361,11 @@
         write.wait()
 
 
-def update(row_slabs, col_slabs, layer_weight, covariance):
-    slabs, streams, _ = row_slabs.shape
-    slab = col_slabs.shape[2]
+def update(row_cross, col_slabs, layer_weight, covariance):
+    _, streams, padded = col_slabs.shape
+    slab = padded - LANES
     tile_rows, tile_cols = covariance.shape
+    slabs = tile_rows // slab
     width = layer_weight.shape[1]
     whole = pl.BlockSpec(memory_space=pltpu.VMEM)
     beyond = pl.BlockSpec(memory_space=pl.ANY)
@@ -352,7 +385,7 @@
         ],
         compiler_params=pltpu.CompilerParams(vmem_limit_bytes=32 << 20),
         name="update",
-    )(row_slabs, col_slabs, layer_weight, in_hbm(covariance))
+    )(row_cross, col_slabs, layer_weight, in_hbm(covariance))
 
 
 def plain_steps(at, jac_all, errors, layer_weight, covariance, slab, cols_n):
@@ -430,10 +463,12 @@
     jac = exchange(payload, ("row", "col"))
     jac = jac.reshape(-1, *jac.shape[2:])
     hi, lo = stage(covariance)
-    row_part, col_part = cross_partial(jac, error, hi, lo, slab)
-    row_own, col_own = slab_sums(exchange(row_part, "col"), exchange(col_part, "row"))
-    row_slabs, col_slabs = exchange(row_own, "col"), exchange(col_own, "row")
-    new_weight, new_cov = update(row_slabs, col_slabs, layer_weight, covariance)
+    row_part, beside = row_partial(jac, error, hi, lo, slab, cols_n)
+    row_cross = lax.psum(row_part, "col")
+    beside = exchange(beside, "col")
+    col_pieces = exchange(col_partial(jac, hi, lo, slab), "row")
+    col_slabs = lax.all_gather(slab_sum(col_pieces, beside), "row", axis=0, tiled=False)
+    new_weight, new_cov = update(row_cross, col_slabs, layer_weight, covariance)
     return new_weight.reshape(-1), new_cov
 
 

time: 86.6 us -> 107 us (1.24)
  blocking collectives: 42.5 us -> 8.84 us
  waiting for transfers between devices: 2.86 us -> 31.2 us
  between operations: 1.31 us -> 14.7 us
  starting transfers between devices: 7.3 us -> 14.6 us
  Pallas kernels: 31.8 us -> 35.2 us
  local copies, waits for them, and re-layouts: 0.01 us -> 1.62 us
    all_to_all x4 -> x0, blocking collectives: 42.5 us -> none  [exchange(): return lax.all_to_all(x, axes, split_axis=0, concat_axis=0, tiled=True)]
    psum x0 -> x1, waiting for transfers between devices: none -> 21.3 us  [on_device(): row_cross = lax.psum(row_part, 'col')]
    all_gather x0 -> x1, blocking collectives: none -> 8.84 us  [on_device(): lax.all_gather(slab_sum(col_pieces, beside), 'row', axis=0, tiled=False)]
    all_to_all x1 -> x3, starting transfers between devices: 7.3 us -> 14.6 us  [exchange(): return lax.all_to_all(x, axes, split_axis=0, concat_axis=0, tiled=True)]
    all_to_all x1 -> x3, waiting for transfers between devices: 2.86 us -> 9.24 us  [exchange(): return lax.all_to_all(x, axes, split_axis=0, concat_axis=0, tiled=True)]
    pallas_call x2 -> x3, Pallas kernels: 10.9 us -> 14.3 us  [the longest x1 7.11 us: row_partial(): pl.pallas_call(functools.partial(row_kernel, col_rows=tile_cols // LANES)...]
    unnamed x4 -> x10, local copies, waits for them, and re-layouts: 0.01 us -> 1.62 us
  transfers between devices with their start and end apart: 1 -> 4, of which waited for: 1 -> 4; matrix products, arithmetic and copies ran while one was open for 0% -> 0% of each run, Pallas kernels for 10% -> 15%
where the time goes in v5:
time: 107 us; the launch traced here: 106 us
  Pallas kernels  35.2 us (33%)
  waiting for transfers between devices  31.2 us (29%)
  between operations  14.7 us (14%)
  starting transfers between devices  14.6 us (14%)
  blocking collectives  8.84 us (8%)
  local copies, waits for them, and re-layouts  1.62 us (2%)
    psum x1, waiting for transfers between devices, on_device(): row_cross = lax.psum(row_part, 'col')  21.3 us
    all_to_all x3, starting transfers between devices, exchange(): return lax.all_to_all(x, axes, split_axis=0, concat_axis=0, tiled=True)  14.6 us
    all_to_all x3, waiting for transfers between devices, exchange(): return lax.all_to_all(x, axes, split_axis=0, concat_axis=0, tiled=True)  9.24 us
    pallas_call x1, Pallas kernels, stage(): pl.pallas_call(stage_kernel, grid=(rows // height,), in_specs=[block], ou...  8.96 us
    all_gather x1, blocking collectives, on_device(): lax.all_gather(slab_sum(col_pieces, beside), 'row', axis=0, tiled=False)  8.84 us
    pallas_call x1, Pallas kernels, update(): pl.pallas_call(update_kernel, in_specs=[whole, whole, whole, beyond], out...  8.32 us
    pallas_call x1, Pallas kernels, row_partial(): pl.pallas_call(functools.partial(row_kernel, col_rows=tile_cols // LANES)...  7.11 us
    pallas_call x1, Pallas kernels, col_partial(): pl.pallas_call(functools.partial(col_kernel, col_rows=tile_cols // LANES)...  5.59 us
  transfers between devices with their start and end apart: 4, of which 4 were waited for; matrix products, arithmetic and copies ran while one was open for 0% of the time, Pallas kernels for 15%

profile of v5, /device:TPU:0, one launch (start us, length us, event | category | flops | bytes accessed | tf_op | source)
XLA Modules:
  0.0 106.2 jit_solution(10831875113307084994)
XLA Ops:
  7.8 3.6 %network.1 = (f32[32,1,24,128]{3,2,1,0:T(8,128)}, f32[1,1,128]{2,1,0:T(1,128)}) custom-call(s32[1,1,256]{2,1,0:T(1,128)} %bitcast.13, s32[1,32,256]{2,1,0:T(8,128)} %ids_ref.1, f32[1,32,256]{2,1,0:T(8,128)} %switch_ref.1, f32[1,64,256]{2,1,0:T(8,128)} %bitcast.12, f32[1,1,256]{2,1,0:T(1,128)} %bitcast.14, f32[1,1,1]{2,1,0:T(1,128)} %bitcast.8.target_ref, ...), custom_call_target="tpu_custom_call" | custom-call | tf_op jit(solution)/shard_map/network/pallas_call | solution.py:101
  11.5 0.0 copy-start.2
  11.5 7.3 %all-to-all-start = ((f32[32,1,24,128]{3,2,1,0:T(8,128)}), f32[32,1,24,128]{3,2,1,0:T(8,128)S(1)}, u32[]{:S(2)}, u32[]{:S(2)}) async-start(f32[32,1,24,128]{3,2,1,0:T(8,128)} %get-tuple-element.10), calls=%async_computation | async-start | bytes 786432 | tf_op jit(solution)/shard_map/all_to_all | solution.py:412
  18.8 9.0 %stage.1 = (bf16[1024,2048]{1,0:T(8,128)(2,1)}, bf16[1024,2048]{1,0:T(8,128)(2,1)}) custom-call(f32[1024,2048]{1,0:T(8,128)} %cov_ref.3), custom_call_target="tpu_custom_call" | custom-call | tf_op jit(solution)/shard_map/stage/pallas_call | solution.py:150
  27.7 2.9 %all-to-all-done = f32[32,1,24,128]{3,2,1,0:T(8,128)S(1)} async-done(((f32[32,1,24,128]{3,2,1,0:T(8,128)}), f32[32,1,24,128]{3,2,1,0:T(8,128)S(1)}, u32[]{:S(2)}, u32[]{:S(2)}) %all-to-all-start) | async-done | bytes 393248 | tf_op jit(solution)/shard_map/all_to_all | solution.py:412
  30.6 0.0 copy-done.2
  30.6 0.0 copy-start.1
  30.6 7.1 %row_cross.1 = (f32[32,1024]{1,0:T(8,128)}, f32[4,32,128]{2,1,0:T(8,128)}) custom-call(f32[32,24,128]{2,1,0:T(8,128)S(1)} %bitcast.9, f32[1,1,128]{2,1,0:T(1,128)S(1)} %copy-done.2, bf16[1024,2048]{1,0:T(8,128)(2,1)} %get-tuple-element.12.hi_ref, bf16[1024,2048]{1,0:T(8,128)(2,1)} %get-tuple-element.13.lo_ref), custom_call_target="tpu_custom_call" | custom-call | tf_op jit(solution)/shard_map/row_cross/pallas_call | solution.py:208
  37.7 3.9 %all-to-all-start.2 = ((f32[4,32,128]{2,1,0:T(8,128)}), f32[4,32,128]{2,1,0:T(8,128)S(1)}, u32[]{:S(2)}, u32[]{:S(2)}) async-start(f32[4,32,128]{2,1,0:T(8,128)} %get-tuple-element.15), calls=%async_computation.2 | async-start | bytes 131072 | tf_op jit(solution)/shard_map/all_to_all | solution.py:412
  41.6 5.6 %col_cross.1 = f32[8,32,256]{2,1,0:T(8,128)} custom-call(f32[32,24,128]{2,1,0:T(8,128)S(1)} %bitcast.10, bf16[1024,2048]{1,0:T(8,128)(2,1)} %get-tuple-element.12.hi_ref, bf16[1024,2048]{1,0:T(8,128)(2,1)} %get-tuple-element.13.lo_ref), custom_call_target="tpu_custom_call" | custom-call | tf_op jit(solution)/shard_map/col_cross/pallas_call | solution.py:265
  47.2 0.2 all-to-all-done.2.beside_ref
  47.4 0.0 copy-start.4
  47.4 3.4 %all-to-all-start.1 = ((f32[8,32,256]{2,1,0:T(8,128)}), f32[8,32,256]{2,1,0:T(8,128)S(1)}, u32[]{:S(2)}, u32[]{:S(2)}) async-start(f32[8,32,256]{2,1,0:T(8,128)} %col_cross.1), calls=%async_computation.1 | async-start | bytes 524288 | tf_op jit(solution)/shard_map/all_to_all | solution.py:412
  50.8 0.0 all-reduce.2.cloned.1.call-start
  50.9 0.7 all-reduce.2.cloned.1.call-update
  51.6 6.1 %all-to-all-done.1.pieces_ref = f32[8,32,256]{2,1,0:T(8,128)S(1)} async-done(((f32[8,32,256]{2,1,0:T(8,128)}), f32[8,32,256]{2,1,0:T(8,128)S(1)}, u32[]{:S(2)}, u32[]{:S(2)}) %all-to-all-start.1) | async-done | bytes 262176 | tf_op jit(solution)/shard_map/all_to_all | solution.py:412
  57.7 0.0 copy-done.4
  57.7 0.0 copy-start.3
  57.7 0.7 copy-done.3
  58.4 1.6 %slab.1 = f32[32,384]{1,0:T(8,128)} custom-call(f32[8,32,256]{2,1,0:T(8,128)} %copy-done.3, f32[4,32,128]{2,1,0:T(8,128)} %copy-done.4), custom_call_target="tpu_custom_call" | custom-call | tf_op jit(solution)/shard_map/slab/pallas_call | solution.py:294
  60.0 8.8 %all-gather = f32[256,384]{1,0:T(8,128)S(1)} all-gather(f32[32,384]{1,0:T(8,128)} %slab.1), channel_id=2, replica_groups=mesh['row'=8,'col'=4] {'row'}, dimensions={0}, use_global_device_ids=true | all-gather | bytes 442368 | tf_op jit(solution)/shard_map/all_gather | solution.py:470
  68.8 21.3 %all-reduce.2.cloned.1.call-done.rows_ref = f32[32,1024]{1,0:T(8,128)} async-done(((f32[32,1024]{1,0:T(8,128)}), f32[32,1024]{1,0:T(8,128)}) %all-reduce.2.cloned.1.call-update) | async-done | bytes 131088 | tf_op jit(solution)/shard_map/psum | solution.py:467
  90.1 0.0 copy-done.1
  90.1 0.0 copy-start
  90.1 0.9 copy-done
  91.0 8.3 %update.1 = (f32[2,128]{1,0:T(2,128)}, f32[1024,2048]{1,0:T(8,128)}) custom-call(f32[32,1024]{1,0:T(8,128)S(1)} %copy-done, f32[8,32,384]{2,1,0:T(8,128)S(1)} %bitcast.11, f32[64,128]{1,0:T(8,128)S(1)} %copy-done.1, f32[1024,2048]{1,0:T(8,128)} %cov_ref.3), custom_call_target="tpu_custom_call" | custom-call | tf_op jit(solution)/shard_map/update/pallas_call | solution.py:372
Async XLA Ops:
  11.5 19.1 %copy-start.2 = (f32[1,1,128]{2,1,0:T(1,128)S(1)}, f32[1,1,128]{2,1,0:T(1,128)}, u32[]{:S(2)}) copy-start(f32[1,1,128]{2,1,0:T(1,128)} %get-tuple-element.11.error_ref) | copy-start | bytes 1540
  11.5 19.1 %all-to-all-start = ((f32[32,1,24,128]{3,2,1,0:T(8,128)}), f32[32,1,24,128]{3,2,1,0:T(8,128)S(1)}, u32[]{:S(2)}, u32[]{:S(2)}) async-start(f32[32,1,24,128]{3,2,1,0:T(8,128)} %get-tuple-element.10), calls=%async_computation | async-start | bytes 786432 | tf_op jit(solution)/shard_map/all_to_all | solution.py:412
  30.6 59.5 %copy-start.1 = (f32[64,128]{1,0:T(8,128)S(1)}, f32[64,128]{1,0:T(8,128)}, u32[]{:S(2)}) copy-start(f32[64,128]{1,0:T(8,128)} %weight_ref.3) | copy-start | bytes 98308
  37.7 9.7 %all-to-all-start.2 = ((f32[4,32,128]{2,1,0:T(8,128)}), f32[4,32,128]{2,1,0:T(8,128)S(1)}, u32[]{:S(2)}, u32[]{:S(2)}) async-start(f32[4,32,128]{2,1,0:T(8,128)} %get-tuple-element.15), calls=%async_computation.2 | async-start | bytes 131072 | tf_op jit(solution)/shard_map/all_to_all | solution.py:412
  47.4 10.3 %copy-start.4 = (f32[4,32,128]{2,1,0:T(8,128)}, f32[4,32,128]{2,1,0:T(8,128)S(1)}, u32[]{:S(2)}) copy-start(f32[4,32,128]{2,1,0:T(8,128)S(1)} %all-to-all-done.2.beside_ref) | copy-start | bytes 196612
  47.4 10.3 %all-to-all-start.1 = ((f32[8,32,256]{2,1,0:T(8,128)}), f32[8,32,256]{2,1,0:T(8,128)S(1)}, u32[]{:S(2)}, u32[]{:S(2)}) async-start(f32[8,32,256]{2,1,0:T(8,128)} %col_cross.1), calls=%async_computation.1 | async-start | bytes 524288 | tf_op jit(solution)/shard_map/all_to_all | solution.py:412
  50.8 39.3 %all-reduce.2.cloned.1.call-start = ((), (), s32[]{:S(2)}) async-start(), calls=%async_computation.3 | async-start | bytes 262144 | tf_op jit(solution)/shard_map/psum | solution.py:467
  57.7 0.7 copy-start.3
  90.1 0.9 copy-start
Sparse Core Ops, SparseCore 0:
  54.0 36.0 all-reduce.1

commit v6 on v4

--- a/solution.py
+++ b/solution.py
@@ -167,53 +167,57 @@
     )
 
 
-def cross_kernel(jac_ref, error_ref, hi_ref, lo_ref, row_ref, col_ref, parts_ref, row_parts_ref, sum_ref, term_ref, *, col_rows):
+def stacked_parts(flat, first, count, streams, stride, into_ref):
+    lanes = flat.shape[1]
+    for i in range(count):
+        parts = split3(flat[pl.ds(first + i, streams, stride=stride), :])
+        for n, part in enumerate(parts):
+            into_ref[n * streams : (n + 1) * streams, i * lanes : (i + 1) * lanes] = part
+
+
+def col_kernel(jac_ref, error_ref, hi_ref, lo_ref, out_ref, parts_ref, sum_ref, *, col_rows):
     streams, rows, lanes = jac_ref.shape
     slab, tile_cols = hi_ref.shape
     slab_rows = slab // lanes
     step = pl.program_id(0)
     flat = jac_ref.reshape(streams * rows, lanes)
+    stacked_parts(flat, col_rows + step * slab_rows, slab_rows, streams, rows, parts_ref.at[:, 0:slab])
+    cross = five_products(parts_ref[:, 0:slab], hi_ref[...], lo_ref[...], ((1,), (0,)))
 
     @pl.when(step == 0)
     def _():
-        term_ref[...] = jnp.zeros_like(term_ref)
-        sum_ref[...] = jnp.zeros_like(sum_ref)
-        for i in range(col_rows):
-            parts = split3(flat[pl.ds(i, streams, stride=rows), :])
-            for n, part in enumerate(parts):
-                parts_ref[n * streams : (n + 1) * streams, i * lanes : (i + 1) * lanes] = part
-
-    hi, lo = hi_ref[...], lo_ref[...]
-    cross = five_products(parts_ref[...], hi, lo, ((1,), (1,)))
-    row_ref[...] = cross
-    term = jnp.zeros((streams, streams), f32)
-    for i in range(slab_rows):
-        own = flat[pl.ds(col_rows + step * slab_rows + i, streams, stride=rows), :]
-        term = term + dot(own, cross[:, i * lanes : (i + 1) * lanes], ((1,), (1,)), highest)
-        for n, part in enumerate(split3(own)):
-            row_parts_ref[n * streams : (n + 1) * streams, i * lanes : (i + 1) * lanes] = part
-    term_ref[:, 0:streams] += term
-    sum_ref[...] += five_products(row_parts_ref[...], hi, lo, ((1,), (0,)))
+        sum_ref[...] = cross
+
+    @pl.when(step > 0)
+    def _():
+        sum_ref[...] += cross
 
     @pl.when(step == pl.num_programs(0) - 1)
     def _():
+        stacked_parts(flat, 0, col_rows, streams, rows, parts_ref)
+        total = sum_ref[...]
+        products = dot(parts_ref[...], jnp.concatenate(split3(total), axis=0), ((1,), (1,)))
+        term = jnp.zeros((streams, streams), f32)
+        for left, right in ((2, 0), (1, 1), (0, 2), (1, 0), (0, 1), (0, 0)):
+            term = term + products[
+                left * streams : (left + 1) * streams, right * streams : (right + 1) * streams
+            ]
         own_at = lax.axis_index("row") * lax.axis_size("col") + lax.axis_index("col")
         stream_at = lax.broadcasted_iota(jnp.int32, (streams, lanes), 0)
-        lane_at = lax.broadcasted_iota(jnp.int32, (streams, lanes), 1)
-        error = jnp.where((stream_at == own_at) & (lane_at >= streams), error_ref[0], 0.0)
-        beside = term_ref[...] + error
+        error = jnp.where(stream_at == own_at, error_ref[0], 0.0)
         for n in range(tile_cols // slab):
-            col_ref[n, :, 0:slab] = sum_ref[:, n * slab : (n + 1) * slab]
-            col_ref[n, :, slab:] = beside
-
-
-def cross_partial(jac, error, hi, lo, slab):
+            out_ref[n, :, 0:slab] = total[:, n * slab : (n + 1) * slab]
+            out_ref[n, :, slab:] = error
+            out_ref[n, :, slab : slab + streams] = term
+
+
+def col_partial(jac, error, hi, lo, slab):
     streams = jac.shape[0]
     tile_rows, tile_cols = hi.shape
-    col_slabs = tile_cols // slab
+    out_shape = (tile_cols // slab, streams, slab + LANES)
     block = pl.BlockSpec((slab, tile_cols), lambda n: (n, 0))
     return pl.pallas_call(
-        functools.partial(cross_kernel, col_rows=tile_cols // LANES),
+        functools.partial(col_kernel, col_rows=tile_cols // LANES),
         grid=(tile_rows // slab,),
         in_specs=[
             pl.BlockSpec(jac.shape, lambda n: (0, 0, 0)),
@@ -221,51 +225,67 @@
             block,
             block,
         ],
-        out_specs=[
-            pl.BlockSpec((None, streams, slab), lambda n: (n, 0, 0)),
-            pl.BlockSpec((col_slabs, streams, slab + LANES), lambda n: (0, 0, 0)),
-        ],
-        out_shape=[
-            jax.ShapeDtypeStruct((tile_rows // slab, streams, slab), f32),
-            jax.ShapeDtypeStruct((col_slabs, streams, slab + LANES), f32),
-        ],
+        out_specs=pl.BlockSpec(out_shape, lambda n: (0, 0, 0)),
+        out_shape=jax.ShapeDtypeStruct(out_shape, f32),
         scratch_shapes=[
             pltpu.VMEM((3 * streams, tile_cols), bf16),
-            pltpu.VMEM((3 * streams, slab), bf16),
             pltpu.VMEM((streams, tile_cols), f32),
-            pltpu.VMEM((streams, LANES), f32),
-        ],
-        compiler_params=pltpu.CompilerParams(vmem_limit_bytes=32 << 20),
-        name="cross",
+        ],
+        compiler_params=pltpu.CompilerParams(vmem_limit_bytes=16 << 20),
+        name="col_cross",
     )(jac, error, in_hbm(hi), in_hbm(lo))
 
 
-def slab_kernel(rows_ref, cols_ref, row_ref, col_ref):
-    slab = rows_ref.shape[2]
-    row = rows_ref[0]
-    for n in range(1, rows_ref.shape[0]):
-        row = row + rows_ref[n]
-    col = cols_ref[0]
-    for n in range(1, cols_ref.shape[0]):
-        col = col + cols_ref[n]
-    for n in range(row_ref.shape[0]):
-        row_ref[n, :, 0:slab] = row
-        row_ref[n, :, slab:] = col[:, slab:]
-    for n in range(col_ref.shape[0]):
-        col_ref[n] = col[:, 0:slab]
-
-
-def slab_sums(row_pieces, col_pieces):
-    rows_n, streams, slab = row_pieces.shape
-    cols_n, _, padded = col_pieces.shape
+def row_kernel(jac_ref, hi_ref, lo_ref, cross_ref, parts_ref):
+    streams, rows, lanes = jac_ref.shape
+    flat = jac_ref.reshape(streams * rows, lanes)
+
+    @pl.when(pl.program_id(0) == 0)
+    def _():
+        stacked_parts(flat, 0, hi_ref.shape[1] // lanes, streams, rows, parts_ref)
+
+    cross_ref[...] = five_products(parts_ref[...], hi_ref[...], lo_ref[...], ((1,), (1,)))
+
+
+def row_partial(jac, hi, lo, slab):
+    streams = jac.shape[0]
+    tile_rows, tile_cols = hi.shape
+    block = pl.BlockSpec((slab, tile_cols), lambda n: (n, 0))
+    return pl.pallas_call(
+        row_kernel,
+        grid=(tile_rows // slab,),
+        in_specs=[pl.BlockSpec(jac.shape, lambda n: (0, 0, 0)), block, block],
+        out_specs=pl.BlockSpec((streams, slab), lambda n: (0, n)),
+        out_shape=jax.ShapeDtypeStruct((streams, tile_rows), f32),
+        scratch_shapes=[pltpu.VMEM((3 * streams, tile_cols), bf16)],
+        compiler_params=pltpu.CompilerParams(vmem_limit_bytes=16 << 20),
+        name="row_cross",
+    )(jac, in_hbm(hi), in_hbm(lo))
+
+
+def slab_kernel(pieces_ref, row_ref, own_ref, out_ref):
+    tile_rows = row_ref.shape[1]
+    slab = own_ref.shape[1]
+    total = pieces_ref[0]
+    for n in range(1, pieces_ref.shape[0]):
+        total = total + pieces_ref[n]
+    own_ref[...] = total[:, 0:slab]
+    for n in range(out_ref.shape[0]):
+        out_ref[n, :, 0:tile_rows] = row_ref[...]
+        out_ref[n, :, tile_rows:] = total[:, slab:]
+
+
+def slab_sum(pieces, row_part, copies):
+    _, streams, padded = pieces.shape
+    tile_rows = row_part.shape[1]
     return pl.pallas_call(
         slab_kernel,
         out_shape=[
-            jax.ShapeDtypeStruct((rows_n, streams, padded), f32),
-            jax.ShapeDtypeStruct((cols_n, streams, slab), f32),
+            jax.ShapeDtypeStruct((streams, padded - LANES), f32),
+            jax.ShapeDtypeStruct((copies, streams, tile_rows + LANES), f32),
         ],
         name="slab",
-    )(row_pieces, col_pieces)
+    )(pieces, row_part)
 
 
 def invert(innovation):
@@ -287,17 +307,20 @@
 def update_kernel(
     rows_ref, cols_ref, weight_ref, cov_ref, new_weight_ref, new_cov_ref, right_ref, tile_ref, in_sems, out_sems
 ):
-    slabs, streams, _ = rows_ref.shape
+    copies, streams, padded = rows_ref.shape
     col_slabs, _, slab = cols_ref.shape
     lanes = weight_ref.shape[1]
+    tile_rows = padded - lanes
+    slabs = tile_rows // slab
     reads = []
     for n in range(slabs):
         here = pl.ds(n * slab, slab)
         reads.append(pltpu.make_async_copy(cov_ref.at[here], tile_ref.at[here], in_sems.at[n]))
         reads[-1].start()
-    beside = rows_ref[0, :, slab:]
-    for n in range(1, slabs):
-        beside = beside + rows_ref[n, :, slab:]
+    total = rows_ref[0]
+    for n in range(1, copies):
+        total = total + rows_ref[n]
+    beside = total[:, tile_rows:]
     inverse = invert(beside[:, 0:streams])
     errors = beside[:, streams : streams + 1]
     for n in range(col_slabs):
@@ -308,7 +331,7 @@
     own_at = (lax.axis_index("row") * slabs + col_at) * (slab // lanes)
     writes = []
     for n in range(slabs):
-        gain = dot(inverse, rows_ref[n, :, 0:slab], ((0,), (0,)), highest)
+        gain = dot(inverse, total[:, n * slab : (n + 1) * slab], ((0,), (0,)), highest)
         hi, mid, lo = split3(gain)
         left = jnp.concatenate([hi, hi, hi, mid, mid, lo], axis=0)
         update = dot(left, right_ref[...], ((0,), (0,)))
@@ -329,10 +352,10 @@
         write.wait()
 
 
-def update(row_slabs, col_slabs, layer_weight, covariance):
-    slabs, streams, _ = row_slabs.shape
-    slab = col_slabs.shape[2]
+def update(row_parts, col_slabs, layer_weight, covariance):
+    _, streams, slab = col_slabs.shape
     tile_rows, tile_cols = covariance.shape
+    slabs = tile_rows // slab
     width = layer_weight.shape[1]
     whole = pl.BlockSpec(memory_space=pltpu.VMEM)
     beyond = pl.BlockSpec(memory_space=pl.ANY)
@@ -352,7 +375,7 @@
         ],
         compiler_params=pltpu.CompilerParams(vmem_limit_bytes=32 << 20),
         name="update",
-    )(row_slabs, col_slabs, layer_weight, in_hbm(covariance))
+    )(row_parts, col_slabs, layer_weight, in_hbm(covariance))
 
 
 def plain_steps(at, jac_all, errors, layer_weight, covariance, slab, cols_n):
@@ -430,10 +453,12 @@
     jac = exchange(payload, ("row", "col"))
     jac = jac.reshape(-1, *jac.shape[2:])
     hi, lo = stage(covariance)
-    row_part, col_part = cross_partial(jac, error, hi, lo, slab)
-    row_own, col_own = slab_sums(exchange(row_part, "col"), exchange(col_part, "row"))
-    row_slabs, col_slabs = exchange(row_own, "col"), exchange(col_own, "row")
-    new_weight, new_cov = update(row_slabs, col_slabs, layer_weight, covariance)
+    col_pieces = exchange(col_partial(jac, error, hi, lo, slab), "row")
+    row_part = row_partial(jac, hi, lo, slab)
+    col_own, row_part = slab_sum(col_pieces, row_part, cols_n)
+    row_parts = exchange(row_part, "col")
+    col_slabs = lax.all_gather(col_own, "row", axis=0, tiled=False)
+    new_weight, new_cov = update(row_parts, col_slabs, layer_weight, covariance)
     return new_weight.reshape(-1), new_cov
 
 

time: 86.6 us -> 72.5 us (0.84)
  blocking collectives: 42.5 us -> 8.53 us
  waiting for transfers between devices: 2.86 us -> 11.4 us
  starting transfers between devices: 7.3 us -> 14.6 us
  Pallas kernels: 31.8 us -> 34.5 us
  local copies, waits for them, and re-layouts: 0.01 us -> 1.39 us
    all_to_all x4 -> x0, blocking collectives: 42.5 us -> none  [exchange(): return lax.all_to_all(x, axes, split_axis=0, concat_axis=0, tiled=True)]
    all_to_all x1 -> x3, waiting for transfers between devices: 2.86 us -> 11.4 us  [exchange(): return lax.all_to_all(x, axes, split_axis=0, concat_axis=0, tiled=True)]
    all_gather x0 -> x1, blocking collectives: none -> 8.53 us  [on_device(): col_slabs = lax.all_gather(col_own, 'row', axis=0, tiled=False)]
    all_to_all x1 -> x3, starting transfers between devices: 7.3 us -> 14.6 us  [exchange(): return lax.all_to_all(x, axes, split_axis=0, concat_axis=0, tiled=True)]
    pallas_call x2 -> x3, Pallas kernels: 10.9 us -> 13.6 us  [the longest x1 6.05 us: col_partial(): pl.pallas_call(functools.partial(col_kernel, col_rows=tile_cols // LANES)...]
    unnamed x4 -> x8, local copies, waits for them, and re-layouts: 0.01 us -> 1.39 us
  transfers between devices with their start and end apart: 1 -> 3, of which waited for: 1 -> 3; matrix products, arithmetic and copies ran while one was open for 0% -> 0% of each run, Pallas kernels for 10% -> 20%
where the time goes in v6:
time: 72.5 us; the launch traced here: 71.8 us
  Pallas kernels  34.5 us (48%)
  starting transfers between devices  14.6 us (20%)
  waiting for transfers between devices  11.4 us (16%)
  blocking collectives  8.53 us (12%)
  local copies, waits for them, and re-layouts  1.39 us (2%)
  between operations  1.32 us (2%)
    all_to_all x3, starting transfers between devices, exchange(): return lax.all_to_all(x, axes, split_axis=0, concat_axis=0, tiled=True)  14.6 us
    all_to_all x3, waiting for transfers between devices, exchange(): return lax.all_to_all(x, axes, split_axis=0, concat_axis=0, tiled=True)  11.4 us
    pallas_call x1, Pallas kernels, stage(): pl.pallas_call(stage_kernel, grid=(rows // height,), in_specs=[block], ou...  8.95 us
    all_gather x1, blocking collectives, on_device(): col_slabs = lax.all_gather(col_own, 'row', axis=0, tiled=False)  8.53 us
    pallas_call x1, Pallas kernels, update(): pl.pallas_call(update_kernel, in_specs=[whole, whole, whole, beyond], out...  8.33 us
    pallas_call x1, Pallas kernels, col_partial(): pl.pallas_call(functools.partial(col_kernel, col_rows=tile_cols // LANES)...  6.05 us
    pallas_call x1, Pallas kernels, row_partial(): pl.pallas_call(row_kernel, grid=(tile_rows // slab,), in_specs=[pl.BlockS...  5.64 us
    pallas_call x1, Pallas kernels, network(): pl.pallas_call(functools.partial(network_kernel, plan=plan), grid=(per_de...  3.66 us
  transfers between devices with their start and end apart: 3, of which 3 were waited for; matrix products, arithmetic and copies ran while one was open for 0% of the time, Pallas kernels for 20%

profile of v6, /device:TPU:0, one launch (start us, length us, event | category | flops | bytes accessed | tf_op | source)
XLA Modules:
  0.0 71.8 jit_solution(4895099680954745824)
XLA Ops:
  1.3 3.7 %network.1 = (f32[32,1,24,128]{3,2,1,0:T(8,128)}, f32[1,1,128]{2,1,0:T(1,128)}) custom-call(s32[1,1,256]{2,1,0:T(1,128)} %bitcast.13, s32[1,32,256]{2,1,0:T(8,128)} %ids_ref.1, f32[1,32,256]{2,1,0:T(8,128)} %switch_ref.1, f32[1,64,256]{2,1,0:T(8,128)} %bitcast.12, f32[1,1,256]{2,1,0:T(1,128)} %bitcast.14, f32[1,1,1]{2,1,0:T(1,128)} %bitcast.8.target_ref, ...), custom_call_target="tpu_custom_call" | custom-call | tf_op jit(solution)/shard_map/network/pallas_call | solution.py:101
  4.9 0.0 copy-start.2
  4.9 7.3 %all-to-all-start = ((f32[32,1,24,128]{3,2,1,0:T(8,128)}), f32[32,1,24,128]{3,2,1,0:T(8,128)S(1)}, u32[]{:S(2)}, u32[]{:S(2)}) async-start(f32[32,1,24,128]{3,2,1,0:T(8,128)} %get-tuple-element.10), calls=%async_computation | async-start | bytes 786432 | tf_op jit(solution)/shard_map/all_to_all | solution.py:402
  12.2 8.9 %stage.1 = (bf16[1024,2048]{1,0:T(8,128)(2,1)}, bf16[1024,2048]{1,0:T(8,128)(2,1)}) custom-call(f32[1024,2048]{1,0:T(8,128)} %cov_ref.3), custom_call_target="tpu_custom_call" | custom-call | tf_op jit(solution)/shard_map/stage/pallas_call | solution.py:150
  21.2 2.9 %all-to-all-done = f32[32,1,24,128]{3,2,1,0:T(8,128)S(1)} async-done(((f32[32,1,24,128]{3,2,1,0:T(8,128)}), f32[32,1,24,128]{3,2,1,0:T(8,128)S(1)}, u32[]{:S(2)}, u32[]{:S(2)}) %all-to-all-start) | async-done | bytes 393248 | tf_op jit(solution)/shard_map/all_to_all | solution.py:402
  24.1 0.0 copy-done.2
  24.1 0.0 copy-start.1
  24.1 6.0 %col_cross.1 = f32[8,32,384]{2,1,0:T(8,128)} custom-call(f32[32,24,128]{2,1,0:T(8,128)S(1)} %bitcast.9, f32[1,1,128]{2,1,0:T(1,128)S(1)} %copy-done.2, bf16[1024,2048]{1,0:T(8,128)(2,1)} %get-tuple-element.12.hi_ref, bf16[1024,2048]{1,0:T(8,128)(2,1)} %get-tuple-element.13.lo_ref), custom_call_target="tpu_custom_call" | custom-call | tf_op jit(solution)/shard_map/col_cross/pallas_call | solution.py:219
  30.1 3.5 %all-to-all-start.1 = ((f32[8,32,384]{2,1,0:T(8,128)}), f32[8,32,384]{2,1,0:T(8,128)S(1)}, u32[]{:S(2)}, u32[]{:S(2)}) async-start(f32[8,32,384]{2,1,0:T(8,128)} %col_cross.1), calls=%async_computation.1 | async-start | bytes 786432 | tf_op jit(solution)/shard_map/all_to_all | solution.py:402
  33.6 5.6 %row_cross.1.row_ref = f32[32,1024]{1,0:T(8,128)S(1)} custom-call(f32[32,24,128]{2,1,0:T(8,128)S(1)} %bitcast.10, bf16[1024,2048]{1,0:T(8,128)(2,1)} %get-tuple-element.12.hi_ref, bf16[1024,2048]{1,0:T(8,128)(2,1)} %get-tuple-element.13.lo_ref), custom_call_target="tpu_custom_call" | custom-call | tf_op jit(solution)/shard_map/row_cross/pallas_call | solution.py:254
  39.2 0.0 copy-start
  39.2 0.6 copy-done
  39.9 2.0 %all-to-all-done.1.pieces_ref = f32[8,32,384]{2,1,0:T(8,128)S(1)} async-done(((f32[8,32,384]{2,1,0:T(8,128)}), f32[8,32,384]{2,1,0:T(8,128)S(1)}, u32[]{:S(2)}, u32[]{:S(2)}) %all-to-all-start.1) | async-done | bytes 393248 | tf_op jit(solution)/shard_map/all_to_all | solution.py:402
  41.9 0.0 copy-start.3
  41.9 0.7 %copy-done.3 = f32[8,32,384]{2,1,0:T(8,128)} copy-done((f32[8,32,384]{2,1,0:T(8,128)}, f32[8,32,384]{2,1,0:T(8,128)S(1)}, u32[]{:S(2)}) %copy-start.3) | copy-done | bytes 393240
  42.6 1.9 %slab.1 = (f32[32,256]{1,0:T(8,128)}, f32[4,32,1152]{2,1,0:T(8,128)}) custom-call(f32[8,32,384]{2,1,0:T(8,128)} %copy-done.3, f32[32,1024]{1,0:T(8,128)} %copy-done), custom_call_target="tpu_custom_call" | custom-call | tf_op jit(solution)/shard_map/slab/pallas_call | solution.py:281
  44.5 3.9 %all-to-all-start.2 = ((f32[4,32,1152]{2,1,0:T(8,128)}), f32[4,32,1152]{2,1,0:T(8,128)S(1)}, u32[]{:S(2)}, u32[]{:S(2)}) async-start(f32[4,32,1152]{2,1,0:T(8,128)} %get-tuple-element.14), calls=%async_computation.2 | async-start | bytes 1179648 | tf_op jit(solution)/shard_map/all_to_all | solution.py:402
  48.4 8.5 %all-gather = f32[256,256]{1,0:T(8,128)S(1)} all-gather(f32[32,256]{1,0:T(8,128)} %get-tuple-element.15), channel_id=2, replica_groups=mesh['row'=8,'col'=4] {'row'}, dimensions={0}, use_global_device_ids=true | all-gather | bytes 294912 | tf_op jit(solution)/shard_map/all_gather | solution.py:460
  56.9 6.6 %all-to-all-done.2.rows_ref = f32[4,32,1152]{2,1,0:T(8,128)S(1)} async-done(((f32[4,32,1152]{2,1,0:T(8,128)}), f32[4,32,1152]{2,1,0:T(8,128)S(1)}, u32[]{:S(2)}, u32[]{:S(2)}) %all-to-all-start.2) | async-done | bytes 589856 | tf_op jit(solution)/shard_map/all_to_all | solution.py:402
  63.4 0.0 copy-done.1
  63.4 8.3 %update.1 = (f32[2,128]{1,0:T(2,128)}, f32[1024,2048]{1,0:T(8,128)}) custom-call(f32[4,32,1152]{2,1,0:T(8,128)S(1)} %all-to-all-done.2.rows_ref, f32[8,32,256]{2,1,0:T(8,128)S(1)} %bitcast.11, f32[64,128]{1,0:T(8,128)S(1)} %copy-done.1, f32[1024,2048]{1,0:T(8,128)} %cov_ref.3), custom_call_target="tpu_custom_call" | custom-call | tf_op jit(solution)/shard_map/update/pallas_call | solution.py:362
Async XLA Ops:
  4.9 19.1 %copy-start.2 = (f32[1,1,128]{2,1,0:T(1,128)S(1)}, f32[1,1,128]{2,1,0:T(1,128)}, u32[]{:S(2)}) copy-start(f32[1,1,128]{2,1,0:T(1,128)} %get-tuple-element.11.error_ref) | copy-start | bytes 1540
  4.9 19.1 %all-to-all-start = ((f32[32,1,24,128]{3,2,1,0:T(8,128)}), f32[32,1,24,128]{3,2,1,0:T(8,128)S(1)}, u32[]{:S(2)}, u32[]{:S(2)}) async-start(f32[32,1,24,128]{3,2,1,0:T(8,128)} %get-tuple-element.10), calls=%async_computation | async-start | bytes 786432 | tf_op jit(solution)/shard_map/all_to_all | solution.py:402
  24.1 39.4 %copy-start.1 = (f32[64,128]{1,0:T(8,128)S(1)}, f32[64,128]{1,0:T(8,128)}, u32[]{:S(2)}) copy-start(f32[64,128]{1,0:T(8,128)} %weight_ref.3) | copy-start | bytes 98308
  30.1 11.7 %all-to-all-start.1 = ((f32[8,32,384]{2,1,0:T(8,128)}), f32[8,32,384]{2,1,0:T(8,128)S(1)}, u32[]{:S(2)}, u32[]{:S(2)}) async-start(f32[8,32,384]{2,1,0:T(8,128)} %col_cross.1), calls=%async_computation.1 | async-start | bytes 786432 | tf_op jit(solution)/shard_map/all_to_all | solution.py:402
  39.2 0.6 copy-start
  41.9 0.7 %copy-start.3 = (f32[8,32,384]{2,1,0:T(8,128)}, f32[8,32,384]{2,1,0:T(8,128)S(1)}, u32[]{:S(2)}) copy-start(f32[8,32,384]{2,1,0:T(8,128)S(1)} %all-to-all-done.1.pieces_ref) | copy-start | bytes 1179652
  44.5 18.9 %all-to-all-start.2 = ((f32[4,32,1152]{2,1,0:T(8,128)}), f32[4,32,1152]{2,1,0:T(8,128)S(1)}, u32[]{:S(2)}, u32[]{:S(2)}) async-start(f32[4,32,1152]{2,1,0:T(8,128)} %get-tuple-element.14), calls=%async_computation.2 | async-start | bytes 1179648 | tf_op jit(solution)/shard_map/all_to_all | solution.py:402

commit v7 on v6

--- a/solution.py
+++ b/solution.py
@@ -175,38 +175,34 @@
             into_ref[n * streams : (n + 1) * streams, i * lanes : (i + 1) * lanes] = part
 
 
-def col_kernel(jac_ref, error_ref, hi_ref, lo_ref, out_ref, parts_ref, sum_ref, *, col_rows):
+def col_kernel(jac_ref, error_ref, hi_ref, lo_ref, out_ref, parts_ref, own_ref, term_ref, *, col_rows):
     streams, rows, lanes = jac_ref.shape
-    slab, tile_cols = hi_ref.shape
+    slab = hi_ref.shape[1]
     slab_rows = slab // lanes
     step = pl.program_id(0)
     flat = jac_ref.reshape(streams * rows, lanes)
-    stacked_parts(flat, col_rows + step * slab_rows, slab_rows, streams, rows, parts_ref.at[:, 0:slab])
-    cross = five_products(parts_ref[:, 0:slab], hi_ref[...], lo_ref[...], ((1,), (0,)))
 
     @pl.when(step == 0)
     def _():
-        sum_ref[...] = cross
-
-    @pl.when(step > 0)
-    def _():
-        sum_ref[...] += cross
+        stacked_parts(flat, col_rows, rows - col_rows, streams, rows, parts_ref)
+        term_ref[...] = jnp.zeros_like(term_ref)
+
+    cross = five_products(parts_ref[...], hi_ref[...], lo_ref[...], ((1,), (0,)))
+    out_ref[step, :, 0:slab] = cross
+    stacked_parts(flat, step * slab_rows, slab_rows, streams, rows, own_ref)
+    term_ref[...] += dot(own_ref[...], jnp.concatenate(split3(cross), axis=0), ((1,), (1,)))
 
     @pl.when(step == pl.num_programs(0) - 1)
     def _():
-        stacked_parts(flat, 0, col_rows, streams, rows, parts_ref)
-        total = sum_ref[...]
-        products = dot(parts_ref[...], jnp.concatenate(split3(total), axis=0), ((1,), (1,)))
         term = jnp.zeros((streams, streams), f32)
         for left, right in ((2, 0), (1, 1), (0, 2), (1, 0), (0, 1), (0, 0)):
-            term = term + products[
+            term = term + term_ref[
                 left * streams : (left + 1) * streams, right * streams : (right + 1) * streams
             ]
         own_at = lax.axis_index("row") * lax.axis_size("col") + lax.axis_index("col")
         stream_at = lax.broadcasted_iota(jnp.int32, (streams, lanes), 0)
         error = jnp.where(stream_at == own_at, error_ref[0], 0.0)
-        for n in range(tile_cols // slab):
-            out_ref[n, :, 0:slab] = total[:, n * slab : (n + 1) * slab]
+        for n in range(out_ref.shape[0]):
             out_ref[n, :, slab:] = error
             out_ref[n, :, slab : slab + streams] = term
 
@@ -215,10 +211,10 @@
     streams = jac.shape[0]
     tile_rows, tile_cols = hi.shape
     out_shape = (tile_cols // slab, streams, slab + LANES)
-    block = pl.BlockSpec((slab, tile_cols), lambda n: (n, 0))
+    block = pl.BlockSpec((tile_rows, slab), lambda n: (0, n))
     return pl.pallas_call(
         functools.partial(col_kernel, col_rows=tile_cols // LANES),
-        grid=(tile_rows // slab,),
+        grid=(tile_cols // slab,),
         in_specs=[
             pl.BlockSpec(jac.shape, lambda n: (0, 0, 0)),
             pl.BlockSpec(error.shape, lambda n: (0, 0, 0)),
@@ -228,8 +224,9 @@
         out_specs=pl.BlockSpec(out_shape, lambda n: (0, 0, 0)),
         out_shape=jax.ShapeDtypeStruct(out_shape, f32),
         scratch_shapes=[
-            pltpu.VMEM((3 * streams, tile_cols), bf16),
-            pltpu.VMEM((streams, tile_cols), f32),
+            pltpu.VMEM((3 * streams, tile_rows), bf16),
+            pltpu.VMEM((3 * streams, slab), bf16),
+            pltpu.VMEM((3 * streams, 3 * streams), f32),
         ],
         compiler_params=pltpu.CompilerParams(vmem_limit_bytes=16 << 20),
         name="col_cross",
@@ -244,10 +241,12 @@
     def _():
         stacked_parts(flat, 0, hi_ref.shape[1] // lanes, streams, rows, parts_ref)
 
-    cross_ref[...] = five_products(parts_ref[...], hi_ref[...], lo_ref[...], ((1,), (1,)))
-
-
-def row_partial(jac, hi, lo, slab):
+    cross = five_products(parts_ref[...], hi_ref[...], lo_ref[...], ((1,), (1,)))
+    for n in range(cross_ref.shape[0]):
+        cross_ref[n] = cross
+
+
+def row_partial(jac, hi, lo, slab, copies):
     streams = jac.shape[0]
     tile_rows, tile_cols = hi.shape
     block = pl.BlockSpec((slab, tile_cols), lambda n: (n, 0))
@@ -255,37 +254,54 @@
         row_kernel,
         grid=(tile_rows // slab,),
         in_specs=[pl.BlockSpec(jac.shape, lambda n: (0, 0, 0)), block, block],
-        out_specs=pl.BlockSpec((streams, slab), lambda n: (0, n)),
-        out_shape=jax.ShapeDtypeStruct((streams, tile_rows), f32),
+        out_specs=pl.BlockSpec((copies, streams, slab), lambda n: (0, 0, n)),
+        out_shape=pltpu.HBM((copies, streams, tile_rows + LANES), f32),
         scratch_shapes=[pltpu.VMEM((3 * streams, tile_cols), bf16)],
         compiler_params=pltpu.CompilerParams(vmem_limit_bytes=16 << 20),
         name="row_cross",
     )(jac, in_hbm(hi), in_hbm(lo))
 
 
-def slab_kernel(pieces_ref, row_ref, own_ref, out_ref):
-    tile_rows = row_ref.shape[1]
+def slab_kernel(pieces_ref, _, own_ref, out_ref, beside_ref, sems):
+    lanes = beside_ref.shape[1]
     slab = own_ref.shape[1]
-    total = pieces_ref[0]
+    copies = out_ref.shape[0]
+    beside = pieces_ref[0, :, slab:]
     for n in range(1, pieces_ref.shape[0]):
-        total = total + pieces_ref[n]
-    own_ref[...] = total[:, 0:slab]
-    for n in range(out_ref.shape[0]):
-        out_ref[n, :, 0:tile_rows] = row_ref[...]
-        out_ref[n, :, tile_rows:] = total[:, slab:]
-
-
-def slab_sum(pieces, row_part, copies):
+        beside = beside + pieces_ref[n, :, slab:]
+    beside_ref[...] = beside
+    writes = []
+    for n in range(copies):
+        place = out_ref.at[n, :, pl.ds(out_ref.shape[2] - lanes, lanes)]
+        writes.append(pltpu.make_async_copy(beside_ref, place, sems.at[n]))
+        writes[-1].start()
+    total = pieces_ref[0, :, 0:slab]
+    for n in range(1, pieces_ref.shape[0]):
+        total = total + pieces_ref[n, :, 0:slab]
+    own_ref[...] = total
+    for write in writes:
+        write.wait()
+
+
+def slab_sum(pieces, row_part):
     _, streams, padded = pieces.shape
-    tile_rows = row_part.shape[1]
+    whole = pl.BlockSpec(memory_space=pltpu.VMEM)
+    beyond = pl.BlockSpec(memory_space=pl.ANY)
     return pl.pallas_call(
         slab_kernel,
+        in_specs=[whole, beyond],
+        out_specs=[whole, beyond],
         out_shape=[
             jax.ShapeDtypeStruct((streams, padded - LANES), f32),
-            jax.ShapeDtypeStruct((copies, streams, tile_rows + LANES), f32),
-        ],
+            pltpu.HBM(row_part.shape, f32),
+        ],
+        scratch_shapes=[
+            pltpu.VMEM((streams, LANES), f32),
+            pltpu.SemaphoreType.DMA((row_part.shape[0],)),
+        ],
+        input_output_aliases={1: 1},
         name="slab",
-    )(pieces, row_part)
+    )(in_hbm(pieces), in_hbm(row_part))
 
 
 def invert(innovation):
@@ -305,16 +321,18 @@
 
 
 def update_kernel(
-    rows_ref, cols_ref, weight_ref, cov_ref, new_weight_ref, new_cov_ref, right_ref, tile_ref, in_sems, out_sems
+    rows_ref, cols_ref, weight_ref, cov_ref, new_weight_ref, new_cov_ref, left_ref, right_ref, tile_ref, in_sems, out_sems
 ):
     copies, streams, padded = rows_ref.shape
     col_slabs, _, slab = cols_ref.shape
     lanes = weight_ref.shape[1]
     tile_rows = padded - lanes
     slabs = tile_rows // slab
+    chunks = in_sems.shape[0]
+    height = tile_rows // chunks
     reads = []
-    for n in range(slabs):
-        here = pl.ds(n * slab, slab)
+    for n in range(chunks):
+        here = pl.ds(n * height, height)
         reads.append(pltpu.make_async_copy(cov_ref.at[here], tile_ref.at[here], in_sems.at[n]))
         reads[-1].start()
     total = rows_ref[0]
@@ -327,23 +345,25 @@
         hi, mid, lo = split3(cols_ref[n])
         for m, part in enumerate((hi, mid, lo, hi, mid, hi)):
             right_ref[m * streams : (m + 1) * streams, n * slab : (n + 1) * slab] = part
-    col_at = lax.axis_index("col")
-    own_at = (lax.axis_index("row") * slabs + col_at) * (slab // lanes)
+    gain = dot(inverse, total[:, 0:tile_rows], ((0,), (0,)), highest)
+    hi, mid, lo = split3(gain)
+    for m, part in enumerate((hi, hi, hi, mid, mid, lo)):
+        left_ref[m * streams : (m + 1) * streams, :] = part
     writes = []
-    for n in range(slabs):
-        gain = dot(inverse, total[:, n * slab : (n + 1) * slab], ((0,), (0,)), highest)
-        hi, mid, lo = split3(gain)
-        left = jnp.concatenate([hi, hi, hi, mid, mid, lo], axis=0)
-        update = dot(left, right_ref[...], ((0,), (0,)))
-        here = pl.ds(n * slab, slab)
+    for n in range(chunks):
+        update = dot(left_ref[:, n * height : (n + 1) * height], right_ref[...], ((0,), (0,)))
+        here = pl.ds(n * height, height)
         reads[n].wait()
         tile_ref[here, :] = (tile_ref[here, :] - update) * (1.0 / forget)
         writes.append(pltpu.make_async_copy(tile_ref.at[here], new_cov_ref.at[here], out_sems.at[n]))
         writes[-1].start()
+    col_at = lax.axis_index("col")
+    own_at = (lax.axis_index("row") * slabs + col_at) * (slab // lanes)
+    for n in range(slabs):
 
         @pl.when(col_at == n)
         def _():
-            moved = jnp.sum(gain * errors, axis=0, keepdims=True)
+            moved = jnp.sum(gain[:, n * slab : (n + 1) * slab] * errors, axis=0, keepdims=True)
             for i in range(slab // lanes):
                 own = weight_ref[pl.ds(own_at + i, 1), :]
                 new_weight_ref[i : i + 1, :] = own + moved[:, i * lanes : (i + 1) * lanes]
@@ -355,7 +375,6 @@
 def update(row_parts, col_slabs, layer_weight, covariance):
     _, streams, slab = col_slabs.shape
     tile_rows, tile_cols = covariance.shape
-    slabs = tile_rows // slab
     width = layer_weight.shape[1]
     whole = pl.BlockSpec(memory_space=pltpu.VMEM)
     beyond = pl.BlockSpec(memory_space=pl.ANY)
@@ -368,10 +387,11 @@
             jax.ShapeDtypeStruct((tile_rows, tile_cols), f32),
         ],
         scratch_shapes=[
+            pltpu.VMEM((6 * streams, tile_rows), bf16),
             pltpu.VMEM((6 * streams, tile_cols), bf16),
             pltpu.VMEM((tile_rows, tile_cols), f32),
-            pltpu.SemaphoreType.DMA((slabs,)),
-            pltpu.SemaphoreType.DMA((slabs,)),
+            pltpu.SemaphoreType.DMA((8,)),
+            pltpu.SemaphoreType.DMA((8,)),
         ],
         compiler_params=pltpu.CompilerParams(vmem_limit_bytes=32 << 20),
         name="update",
@@ -454,8 +474,8 @@
     jac = jac.reshape(-1, *jac.shape[2:])
     hi, lo = stage(covariance)
     col_pieces = exchange(col_partial(jac, error, hi, lo, slab), "row")
-    row_part = row_partial(jac, hi, lo, slab)
-    col_own, row_part = slab_sum(col_pieces, row_part, cols_n)
+    row_part = row_partial(jac, hi, lo, slab, cols_n)
+    col_own, row_part = slab_sum(col_pieces, row_part)
     row_parts = exchange(row_part, "col")
     col_slabs = lax.all_gather(col_own, "row", axis=0, tiled=False)
     new_weight, new_cov = update(row_parts, col_slabs, layer_weight, covariance)

time: 72.5 us -> 75.5 us (1.041)
  Pallas kernels: 34.5 us -> 37.8 us
    pallas_call x1, Pallas kernels: 6.05 us -> 8.41 us  [col_partial(): pl.pallas_call(functools.partial(col_kernel, col_rows=tile_cols // LANES)...]
  transfers between devices with their start and end apart: 3 -> 3, of which waited for: 3 -> 3; matrix products, arithmetic and copies ran while one was open for 0% -> 0% of each run, Pallas kernels for 20% -> 21%
where the time goes in v7:
time: 75.5 us; the launch traced here: 74.5 us
  Pallas kernels  37.8 us (50%)
  starting transfers between devices  14.8 us (20%)
  waiting for transfers between devices  11.4 us (15%)
  blocking collectives  8.53 us (11%)
  between operations  1.31 us (2%)
    all_to_all x3, starting transfers between devices, exchange(): return lax.all_to_all(x, axes, split_axis=0, concat_axis=0, tiled=True)  14.8 us
    all_to_all x3, waiting for transfers between devices, exchange(): return lax.all_to_all(x, axes, split_axis=0, concat_axis=0, tiled=True)  11.4 us
    pallas_call x1, Pallas kernels, stage(): pl.pallas_call(stage_kernel, grid=(rows // height,), in_specs=[block], ou...  8.95 us
    all_gather x1, blocking collectives, on_device(): col_slabs = lax.all_gather(col_own, 'row', axis=0, tiled=False)  8.53 us
    pallas_call x1, Pallas kernels, col_partial(): pl.pallas_call(functools.partial(col_kernel, col_rows=tile_cols // LANES)...  8.41 us
    pallas_call x1, Pallas kernels, update(): pl.pallas_call(update_kernel, in_specs=[whole, whole, whole, beyond], out...  8.13 us
    pallas_call x1, Pallas kernels, row_partial(): pl.pallas_call(row_kernel, grid=(tile_rows // slab,), in_specs=[pl.BlockS...  6.34 us
    pallas_call x1, Pallas kernels, network(): pl.pallas_call(functools.partial(network_kernel, plan=plan), grid=(per_de...  3.66 us
  transfers between devices with their start and end apart: 3, of which 3 were waited for; matrix products, arithmetic and copies ran while one was open for 0% of the time, Pallas kernels for 21%

profile of v7, /device:TPU:0, one launch (start us, length us, event | category | flops | bytes accessed | tf_op | source)
XLA Modules:
  0.0 74.5 jit_solution(6340942131270651841)
XLA Ops:
  1.3 3.7 %network.1 = (f32[32,1,24,128]{3,2,1,0:T(8,128)}, f32[1,1,128]{2,1,0:T(1,128)}) custom-call(s32[1,1,256]{2,1,0:T(1,128)} %bitcast.13, s32[1,32,256]{2,1,0:T(8,128)} %ids_ref.1, f32[1,32,256]{2,1,0:T(8,128)} %switch_ref.1, f32[1,64,256]{2,1,0:T(8,128)} %bitcast.12, f32[1,1,256]{2,1,0:T(1,128)} %bitcast.14, f32[1,1,1]{2,1,0:T(1,128)} %bitcast.8.target_ref, ...), custom_call_target="tpu_custom_call" | custom-call | tf_op jit(solution)/shard_map/network/pallas_call | solution.py:101
  4.9 0.0 copy-start.1
  4.9 7.3 %all-to-all-start = ((f32[32,1,24,128]{3,2,1,0:T(8,128)}), f32[32,1,24,128]{3,2,1,0:T(8,128)S(1)}, u32[]{:S(2)}, u32[]{:S(2)}) async-start(f32[32,1,24,128]{3,2,1,0:T(8,128)} %get-tuple-element.10), calls=%async_computation | async-start | bytes 786432 | tf_op jit(solution)/shard_map/all_to_all | solution.py:422
  12.2 9.0 %stage.1 = (bf16[1024,2048]{1,0:T(8,128)(2,1)}, bf16[1024,2048]{1,0:T(8,128)(2,1)}) custom-call(f32[1024,2048]{1,0:T(8,128)} %cov_ref.3), custom_call_target="tpu_custom_call" | custom-call | tf_op jit(solution)/shard_map/stage/pallas_call | solution.py:150
  21.2 2.9 %all-to-all-done = f32[32,1,24,128]{3,2,1,0:T(8,128)S(1)} async-done(((f32[32,1,24,128]{3,2,1,0:T(8,128)}), f32[32,1,24,128]{3,2,1,0:T(8,128)S(1)}, u32[]{:S(2)}, u32[]{:S(2)}) %all-to-all-start) | async-done | bytes 393248 | tf_op jit(solution)/shard_map/all_to_all | solution.py:422
  24.1 0.0 copy-done.1
  24.1 8.4 %col_cross.1 = f32[8,32,384]{2,1,0:T(8,128)} custom-call(f32[32,24,128]{2,1,0:T(8,128)S(1)} %bitcast.9, f32[1,1,128]{2,1,0:T(1,128)S(1)} %copy-done.1, bf16[1024,2048]{1,0:T(8,128)(2,1)} %get-tuple-element.12.hi_ref, bf16[1024,2048]{1,0:T(8,128)(2,1)} %get-tuple-element.13.lo_ref), custom_call_target="tpu_custom_call" | custom-call | tf_op jit(solution)/shard_map/col_cross/pallas_call | solution.py:215
  32.5 0.0 copy-start
  32.5 3.6 %all-to-all-start.1 = ((f32[8,32,384]{2,1,0:T(8,128)}), f32[8,32,384]{2,1,0:T(8,128)S(1)}, u32[]{:S(2)}, u32[]{:S(2)}) async-start(f32[8,32,384]{2,1,0:T(8,128)} %col_cross.1), calls=%async_computation.1 | async-start | bytes 786432 | tf_op jit(solution)/shard_map/all_to_all | solution.py:422
  36.1 6.3 %row_cross.1._ = f32[4,32,1152]{2,1,0:T(8,128)} custom-call(f32[32,24,128]{2,1,0:T(8,128)S(1)} %bitcast.10, bf16[1024,2048]{1,0:T(8,128)(2,1)} %get-tuple-element.12.hi_ref, bf16[1024,2048]{1,0:T(8,128)(2,1)} %get-tuple-element.13.lo_ref), custom_call_target="tpu_custom_call" | custom-call | tf_op jit(solution)/shard_map/row_cross/pallas_call | solution.py:253
  42.4 1.9 %all-to-all-done.1.pieces_ref = f32[8,32,384]{2,1,0:T(8,128)S(1)} async-done(((f32[8,32,384]{2,1,0:T(8,128)}), f32[8,32,384]{2,1,0:T(8,128)S(1)}, u32[]{:S(2)}, u32[]{:S(2)}) %all-to-all-start.1) | async-done | bytes 393248 | tf_op jit(solution)/shard_map/all_to_all | solution.py:422
  44.4 0.0 copy-start.2
  44.4 0.7 copy-done.2
  45.1 2.3 %slab.1 = (f32[32,256]{1,0:T(8,128)}, f32[4,32,1152]{2,1,0:T(8,128)}) custom-call(f32[8,32,384]{2,1,0:T(8,128)} %copy-done.2, f32[4,32,1152]{2,1,0:T(8,128)} %row_cross.1._), custom_call_target="tpu_custom_call", output_to_operand_aliasing={{1}: (1, {})} | custom-call | tf_op jit(solution)/shard_map/slab/pallas_call | solution.py:290
  47.4 3.9 %all-to-all-start.2 = ((f32[4,32,1152]{2,1,0:T(8,128)}), f32[4,32,1152]{2,1,0:T(8,128)S(1)}, u32[]{:S(2)}, u32[]{:S(2)}) async-start(f32[4,32,1152]{2,1,0:T(8,128)} %get-tuple-element.14), calls=%async_computation.2 | async-start | bytes 1179648 | tf_op jit(solution)/shard_map/all_to_all | solution.py:422
  51.3 8.5 %all-gather = f32[256,256]{1,0:T(8,128)S(1)} all-gather(f32[32,256]{1,0:T(8,128)} %get-tuple-element.15), channel_id=2, replica_groups=mesh['row'=8,'col'=4] {'row'}, dimensions={0}, use_global_device_ids=true | all-gather | bytes 294912 | tf_op jit(solution)/shard_map/all_gather | solution.py:480
  59.8 6.6 %all-to-all-done.2.rows_ref = f32[4,32,1152]{2,1,0:T(8,128)S(1)} async-done(((f32[4,32,1152]{2,1,0:T(8,128)}), f32[4,32,1152]{2,1,0:T(8,128)S(1)}, u32[]{:S(2)}, u32[]{:S(2)}) %all-to-all-start.2) | async-done | bytes 589856 | tf_op jit(solution)/shard_map/all_to_all | solution.py:422
  66.4 0.0 copy-done
  66.4 8.1 %update.1 = (f32[2,128]{1,0:T(2,128)}, f32[1024,2048]{1,0:T(8,128)}) custom-call(f32[4,32,1152]{2,1,0:T(8,128)S(1)} %all-to-all-done.2.rows_ref, f32[8,32,256]{2,1,0:T(8,128)S(1)} %bitcast.11, f32[64,128]{1,0:T(8,128)S(1)} %copy-done, f32[1024,2048]{1,0:T(8,128)} %cov_ref.3), custom_call_target="tpu_custom_call" | custom-call | tf_op jit(solution)/shard_map/update/pallas_call | solution.py:381
Async XLA Ops:
  4.9 19.1 %copy-start.1 = (f32[1,1,128]{2,1,0:T(1,128)S(1)}, f32[1,1,128]{2,1,0:T(1,128)}, u32[]{:S(2)}) copy-start(f32[1,1,128]{2,1,0:T(1,128)} %get-tuple-element.11.error_ref) | copy-start | bytes 1540
  4.9 19.1 %all-to-all-start = ((f32[32,1,24,128]{3,2,1,0:T(8,128)}), f32[32,1,24,128]{3,2,1,0:T(8,128)S(1)}, u32[]{:S(2)}, u32[]{:S(2)}) async-start(f32[32,1,24,128]{3,2,1,0:T(8,128)} %get-tuple-element.10), calls=%async_computation | async-start | bytes 786432 | tf_op jit(solution)/shard_map/all_to_all | solution.py:422
  32.5 33.9 %copy-start = (f32[64,128]{1,0:T(8,128)S(1)}, f32[64,128]{1,0:T(8,128)}, u32[]{:S(2)}) copy-start(f32[64,128]{1,0:T(8,128)} %weight_ref.3) | copy-start | bytes 98308
  32.5 11.9 %all-to-all-start.1 = ((f32[8,32,384]{2,1,0:T(8,128)}), f32[8,32,384]{2,1,0:T(8,128)S(1)}, u32[]{:S(2)}, u32[]{:S(2)}) async-start(f32[8,32,384]{2,1,0:T(8,128)} %col_cross.1), calls=%async_computation.1 | async-start | bytes 786432 | tf_op jit(solution)/shard_map/all_to_all | solution.py:422
  44.4 0.7 %copy-start.2 = (f32[8,32,384]{2,1,0:T(8,128)}, f32[8,32,384]{2,1,0:T(8,128)S(1)}, u32[]{:S(2)}) copy-start(f32[8,32,384]{2,1,0:T(8,128)S(1)} %all-to-all-done.1.pieces_ref) | copy-start | bytes 1179652
  47.4 19.0 %all-to-all-start.2 = ((f32[4,32,1152]{2,1,0:T(8,128)}), f32[4,32,1152]{2,1,0:T(8,128)S(1)}, u32[]{:S(2)}, u32[]{:S(2)}) async-start(f32[4,32,1152]{2,1,0:T(8,128)} %get-tuple-element.14), calls=%async_computation.2 | async-start | bytes 1179648 | tf_op jit(solution)/shard_map/all_to_all | solution.py:422

commit v8 on v6

--- a/solution.py
+++ b/solution.py
@@ -36,6 +36,10 @@
 def split2(x):
     hi = x.astype(bf16)
     return hi, (x - hi.astype(f32)).astype(bf16)
+
+
+def limit(mib):
+    return pltpu.CompilerParams(vmem_limit_bytes=mib << 20)
 
 
 def network_kernel(
@@ -121,6 +125,7 @@
             jax.ShapeDtypeStruct((per_dev, 1, width), f32),
         ],
         scratch_shapes=[pltpu.VMEM((atoms, atoms), f32)],
+        compiler_params=limit(8),
         name="network",
     )(
         atom_types.reshape(per_dev, 1, atoms),
@@ -135,10 +140,6 @@
     )
 
 
-def in_hbm(x):
-    return pltpu.with_memory_space_constraint(x, pltpu.HBM)
-
-
 def stage_kernel(cov_ref, hi_ref, lo_ref):
     hi_ref[...], lo_ref[...] = split2(cov_ref[...])
 
@@ -152,10 +153,10 @@
         grid=(rows // height,),
         in_specs=[block],
         out_specs=[block] * 2,
-        out_shape=[pltpu.HBM((rows, cols), bf16)] * 2,
-        compiler_params=pltpu.CompilerParams(vmem_limit_bytes=16 << 20),
+        out_shape=[jax.ShapeDtypeStruct((rows, cols), bf16)] * 2,
+        compiler_params=limit(12),
         name="stage",
-    )(in_hbm(covariance))
+    )(covariance)
 
 
 def five_products(parts, hi, lo, contract):
@@ -175,18 +176,19 @@
             into_ref[n * streams : (n + 1) * streams, i * lanes : (i + 1) * lanes] = part
 
 
-def col_kernel(jac_ref, error_ref, hi_ref, lo_ref, out_ref, parts_ref, sum_ref, *, col_rows):
+def col_kernel(jac_ref, error_ref, hi_ref, lo_ref, out_ref, parts_ref, own_ref, sum_ref, *, col_rows):
     streams, rows, lanes = jac_ref.shape
     slab, tile_cols = hi_ref.shape
     slab_rows = slab // lanes
     step = pl.program_id(0)
     flat = jac_ref.reshape(streams * rows, lanes)
-    stacked_parts(flat, col_rows + step * slab_rows, slab_rows, streams, rows, parts_ref.at[:, 0:slab])
-    cross = five_products(parts_ref[:, 0:slab], hi_ref[...], lo_ref[...], ((1,), (0,)))
+    stacked_parts(flat, col_rows + step * slab_rows, slab_rows, streams, rows, own_ref)
+    cross = five_products(own_ref[...], hi_ref[...], lo_ref[...], ((1,), (0,)))
 
     @pl.when(step == 0)
     def _():
         sum_ref[...] = cross
+        stacked_parts(flat, 0, col_rows, streams, rows, parts_ref)
 
     @pl.when(step > 0)
     def _():
@@ -194,7 +196,6 @@
 
     @pl.when(step == pl.num_programs(0) - 1)
     def _():
-        stacked_parts(flat, 0, col_rows, streams, rows, parts_ref)
         total = sum_ref[...]
         products = dot(parts_ref[...], jnp.concatenate(split3(total), axis=0), ((1,), (1,)))
         term = jnp.zeros((streams, streams), f32)
@@ -229,11 +230,12 @@
         out_shape=jax.ShapeDtypeStruct(out_shape, f32),
         scratch_shapes=[
             pltpu.VMEM((3 * streams, tile_cols), bf16),
+            pltpu.VMEM((3 * streams, slab), bf16),
             pltpu.VMEM((streams, tile_cols), f32),
         ],
-        compiler_params=pltpu.CompilerParams(vmem_limit_bytes=16 << 20),
+        compiler_params=limit(12),
         name="col_cross",
-    )(jac, error, in_hbm(hi), in_hbm(lo))
+    )(jac, error, hi, lo)
 
 
 def row_kernel(jac_ref, hi_ref, lo_ref, cross_ref, parts_ref):
@@ -258,9 +260,9 @@
         out_specs=pl.BlockSpec((streams, slab), lambda n: (0, n)),
         out_shape=jax.ShapeDtypeStruct((streams, tile_rows), f32),
         scratch_shapes=[pltpu.VMEM((3 * streams, tile_cols), bf16)],
-        compiler_params=pltpu.CompilerParams(vmem_limit_bytes=16 << 20),
+        compiler_params=limit(12),
         name="row_cross",
-    )(jac, in_hbm(hi), in_hbm(lo))
+    )(jac, hi, lo)
 
 
 def slab_kernel(pieces_ref, row_ref, own_ref, out_ref):
@@ -284,6 +286,7 @@
             jax.ShapeDtypeStruct((streams, padded - LANES), f32),
             jax.ShapeDtypeStruct((copies, streams, tile_rows + LANES), f32),
         ],
+        compiler_params=limit(8),
         name="slab",
     )(pieces, row_part)
 
@@ -305,16 +308,18 @@
 
 
 def update_kernel(
-    rows_ref, cols_ref, weight_ref, cov_ref, new_weight_ref, new_cov_ref, right_ref, tile_ref, in_sems, out_sems
+    rows_ref, cols_ref, weight_ref, cov_ref, new_weight_ref, new_cov_ref, left_ref, right_ref, tile_ref, in_sems, out_sems
 ):
     copies, streams, padded = rows_ref.shape
     col_slabs, _, slab = cols_ref.shape
     lanes = weight_ref.shape[1]
     tile_rows = padded - lanes
     slabs = tile_rows // slab
+    chunks = in_sems.shape[0]
+    height = tile_rows // chunks
     reads = []
-    for n in range(slabs):
-        here = pl.ds(n * slab, slab)
+    for n in range(chunks):
+        here = pl.ds(n * height, height)
         reads.append(pltpu.make_async_copy(cov_ref.at[here], tile_ref.at[here], in_sems.at[n]))
         reads[-1].start()
     total = rows_ref[0]
@@ -327,23 +332,25 @@
         hi, mid, lo = split3(cols_ref[n])
         for m, part in enumerate((hi, mid, lo, hi, mid, hi)):
             right_ref[m * streams : (m + 1) * streams, n * slab : (n + 1) * slab] = part
-    col_at = lax.axis_index("col")
-    own_at = (lax.axis_index("row") * slabs + col_at) * (slab // lanes)
+    gain = dot(inverse, total[:, 0:tile_rows], ((0,), (0,)), highest)
+    hi, mid, lo = split3(gain)
+    for m, part in enumerate((hi, hi, hi, mid, mid, lo)):
+        left_ref[m * streams : (m + 1) * streams, :] = part
     writes = []
-    for n in range(slabs):
-        gain = dot(inverse, total[:, n * slab : (n + 1) * slab], ((0,), (0,)), highest)
-        hi, mid, lo = split3(gain)
-        left = jnp.concatenate([hi, hi, hi, mid, mid, lo], axis=0)
-        update = dot(left, right_ref[...], ((0,), (0,)))
-        here = pl.ds(n * slab, slab)
+    for n in range(chunks):
+        update = dot(left_ref[:, n * height : (n + 1) * height], right_ref[...], ((0,), (0,)))
+        here = pl.ds(n * height, height)
         reads[n].wait()
         tile_ref[here, :] = (tile_ref[here, :] - update) * (1.0 / forget)
         writes.append(pltpu.make_async_copy(tile_ref.at[here], new_cov_ref.at[here], out_sems.at[n]))
         writes[-1].start()
+    col_at = lax.axis_index("col")
+    own_at = (lax.axis_index("row") * slabs + col_at) * (slab // lanes)
+    for n in range(slabs):
 
         @pl.when(col_at == n)
         def _():
-            moved = jnp.sum(gain * errors, axis=0, keepdims=True)
+            moved = jnp.sum(gain[:, n * slab : (n + 1) * slab] * errors, axis=0, keepdims=True)
             for i in range(slab // lanes):
                 own = weight_ref[pl.ds(own_at + i, 1), :]
                 new_weight_ref[i : i + 1, :] = own + moved[:, i * lanes : (i + 1) * lanes]
@@ -355,7 +362,6 @@
 def update(row_parts, col_slabs, layer_weight, covariance):
     _, streams, slab = col_slabs.shape
     tile_rows, tile_cols = covariance.shape
-    slabs = tile_rows // slab
     width = layer_weight.shape[1]
     whole = pl.BlockSpec(memory_space=pltpu.VMEM)
     beyond = pl.BlockSpec(memory_space=pl.ANY)
@@ -368,14 +374,15 @@
             jax.ShapeDtypeStruct((tile_rows, tile_cols), f32),
         ],
         scratch_shapes=[
+            pltpu.VMEM((6 * streams, tile_rows), bf16),
             pltpu.VMEM((6 * streams, tile_cols), bf16),
             pltpu.VMEM((tile_rows, tile_cols), f32),
-            pltpu.SemaphoreType.DMA((slabs,)),
-            pltpu.SemaphoreType.DMA((slabs,)),
-        ],
-        compiler_params=pltpu.CompilerParams(vmem_limit_bytes=32 << 20),
+            pltpu.SemaphoreType.DMA((8,)),
+            pltpu.SemaphoreType.DMA((8,)),
+        ],
+        compiler_params=limit(20),
         name="update",
-    )(row_parts, col_slabs, layer_weight, in_hbm(covariance))
+    )(row_parts, col_slabs, layer_weight, covariance)
 
 
 def plain_steps(at, jac_all, errors, layer_weight, covariance, slab, cols_n):

time: 72.5 us -> 80.4 us (1.11)
  local copies, waits for them, and re-layouts: 1.39 us -> 25.3 us
  Pallas kernels: 34.5 us -> 18 us
    unnamed x8 -> x34, local copies, waits for them, and re-layouts: 1.39 us -> 25.3 us
    pallas_call x1, Pallas kernels: 8.95 us -> 1.23 us  [stage(): pl.pallas_call(stage_kernel, grid=(rows // height,), in_specs=[block], ou...]
    pallas_call x1, Pallas kernels: 6.05 us -> 3.19 us  [col_partial(): pl.pallas_call(functools.partial(col_kernel, col_rows=tile_cols // LANES)...]
    pallas_call x1, Pallas kernels: 5.64 us -> 3.15 us  [row_partial(): pl.pallas_call(row_kernel, grid=(tile_rows // slab,), in_specs=[pl.BlockS...]
    pallas_call x1, Pallas kernels: 8.33 us -> 6.81 us  [update(): pl.pallas_call(update_kernel, in_specs=[whole, whole, whole, beyond], out...]
    pallas_call x1, Pallas kernels: 1.89 us -> 0.85 us  [slab_sum(): pl.pallas_call(slab_kernel, out_shape=[jax.ShapeDtypeStruct((streams, pad...]
    pallas_call x1, Pallas kernels: 3.66 us -> 2.77 us  [network(): pl.pallas_call(functools.partial(network_kernel, plan=plan), grid=(per_de...]
  transfers between devices with their start and end apart: 3 -> 3, of which waited for: 3 -> 3; matrix products, arithmetic and copies ran while one was open for 0% -> 0% of each run, Pallas kernels for 20% -> 6%
where the time goes in v8:
time: 80.4 us; the launch traced here: 79.5 us
  local copies, waits for them, and re-layouts  25.3 us (31%)
  Pallas kernels  18 us (22%)
  starting transfers between devices  14.6 us (18%)
  waiting for transfers between devices  11.3 us (14%)
  blocking collectives  9 us (11%)
  between operations  1.36 us (2%)
    unnamed x34, local copies, waits for them, and re-layouts  25.3 us
    all_to_all x3, starting transfers between devices, exchange(): return lax.all_to_all(x, axes, split_axis=0, concat_axis=0, tiled=True)  14.6 us
    all_to_all x3, waiting for transfers between devices, exchange(): return lax.all_to_all(x, axes, split_axis=0, concat_axis=0, tiled=True)  11.3 us
    all_gather x1, blocking collectives, on_device(): col_slabs = lax.all_gather(col_own, 'row', axis=0, tiled=False)  9 us
    pallas_call x1, Pallas kernels, update(): pl.pallas_call(update_kernel, in_specs=[whole, whole, whole, beyond], out...  6.81 us
    pallas_call x1, Pallas kernels, col_partial(): pl.pallas_call(functools.partial(col_kernel, col_rows=tile_cols // LANES)...  3.19 us
    pallas_call x1, Pallas kernels, row_partial(): pl.pallas_call(row_kernel, grid=(tile_rows // slab,), in_specs=[pl.BlockS...  3.15 us
    pallas_call x1, Pallas kernels, network(): pl.pallas_call(functools.partial(network_kernel, plan=plan), grid=(per_de...  2.77 us
  transfers between devices with their start and end apart: 3, of which 3 were waited for; matrix products, arithmetic and copies ran while one was open for 0% of the time, Pallas kernels for 6%

profile of v8, /device:TPU:0, one launch (start us, length us, event | category | flops | bytes accessed | tf_op | source)
XLA Modules:
  0.0 79.5 jit_solution(14351768716900102132)
XLA Ops:
  1.3 0.0 copy-start.8
  1.3 0.7 copy-done.8
  2.0 0.0 copy-start.10
  2.0 0.8 %copy-done.10 = f32[1,256,64]{1,2,0:T(8,128)S(1)} copy-done((f32[1,256,64]{1,2,0:T(8,128)S(1)}, f32[1,256,64]{1,2,0:T(8,128)}, u32[]{:S(2)}) %copy-start.10) | copy-done | bytes 65560
  2.9 0.0 copy-start.11
  2.9 0.8 copy-done.11
  3.6 0.0 copy-start.12
  3.6 0.8 copy-done.12
  4.4 0.0 copy-start.13
  4.4 0.7 copy-done.13
  5.1 0.0 copy-start.14
  5.1 0.7 copy-done.14
  5.8 0.0 copy-start.15
  5.8 0.7 copy-done.15
  6.4 0.0 copy-start.16
  6.4 0.7 copy-done.16
  7.1 2.8 %network.1 = (f32[32,1,24,128]{3,2,1,0:T(8,128)}, f32[1,1,128]{2,1,0:T(1,128)S(1)}) custom-call(s32[1,1,256]{2,1,0:T(1,128)S(1)} %bitcast.13, s32[1,32,256]{2,1,0:T(8,128)S(1)} %copy-done.11, f32[1,32,256]{2,1,0:T(8,128)S(1)} %copy-done.12, f32[1,64,256]{2,1,0:T(8,128)S(1)} %bitcast.12, f32[1,1,256]{2,1,0:T(1,128)S(1)} %bitcast.14, ...), custom_call_target="tpu_custom_call" | custom-call | tf_op jit(solution)/shard_map/network/pallas_call | solution.py:105
  9.9 7.3 %all-to-all-start = ((f32[32,1,24,128]{3,2,1,0:T(8,128)}), f32[32,1,24,128]{3,2,1,0:T(8,128)S(1)}, u32[]{:S(2)}, u32[]{:S(2)}) async-start(f32[32,1,24,128]{3,2,1,0:T(8,128)} %get-tuple-element.10), calls=%async_computation | async-start | bytes 786432 | tf_op jit(solution)/shard_map/all_to_all | solution.py:409
  17.2 0.0 copy-start
  17.2 3.4 %copy-done = f32[1024,2048]{1,0:T(8,128)S(1)} copy-done((f32[1024,2048]{1,0:T(8,128)S(1)}, f32[1024,2048]{1,0:T(8,128)}, u32[]{:S(2)}) %copy-start) | copy-done | bytes 8388632
  20.6 1.2 %stage.1 = (bf16[1024,2048]{1,0:T(8,128)(2,1)S(1)}, bf16[1024,2048]{1,0:T(8,128)(2,1)S(1)}) custom-call(f32[1024,2048]{1,0:T(8,128)S(1)} %copy-done), custom_call_target="tpu_custom_call" | custom-call | tf_op jit(solution)/shard_map/stage/pallas_call | solution.py:151
  21.8 0.0 copy-start.2
  21.8 2.0 %copy-done.2 = bf16[1024,2048]{1,0:T(8,128)(2,1)} copy-done((bf16[1024,2048]{1,0:T(8,128)(2,1)}, bf16[1024,2048]{1,0:T(8,128)(2,1)S(1)}, u32[]{:S(2)}) %copy-start.2) | copy-done | bytes 4194328
  23.8 0.0 copy-start.5
  23.8 1.9 %copy-done.5 = bf16[1024,2048]{1,0:T(8,128)(2,1)} copy-done((bf16[1024,2048]{1,0:T(8,128)(2,1)}, bf16[1024,2048]{1,0:T(8,128)(2,1)S(1)}, u32[]{:S(2)}) %copy-start.5) | copy-done | bytes 4194328
  25.7 3.2 %all-to-all-done = f32[32,1,24,128]{3,2,1,0:T(8,128)S(1)} async-done(((f32[32,1,24,128]{3,2,1,0:T(8,128)}), f32[32,1,24,128]{3,2,1,0:T(8,128)S(1)}, u32[]{:S(2)}, u32[]{:S(2)}) %all-to-all-start) | async-done | bytes 393248 | tf_op jit(solution)/shard_map/all_to_all | solution.py:409
  29.0 0.0 copy-start.3
  29.0 2.2 %copy-done.3 = bf16[1024,2048]{1,0:T(8,128)(2,1)S(1)} copy-done((bf16[1024,2048]{1,0:T(8,128)(2,1)S(1)}, bf16[1024,2048]{1,0:T(8,128)(2,1)}, u32[]{:S(2)}) %copy-start.3) | copy-done | bytes 4194328
  31.2 0.0 copy-start.6
  31.2 2.2 %copy-done.6 = bf16[1024,2048]{1,0:T(8,128)(2,1)S(1)} copy-done((bf16[1024,2048]{1,0:T(8,128)(2,1)S(1)}, bf16[1024,2048]{1,0:T(8,128)(2,1)}, u32[]{:S(2)}) %copy-start.6) | copy-done | bytes 4194328
  33.4 0.0 copy-start.9
  33.4 3.2 %col_cross.1 = f32[8,32,384]{2,1,0:T(8,128)} custom-call(f32[32,24,128]{2,1,0:T(8,128)S(1)} %bitcast.9, f32[1,1,128]{2,1,0:T(1,128)S(1)} %get-tuple-element.11.error_ref, bf16[1024,2048]{1,0:T(8,128)(2,1)S(1)} %copy-done.3, bf16[1024,2048]{1,0:T(8,128)(2,1)S(1)} %copy-done.6), custom_call_target="tpu_custom_call" | custom-call | tf_op jit(solution)/shard_map/col_cross/pallas_call | solution.py:220
  36.6 3.5 %all-to-all-start.1 = ((f32[8,32,384]{2,1,0:T(8,128)}), f32[8,32,384]{2,1,0:T(8,128)S(1)}, u32[]{:S(2)}, u32[]{:S(2)}) async-start(f32[8,32,384]{2,1,0:T(8,128)} %col_cross.1), calls=%async_computation.1 | async-start | bytes 786432 | tf_op jit(solution)/shard_map/all_to_all | solution.py:409
  40.0 0.0 copy-start.4
  40.0 2.2 %copy-done.4 = bf16[1024,2048]{1,0:T(8,128)(2,1)S(1)} copy-done((bf16[1024,2048]{1,0:T(8,128)(2,1)S(1)}, bf16[1024,2048]{1,0:T(8,128)(2,1)}, u32[]{:S(2)}) %copy-start.4) | copy-done | bytes 4194328
  42.2 0.0 copy-start.7
  42.2 2.2 %copy-done.7 = bf16[1024,2048]{1,0:T(8,128)(2,1)S(1)} copy-done((bf16[1024,2048]{1,0:T(8,128)(2,1)S(1)}, bf16[1024,2048]{1,0:T(8,128)(2,1)}, u32[]{:S(2)}) %copy-start.7) | copy-done | bytes 4194328
  44.4 3.2 %row_cross.1.row_ref = f32[32,1024]{1,0:T(8,128)S(1)} custom-call(f32[32,24,128]{2,1,0:T(8,128)S(1)} %bitcast.10, bf16[1024,2048]{1,0:T(8,128)(2,1)S(1)} %copy-done.4, bf16[1024,2048]{1,0:T(8,128)(2,1)S(1)} %copy-done.7), custom_call_target="tpu_custom_call" | custom-call | tf_op jit(solution)/shard_map/row_cross/pallas_call | solution.py:256
  47.6 0.7 all-to-all-done.1.pieces_ref
  48.3 0.9 %slab.1 = (f32[32,256]{1,0:T(8,128)S(1)}, f32[4,32,1152]{2,1,0:T(8,128)}) custom-call(f32[8,32,384]{2,1,0:T(8,128)S(1)} %all-to-all-done.1.pieces_ref, f32[32,1024]{1,0:T(8,128)S(1)} %row_cross.1.row_ref), custom_call_target="tpu_custom_call" | custom-call | tf_op jit(solution)/shard_map/slab/pallas_call | solution.py:283
  49.2 3.9 %all-to-all-start.2 = ((f32[4,32,1152]{2,1,0:T(8,128)}), f32[4,32,1152]{2,1,0:T(8,128)S(1)}, u32[]{:S(2)}, u32[]{:S(2)}) async-start(f32[4,32,1152]{2,1,0:T(8,128)} %get-tuple-element.14), calls=%async_computation.2 | async-start | bytes 1179648 | tf_op jit(solution)/shard_map/all_to_all | solution.py:409
  53.0 9.0 %all-gather = f32[256,256]{1,0:T(8,128)S(1)} all-gather(f32[32,256]{1,0:T(8,128)S(1)} %get-tuple-element.15), channel_id=2, replica_groups=mesh['row'=8,'col'=4] {'row'}, dimensions={0}, use_global_device_ids=true | all-gather | bytes 294912 | tf_op jit(solution)/shard_map/all_gather | solution.py:467
  62.0 7.3 %all-to-all-done.2.rows_ref = f32[4,32,1152]{2,1,0:T(8,128)S(1)} async-done(((f32[4,32,1152]{2,1,0:T(8,128)}), f32[4,32,1152]{2,1,0:T(8,128)S(1)}, u32[]{:S(2)}, u32[]{:S(2)}) %all-to-all-start.2) | async-done | bytes 589856 | tf_op jit(solution)/shard_map/all_to_all | solution.py:409
  69.3 0.0 copy-done.9
  69.4 0.0 copy-start.1
  69.4 3.4 %copy-done.1 = f32[1024,2048]{1,0:T(8,128)S(1)} copy-done((f32[1024,2048]{1,0:T(8,128)S(1)}, f32[1024,2048]{1,0:T(8,128)}, u32[]{:S(2)}) %copy-start.1) | copy-done | bytes 8388632
  72.7 6.8 %update.1 = (f32[2,128]{1,0:T(2,128)}, f32[1024,2048]{1,0:T(8,128)}) custom-call(f32[4,32,1152]{2,1,0:T(8,128)S(1)} %all-to-all-done.2.rows_ref, f32[8,32,256]{2,1,0:T(8,128)S(1)} %bitcast.11, f32[64,128]{1,0:T(8,128)S(1)} %copy-done.9, f32[1024,2048]{1,0:T(8,128)S(1)} %copy-done.1), custom_call_target="tpu_custom_call" | custom-call | tf_op jit(solution)/shard_map/update/pallas_call | solution.py:368
Async XLA Ops:
  1.3 0.8 copy-start.8
  2.0 0.8 %copy-start.10 = (f32[1,256,64]{1,2,0:T(8,128)S(1)}, f32[1,256,64]{1,2,0:T(8,128)}, u32[]{:S(2)}) copy-start(f32[1,256,64]{1,2,0:T(8,128)} %param.13) | copy-start | bytes 196612
  2.9 0.8 copy-start.11
  3.6 0.8 copy-start.12
  4.4 0.7 copy-start.13
  5.1 0.7 copy-start.14
  5.8 0.7 copy-start.15
  6.4 0.7 copy-start.16
  9.9 19.1 %all-to-all-start = ((f32[32,1,24,128]{3,2,1,0:T(8,128)}), f32[32,1,24,128]{3,2,1,0:T(8,128)S(1)}, u32[]{:S(2)}, u32[]{:S(2)}) async-start(f32[32,1,24,128]{3,2,1,0:T(8,128)} %get-tuple-element.10), calls=%async_computation | async-start | bytes 786432 | tf_op jit(solution)/shard_map/all_to_all | solution.py:409
  17.2 3.4 %copy-start = (f32[1024,2048]{1,0:T(8,128)S(1)}, f32[1024,2048]{1,0:T(8,128)}, u32[]{:S(2)}) copy-start(f32[1024,2048]{1,0:T(8,128)} %cov_ref.3) | copy-start | bytes 25165828
  21.8 2.0 %copy-start.2 = (bf16[1024,2048]{1,0:T(8,128)(2,1)}, bf16[1024,2048]{1,0:T(8,128)(2,1)S(1)}, u32[]{:S(2)}) copy-start(bf16[1024,2048]{1,0:T(8,128)(2,1)S(1)} %get-tuple-element.12.hi_ref) | copy-start | bytes 12582916
  23.8 1.9 %copy-start.5 = (bf16[1024,2048]{1,0:T(8,128)(2,1)}, bf16[1024,2048]{1,0:T(8,128)(2,1)S(1)}, u32[]{:S(2)}) copy-start(bf16[1024,2048]{1,0:T(8,128)(2,1)S(1)} %get-tuple-element.13.lo_ref) | copy-start | bytes 12582916
  29.0 2.2 %copy-start.3 = (bf16[1024,2048]{1,0:T(8,128)(2,1)S(1)}, bf16[1024,2048]{1,0:T(8,128)(2,1)}, u32[]{:S(2)}) copy-start(bf16[1024,2048]{1,0:T(8,128)(2,1)} %copy-done.2) | copy-start | bytes 12582916
  31.2 2.2 %copy-start.6 = (bf16[1024,2048]{1,0:T(8,128)(2,1)S(1)}, bf16[1024,2048]{1,0:T(8,128)(2,1)}, u32[]{:S(2)}) copy-start(bf16[1024,2048]{1,0:T(8,128)(2,1)} %copy-done.5) | copy-start | bytes 12582916
  33.4 36.0 %copy-start.9 = (f32[64,128]{1,0:T(8,128)S(1)}, f32[64,128]{1,0:T(8,128)}, u32[]{:S(2)}) copy-start(f32[64,128]{1,0:T(8,128)} %weight_ref.3) | copy-start | bytes 98308
  36.6 11.7 %all-to-all-start.1 = ((f32[8,32,384]{2,1,0:T(8,128)}), f32[8,32,384]{2,1,0:T(8,128)S(1)}, u32[]{:S(2)}, u32[]{:S(2)}) async-start(f32[8,32,384]{2,1,0:T(8,128)} %col_cross.1), calls=%async_computation.1 | async-start | bytes 786432 | tf_op jit(solution)/shard_map/all_to_all | solution.py:409
  40.0 2.2 %copy-start.4 = (bf16[1024,2048]{1,0:T(8,128)(2,1)S(1)}, bf16[1024,2048]{1,0:T(8,128)(2,1)}, u32[]{:S(2)}) copy-start(bf16[1024,2048]{1,0:T(8,128)(2,1)} %copy-done.2) | copy-start | bytes 12582916
  42.2 2.2 %copy-start.7 = (bf16[1024,2048]{1,0:T(8,128)(2,1)S(1)}, bf16[1024,2048]{1,0:T(8,128)(2,1)}, u32[]{:S(2)}) copy-start(bf16[1024,2048]{1,0:T(8,128)(2,1)} %copy-done.5) | copy-start | bytes 12582916
  49.2 20.2 %all-to-all-start.2 = ((f32[4,32,1152]{2,1,0:T(8,128)}), f32[4,32,1152]{2,1,0:T(8,128)S(1)}, u32[]{:S(2)}, u32[]{:S(2)}) async-start(f32[4,32,1152]{2,1,0:T(8,128)} %get-tuple-element.14), calls=%async_computation.2 | async-start | bytes 1179648 | tf_op jit(solution)/shard_map/all_to_all | solution.py:409
  69.4 3.4 %copy-start.1 = (f32[1024,2048]{1,0:T(8,128)S(1)}, f32[1024,2048]{1,0:T(8,128)}, u32[]{:S(2)}) copy-start(f32[1024,2048]{1,0:T(8,128)} %cov_ref.3) | copy-start | bytes 25165828

commit v9 on v8

--- a/solution.py
+++ b/solution.py
@@ -125,7 +125,6 @@
             jax.ShapeDtypeStruct((per_dev, 1, width), f32),
         ],
         scratch_shapes=[pltpu.VMEM((atoms, atoms), f32)],
-        compiler_params=limit(8),
         name="network",
     )(
         atom_types.reshape(per_dev, 1, atoms),
@@ -140,6 +139,14 @@
     )
 
 
+def in_hbm(x):
+    return pltpu.with_memory_space_constraint(x, pltpu.HBM)
+
+
+def in_vmem(x):
+    return pltpu.with_memory_space_constraint(x, pltpu.VMEM)
+
+
 def stage_kernel(cov_ref, hi_ref, lo_ref):
     hi_ref[...], lo_ref[...] = split2(cov_ref[...])
 
@@ -153,10 +160,10 @@
         grid=(rows // height,),
         in_specs=[block],
         out_specs=[block] * 2,
-        out_shape=[jax.ShapeDtypeStruct((rows, cols), bf16)] * 2,
+        out_shape=[pltpu.HBM((rows, cols), bf16)] * 2,
         compiler_params=limit(12),
         name="stage",
-    )(covariance)
+    )(in_hbm(covariance))
 
 
 def five_products(parts, hi, lo, contract):
@@ -235,7 +242,7 @@
         ],
         compiler_params=limit(12),
         name="col_cross",
-    )(jac, error, hi, lo)
+    )(jac, error, in_hbm(hi), in_hbm(lo))
 
 
 def row_kernel(jac_ref, hi_ref, lo_ref, cross_ref, parts_ref):
@@ -262,7 +269,7 @@
         scratch_shapes=[pltpu.VMEM((3 * streams, tile_cols), bf16)],
         compiler_params=limit(12),
         name="row_cross",
-    )(jac, hi, lo)
+    )(jac, in_hbm(hi), in_hbm(lo))
 
 
 def slab_kernel(pieces_ref, row_ref, own_ref, out_ref):
@@ -307,8 +314,28 @@
     return inverse / bound
 
 
+def head_kernel(cov_ref, _, head_ref, sem):
+    copy = pltpu.make_async_copy(cov_ref.at[pl.ds(0, head_ref.shape[0])], head_ref, sem)
+    copy.start()
+    copy.wait()
+
+
+def read_head(covariance, col_slabs):
+    beyond = pl.BlockSpec(memory_space=pl.ANY)
+    rows, cols = covariance.shape
+    return pl.pallas_call(
+        head_kernel,
+        in_specs=[beyond, beyond],
+        out_specs=pl.BlockSpec(memory_space=pltpu.VMEM),
+        out_shape=pltpu.VMEM((rows // 4, cols), f32),
+        scratch_shapes=[pltpu.SemaphoreType.DMA],
+        compiler_params=limit(2),
+        name="head",
+    )(in_hbm(covariance), col_slabs)
+
+
 def update_kernel(
-    rows_ref, cols_ref, weight_ref, cov_ref, new_weight_ref, new_cov_ref, left_ref, right_ref, tile_ref, in_sems, out_sems
+    rows_ref, cols_ref, weight_ref, head_ref, cov_ref, new_weight_ref, new_cov_ref, left_ref, right_ref, tile_ref, in_sems, out_sems
 ):
     copies, streams, padded = rows_ref.shape
     col_slabs, _, slab = cols_ref.shape
@@ -317,8 +344,9 @@
     slabs = tile_rows // slab
     chunks = in_sems.shape[0]
     height = tile_rows // chunks
+    held = head_ref.shape[0] // height
     reads = []
-    for n in range(chunks):
+    for n in range(held, chunks):
         here = pl.ds(n * height, height)
         reads.append(pltpu.make_async_copy(cov_ref.at[here], tile_ref.at[here], in_sems.at[n]))
         reads[-1].start()
@@ -340,8 +368,10 @@
     for n in range(chunks):
         update = dot(left_ref[:, n * height : (n + 1) * height], right_ref[...], ((0,), (0,)))
         here = pl.ds(n * height, height)
-        reads[n].wait()
-        tile_ref[here, :] = (tile_ref[here, :] - update) * (1.0 / forget)
+        if n >= held:
+            reads[n - held].wait()
+        before = head_ref if n < held else tile_ref
+        tile_ref[here, :] = (before[here, :] - update) * (1.0 / forget)
         writes.append(pltpu.make_async_copy(tile_ref.at[here], new_cov_ref.at[here], out_sems.at[n]))
         writes[-1].start()
     col_at = lax.axis_index("col")
@@ -359,7 +389,7 @@
         write.wait()
 
 
-def update(row_parts, col_slabs, layer_weight, covariance):
+def update(row_parts, col_slabs, layer_weight, head, covariance):
     _, streams, slab = col_slabs.shape
     tile_rows, tile_cols = covariance.shape
     width = layer_weight.shape[1]
@@ -367,7 +397,7 @@
     beyond = pl.BlockSpec(memory_space=pl.ANY)
     return pl.pallas_call(
         update_kernel,
-        in_specs=[whole, whole, whole, beyond],
+        in_specs=[whole, whole, whole, whole, beyond],
         out_specs=[whole, beyond],
         out_shape=[
             jax.ShapeDtypeStruct((slab // width, width), f32),
@@ -382,7 +412,7 @@
         ],
         compiler_params=limit(20),
         name="update",
-    )(row_parts, col_slabs, layer_weight, covariance)
+    )(row_parts, col_slabs, layer_weight, in_vmem(head), in_hbm(covariance))
 
 
 def plain_steps(at, jac_all, errors, layer_weight, covariance, slab, cols_n):
@@ -465,7 +495,8 @@
     col_own, row_part = slab_sum(col_pieces, row_part, cols_n)
     row_parts = exchange(row_part, "col")
     col_slabs = lax.all_gather(col_own, "row", axis=0, tiled=False)
-    new_weight, new_cov = update(row_parts, col_slabs, layer_weight, covariance)
+    head = read_head(covariance, col_slabs)
+    new_weight, new_cov = update(row_parts, col_slabs, layer_weight, head, covariance)
     return new_weight.reshape(-1), new_cov
 
 

time: 80.4 us -> 69 us (0.86)
  local copies, waits for them, and re-layouts: 25.3 us -> 0.01 us
  Pallas kernels: 18 us -> 34.1 us
  waiting for transfers between devices: 11.3 us -> 9.97 us
    unnamed x34 -> x4, local copies, waits for them, and re-layouts: 25.3 us -> 0.01 us
    pallas_call x1, Pallas kernels: 1.23 us -> 8.96 us  [stage(): pl.pallas_call(stage_kernel, grid=(rows // height,), in_specs=[block], ou...]
    pallas_call x1, Pallas kernels: 3.19 us -> 6.02 us  [col_partial(): pl.pallas_call(functools.partial(col_kernel, col_rows=tile_cols // LANES)...]
    pallas_call x1, Pallas kernels: 3.15 us -> 5.64 us  [row_partial(): pl.pallas_call(row_kernel, grid=(tile_rows // slab,), in_specs=[pl.BlockS...]
    pallas_call x1 -> x2, Pallas kernels: 6.81 us -> 8.94 us  [the longest x1 7.34 us: update(): pl.pallas_call(update_kernel, in_specs=[whole, whole, whole, whole, beyon...]
    all_to_all x3, waiting for transfers between devices: 11.3 us -> 9.97 us  [exchange(): return lax.all_to_all(x, axes, split_axis=0, concat_axis=0, tiled=True)]
    pallas_call x1, Pallas kernels: 2.77 us -> 3.65 us  [network(): pl.pallas_call(functools.partial(network_kernel, plan=plan), grid=(per_de...]
  transfers between devices with their start and end apart: 3 -> 3, of which waited for: 3 -> 3; matrix products, arithmetic and copies ran while one was open for 0% -> 0% of each run, Pallas kernels for 6% -> 24%
where the time goes in v9:
time: 69 us; the launch traced here: 68.3 us
  Pallas kernels  34.1 us (49%)
  starting transfers between devices  14.6 us (21%)
  waiting for transfers between devices  9.97 us (14%)
  blocking collectives  8.33 us (12%)
  between operations  1.32 us (2%)
    all_to_all x3, starting transfers between devices, exchange(): return lax.all_to_all(x, axes, split_axis=0, concat_axis=0, tiled=True)  14.6 us
    all_to_all x3, waiting for transfers between devices, exchange(): return lax.all_to_all(x, axes, split_axis=0, concat_axis=0, tiled=True)  9.97 us
    pallas_call x1, Pallas kernels, stage(): pl.pallas_call(stage_kernel, grid=(rows // height,), in_specs=[block], ou...  8.96 us
    all_gather x1, blocking collectives, on_device(): col_slabs = lax.all_gather(col_own, 'row', axis=0, tiled=False)  8.33 us
    pallas_call x1, Pallas kernels, update(): pl.pallas_call(update_kernel, in_specs=[whole, whole, whole, whole, beyon...  7.34 us
    pallas_call x1, Pallas kernels, col_partial(): pl.pallas_call(functools.partial(col_kernel, col_rows=tile_cols // LANES)...  6.02 us
    pallas_call x1, Pallas kernels, row_partial(): pl.pallas_call(row_kernel, grid=(tile_rows // slab,), in_specs=[pl.BlockS...  5.64 us
    pallas_call x1, Pallas kernels, network(): pl.pallas_call(functools.partial(network_kernel, plan=plan), grid=(per_de...  3.65 us
  transfers between devices with their start and end apart: 3, of which 3 were waited for; matrix products, arithmetic and copies ran while one was open for 0% of the time, Pallas kernels for 24%

profile of v9, /device:TPU:0, one launch (start us, length us, event | category | flops | bytes accessed | tf_op | source)
XLA Modules:
  0.0 68.3 jit_solution(5590626328522411913)
XLA Ops:
  1.3 3.6 %network.1 = (f32[32,1,24,128]{3,2,1,0:T(8,128)}, f32[1,1,128]{2,1,0:T(1,128)}) custom-call(s32[1,1,256]{2,1,0:T(1,128)} %bitcast.14, s32[1,32,256]{2,1,0:T(8,128)} %ids_ref.1, f32[1,32,256]{2,1,0:T(8,128)} %switch_ref.1, f32[1,64,256]{2,1,0:T(8,128)} %bitcast.13, f32[1,1,256]{2,1,0:T(1,128)} %bitcast.15, f32[1,1,1]{2,1,0:T(1,128)} %bitcast.8.target_ref, ...), custom_call_target="tpu_custom_call" | custom-call | tf_op jit(solution)/shard_map/network/pallas_call | solution.py:105
  4.9 7.3 %all-to-all-start = ((f32[32,1,24,128]{3,2,1,0:T(8,128)}), f32[32,1,24,128]{3,2,1,0:T(8,128)S(1)}, u32[]{:S(2)}, u32[]{:S(2)}) async-start(f32[32,1,24,128]{3,2,1,0:T(8,128)} %get-tuple-element.10), calls=%async_computation | async-start | bytes 786432 | tf_op jit(solution)/shard_map/all_to_all | solution.py:439
  12.2 0.0 copy-start.1
  12.2 9.0 %stage.1 = (bf16[1024,2048]{1,0:T(8,128)(2,1)}, bf16[1024,2048]{1,0:T(8,128)(2,1)}) custom-call(f32[1024,2048]{1,0:T(8,128)} %cov_ref.5), custom_call_target="tpu_custom_call" | custom-call | tf_op jit(solution)/shard_map/stage/pallas_call | solution.py:158
  21.2 2.9 %all-to-all-done = f32[32,1,24,128]{3,2,1,0:T(8,128)S(1)} async-done(((f32[32,1,24,128]{3,2,1,0:T(8,128)}), f32[32,1,24,128]{3,2,1,0:T(8,128)S(1)}, u32[]{:S(2)}, u32[]{:S(2)}) %all-to-all-start) | async-done | bytes 393248 | tf_op jit(solution)/shard_map/all_to_all | solution.py:439
  24.1 0.0 copy-done.1
  24.1 6.0 %col_cross.1 = f32[8,32,384]{2,1,0:T(8,128)} custom-call(f32[32,24,128]{2,1,0:T(8,128)S(1)} %bitcast.9, f32[1,1,128]{2,1,0:T(1,128)S(1)} %copy-done.1, bf16[1024,2048]{1,0:T(8,128)(2,1)} %get-tuple-element.12.hi_ref, bf16[1024,2048]{1,0:T(8,128)(2,1)} %get-tuple-element.13.lo_ref), custom_call_target="tpu_custom_call" | custom-call | tf_op jit(solution)/shard_map/col_cross/pallas_call | solution.py:227
  30.1 3.5 %all-to-all-start.1 = ((f32[8,32,384]{2,1,0:T(8,128)}), f32[8,32,384]{2,1,0:T(8,128)S(1)}, u32[]{:S(2)}, u32[]{:S(2)}) async-start(f32[8,32,384]{2,1,0:T(8,128)} %col_cross.1), calls=%async_computation.1 | async-start | bytes 786432 | tf_op jit(solution)/shard_map/all_to_all | solution.py:439
  33.5 5.6 %row_cross.1.row_ref = f32[32,1024]{1,0:T(8,128)S(1)} custom-call(f32[32,24,128]{2,1,0:T(8,128)S(1)} %bitcast.10, bf16[1024,2048]{1,0:T(8,128)(2,1)} %get-tuple-element.12.hi_ref, bf16[1024,2048]{1,0:T(8,128)(2,1)} %get-tuple-element.13.lo_ref), custom_call_target="tpu_custom_call" | custom-call | tf_op jit(solution)/shard_map/row_cross/pallas_call | solution.py:263
  39.2 2.6 %all-to-all-done.1.pieces_ref = f32[8,32,384]{2,1,0:T(8,128)S(1)} async-done(((f32[8,32,384]{2,1,0:T(8,128)}), f32[8,32,384]{2,1,0:T(8,128)S(1)}, u32[]{:S(2)}, u32[]{:S(2)}) %all-to-all-start.1) | async-done | bytes 393248 | tf_op jit(solution)/shard_map/all_to_all | solution.py:439
  41.8 0.9 %slab.1 = (f32[32,256]{1,0:T(8,128)S(1)}, f32[4,32,1152]{2,1,0:T(8,128)}) custom-call(f32[8,32,384]{2,1,0:T(8,128)S(1)} %all-to-all-done.1.pieces_ref, f32[32,1024]{1,0:T(8,128)S(1)} %row_cross.1.row_ref), custom_call_target="tpu_custom_call" | custom-call | tf_op jit(solution)/shard_map/slab/pallas_call | solution.py:290
  42.7 3.9 %all-to-all-start.2 = ((f32[4,32,1152]{2,1,0:T(8,128)}), f32[4,32,1152]{2,1,0:T(8,128)S(1)}, u32[]{:S(2)}, u32[]{:S(2)}) async-start(f32[4,32,1152]{2,1,0:T(8,128)} %get-tuple-element.14), calls=%async_computation.2 | async-start | bytes 1179648 | tf_op jit(solution)/shard_map/all_to_all | solution.py:439
  46.5 8.3 %all-gather = f32[256,256]{1,0:T(8,128)S(1)} all-gather(f32[32,256]{1,0:T(8,128)S(1)} %get-tuple-element.15), channel_id=2, replica_groups=mesh['row'=8,'col'=4] {'row'}, dimensions={0}, use_global_device_ids=true | all-gather | bytes 294912 | tf_op jit(solution)/shard_map/all_gather | solution.py:497
  54.9 0.0 copy-start
  54.9 1.6 %head.1.head_ref = f32[256,2048]{1,0:T(8,128)S(1)} custom-call(f32[1024,2048]{1,0:T(8,128)} %cov_ref.5, f32[8,32,256]{2,1,0:T(8,128)S(1)} %bitcast.11), custom_call_target="tpu_custom_call" | custom-call | tf_op jit(solution)/shard_map/head/pallas_call | solution.py:326
  56.5 4.5 %all-to-all-done.2.rows_ref = f32[4,32,1152]{2,1,0:T(8,128)S(1)} async-done(((f32[4,32,1152]{2,1,0:T(8,128)}), f32[4,32,1152]{2,1,0:T(8,128)S(1)}, u32[]{:S(2)}, u32[]{:S(2)}) %all-to-all-start.2) | async-done | bytes 589856 | tf_op jit(solution)/shard_map/all_to_all | solution.py:439
  61.0 0.0 copy-done
  61.0 7.3 %update.1 = (f32[2,128]{1,0:T(2,128)}, f32[1024,2048]{1,0:T(8,128)}) custom-call(f32[4,32,1152]{2,1,0:T(8,128)S(1)} %all-to-all-done.2.rows_ref, f32[8,32,256]{2,1,0:T(8,128)S(1)} %bitcast.12, f32[64,128]{1,0:T(8,128)S(1)} %copy-done, f32[256,2048]{1,0:T(8,128)S(1)} %head.1.head_ref, f32[1024,2048]{1,0:T(8,128)} %cov_ref.5), custom_call_target="tpu_custom_call" | custom-call | tf_op jit(solution)/shard_map/update/pallas_call | solution.py:398
Async XLA Ops:
  4.9 19.1 %all-to-all-start = ((f32[32,1,24,128]{3,2,1,0:T(8,128)}), f32[32,1,24,128]{3,2,1,0:T(8,128)S(1)}, u32[]{:S(2)}, u32[]{:S(2)}) async-start(f32[32,1,24,128]{3,2,1,0:T(8,128)} %get-tuple-element.10), calls=%async_computation | async-start | bytes 786432 | tf_op jit(solution)/shard_map/all_to_all | solution.py:439
  12.2 11.8 %copy-start.1 = (f32[1,1,128]{2,1,0:T(1,128)S(1)}, f32[1,1,128]{2,1,0:T(1,128)}, u32[]{:S(2)}) copy-start(f32[1,1,128]{2,1,0:T(1,128)} %get-tuple-element.11.error_ref) | copy-start | bytes 1540
  30.1 11.7 %all-to-all-start.1 = ((f32[8,32,384]{2,1,0:T(8,128)}), f32[8,32,384]{2,1,0:T(8,128)S(1)}, u32[]{:S(2)}, u32[]{:S(2)}) async-start(f32[8,32,384]{2,1,0:T(8,128)} %col_cross.1), calls=%async_computation.1 | async-start | bytes 786432 | tf_op jit(solution)/shard_map/all_to_all | solution.py:439
  42.7 18.3 %all-to-all-start.2 = ((f32[4,32,1152]{2,1,0:T(8,128)}), f32[4,32,1152]{2,1,0:T(8,128)S(1)}, u32[]{:S(2)}, u32[]{:S(2)}) async-start(f32[4,32,1152]{2,1,0:T(8,128)} %get-tuple-element.14), calls=%async_computation.2 | async-start | bytes 1179648 | tf_op jit(solution)/shard_map/all_to_all | solution.py:439
  54.9 6.1 %copy-start = (f32[64,128]{1,0:T(8,128)S(1)}, f32[64,128]{1,0:T(8,128)}, u32[]{:S(2)}) copy-start(f32[64,128]{1,0:T(8,128)} %weight_ref.3) | copy-start | bytes 98308

commit v10 on v9

--- a/solution.py
+++ b/solution.py
@@ -40,6 +40,15 @@
 
 def limit(mib):
     return pltpu.CompilerParams(vmem_limit_bytes=mib << 20)
+
+
+def five_products(parts, hi, lo, contract):
+    streams = parts.shape[0] // 3
+    by_hi = dot(parts, hi, contract)
+    by_lo = dot(parts[0 : 2 * streams], lo, contract)
+    return by_hi[0:streams] + (
+        by_hi[streams : 2 * streams] + by_lo[0:streams] + (by_hi[2 * streams :] + by_lo[streams:])
+    )
 
 
 def network_kernel(
@@ -71,7 +80,8 @@
     type_at = lax.broadcasted_iota(jnp.int32, (n_types, atoms), 0)
     onehot = (types_ref[...] == type_at).astype(f32)
     mixed = env_ref[...] + dot(embed_ref[...], onehot, ((0,), (0,)), highest)
-    descriptor = dot(mixed, mix, ((1,), (0,)), highest) * (1.0 / math.sqrt(neighbours))
+    parts = jnp.concatenate(split3(mixed), axis=0)
+    descriptor = five_products(parts, *split2(mix), ((1,), (0,))) * (1.0 / math.sqrt(neighbours))
     hidden = jnp.tanh(descriptor)
     activity = jnp.tanh(dot(hidden, weight_ref[...], ((0,), (0,)), highest))
     out_weight = out_weight_ref[...]
@@ -80,7 +90,8 @@
     weighted = dot(force, activity, ((1,), (0,)), highest)
     predicted = jnp.sum(weighted * out_weight, axis=1, keepdims=True) * scale
     slopes = out_weight * (1.0 - activity * activity)
-    jacobian = dot(hidden * force, slopes, ((1,), (0,)), highest) * scale
+    parts = jnp.concatenate(split3(hidden * force), axis=0)
+    jacobian = five_products(parts, *split2(slopes), ((1,), (0,))) * scale
     error_ref[...] = jnp.broadcast_to(target_ref[...] - predicted, error_ref.shape)
     for block, pieces in enumerate(plan):
         at = 0
@@ -147,32 +158,32 @@
     return pltpu.with_memory_space_constraint(x, pltpu.VMEM)
 
 
-def stage_kernel(cov_ref, hi_ref, lo_ref):
-    hi_ref[...], lo_ref[...] = split2(cov_ref[...])
-
-
-def stage(covariance):
+def stage_kernel(cov_ref, hi_ref, lo_ref, hi_head_ref, lo_head_ref, *, head_steps):
+    hi, lo = split2(cov_ref[...])
+    hi_ref[...] = hi
+    lo_ref[...] = lo
+
+    @pl.when(pl.program_id(0) < head_steps)
+    def _():
+        hi_head_ref[...] = hi
+        lo_head_ref[...] = lo
+
+
+def stage(covariance, head):
     rows, cols = covariance.shape
-    height = rows // 8
+    height = min(rows // 8, head)
+    head_steps = head // height
     block = pl.BlockSpec((height, cols), lambda n: (n, 0))
-    return pl.pallas_call(
-        stage_kernel,
+    head_block = pl.BlockSpec((height, cols), lambda n: (jnp.minimum(n, head_steps - 1), 0))
+    return pl.pallas_call(
+        functools.partial(stage_kernel, head_steps=head_steps),
         grid=(rows // height,),
         in_specs=[block],
-        out_specs=[block] * 2,
-        out_shape=[pltpu.HBM((rows, cols), bf16)] * 2,
+        out_specs=[block, block, head_block, head_block],
+        out_shape=[pltpu.HBM((rows, cols), bf16)] * 2 + [pltpu.VMEM((head, cols), bf16)] * 2,
         compiler_params=limit(12),
         name="stage",
     )(in_hbm(covariance))
-
-
-def five_products(parts, hi, lo, contract):
-    streams = parts.shape[0] // 3
-    by_hi = dot(parts, hi, contract)
-    by_lo = dot(parts[0 : 2 * streams], lo, contract)
-    return by_hi[0:streams] + (
-        by_hi[streams : 2 * streams] + by_lo[0:streams] + (by_hi[2 * streams :] + by_lo[streams:])
-    )
 
 
 def stacked_parts(flat, first, count, streams, stride, into_ref):
@@ -183,66 +194,85 @@
             into_ref[n * streams : (n + 1) * streams, i * lanes : (i + 1) * lanes] = part
 
 
-def col_kernel(jac_ref, error_ref, hi_ref, lo_ref, out_ref, parts_ref, own_ref, sum_ref, *, col_rows):
+def col_kernel(
+    jac_ref,
+    error_ref,
+    hi_head_ref,
+    lo_head_ref,
+    hi_ref,
+    lo_ref,
+    out_ref,
+    own_ref,
+    parts_ref,
+    sum_ref,
+    hi_rest_ref,
+    lo_rest_ref,
+    sems,
+    *,
+    col_rows,
+):
     streams, rows, lanes = jac_ref.shape
-    slab, tile_cols = hi_ref.shape
-    slab_rows = slab // lanes
-    step = pl.program_id(0)
+    head, tile_cols = hi_head_ref.shape
+    slab = out_ref.shape[2] - lanes
+    chunks = sems.shape[0]
+    copies = []
+    for n in range(chunks):
+        source, target = pl.ds((n + 1) * head, head), pl.ds(n * head, head)
+        copies.append(
+            (
+                pltpu.make_async_copy(hi_ref.at[source], hi_rest_ref.at[target], sems.at[n, 0]),
+                pltpu.make_async_copy(lo_ref.at[source], lo_rest_ref.at[target], sems.at[n, 1]),
+            )
+        )
+        for copy in copies[-1]:
+            copy.start()
     flat = jac_ref.reshape(streams * rows, lanes)
-    stacked_parts(flat, col_rows + step * slab_rows, slab_rows, streams, rows, own_ref)
-    cross = five_products(own_ref[...], hi_ref[...], lo_ref[...], ((1,), (0,)))
-
-    @pl.when(step == 0)
-    def _():
-        sum_ref[...] = cross
-        stacked_parts(flat, 0, col_rows, streams, rows, parts_ref)
-
-    @pl.when(step > 0)
-    def _():
-        sum_ref[...] += cross
-
-    @pl.when(step == pl.num_programs(0) - 1)
-    def _():
-        total = sum_ref[...]
-        products = dot(parts_ref[...], jnp.concatenate(split3(total), axis=0), ((1,), (1,)))
-        term = jnp.zeros((streams, streams), f32)
-        for left, right in ((2, 0), (1, 1), (0, 2), (1, 0), (0, 1), (0, 0)):
-            term = term + products[
-                left * streams : (left + 1) * streams, right * streams : (right + 1) * streams
-            ]
-        own_at = lax.axis_index("row") * lax.axis_size("col") + lax.axis_index("col")
-        stream_at = lax.broadcasted_iota(jnp.int32, (streams, lanes), 0)
-        error = jnp.where(stream_at == own_at, error_ref[0], 0.0)
-        for n in range(tile_cols // slab):
-            out_ref[n, :, 0:slab] = total[:, n * slab : (n + 1) * slab]
-            out_ref[n, :, slab:] = error
-            out_ref[n, :, slab : slab + streams] = term
-
-
-def col_partial(jac, error, hi, lo, slab):
+    stacked_parts(flat, col_rows, rows - col_rows, streams, rows, own_ref)
+    sum_ref[...] = five_products(own_ref[:, 0:head], hi_head_ref[...], lo_head_ref[...], ((1,), (0,)))
+    stacked_parts(flat, 0, col_rows, streams, rows, parts_ref)
+    for n in range(chunks):
+        for copy in copies[n]:
+            copy.wait()
+        here = slice(n * head, (n + 1) * head)
+        sum_ref[...] += five_products(
+            own_ref[:, (n + 1) * head : (n + 2) * head], hi_rest_ref[here, :], lo_rest_ref[here, :], ((1,), (0,))
+        )
+    total = sum_ref[...]
+    products = dot(parts_ref[...], jnp.concatenate(split3(total), axis=0), ((1,), (1,)))
+    term = jnp.zeros((streams, streams), f32)
+    for left, right in ((2, 0), (1, 1), (0, 2), (1, 0), (0, 1), (0, 0)):
+        term = term + products[left * streams : (left + 1) * streams, right * streams : (right + 1) * streams]
+    own_at = lax.axis_index("row") * lax.axis_size("col") + lax.axis_index("col")
+    stream_at = lax.broadcasted_iota(jnp.int32, (streams, lanes), 0)
+    error = jnp.where(stream_at == own_at, error_ref[0], 0.0)
+    for n in range(tile_cols // slab):
+        out_ref[n, :, 0:slab] = total[:, n * slab : (n + 1) * slab]
+        out_ref[n, :, slab:] = error
+        out_ref[n, :, slab : slab + streams] = term
+
+
+def col_partial(jac, error, hi_head, lo_head, hi, lo, slab):
     streams = jac.shape[0]
     tile_rows, tile_cols = hi.shape
-    out_shape = (tile_cols // slab, streams, slab + LANES)
-    block = pl.BlockSpec((slab, tile_cols), lambda n: (n, 0))
+    head = hi_head.shape[0]
+    whole = pl.BlockSpec(memory_space=pltpu.VMEM)
+    beyond = pl.BlockSpec(memory_space=pl.ANY)
     return pl.pallas_call(
         functools.partial(col_kernel, col_rows=tile_cols // LANES),
-        grid=(tile_rows // slab,),
-        in_specs=[
-            pl.BlockSpec(jac.shape, lambda n: (0, 0, 0)),
-            pl.BlockSpec(error.shape, lambda n: (0, 0, 0)),
-            block,
-            block,
-        ],
-        out_specs=pl.BlockSpec(out_shape, lambda n: (0, 0, 0)),
-        out_shape=jax.ShapeDtypeStruct(out_shape, f32),
+        in_specs=[whole] * 4 + [beyond] * 2,
+        out_specs=whole,
+        out_shape=jax.ShapeDtypeStruct((tile_cols // slab, streams, slab + LANES), f32),
         scratch_shapes=[
+            pltpu.VMEM((3 * streams, tile_rows), bf16),
             pltpu.VMEM((3 * streams, tile_cols), bf16),
-            pltpu.VMEM((3 * streams, slab), bf16),
             pltpu.VMEM((streams, tile_cols), f32),
-        ],
-        compiler_params=limit(12),
+            pltpu.VMEM((tile_rows - head, tile_cols), bf16),
+            pltpu.VMEM((tile_rows - head, tile_cols), bf16),
+            pltpu.SemaphoreType.DMA((tile_rows // head - 1, 2)),
+        ],
+        compiler_params=limit(16),
         name="col_cross",
-    )(jac, error, in_hbm(hi), in_hbm(lo))
+    )(jac, error, in_vmem(hi_head), in_vmem(lo_head), in_hbm(hi), in_hbm(lo))
 
 
 def row_kernel(jac_ref, hi_ref, lo_ref, cross_ref, parts_ref):
@@ -489,8 +519,8 @@
     payload, error = run_network(plan)
     jac = exchange(payload, ("row", "col"))
     jac = jac.reshape(-1, *jac.shape[2:])
-    hi, lo = stage(covariance)
-    col_pieces = exchange(col_partial(jac, error, hi, lo, slab), "row")
+    hi, lo, hi_head, lo_head = stage(covariance, tile_rows // 4)
+    col_pieces = exchange(col_partial(jac, error, hi_head, lo_head, hi, lo, slab), "row")
     row_part = row_partial(jac, hi, lo, slab)
     col_own, row_part = slab_sum(col_pieces, row_part, cols_n)
     row_parts = exchange(row_part, "col")

time: 69 us -> 67.6 us (0.980)
  Pallas kernels: 34.1 us -> 33 us
    pallas_call x1, Pallas kernels: 6.02 us -> 4.67 us  [col_partial(): pl.pallas_call(functools.partial(col_kernel, col_rows=tile_cols // LANES)...]
  transfers between devices with their start and end apart: 3 -> 3, of which waited for: 3 -> 3; matrix products, arithmetic and copies ran while one was open for 0% -> 0% of each run, Pallas kernels for 24% -> 25%
where the time goes in v10:
time: 67.6 us; the launch traced here: 66.9 us
  Pallas kernels  33 us (49%)
  starting transfers between devices  14.6 us (22%)
  waiting for transfers between devices  9.55 us (14%)
  blocking collectives  8.33 us (12%)
  between operations  1.33 us (2%)
    all_to_all x3, starting transfers between devices, exchange(): return lax.all_to_all(x, axes, split_axis=0, concat_axis=0, tiled=True)  14.6 us
    all_to_all x3, waiting for transfers between devices, exchange(): return lax.all_to_all(x, axes, split_axis=0, concat_axis=0, tiled=True)  9.55 us
    pallas_call x1, Pallas kernels, stage(): pl.pallas_call(functools.partial(stage_kernel, head_steps=head_steps), gr...  9.37 us
    all_gather x1, blocking collectives, on_device(): col_slabs = lax.all_gather(col_own, 'row', axis=0, tiled=False)  8.33 us
    pallas_call x1, Pallas kernels, update(): pl.pallas_call(update_kernel, in_specs=[whole, whole, whole, whole, beyon...  7.34 us
    pallas_call x1, Pallas kernels, row_partial(): pl.pallas_call(row_kernel, grid=(tile_rows // slab,), in_specs=[pl.BlockS...  5.64 us
    pallas_call x1, Pallas kernels, col_partial(): pl.pallas_call(functools.partial(col_kernel, col_rows=tile_cols // LANES)...  4.67 us
    pallas_call x1, Pallas kernels, network(): pl.pallas_call(functools.partial(network_kernel, plan=plan), grid=(per_de...  3.56 us
  transfers between devices with their start and end apart: 3, of which 3 were waited for; matrix products, arithmetic and copies ran while one was open for 0% of the time, Pallas kernels for 25%

profile of v10, /device:TPU:0, one launch (start us, length us, event | category | flops | bytes accessed | tf_op | source)
XLA Modules:
  0.0 66.9 jit_solution(5636927598238988193)
XLA Ops:
  1.3 3.6 %network.1 = (f32[32,1,24,128]{3,2,1,0:T(8,128)}, f32[1,1,128]{2,1,0:T(1,128)}) custom-call(s32[1,1,256]{2,1,0:T(1,128)} %bitcast.14, s32[1,32,256]{2,1,0:T(8,128)} %ids_ref.1, f32[1,32,256]{2,1,0:T(8,128)} %switch_ref.1, f32[1,64,256]{2,1,0:T(8,128)} %bitcast.13, f32[1,1,256]{2,1,0:T(1,128)} %bitcast.15, f32[1,1,1]{2,1,0:T(1,128)} %bitcast.8.target_ref, ...), custom_call_target="tpu_custom_call" | custom-call | tf_op jit(solution)/shard_map/network/pallas_call | solution.py:116
  4.8 7.3 %all-to-all-start = ((f32[32,1,24,128]{3,2,1,0:T(8,128)}), f32[32,1,24,128]{3,2,1,0:T(8,128)S(1)}, u32[]{:S(2)}, u32[]{:S(2)}) async-start(f32[32,1,24,128]{3,2,1,0:T(8,128)} %get-tuple-element.12), calls=%async_computation | async-start | bytes 786432 | tf_op jit(solution)/shard_map/all_to_all | solution.py:469
  12.1 0.0 copy-start.1
  12.2 9.4 %stage.1 = (bf16[1024,2048]{1,0:T(8,128)(2,1)}, bf16[1024,2048]{1,0:T(8,128)(2,1)}, bf16[256,2048]{1,0:T(8,128)(2,1)S(1)}, bf16[256,2048]{1,0:T(8,128)(2,1)S(1)}) custom-call(f32[1024,2048]{1,0:T(8,128)} %cov_ref.5), custom_call_target="tpu_custom_call" | custom-call | tf_op jit(solution)/shard_map/stage/pallas_call | solution.py:178
  21.5 2.4 %all-to-all-done = f32[32,1,24,128]{3,2,1,0:T(8,128)S(1)} async-done(((f32[32,1,24,128]{3,2,1,0:T(8,128)}), f32[32,1,24,128]{3,2,1,0:T(8,128)S(1)}, u32[]{:S(2)}, u32[]{:S(2)}) %all-to-all-start) | async-done | bytes 393248 | tf_op jit(solution)/shard_map/all_to_all | solution.py:469
  24.0 0.0 copy-done.1
  24.0 4.7 %col_cross.1 = f32[8,32,384]{2,1,0:T(8,128)} custom-call(f32[32,24,128]{2,1,0:T(8,128)S(1)} %bitcast.9, f32[1,1,128]{2,1,0:T(1,128)S(1)} %copy-done.1, bf16[256,2048]{1,0:T(8,128)(2,1)S(1)} %get-tuple-element.14.hi_head_ref, bf16[256,2048]{1,0:T(8,128)(2,1)S(1)} %get-tuple-element.15.lo_head_ref, bf16[1024,2048]{1,0:T(8,128)(2,1)} %get-tuple-element.16.hi_ref, ...), custom_call_target="tpu_custom_call" | custom-call | tf_op jit(solution)/shard_map/col_cross/pallas_call | solution.py:260
  28.7 3.5 %all-to-all-start.1 = ((f32[8,32,384]{2,1,0:T(8,128)}), f32[8,32,384]{2,1,0:T(8,128)S(1)}, u32[]{:S(2)}, u32[]{:S(2)}) async-start(f32[8,32,384]{2,1,0:T(8,128)} %col_cross.1), calls=%async_computation.1 | async-start | bytes 786432 | tf_op jit(solution)/shard_map/all_to_all | solution.py:469
  32.1 5.6 %row_cross.1.row_ref = f32[32,1024]{1,0:T(8,128)S(1)} custom-call(f32[32,24,128]{2,1,0:T(8,128)S(1)} %bitcast.10, bf16[1024,2048]{1,0:T(8,128)(2,1)} %get-tuple-element.16.hi_ref, bf16[1024,2048]{1,0:T(8,128)(2,1)} %get-tuple-element.17.lo_ref), custom_call_target="tpu_custom_call" | custom-call | tf_op jit(solution)/shard_map/row_cross/pallas_call | solution.py:293
  37.8 2.6 %all-to-all-done.1.pieces_ref = f32[8,32,384]{2,1,0:T(8,128)S(1)} async-done(((f32[8,32,384]{2,1,0:T(8,128)}), f32[8,32,384]{2,1,0:T(8,128)S(1)}, u32[]{:S(2)}, u32[]{:S(2)}) %all-to-all-start.1) | async-done | bytes 393248 | tf_op jit(solution)/shard_map/all_to_all | solution.py:469
  40.4 0.9 %slab.1 = (f32[32,256]{1,0:T(8,128)S(1)}, f32[4,32,1152]{2,1,0:T(8,128)}) custom-call(f32[8,32,384]{2,1,0:T(8,128)S(1)} %all-to-all-done.1.pieces_ref, f32[32,1024]{1,0:T(8,128)S(1)} %row_cross.1.row_ref), custom_call_target="tpu_custom_call" | custom-call | tf_op jit(solution)/shard_map/slab/pallas_call | solution.py:320
  41.3 3.9 %all-to-all-start.2 = ((f32[4,32,1152]{2,1,0:T(8,128)}), f32[4,32,1152]{2,1,0:T(8,128)S(1)}, u32[]{:S(2)}, u32[]{:S(2)}) async-start(f32[4,32,1152]{2,1,0:T(8,128)} %get-tuple-element.18), calls=%async_computation.2 | async-start | bytes 1179648 | tf_op jit(solution)/shard_map/all_to_all | solution.py:469
  45.1 8.3 %all-gather = f32[256,256]{1,0:T(8,128)S(1)} all-gather(f32[32,256]{1,0:T(8,128)S(1)} %get-tuple-element.19), channel_id=2, replica_groups=mesh['row'=8,'col'=4] {'row'}, dimensions={0}, use_global_device_ids=true | all-gather | bytes 294912 | tf_op jit(solution)/shard_map/all_gather | solution.py:527
  53.5 0.0 copy-start
  53.5 1.6 %head.1.head_ref = f32[256,2048]{1,0:T(8,128)S(1)} custom-call(f32[1024,2048]{1,0:T(8,128)} %cov_ref.5, f32[8,32,256]{2,1,0:T(8,128)S(1)} %bitcast.11), custom_call_target="tpu_custom_call" | custom-call | tf_op jit(solution)/shard_map/head/pallas_call | solution.py:356
  55.1 4.5 %all-to-all-done.2.rows_ref = f32[4,32,1152]{2,1,0:T(8,128)S(1)} async-done(((f32[4,32,1152]{2,1,0:T(8,128)}), f32[4,32,1152]{2,1,0:T(8,128)S(1)}, u32[]{:S(2)}, u32[]{:S(2)}) %all-to-all-start.2) | async-done | bytes 589856 | tf_op jit(solution)/shard_map/all_to_all | solution.py:469
  59.6 0.0 copy-done
  59.6 7.3 %update.1 = (f32[2,128]{1,0:T(2,128)}, f32[1024,2048]{1,0:T(8,128)}) custom-call(f32[4,32,1152]{2,1,0:T(8,128)S(1)} %all-to-all-done.2.rows_ref, f32[8,32,256]{2,1,0:T(8,128)S(1)} %bitcast.12, f32[64,128]{1,0:T(8,128)S(1)} %copy-done, f32[256,2048]{1,0:T(8,128)S(1)} %head.1.head_ref, f32[1024,2048]{1,0:T(8,128)} %cov_ref.5), custom_call_target="tpu_custom_call" | custom-call | tf_op jit(solution)/shard_map/update/pallas_call | solution.py:428
Async XLA Ops:
  4.8 19.1 %all-to-all-start = ((f32[32,1,24,128]{3,2,1,0:T(8,128)}), f32[32,1,24,128]{3,2,1,0:T(8,128)S(1)}, u32[]{:S(2)}, u32[]{:S(2)}) async-start(f32[32,1,24,128]{3,2,1,0:T(8,128)} %get-tuple-element.12), calls=%async_computation | async-start | bytes 786432 | tf_op jit(solution)/shard_map/all_to_all | solution.py:469
  12.1 11.8 %copy-start.1 = (f32[1,1,128]{2,1,0:T(1,128)S(1)}, f32[1,1,128]{2,1,0:T(1,128)}, u32[]{:S(2)}) copy-start(f32[1,1,128]{2,1,0:T(1,128)} %get-tuple-element.13.error_ref) | copy-start | bytes 1540
  28.7 11.7 %all-to-all-start.1 = ((f32[8,32,384]{2,1,0:T(8,128)}), f32[8,32,384]{2,1,0:T(8,128)S(1)}, u32[]{:S(2)}, u32[]{:S(2)}) async-start(f32[8,32,384]{2,1,0:T(8,128)} %col_cross.1), calls=%async_computation.1 | async-start | bytes 786432 | tf_op jit(solution)/shard_map/all_to_all | solution.py:469
  41.3 18.3 %all-to-all-start.2 = ((f32[4,32,1152]{2,1,0:T(8,128)}), f32[4,32,1152]{2,1,0:T(8,128)S(1)}, u32[]{:S(2)}, u32[]{:S(2)}) async-start(f32[4,32,1152]{2,1,0:T(8,128)} %get-tuple-element.18), calls=%async_computation.2 | async-start | bytes 1179648 | tf_op jit(solution)/shard_map/all_to_all | solution.py:469
  53.5 6.1 %copy-start = (f32[64,128]{1,0:T(8,128)S(1)}, f32[64,128]{1,0:T(8,128)}, u32[]{:S(2)}) copy-start(f32[64,128]{1,0:T(8,128)} %weight_ref.3) | copy-start | bytes 98308

commit v11 on v10

--- a/solution.py
+++ b/solution.py
@@ -62,7 +62,6 @@
     weight_ref,
     out_weight_ref,
     payload_ref,
-    error_ref,
     mix_ref,
     *,
     plan,
@@ -92,12 +91,14 @@
     slopes = out_weight * (1.0 - activity * activity)
     parts = jnp.concatenate(split3(hidden * force), axis=0)
     jacobian = five_products(parts, *split2(slopes), ((1,), (0,))) * scale
-    error_ref[...] = jnp.broadcast_to(target_ref[...] - predicted, error_ref.shape)
+    error = target_ref[...] - predicted
     for block, pieces in enumerate(plan):
         at = 0
         for start, size in pieces:
             payload_ref[block, at : at + size, :] = jacobian[start : start + size, :]
             at += size
+        rest = payload_ref.shape[1] - at
+        payload_ref[block, at:, :] = jnp.broadcast_to(error, (rest, jacobian.shape[1]))
 
 
 def network(
@@ -105,7 +106,8 @@
 ):
     per_dev, neighbours, atoms = neighbor_ids.shape
     hin, width = layer_weight.shape
-    blocks, rows = len(plan), sum(size for _, size in plan[0])
+    blocks = len(plan)
+    rows = pl.cdiv(sum(size for _, size in plan[0]) + 1, SUBLANES) * SUBLANES
 
     def per_stream(*shape):
         return pl.BlockSpec((None,) + shape, lambda s: (s,) + (0,) * len(shape))
@@ -127,14 +129,8 @@
             shared(layer_weight.shape),
             shared((1, width)),
         ],
-        out_specs=[
-            pl.BlockSpec((blocks, None, rows, width), lambda s: (0, s, 0, 0)),
-            per_stream(1, width),
-        ],
-        out_shape=[
-            jax.ShapeDtypeStruct((blocks, per_dev, rows, width), f32),
-            jax.ShapeDtypeStruct((per_dev, 1, width), f32),
-        ],
+        out_specs=pl.BlockSpec((blocks, None, rows, width), lambda s: (0, s, 0, 0)),
+        out_shape=jax.ShapeDtypeStruct((blocks, per_dev, rows, width), f32),
         scratch_shapes=[pltpu.VMEM((atoms, atoms), f32)],
         name="network",
     )(
@@ -174,13 +170,14 @@
     height = min(rows // 8, head)
     head_steps = head // height
     block = pl.BlockSpec((height, cols), lambda n: (n, 0))
+    rest_block = pl.BlockSpec((height, cols), lambda n: (jnp.maximum(n - head_steps, 0), 0))
     head_block = pl.BlockSpec((height, cols), lambda n: (jnp.minimum(n, head_steps - 1), 0))
     return pl.pallas_call(
         functools.partial(stage_kernel, head_steps=head_steps),
         grid=(rows // height,),
         in_specs=[block],
-        out_specs=[block, block, head_block, head_block],
-        out_shape=[pltpu.HBM((rows, cols), bf16)] * 2 + [pltpu.VMEM((head, cols), bf16)] * 2,
+        out_specs=[rest_block, rest_block, head_block, head_block],
+        out_shape=[pltpu.HBM((rows - head, cols), bf16)] * 2 + [pltpu.VMEM((head, cols), bf16)] * 2,
         compiler_params=limit(12),
         name="stage",
     )(in_hbm(covariance))
@@ -194,138 +191,109 @@
             into_ref[n * streams : (n + 1) * streams, i * lanes : (i + 1) * lanes] = part
 
 
-def col_kernel(
-    jac_ref,
-    error_ref,
-    hi_head_ref,
-    lo_head_ref,
-    hi_ref,
-    lo_ref,
-    out_ref,
-    own_ref,
-    parts_ref,
-    sum_ref,
-    hi_rest_ref,
-    lo_rest_ref,
-    sems,
-    *,
-    col_rows,
-):
+def col_kernel(jac_ref, hi_head_ref, lo_head_ref, hi_ref, lo_ref, out_ref, parts_ref, hi_rest_ref, lo_rest_ref, sums_ref, sems):
     streams, rows, lanes = jac_ref.shape
     head, tile_cols = hi_head_ref.shape
-    slab = out_ref.shape[2] - lanes
+    slabs, _, slab = out_ref.shape
     chunks = sems.shape[0]
     copies = []
     for n in range(chunks):
-        source, target = pl.ds((n + 1) * head, head), pl.ds(n * head, head)
+        here = pl.ds(n * head, head)
         copies.append(
             (
-                pltpu.make_async_copy(hi_ref.at[source], hi_rest_ref.at[target], sems.at[n, 0]),
-                pltpu.make_async_copy(lo_ref.at[source], lo_rest_ref.at[target], sems.at[n, 1]),
+                pltpu.make_async_copy(hi_ref.at[here], hi_rest_ref.at[here], sems.at[n, 0]),
+                pltpu.make_async_copy(lo_ref.at[here], lo_rest_ref.at[here], sems.at[n, 1]),
             )
         )
         for copy in copies[-1]:
             copy.start()
     flat = jac_ref.reshape(streams * rows, lanes)
-    stacked_parts(flat, col_rows, rows - col_rows, streams, rows, own_ref)
-    sum_ref[...] = five_products(own_ref[:, 0:head], hi_head_ref[...], lo_head_ref[...], ((1,), (0,)))
-    stacked_parts(flat, 0, col_rows, streams, rows, parts_ref)
+    stacked_parts(flat, 0, parts_ref.shape[1] // lanes, streams, rows, parts_ref)
+    sums_ref[...] = five_products(parts_ref[:, 0:head], hi_head_ref[...], lo_head_ref[...], ((1,), (0,)))
     for n in range(chunks):
         for copy in copies[n]:
             copy.wait()
         here = slice(n * head, (n + 1) * head)
-        sum_ref[...] += five_products(
-            own_ref[:, (n + 1) * head : (n + 2) * head], hi_rest_ref[here, :], lo_rest_ref[here, :], ((1,), (0,))
+        sums_ref[...] += five_products(
+            parts_ref[:, (n + 1) * head : (n + 2) * head], hi_rest_ref[here, :], lo_rest_ref[here, :], ((1,), (0,))
         )
-    total = sum_ref[...]
-    products = dot(parts_ref[...], jnp.concatenate(split3(total), axis=0), ((1,), (1,)))
-    term = jnp.zeros((streams, streams), f32)
-    for left, right in ((2, 0), (1, 1), (0, 2), (1, 0), (0, 1), (0, 0)):
-        term = term + products[left * streams : (left + 1) * streams, right * streams : (right + 1) * streams]
-    own_at = lax.axis_index("row") * lax.axis_size("col") + lax.axis_index("col")
-    stream_at = lax.broadcasted_iota(jnp.int32, (streams, lanes), 0)
-    error = jnp.where(stream_at == own_at, error_ref[0], 0.0)
-    for n in range(tile_cols // slab):
-        out_ref[n, :, 0:slab] = total[:, n * slab : (n + 1) * slab]
-        out_ref[n, :, slab:] = error
-        out_ref[n, :, slab : slab + streams] = term
-
-
-def col_partial(jac, error, hi_head, lo_head, hi, lo, slab):
+    for n in range(slabs):
+        out_ref[n] = sums_ref[:, n * slab : (n + 1) * slab]
+
+
+def col_partial(jac, hi_head, lo_head, hi, lo, slab):
     streams = jac.shape[0]
-    tile_rows, tile_cols = hi.shape
+    rest, tile_cols = hi.shape
     head = hi_head.shape[0]
     whole = pl.BlockSpec(memory_space=pltpu.VMEM)
     beyond = pl.BlockSpec(memory_space=pl.ANY)
     return pl.pallas_call(
-        functools.partial(col_kernel, col_rows=tile_cols // LANES),
-        in_specs=[whole] * 4 + [beyond] * 2,
+        col_kernel,
+        in_specs=[whole] * 3 + [beyond] * 2,
         out_specs=whole,
-        out_shape=jax.ShapeDtypeStruct((tile_cols // slab, streams, slab + LANES), f32),
+        out_shape=jax.ShapeDtypeStruct((tile_cols // slab, streams, slab), f32),
         scratch_shapes=[
-            pltpu.VMEM((3 * streams, tile_rows), bf16),
-            pltpu.VMEM((3 * streams, tile_cols), bf16),
+            pltpu.VMEM((3 * streams, head + rest), bf16),
+            pltpu.VMEM((rest, tile_cols), bf16),
+            pltpu.VMEM((rest, tile_cols), bf16),
             pltpu.VMEM((streams, tile_cols), f32),
-            pltpu.VMEM((tile_rows - head, tile_cols), bf16),
-            pltpu.VMEM((tile_rows - head, tile_cols), bf16),
-            pltpu.SemaphoreType.DMA((tile_rows // head - 1, 2)),
+            pltpu.SemaphoreType.DMA((rest // head, 2)),
         ],
         compiler_params=limit(16),
         name="col_cross",
-    )(jac, error, in_vmem(hi_head), in_vmem(lo_head), in_hbm(hi), in_hbm(lo))
-
-
-def row_kernel(jac_ref, hi_ref, lo_ref, cross_ref, parts_ref):
+    )(jac, in_vmem(hi_head), in_vmem(lo_head), in_hbm(hi), in_hbm(lo))
+
+
+def slab_kernel(pieces_ref, jac_ref, own_ref, out_ref, error_ref, *, first):
     streams, rows, lanes = jac_ref.shape
-    flat = jac_ref.reshape(streams * rows, lanes)
-
-    @pl.when(pl.program_id(0) == 0)
-    def _():
-        stacked_parts(flat, 0, hi_ref.shape[1] // lanes, streams, rows, parts_ref)
-
-    cross_ref[...] = five_products(parts_ref[...], hi_ref[...], lo_ref[...], ((1,), (1,)))
-
-
-def row_partial(jac, hi, lo, slab):
-    streams = jac.shape[0]
-    tile_rows, tile_cols = hi.shape
-    block = pl.BlockSpec((slab, tile_cols), lambda n: (n, 0))
-    return pl.pallas_call(
-        row_kernel,
-        grid=(tile_rows // slab,),
-        in_specs=[pl.BlockSpec(jac.shape, lambda n: (0, 0, 0)), block, block],
-        out_specs=pl.BlockSpec((streams, slab), lambda n: (0, n)),
-        out_shape=jax.ShapeDtypeStruct((streams, tile_rows), f32),
-        scratch_shapes=[pltpu.VMEM((3 * streams, tile_cols), bf16)],
-        compiler_params=limit(12),
-        name="row_cross",
-    )(jac, in_hbm(hi), in_hbm(lo))
-
-
-def slab_kernel(pieces_ref, row_ref, own_ref, out_ref):
-    tile_rows = row_ref.shape[1]
     slab = own_ref.shape[1]
     total = pieces_ref[0]
     for n in range(1, pieces_ref.shape[0]):
         total = total + pieces_ref[n]
-    own_ref[...] = total[:, 0:slab]
-    for n in range(out_ref.shape[0]):
-        out_ref[n, :, 0:tile_rows] = row_ref[...]
-        out_ref[n, :, tile_rows:] = total[:, slab:]
-
-
-def slab_sum(pieces, row_part, copies):
-    _, streams, padded = pieces.shape
-    tile_rows = row_part.shape[1]
-    return pl.pallas_call(
-        slab_kernel,
+    own_ref[...] = total
+    out_ref[:, 0:slab] = total
+    flat = jac_ref.reshape(streams * rows, lanes)
+    term = jnp.zeros((streams, streams), f32)
+    for i in range(slab // lanes):
+        own = flat[pl.ds(first + i, streams, stride=rows), :]
+        term = term + dot(own, total[:, i * lanes : (i + 1) * lanes], ((1,), (1,)), highest)
+    out_ref[:, slab:] = jnp.zeros((streams, lanes), f32)
+    out_ref[:, slab : slab + streams] = term
+    error_ref[...] = flat[pl.ds(first + slab // lanes, streams, stride=rows), :]
+
+
+def slab_sum(pieces, jac, first):
+    _, streams, slab = pieces.shape
+    return pl.pallas_call(
+        functools.partial(slab_kernel, first=first),
         out_shape=[
-            jax.ShapeDtypeStruct((streams, padded - LANES), f32),
-            jax.ShapeDtypeStruct((copies, streams, tile_rows + LANES), f32),
+            jax.ShapeDtypeStruct((streams, slab), f32),
+            jax.ShapeDtypeStruct((streams, slab + LANES), f32),
+            jax.ShapeDtypeStruct((streams, LANES), f32),
         ],
         compiler_params=limit(8),
         name="slab",
-    )(pieces, row_part)
+    )(pieces, jac)
+
+
+def term_kernel(own_ref, cols_ref, out_ref):
+    slab = own_ref.shape[1]
+    term = cols_ref[0, :, slab:]
+    for n in range(1, cols_ref.shape[0]):
+        term = term + cols_ref[n, :, slab:]
+    for n in range(out_ref.shape[0]):
+        out_ref[n, :, 0:slab] = own_ref[...]
+        out_ref[n, :, slab:] = term
+
+
+def with_terms(own, col_slabs, copies):
+    _, streams, padded = col_slabs.shape
+    return pl.pallas_call(
+        term_kernel,
+        out_shape=jax.ShapeDtypeStruct((copies, streams, padded), f32),
+        compiler_params=limit(8),
+        name="term",
+    )(own, col_slabs)
 
 
 def invert(innovation):
@@ -365,13 +333,13 @@
 
 
 def update_kernel(
-    rows_ref, cols_ref, weight_ref, head_ref, cov_ref, new_weight_ref, new_cov_ref, left_ref, right_ref, tile_ref, in_sems, out_sems
+    rows_ref, cols_ref, error_ref, weight_ref, head_ref, cov_ref, new_weight_ref, new_cov_ref, left_ref, right_ref, tile_ref, in_sems, out_sems
 ):
-    copies, streams, padded = rows_ref.shape
-    col_slabs, _, slab = cols_ref.shape
+    slabs, streams, padded = rows_ref.shape
+    col_slabs = cols_ref.shape[0]
     lanes = weight_ref.shape[1]
-    tile_rows = padded - lanes
-    slabs = tile_rows // slab
+    slab = padded - lanes
+    tile_rows = slabs * slab
     chunks = in_sems.shape[0]
     height = tile_rows // chunks
     held = head_ref.shape[0] // height
@@ -380,17 +348,17 @@
         here = pl.ds(n * height, height)
         reads.append(pltpu.make_async_copy(cov_ref.at[here], tile_ref.at[here], in_sems.at[n]))
         reads[-1].start()
-    total = rows_ref[0]
-    for n in range(1, copies):
-        total = total + rows_ref[n]
-    beside = total[:, tile_rows:]
-    inverse = invert(beside[:, 0:streams])
-    errors = beside[:, streams : streams + 1]
+    term = rows_ref[0, :, slab:]
+    for n in range(1, slabs):
+        term = term + rows_ref[n, :, slab:]
+    inverse = invert(term[:, 0:streams])
+    errors = error_ref[:, 0:1]
     for n in range(col_slabs):
-        hi, mid, lo = split3(cols_ref[n])
+        hi, mid, lo = split3(cols_ref[n, :, 0:slab])
         for m, part in enumerate((hi, mid, lo, hi, mid, hi)):
             right_ref[m * streams : (m + 1) * streams, n * slab : (n + 1) * slab] = part
-    gain = dot(inverse, total[:, 0:tile_rows], ((0,), (0,)), highest)
+    cross = jnp.concatenate([rows_ref[n, :, 0:slab] for n in range(slabs)], axis=1)
+    gain = dot(inverse, cross, ((0,), (0,)), highest)
     hi, mid, lo = split3(gain)
     for m, part in enumerate((hi, hi, hi, mid, mid, lo)):
         left_ref[m * streams : (m + 1) * streams, :] = part
@@ -419,15 +387,16 @@
         write.wait()
 
 
-def update(row_parts, col_slabs, layer_weight, head, covariance):
-    _, streams, slab = col_slabs.shape
+def update(row_slabs, col_slabs, errors, layer_weight, head, covariance):
+    _, streams, padded = col_slabs.shape
+    slab = padded - LANES
     tile_rows, tile_cols = covariance.shape
     width = layer_weight.shape[1]
     whole = pl.BlockSpec(memory_space=pltpu.VMEM)
     beyond = pl.BlockSpec(memory_space=pl.ANY)
     return pl.pallas_call(
         update_kernel,
-        in_specs=[whole, whole, whole, whole, beyond],
+        in_specs=[whole] * 5 + [beyond],
         out_specs=[whole, beyond],
         out_shape=[
             jax.ShapeDtypeStruct((slab // width, width), f32),
@@ -442,7 +411,7 @@
         ],
         compiler_params=limit(20),
         name="update",
-    )(row_parts, col_slabs, layer_weight, in_vmem(head), in_hbm(covariance))
+    )(row_slabs, col_slabs, errors, layer_weight, in_vmem(head), in_hbm(covariance))
 
 
 def plain_steps(at, jac_all, errors, layer_weight, covariance, slab, cols_n):
@@ -510,23 +479,23 @@
         and streams < LANES
     )
     if not kernels:
-        payload, error = run_network([[(0, hin)]])
-        jac_all = lax.all_gather(payload[0], ("row", "col"), axis=0, tiled=True)
-        errors = lax.all_gather(error[:, 0, 0], ("row", "col"), axis=0, tiled=True)
-        return plain_steps(at, jac_all, errors, layer_weight, covariance, slab, cols_n)
-    row_size, col_size = tile_rows // LANES, tile_cols // LANES
-    plan = [[(c * col_size, col_size), (r * row_size, row_size)] for r in range(rows_n) for c in range(cols_n)]
-    payload, error = run_network(plan)
-    jac = exchange(payload, ("row", "col"))
+        payload = run_network([[(0, hin)]])[0]
+        jac_all = lax.all_gather(payload, ("row", "col"), axis=0, tiled=True)
+        return plain_steps(at, jac_all[:, 0:hin], jac_all[:, hin, 0], layer_weight, covariance, slab, cols_n)
+    row_size, slab_size = tile_rows // LANES, slab // LANES
+    devices = [(r, c) for r in range(rows_n) for c in range(cols_n)]
+    plan = [[(r * row_size, row_size), ((c * rows_n + r) * slab_size, slab_size)] for r, c in devices]
+    jac = exchange(run_network(plan), ("row", "col"))
     jac = jac.reshape(-1, *jac.shape[2:])
     hi, lo, hi_head, lo_head = stage(covariance, tile_rows // 4)
-    col_pieces = exchange(col_partial(jac, error, hi_head, lo_head, hi, lo, slab), "row")
-    row_part = row_partial(jac, hi, lo, slab)
-    col_own, row_part = slab_sum(col_pieces, row_part, cols_n)
-    row_parts = exchange(row_part, "col")
-    col_slabs = lax.all_gather(col_own, "row", axis=0, tiled=False)
+    pieces = exchange(col_partial(jac, hi_head, lo_head, hi, lo, slab), "row")
+    col_own, with_term, errors = slab_sum(pieces, jac, row_size)
+    to_row = [(r * cols_n + c, c * rows_n + r) for r, c in devices]
+    row_own = lax.ppermute(col_own, ("row", "col"), to_row)
+    col_slabs = lax.all_gather(with_term, "row", axis=0, tiled=False)
+    row_slabs = exchange(with_terms(row_own, col_slabs, cols_n), "col")
     head = read_head(covariance, col_slabs)
-    new_weight, new_cov = update(row_parts, col_slabs, layer_weight, head, covariance)
+    new_weight, new_cov = update(row_slabs, col_slabs, errors, layer_weight, head, covariance)
     return new_weight.reshape(-1), new_cov
 
 

time: 67.6 us -> 69.3 us (1.025)
  blocking collectives: 8.33 us -> 22.5 us
  Pallas kernels: 33 us -> 25.4 us
  starting transfers between devices: 14.6 us -> 11.3 us
  waiting for transfers between devices: 9.55 us -> 8.16 us
    all_to_all x0 -> x1, blocking collectives: none -> 9.35 us  [exchange(): return lax.all_to_all(x, axes, split_axis=0, concat_axis=0, tiled=True)]
    pallas_call x4, Pallas kernels: 18.5 us -> 11.6 us  [the longest x1 7.35 us: update(): pl.pallas_call(update_kernel, in_specs=[whole] * 5 + [beyond], out_specs=...]
    all_gather x1, blocking collectives: 8.33 us -> 13.1 us  [on_device(): col_slabs = lax.all_gather(with_term, 'row', axis=0, tiled=False)]
    all_to_all x3 -> x2, starting transfers between devices: 14.6 us -> 10.7 us  [exchange(): return lax.all_to_all(x, axes, split_axis=0, concat_axis=0, tiled=True)]
    all_to_all x3 -> x2, waiting for transfers between devices: 9.55 us -> 8.15 us  [exchange(): return lax.all_to_all(x, axes, split_axis=0, concat_axis=0, tiled=True)]
    pallas_call x1, Pallas kernels: 9.37 us -> 8.65 us  [stage(): pl.pallas_call(functools.partial(stage_kernel, head_steps=head_steps), gr...]
  transfers between devices with their start and end apart: 3 -> 3, of which waited for: 3 -> 2; matrix products, arithmetic and copies ran while one was open for 0% -> 0% of each run, Pallas kernels for 25% -> 15%
where the time goes in v11:
time: 69.3 us; the launch traced here: 68.7 us
  Pallas kernels  25.4 us (37%)
  blocking collectives  22.5 us (32%)
  starting transfers between devices  11.3 us (16%)
  waiting for transfers between devices  8.16 us (12%)
  between operations  1.33 us (2%)
    all_gather x1, blocking collectives, on_device(): col_slabs = lax.all_gather(with_term, 'row', axis=0, tiled=False)  13.1 us
    all_to_all x2, starting transfers between devices, exchange(): return lax.all_to_all(x, axes, split_axis=0, concat_axis=0, tiled=True)  10.7 us
    all_to_all x1, blocking collectives, exchange(): return lax.all_to_all(x, axes, split_axis=0, concat_axis=0, tiled=True)  9.35 us
    pallas_call x1, Pallas kernels, stage(): pl.pallas_call(functools.partial(stage_kernel, head_steps=head_steps), gr...  8.65 us
    all_to_all x2, waiting for transfers between devices, exchange(): return lax.all_to_all(x, axes, split_axis=0, concat_axis=0, tiled=True)  8.15 us
    pallas_call x1, Pallas kernels, update(): pl.pallas_call(update_kernel, in_specs=[whole] * 5 + [beyond], out_specs=...  7.35 us
    pallas_call x1, Pallas kernels, network(): pl.pallas_call(functools.partial(network_kernel, plan=plan), grid=(per_de...  3.55 us
    pallas_call x1, Pallas kernels, col_partial(): pl.pallas_call(col_kernel, in_specs=[whole] * 3 + [beyond] * 2, out_specs...  3.37 us
  transfers between devices with their start and end apart: 3, of which 2 were waited for; matrix products, arithmetic and copies ran while one was open for 0% of the time, Pallas kernels for 15%

profile of v11, /device:TPU:0, one launch (start us, length us, event | category | flops | bytes accessed | tf_op | source)
XLA Modules:
  0.0 68.7 jit_solution(2630173130512467497)
XLA Ops:
  1.3 3.5 %network.1 = f32[32,1,16,128]{3,2,1,0:T(8,128)} custom-call(s32[1,1,256]{2,1,0:T(1,128)} %bitcast.15, s32[1,32,256]{2,1,0:T(8,128)} %ids_ref.1, f32[1,32,256]{2,1,0:T(8,128)} %switch_ref.1, f32[1,64,256]{2,1,0:T(8,128)} %bitcast.14, f32[1,1,256]{2,1,0:T(1,128)} %bitcast.16, f32[1,1,1]{2,1,0:T(1,128)} %bitcast.8.target_ref, f32[4,64]{1,0:T(4,128)} %embed_ref.1, ...), custom_call_target="tpu_custom_call" | custom-call | tf_op jit(solution)/shard_map/network/pallas_call | solution.py:118
  4.8 7.3 %all-to-all-start = ((f32[32,1,16,128]{3,2,1,0:T(8,128)}), f32[32,1,16,128]{3,2,1,0:T(8,128)S(1)}, u32[]{:S(2)}, u32[]{:S(2)}) async-start(f32[32,1,16,128]{3,2,1,0:T(8,128)} %network.1), calls=%async_computation | async-start | bytes 524288 | tf_op jit(solution)/shard_map/all_to_all | solution.py:438
  12.1 8.6 %stage.1 = (bf16[768,2048]{1,0:T(8,128)(2,1)}, bf16[768,2048]{1,0:T(8,128)(2,1)}, bf16[256,2048]{1,0:T(8,128)(2,1)S(1)}, bf16[256,2048]{1,0:T(8,128)(2,1)S(1)}) custom-call(f32[1024,2048]{1,0:T(8,128)} %cov_ref.5), custom_call_target="tpu_custom_call" | custom-call | tf_op jit(solution)/shard_map/stage/pallas_call | solution.py:175
  20.8 1.6 %all-to-all-done = f32[32,1,16,128]{3,2,1,0:T(8,128)S(1)} async-done(((f32[32,1,16,128]{3,2,1,0:T(8,128)}), f32[32,1,16,128]{3,2,1,0:T(8,128)S(1)}, u32[]{:S(2)}, u32[]{:S(2)}) %all-to-all-start) | async-done | bytes 262176 | tf_op jit(solution)/shard_map/all_to_all | solution.py:438
  22.3 3.4 %col_cross.1 = f32[8,32,256]{2,1,0:T(8,128)S(1)} custom-call(f32[32,16,128]{2,1,0:T(8,128)S(1)} %bitcast.12, bf16[256,2048]{1,0:T(8,128)(2,1)S(1)} %get-tuple-element.11.hi_head_ref, bf16[256,2048]{1,0:T(8,128)(2,1)S(1)} %get-tuple-element.12.lo_head_ref, bf16[768,2048]{1,0:T(8,128)(2,1)} %get-tuple-element.13.hi_ref, bf16[768,2048]{1,0:T(8,128)(2,1)} %get-tuple-element.14.lo_ref), custom_call_target="tpu_custom_call" | custom-call | tf_op jit(solution)/shard_map/col_cross/pallas_call | solution.py:230
  25.7 9.3 %all_to_all.15.pieces_ref = f32[8,32,256]{2,1,0:T(8,128)S(1)} all-to-all(f32[8,32,256]{2,1,0:T(8,128)S(1)} %col_cross.1), channel_id=1, replica_groups=mesh['row'=8,'col'=4] {'row'}, dimensions={0} | all-to-all | bytes 524288 | tf_op jit(solution)/shard_map/all_to_all | solution.py:438
  35.0 0.2 slab.1
  35.2 0.7 collective-permute-start
  35.9 13.1 %all-gather = f32[256,384]{1,0:T(8,128)S(1)} all-gather(f32[32,384]{1,0:T(8,128)S(1)} %get-tuple-element.16), channel_id=2, replica_groups=mesh['row'=8,'col'=4] {'row'}, dimensions={0}, use_global_device_ids=true | all-gather | bytes 442368 | tf_op jit(solution)/shard_map/all_gather | solution.py:495
  49.0 0.0 collective-permute-done.own_ref
  49.0 0.7 %term.1 = f32[4,32,384]{2,1,0:T(8,128)} custom-call(f32[32,256]{1,0:T(8,128)S(1)} %collective-permute-done.own_ref, f32[8,32,384]{2,1,0:T(8,128)S(1)} %bitcast.9), custom_call_target="tpu_custom_call" | custom-call | tf_op jit(solution)/shard_map/term/pallas_call | solution.py:291
  49.7 3.4 %all-to-all-start.2 = ((f32[4,32,384]{2,1,0:T(8,128)}), f32[4,32,384]{2,1,0:T(8,128)S(1)}, u32[]{:S(2)}, u32[]{:S(2)}) async-start(f32[4,32,384]{2,1,0:T(8,128)} %term.1), calls=%async_computation.2 | async-start | bytes 393216 | tf_op jit(solution)/shard_map/all_to_all | solution.py:438
  53.1 0.0 copy-start
  53.1 1.6 %head.1.head_ref = f32[256,2048]{1,0:T(8,128)S(1)} custom-call(f32[1024,2048]{1,0:T(8,128)} %cov_ref.5, f32[8,32,384]{2,1,0:T(8,128)S(1)} %bitcast.10), custom_call_target="tpu_custom_call" | custom-call | tf_op jit(solution)/shard_map/head/pallas_call | solution.py:324
  54.7 6.6 %all-to-all-done.2.rows_ref = f32[4,32,384]{2,1,0:T(8,128)S(1)} async-done(((f32[4,32,384]{2,1,0:T(8,128)}), f32[4,32,384]{2,1,0:T(8,128)S(1)}, u32[]{:S(2)}, u32[]{:S(2)}) %all-to-all-start.2) | async-done | bytes 196640 | tf_op jit(solution)/shard_map/all_to_all | solution.py:438
  61.3 0.0 copy-done
  61.3 7.4 %update.1 = (f32[2,128]{1,0:T(2,128)}, f32[1024,2048]{1,0:T(8,128)}) custom-call(f32[4,32,384]{2,1,0:T(8,128)S(1)} %all-to-all-done.2.rows_ref, f32[8,32,384]{2,1,0:T(8,128)S(1)} %bitcast.11, f32[32,128]{1,0:T(8,128)S(1)} %get-tuple-element.17.error_ref, f32[64,128]{1,0:T(8,128)S(1)} %copy-done, f32[256,2048]{1,0:T(8,128)S(1)} %head.1.head_ref, ...), custom_call_target="tpu_custom_call" | custom-call | tf_op jit(solution)/shard_map/update/pallas_call | solution.py:397
Async XLA Ops:
  4.8 17.5 %all-to-all-start = ((f32[32,1,16,128]{3,2,1,0:T(8,128)}), f32[32,1,16,128]{3,2,1,0:T(8,128)S(1)}, u32[]{:S(2)}, u32[]{:S(2)}) async-start(f32[32,1,16,128]{3,2,1,0:T(8,128)} %network.1), calls=%async_computation | async-start | bytes 524288 | tf_op jit(solution)/shard_map/all_to_all | solution.py:438
  35.2 13.8 %collective-permute-start = (f32[32,256]{1,0:T(8,128)S(1)}, f32[32,256]{1,0:T(8,128)S(1)}, u32[]{:S(2)}, u32[]{:S(2)}) collective-permute-start(f32[32,256]{1,0:T(8,128)S(1)} %get-tuple-element.15), channel_id=1, source_target_pairs={{0,0},{1,8},{2,16},{3,24},{4,1},{5,9},{6,17},{7,25},{8,2},{9,10},{... | collective-permute-start | bytes 98312 | tf_op jit(solution)/shard_map/ppermute | solution.py:494
  49.7 11.6 %all-to-all-start.2 = ((f32[4,32,384]{2,1,0:T(8,128)}), f32[4,32,384]{2,1,0:T(8,128)S(1)}, u32[]{:S(2)}, u32[]{:S(2)}) async-start(f32[4,32,384]{2,1,0:T(8,128)} %term.1), calls=%async_computation.2 | async-start | bytes 393216 | tf_op jit(solution)/shard_map/all_to_all | solution.py:438
  53.1 8.2 %copy-start = (f32[64,128]{1,0:T(8,128)S(1)}, f32[64,128]{1,0:T(8,128)}, u32[]{:S(2)}) copy-start(f32[64,128]{1,0:T(8,128)} %weight_ref.3) | copy-start | bytes 98308

commit v12 on v11

--- a/solution.py
+++ b/solution.py
@@ -165,7 +165,7 @@
         lo_head_ref[...] = lo
 
 
-def stage(covariance, head):
+def stage(covariance, head, tail):
     rows, cols = covariance.shape
     height = min(rows // 8, head)
     head_steps = head // height
@@ -174,10 +174,10 @@
     head_block = pl.BlockSpec((height, cols), lambda n: (jnp.minimum(n, head_steps - 1), 0))
     return pl.pallas_call(
         functools.partial(stage_kernel, head_steps=head_steps),
-        grid=(rows // height,),
+        grid=((rows - tail) // height,),
         in_specs=[block],
         out_specs=[rest_block, rest_block, head_block, head_block],
-        out_shape=[pltpu.HBM((rows - head, cols), bf16)] * 2 + [pltpu.VMEM((head, cols), bf16)] * 2,
+        out_shape=[pltpu.HBM((rows - head - tail, cols), bf16)] * 2 + [pltpu.VMEM((head, cols), bf16)] * 2,
         compiler_params=limit(12),
         name="stage",
     )(in_hbm(covariance))
@@ -191,7 +191,22 @@
             into_ref[n * streams : (n + 1) * streams, i * lanes : (i + 1) * lanes] = part
 
 
-def col_kernel(jac_ref, hi_head_ref, lo_head_ref, hi_ref, lo_ref, out_ref, parts_ref, hi_rest_ref, lo_rest_ref, sums_ref, sems):
+def col_kernel(
+    jac_ref,
+    hi_head_ref,
+    lo_head_ref,
+    hi_ref,
+    lo_ref,
+    cov_ref,
+    out_ref,
+    parts_ref,
+    hi_rest_ref,
+    lo_rest_ref,
+    tail_ref,
+    sums_ref,
+    sems,
+    tail_sem,
+):
     streams, rows, lanes = jac_ref.shape
     head, tile_cols = hi_head_ref.shape
     slabs, _, slab = out_ref.shape
@@ -207,6 +222,9 @@
         )
         for copy in copies[-1]:
             copy.start()
+    tail = tail_ref.shape[0]
+    last = pltpu.make_async_copy(cov_ref.at[pl.ds(cov_ref.shape[0] - tail, tail)], tail_ref, tail_sem)
+    last.start()
     flat = jac_ref.reshape(streams * rows, lanes)
     stacked_parts(flat, 0, parts_ref.shape[1] // lanes, streams, rows, parts_ref)
     sums_ref[...] = five_products(parts_ref[:, 0:head], hi_head_ref[...], lo_head_ref[...], ((1,), (0,)))
@@ -217,31 +235,51 @@
         sums_ref[...] += five_products(
             parts_ref[:, (n + 1) * head : (n + 2) * head], hi_rest_ref[here, :], lo_rest_ref[here, :], ((1,), (0,))
         )
+    last.wait()
+    sums_ref[...] += five_products(
+        parts_ref[:, parts_ref.shape[1] - tail :], *split2(tail_ref[...]), ((1,), (0,))
+    )
     for n in range(slabs):
         out_ref[n] = sums_ref[:, n * slab : (n + 1) * slab]
 
 
-def col_partial(jac, hi_head, lo_head, hi, lo, slab):
+def col_partial(jac, hi_head, lo_head, hi, lo, covariance, slab):
     streams = jac.shape[0]
     rest, tile_cols = hi.shape
     head = hi_head.shape[0]
+    tail = covariance.shape[0] - head - rest
     whole = pl.BlockSpec(memory_space=pltpu.VMEM)
     beyond = pl.BlockSpec(memory_space=pl.ANY)
     return pl.pallas_call(
         col_kernel,
-        in_specs=[whole] * 3 + [beyond] * 2,
+        in_specs=[whole] * 3 + [beyond] * 3,
         out_specs=whole,
         out_shape=jax.ShapeDtypeStruct((tile_cols // slab, streams, slab), f32),
         scratch_shapes=[
-            pltpu.VMEM((3 * streams, head + rest), bf16),
+            pltpu.VMEM((3 * streams, covariance.shape[0]), bf16),
             pltpu.VMEM((rest, tile_cols), bf16),
             pltpu.VMEM((rest, tile_cols), bf16),
+            pltpu.VMEM((tail, tile_cols), f32),
             pltpu.VMEM((streams, tile_cols), f32),
             pltpu.SemaphoreType.DMA((rest // head, 2)),
+            pltpu.SemaphoreType.DMA,
         ],
         compiler_params=limit(16),
         name="col_cross",
-    )(jac, in_vmem(hi_head), in_vmem(lo_head), in_hbm(hi), in_hbm(lo))
+    )(jac, in_vmem(hi_head), in_vmem(lo_head), in_hbm(hi), in_hbm(lo), in_hbm(covariance))
+
+
+def packed(term):
+    streams = term.shape[0]
+    groups = LANES // streams
+    height = streams // groups
+    return jnp.concatenate([term[n * height : (n + 1) * height] for n in range(groups)], axis=1)
+
+
+def unpacked(rows, streams):
+    return jnp.concatenate(
+        [rows[:, n * streams : (n + 1) * streams] for n in range(LANES // streams)], axis=0
+    )
 
 
 def slab_kernel(pieces_ref, jac_ref, own_ref, out_ref, error_ref, *, first):
@@ -251,14 +289,14 @@
     for n in range(1, pieces_ref.shape[0]):
         total = total + pieces_ref[n]
     own_ref[...] = total
-    out_ref[:, 0:slab] = total
     flat = jac_ref.reshape(streams * rows, lanes)
     term = jnp.zeros((streams, streams), f32)
     for i in range(slab // lanes):
         own = flat[pl.ds(first + i, streams, stride=rows), :]
-        term = term + dot(own, total[:, i * lanes : (i + 1) * lanes], ((1,), (1,)), highest)
-    out_ref[:, slab:] = jnp.zeros((streams, lanes), f32)
-    out_ref[:, slab : slab + streams] = term
+        here = total[:, i * lanes : (i + 1) * lanes]
+        term = term + dot(own, here, ((1,), (1,)), highest)
+        out_ref[i * streams : (i + 1) * streams, :] = here
+    out_ref[slab // lanes * streams :, :] = packed(term)
     error_ref[...] = flat[pl.ds(first + slab // lanes, streams, stride=rows), :]
 
 
@@ -268,7 +306,7 @@
         functools.partial(slab_kernel, first=first),
         out_shape=[
             jax.ShapeDtypeStruct((streams, slab), f32),
-            jax.ShapeDtypeStruct((streams, slab + LANES), f32),
+            jax.ShapeDtypeStruct((streams * (slab + streams) // LANES, LANES), f32),
             jax.ShapeDtypeStruct((streams, LANES), f32),
         ],
         compiler_params=limit(8),
@@ -277,20 +315,22 @@
 
 
 def term_kernel(own_ref, cols_ref, out_ref):
-    slab = own_ref.shape[1]
-    term = cols_ref[0, :, slab:]
+    streams, slab = own_ref.shape
+    _, lanes = out_ref.shape[1:]
+    under = slab // lanes * streams
+    term = cols_ref[0, under:, :]
     for n in range(1, cols_ref.shape[0]):
-        term = term + cols_ref[n, :, slab:]
+        term = term + cols_ref[n, under:, :]
     for n in range(out_ref.shape[0]):
-        out_ref[n, :, 0:slab] = own_ref[...]
-        out_ref[n, :, slab:] = term
+        for i in range(slab // lanes):
+            out_ref[n, i * streams : (i + 1) * streams, :] = own_ref[:, i * lanes : (i + 1) * lanes]
+        out_ref[n, under:, :] = term
 
 
 def with_terms(own, col_slabs, copies):
-    _, streams, padded = col_slabs.shape
     return pl.pallas_call(
         term_kernel,
-        out_shape=jax.ShapeDtypeStruct((copies, streams, padded), f32),
+        out_shape=jax.ShapeDtypeStruct((copies,) + col_slabs.shape[1:], f32),
         compiler_params=limit(8),
         name="term",
     )(own, col_slabs)
@@ -312,34 +352,43 @@
     return inverse / bound
 
 
-def head_kernel(cov_ref, _, head_ref, sem):
+def head_kernel(cov_ref, cols_ref, head_ref, right_ref, sem):
     copy = pltpu.make_async_copy(cov_ref.at[pl.ds(0, head_ref.shape[0])], head_ref, sem)
     copy.start()
+    streams = right_ref.shape[0] // 6
+    slabs, _, lanes = cols_ref.shape
+    per_slab = right_ref.shape[1] // slabs // lanes
+    for n in range(slabs):
+        for i in range(per_slab):
+            hi, mid, lo = split3(cols_ref[n, i * streams : (i + 1) * streams, :])
+            at = (n * per_slab + i) * lanes
+            for m, part in enumerate((hi, mid, lo, hi, mid, hi)):
+                right_ref[m * streams : (m + 1) * streams, at : at + lanes] = part
     copy.wait()
 
 
-def read_head(covariance, col_slabs):
-    beyond = pl.BlockSpec(memory_space=pl.ANY)
+def read_head(covariance, col_slabs, streams):
     rows, cols = covariance.shape
+    whole = pl.BlockSpec(memory_space=pltpu.VMEM)
     return pl.pallas_call(
         head_kernel,
-        in_specs=[beyond, beyond],
-        out_specs=pl.BlockSpec(memory_space=pltpu.VMEM),
-        out_shape=pltpu.VMEM((rows // 4, cols), f32),
+        in_specs=[pl.BlockSpec(memory_space=pl.ANY), whole],
+        out_specs=[whole, whole],
+        out_shape=[pltpu.VMEM((rows // 4, cols), f32), pltpu.VMEM((6 * streams, cols), bf16)],
         scratch_shapes=[pltpu.SemaphoreType.DMA],
-        compiler_params=limit(2),
+        compiler_params=limit(4),
         name="head",
     )(in_hbm(covariance), col_slabs)
 
 
 def update_kernel(
-    rows_ref, cols_ref, error_ref, weight_ref, head_ref, cov_ref, new_weight_ref, new_cov_ref, left_ref, right_ref, tile_ref, in_sems, out_sems
+    rows_ref, right_ref, error_ref, weight_ref, head_ref, cov_ref, new_weight_ref, new_cov_ref, left_ref, tile_ref, in_sems, out_sems
 ):
-    slabs, streams, padded = rows_ref.shape
-    col_slabs = cols_ref.shape[0]
-    lanes = weight_ref.shape[1]
-    slab = padded - lanes
-    tile_rows = slabs * slab
+    slabs, _, lanes = rows_ref.shape
+    streams = error_ref.shape[0]
+    tile_rows = cov_ref.shape[0]
+    slab = tile_rows // slabs
+    under = slab // lanes * streams
     chunks = in_sems.shape[0]
     height = tile_rows // chunks
     held = head_ref.shape[0] // height
@@ -348,16 +397,14 @@
         here = pl.ds(n * height, height)
         reads.append(pltpu.make_async_copy(cov_ref.at[here], tile_ref.at[here], in_sems.at[n]))
         reads[-1].start()
-    term = rows_ref[0, :, slab:]
+    term = rows_ref[0, under:, :]
     for n in range(1, slabs):
-        term = term + rows_ref[n, :, slab:]
-    inverse = invert(term[:, 0:streams])
+        term = term + rows_ref[n, under:, :]
+    inverse = invert(unpacked(term, streams))
     errors = error_ref[:, 0:1]
-    for n in range(col_slabs):
-        hi, mid, lo = split3(cols_ref[n, :, 0:slab])
-        for m, part in enumerate((hi, mid, lo, hi, mid, hi)):
-            right_ref[m * streams : (m + 1) * streams, n * slab : (n + 1) * slab] = part
-    cross = jnp.concatenate([rows_ref[n, :, 0:slab] for n in range(slabs)], axis=1)
+    cross = jnp.concatenate(
+        [rows_ref[n, i : i + streams, :] for n in range(slabs) for i in range(0, under, streams)], axis=1
+    )
     gain = dot(inverse, cross, ((0,), (0,)), highest)
     hi, mid, lo = split3(gain)
     for m, part in enumerate((hi, hi, hi, mid, mid, lo)):
@@ -387,10 +434,10 @@
         write.wait()
 
 
-def update(row_slabs, col_slabs, errors, layer_weight, head, covariance):
-    _, streams, padded = col_slabs.shape
-    slab = padded - LANES
+def update(row_slabs, right, errors, layer_weight, head, covariance):
+    streams = errors.shape[0]
     tile_rows, tile_cols = covariance.shape
+    slab = tile_rows // row_slabs.shape[0]
     width = layer_weight.shape[1]
     whole = pl.BlockSpec(memory_space=pltpu.VMEM)
     beyond = pl.BlockSpec(memory_space=pl.ANY)
@@ -404,14 +451,13 @@
         ],
         scratch_shapes=[
             pltpu.VMEM((6 * streams, tile_rows), bf16),
-            pltpu.VMEM((6 * streams, tile_cols), bf16),
             pltpu.VMEM((tile_rows, tile_cols), f32),
             pltpu.SemaphoreType.DMA((8,)),
             pltpu.SemaphoreType.DMA((8,)),
         ],
         compiler_params=limit(20),
         name="update",
-    )(row_slabs, col_slabs, errors, layer_weight, in_vmem(head), in_hbm(covariance))
+    )(row_slabs, in_vmem(right), errors, layer_weight, in_vmem(head), in_hbm(covariance))
 
 
 def plain_steps(at, jac_all, errors, layer_weight, covariance, slab, cols_n):
@@ -476,7 +522,8 @@
         and tile_rows % (SUBLANES * LANES) == 0
         and tile_cols % (SUBLANES * LANES) == 0
         and rows_n * slab == tile_cols
-        and streams < LANES
+        and LANES % streams == 0
+        and streams * streams % (SUBLANES * LANES) == 0
     )
     if not kernels:
         payload = run_network([[(0, hin)]])[0]
@@ -487,15 +534,15 @@
     plan = [[(r * row_size, row_size), ((c * rows_n + r) * slab_size, slab_size)] for r, c in devices]
     jac = exchange(run_network(plan), ("row", "col"))
     jac = jac.reshape(-1, *jac.shape[2:])
-    hi, lo, hi_head, lo_head = stage(covariance, tile_rows // 4)
-    pieces = exchange(col_partial(jac, hi_head, lo_head, hi, lo, slab), "row")
+    hi, lo, hi_head, lo_head = stage(covariance, tile_rows // 4, tile_rows // 4)
+    pieces = exchange(col_partial(jac, hi_head, lo_head, hi, lo, covariance, slab), "row")
     col_own, with_term, errors = slab_sum(pieces, jac, row_size)
     to_row = [(r * cols_n + c, c * rows_n + r) for r, c in devices]
     row_own = lax.ppermute(col_own, ("row", "col"), to_row)
     col_slabs = lax.all_gather(with_term, "row", axis=0, tiled=False)
     row_slabs = exchange(with_terms(row_own, col_slabs, cols_n), "col")
-    head = read_head(covariance, col_slabs)
-    new_weight, new_cov = update(row_slabs, col_slabs, errors, layer_weight, head, covariance)
+    head, right = read_head(covariance, col_slabs, streams)
+    new_weight, new_cov = update(row_slabs, right, errors, layer_weight, head, covariance)
     return new_weight.reshape(-1), new_cov
 
 

time: 69.3 us -> 66.3 us (0.957)
  Pallas kernels: 25.4 us -> 23.4 us
  blocking collectives: 22.5 us -> 20.8 us
  waiting for transfers between devices: 8.16 us -> 8.92 us
    pallas_call x1, Pallas kernels: 8.65 us -> 6.43 us  [stage(): pl.pallas_call(functools.partial(stage_kernel, head_steps=head_steps), gr...]
    all_gather x1, blocking collectives: 13.1 us -> 11.5 us  [on_device(): col_slabs = lax.all_gather(with_term, 'row', axis=0, tiled=False)]
    all_to_all x2, waiting for transfers between devices: 8.15 us -> 8.92 us  [exchange(): return lax.all_to_all(x, axes, split_axis=0, concat_axis=0, tiled=True)]
  transfers between devices with their start and end apart: 3 -> 3, of which waited for: 2 -> 2; matrix products, arithmetic and copies ran while one was open for 0% -> 0% of each run, Pallas kernels for 15% -> 12%
where the time goes in v12:
time: 66.3 us; the launch traced here: 65.8 us
  Pallas kernels  23.4 us (35%)
  blocking collectives  20.8 us (31%)
  starting transfers between devices  11.3 us (17%)
  waiting for transfers between devices  8.92 us (13%)
  between operations  1.33 us (2%)
    all_gather x1, blocking collectives, on_device(): col_slabs = lax.all_gather(with_term, 'row', axis=0, tiled=False)  11.5 us
    all_to_all x2, starting transfers between devices, exchange(): return lax.all_to_all(x, axes, split_axis=0, concat_axis=0, tiled=True)  10.6 us
    all_to_all x1, blocking collectives, exchange(): return lax.all_to_all(x, axes, split_axis=0, concat_axis=0, tiled=True)  9.35 us
    all_to_all x2, waiting for transfers between devices, exchange(): return lax.all_to_all(x, axes, split_axis=0, concat_axis=0, tiled=True)  8.92 us
    pallas_call x1, Pallas kernels, update(): pl.pallas_call(update_kernel, in_specs=[whole] * 5 + [beyond], out_specs=...  7.42 us
    pallas_call x1, Pallas kernels, stage(): pl.pallas_call(functools.partial(stage_kernel, head_steps=head_steps), gr...  6.43 us
    pallas_call x1, Pallas kernels, network(): pl.pallas_call(functools.partial(network_kernel, plan=plan), grid=(per_de...  3.54 us
    pallas_call x1, Pallas kernels, col_partial(): pl.pallas_call(col_kernel, in_specs=[whole] * 3 + [beyond] * 3, out_specs...  3.47 us
  transfers between devices with their start and end apart: 3, of which 2 were waited for; matrix products, arithmetic and copies ran while one was open for 0% of the time, Pallas kernels for 12%

profile of v12, /device:TPU:0, one launch (start us, length us, event | category | flops | bytes accessed | tf_op | source)
XLA Modules:
  0.0 65.8 jit_solution(11551552090715334690)
XLA Ops:
  1.3 3.5 %network.1 = f32[32,1,16,128]{3,2,1,0:T(8,128)} custom-call(s32[1,1,256]{2,1,0:T(1,128)} %bitcast.14, s32[1,32,256]{2,1,0:T(8,128)} %ids_ref.1, f32[1,32,256]{2,1,0:T(8,128)} %switch_ref.1, f32[1,64,256]{2,1,0:T(8,128)} %bitcast.13, f32[1,1,256]{2,1,0:T(1,128)} %bitcast.15, f32[1,1,1]{2,1,0:T(1,128)} %bitcast.8.target_ref, f32[4,64]{1,0:T(4,128)} %embed_ref.1, ...), custom_call_target="tpu_custom_call" | custom-call | tf_op jit(solution)/shard_map/network/pallas_call | solution.py:118
  4.8 7.3 %all-to-all-start = ((f32[32,1,16,128]{3,2,1,0:T(8,128)}), f32[32,1,16,128]{3,2,1,0:T(8,128)S(1)}, u32[]{:S(2)}, u32[]{:S(2)}) async-start(f32[32,1,16,128]{3,2,1,0:T(8,128)} %network.1), calls=%async_computation | async-start | bytes 524288 | tf_op jit(solution)/shard_map/all_to_all | solution.py:484
  12.1 6.4 %stage.1 = (bf16[512,2048]{1,0:T(8,128)(2,1)}, bf16[512,2048]{1,0:T(8,128)(2,1)}, bf16[256,2048]{1,0:T(8,128)(2,1)S(1)}, bf16[256,2048]{1,0:T(8,128)(2,1)S(1)}) custom-call(f32[1024,2048]{1,0:T(8,128)} %cov_ref.7), custom_call_target="tpu_custom_call" | custom-call | tf_op jit(solution)/shard_map/stage/pallas_call | solution.py:175
  18.5 3.8 %all-to-all-done = f32[32,1,16,128]{3,2,1,0:T(8,128)S(1)} async-done(((f32[32,1,16,128]{3,2,1,0:T(8,128)}), f32[32,1,16,128]{3,2,1,0:T(8,128)S(1)}, u32[]{:S(2)}, u32[]{:S(2)}) %all-to-all-start) | async-done | bytes 262176 | tf_op jit(solution)/shard_map/all_to_all | solution.py:484
  22.3 3.5 %col_cross.1 = f32[8,32,256]{2,1,0:T(8,128)S(1)} custom-call(f32[32,16,128]{2,1,0:T(8,128)S(1)} %bitcast.11, bf16[256,2048]{1,0:T(8,128)(2,1)S(1)} %get-tuple-element.13.hi_head_ref, bf16[256,2048]{1,0:T(8,128)(2,1)S(1)} %get-tuple-element.14.lo_head_ref, bf16[512,2048]{1,0:T(8,128)(2,1)} %get-tuple-element.15.hi_ref, ...), custom_call_target="tpu_custom_call" | custom-call | tf_op jit(solution)/shard_map/col_cross/pallas_call | solution.py:253
  25.8 9.3 %all_to_all.15.pieces_ref = f32[8,32,256]{2,1,0:T(8,128)S(1)} all-to-all(f32[8,32,256]{2,1,0:T(8,128)S(1)} %col_cross.1), channel_id=1, replica_groups=mesh['row'=8,'col'=4] {'row'}, dimensions={0} | all-to-all | bytes 524288 | tf_op jit(solution)/shard_map/all_to_all | solution.py:484
  35.1 0.3 slab.1
  35.4 0.7 %collective-permute-start = (f32[32,256]{1,0:T(8,128)S(1)}, f32[32,256]{1,0:T(8,128)S(1)}, u32[]{:S(2)}, u32[]{:S(2)}) collective-permute-start(f32[32,256]{1,0:T(8,128)S(1)} %get-tuple-element.17), channel_id=1, source_target_pairs={{0,0},{1,8},{2,16},{3,24},{4,1},{5,9},{6,17},{7,25},{8,2},{9,10},{... | collective-permute-start | bytes 98312 | tf_op jit(solution)/shard_map/ppermute | solution.py:541
  36.1 11.5 %all-gather = f32[576,128]{1,0:T(8,128)S(1)} all-gather(f32[72,128]{1,0:T(8,128)S(1)} %get-tuple-element.18), channel_id=2, replica_groups=mesh['row'=8,'col'=4] {'row'}, dimensions={0}, use_global_device_ids=true | all-gather | bytes 331776 | tf_op jit(solution)/shard_map/all_gather | solution.py:542
  47.5 0.0 collective-permute-done.own_ref
  47.5 0.7 %term.1 = f32[4,72,128]{2,1,0:T(8,128)} custom-call(f32[32,256]{1,0:T(8,128)S(1)} %collective-permute-done.own_ref, f32[8,72,128]{2,1,0:T(8,128)S(1)} %bitcast.9), custom_call_target="tpu_custom_call" | custom-call | tf_op jit(solution)/shard_map/term/pallas_call | solution.py:331
  48.2 3.3 %all-to-all-start.2 = ((f32[4,72,128]{2,1,0:T(8,128)}), f32[4,72,128]{2,1,0:T(8,128)S(1)}, u32[]{:S(2)}, u32[]{:S(2)}) async-start(f32[4,72,128]{2,1,0:T(8,128)} %term.1), calls=%async_computation.2 | async-start | bytes 294912 | tf_op jit(solution)/shard_map/all_to_all | solution.py:484
  51.6 0.0 copy-start
  51.6 1.6 %head.1 = (f32[256,2048]{1,0:T(8,128)S(1)}, bf16[192,2048]{1,0:T(8,128)(2,1)S(1)}) custom-call(f32[1024,2048]{1,0:T(8,128)} %cov_ref.7, f32[8,72,128]{2,1,0:T(8,128)S(1)} %bitcast.10), custom_call_target="tpu_custom_call" | custom-call | tf_op jit(solution)/shard_map/head/pallas_call | solution.py:373
  53.2 5.2 %all-to-all-done.2.rows_ref = f32[4,72,128]{2,1,0:T(8,128)S(1)} async-done(((f32[4,72,128]{2,1,0:T(8,128)}), f32[4,72,128]{2,1,0:T(8,128)S(1)}, u32[]{:S(2)}, u32[]{:S(2)}) %all-to-all-start.2) | async-done | bytes 147488 | tf_op jit(solution)/shard_map/all_to_all | solution.py:484
  58.3 0.0 copy-done
  58.3 7.4 %update.1 = (f32[2,128]{1,0:T(2,128)}, f32[1024,2048]{1,0:T(8,128)}) custom-call(f32[4,72,128]{2,1,0:T(8,128)S(1)} %all-to-all-done.2.rows_ref, bf16[192,2048]{1,0:T(8,128)(2,1)S(1)} %get-tuple-element.19.right_ref, f32[32,128]{1,0:T(8,128)S(1)} %get-tuple-element.20.error_ref, f32[64,128]{1,0:T(8,128)S(1)} %copy-done, ...), custom_call_target="tpu_custom_call" | custom-call | tf_op jit(solution)/shard_map/update/pallas_call | solution.py:444
Async XLA Ops:
  4.8 17.5 %all-to-all-start = ((f32[32,1,16,128]{3,2,1,0:T(8,128)}), f32[32,1,16,128]{3,2,1,0:T(8,128)S(1)}, u32[]{:S(2)}, u32[]{:S(2)}) async-start(f32[32,1,16,128]{3,2,1,0:T(8,128)} %network.1), calls=%async_computation | async-start | bytes 524288 | tf_op jit(solution)/shard_map/all_to_all | solution.py:484
  35.4 12.1 %collective-permute-start = (f32[32,256]{1,0:T(8,128)S(1)}, f32[32,256]{1,0:T(8,128)S(1)}, u32[]{:S(2)}, u32[]{:S(2)}) collective-permute-start(f32[32,256]{1,0:T(8,128)S(1)} %get-tuple-element.17), channel_id=1, source_target_pairs={{0,0},{1,8},{2,16},{3,24},{4,1},{5,9},{6,17},{7,25},{8,2},{9,10},{... | collective-permute-start | bytes 98312 | tf_op jit(solution)/shard_map/ppermute | solution.py:541
  48.2 10.1 %all-to-all-start.2 = ((f32[4,72,128]{2,1,0:T(8,128)}), f32[4,72,128]{2,1,0:T(8,128)S(1)}, u32[]{:S(2)}, u32[]{:S(2)}) async-start(f32[4,72,128]{2,1,0:T(8,128)} %term.1), calls=%async_computation.2 | async-start | bytes 294912 | tf_op jit(solution)/shard_map/all_to_all | solution.py:484
  51.6 6.8 %copy-start = (f32[64,128]{1,0:T(8,128)S(1)}, f32[64,128]{1,0:T(8,128)}, u32[]{:S(2)}) copy-start(f32[64,128]{1,0:T(8,128)} %weight_ref.3) | copy-start | bytes 98308

commit v13 on v12

--- a/solution.py
+++ b/solution.py
@@ -352,37 +352,28 @@
     return inverse / bound
 
 
-def head_kernel(cov_ref, cols_ref, head_ref, right_ref, sem):
+def head_kernel(cov_ref, _, head_ref, sem):
     copy = pltpu.make_async_copy(cov_ref.at[pl.ds(0, head_ref.shape[0])], head_ref, sem)
     copy.start()
-    streams = right_ref.shape[0] // 6
-    slabs, _, lanes = cols_ref.shape
-    per_slab = right_ref.shape[1] // slabs // lanes
-    for n in range(slabs):
-        for i in range(per_slab):
-            hi, mid, lo = split3(cols_ref[n, i * streams : (i + 1) * streams, :])
-            at = (n * per_slab + i) * lanes
-            for m, part in enumerate((hi, mid, lo, hi, mid, hi)):
-                right_ref[m * streams : (m + 1) * streams, at : at + lanes] = part
     copy.wait()
 
 
-def read_head(covariance, col_slabs, streams):
+def read_head(covariance, after):
+    beyond = pl.BlockSpec(memory_space=pl.ANY)
     rows, cols = covariance.shape
-    whole = pl.BlockSpec(memory_space=pltpu.VMEM)
     return pl.pallas_call(
         head_kernel,
-        in_specs=[pl.BlockSpec(memory_space=pl.ANY), whole],
-        out_specs=[whole, whole],
-        out_shape=[pltpu.VMEM((rows // 4, cols), f32), pltpu.VMEM((6 * streams, cols), bf16)],
+        in_specs=[beyond, beyond],
+        out_specs=pl.BlockSpec(memory_space=pltpu.VMEM),
+        out_shape=pltpu.VMEM((rows // 4, cols), f32),
         scratch_shapes=[pltpu.SemaphoreType.DMA],
-        compiler_params=limit(4),
+        compiler_params=limit(2),
         name="head",
-    )(in_hbm(covariance), col_slabs)
+    )(in_hbm(covariance), after)
 
 
 def update_kernel(
-    rows_ref, right_ref, error_ref, weight_ref, head_ref, cov_ref, new_weight_ref, new_cov_ref, left_ref, tile_ref, in_sems, out_sems
+    rows_ref, cols_ref, error_ref, weight_ref, head_ref, cov_ref, new_weight_ref, new_cov_ref, left_ref, right_ref, tile_ref, in_sems, out_sems
 ):
     slabs, _, lanes = rows_ref.shape
     streams = error_ref.shape[0]
@@ -402,6 +393,12 @@
         term = term + rows_ref[n, under:, :]
     inverse = invert(unpacked(term, streams))
     errors = error_ref[:, 0:1]
+    for n in range(cols_ref.shape[0]):
+        for i in range(slab // lanes):
+            hi, mid, lo = split3(cols_ref[n, i * streams : (i + 1) * streams, :])
+            at = n * slab + i * lanes
+            for m, part in enumerate((hi, mid, lo, hi, mid, hi)):
+                right_ref[m * streams : (m + 1) * streams, at : at + lanes] = part
     cross = jnp.concatenate(
         [rows_ref[n, i : i + streams, :] for n in range(slabs) for i in range(0, under, streams)], axis=1
     )
@@ -434,7 +431,7 @@
         write.wait()
 
 
-def update(row_slabs, right, errors, layer_weight, head, covariance):
+def update(row_slabs, col_slabs, errors, layer_weight, head, covariance):
     streams = errors.shape[0]
     tile_rows, tile_cols = covariance.shape
     slab = tile_rows // row_slabs.shape[0]
@@ -451,13 +448,14 @@
         ],
         scratch_shapes=[
             pltpu.VMEM((6 * streams, tile_rows), bf16),
+            pltpu.VMEM((6 * streams, tile_cols), bf16),
             pltpu.VMEM((tile_rows, tile_cols), f32),
             pltpu.SemaphoreType.DMA((8,)),
             pltpu.SemaphoreType.DMA((8,)),
         ],
         compiler_params=limit(20),
         name="update",
-    )(row_slabs, in_vmem(right), errors, layer_weight, in_vmem(head), in_hbm(covariance))
+    )(row_slabs, col_slabs, errors, layer_weight, in_vmem(head), in_hbm(covariance))
 
 
 def plain_steps(at, jac_all, errors, layer_weight, covariance, slab, cols_n):
@@ -534,15 +532,16 @@
     plan = [[(r * row_size, row_size), ((c * rows_n + r) * slab_size, slab_size)] for r, c in devices]
     jac = exchange(run_network(plan), ("row", "col"))
     jac = jac.reshape(-1, *jac.shape[2:])
-    hi, lo, hi_head, lo_head = stage(covariance, tile_rows // 4, tile_rows // 4)
-    pieces = exchange(col_partial(jac, hi_head, lo_head, hi, lo, covariance, slab), "row")
+    hi, lo, hi_head, lo_head = stage(covariance, tile_rows // 8 * 3, tile_rows // 4)
+    col_part = col_partial(jac, hi_head, lo_head, hi, lo, covariance, slab)
+    pieces = exchange(col_part, "row")
+    head = read_head(covariance, col_part)
     col_own, with_term, errors = slab_sum(pieces, jac, row_size)
     to_row = [(r * cols_n + c, c * rows_n + r) for r, c in devices]
     row_own = lax.ppermute(col_own, ("row", "col"), to_row)
     col_slabs = lax.all_gather(with_term, "row", axis=0, tiled=False)
     row_slabs = exchange(with_terms(row_own, col_slabs, cols_n), "col")
-    head, right = read_head(covariance, col_slabs, streams)
-    new_weight, new_cov = update(row_slabs, right, errors, layer_weight, head, covariance)
+    new_weight, new_cov = update(row_slabs, col_slabs, errors, layer_weight, head, covariance)
     return new_weight.reshape(-1), new_cov
 
 

time: 66.3 us -> 65.9 us (level)
  local copies, waits for them, and re-layouts: 0.01 us -> 2.57 us
  Pallas kernels: 23.4 us -> 21.2 us
  waiting for transfers between devices: 8.92 us -> 8.03 us
    unnamed x2 -> x6, local copies, waits for them, and re-layouts: 0.01 us -> 2.57 us
    pallas_call x1, Pallas kernels: 7.42 us -> 5.86 us  [update(): pl.pallas_call(update_kernel, in_specs=[whole] * 5 + [beyond], out_specs=...]
    all_to_all x2, waiting for transfers between devices: 8.92 us -> 8.03 us  [exchange(): return lax.all_to_all(x, axes, split_axis=0, concat_axis=0, tiled=True)]
where the time goes in v13:
time: 65.9 us; the launch traced here: 65.4 us
  Pallas kernels  21.2 us (32%)
  blocking collectives  20.9 us (32%)
  starting transfers between devices  11.3 us (17%)
  waiting for transfers between devices  8.03 us (12%)
  local copies, waits for them, and re-layouts  2.57 us (4%)
  between operations  1.33 us (2%)
    all_gather x1, blocking collectives, on_device(): col_slabs = lax.all_gather(with_term, 'row', axis=0, tiled=False)  11.6 us
    all_to_all x2, starting transfers between devices, exchange(): return lax.all_to_all(x, axes, split_axis=0, concat_axis=0, tiled=True)  10.6 us
    all_to_all x1, blocking collectives, exchange(): return lax.all_to_all(x, axes, split_axis=0, concat_axis=0, tiled=True)  9.35 us
    all_to_all x2, waiting for transfers between devices, exchange(): return lax.all_to_all(x, axes, split_axis=0, concat_axis=0, tiled=True)  8.03 us
    pallas_call x1, Pallas kernels, stage(): pl.pallas_call(functools.partial(stage_kernel, head_steps=head_steps), gr...  6.17 us
    pallas_call x1, Pallas kernels, update(): pl.pallas_call(update_kernel, in_specs=[whole] * 5 + [beyond], out_specs=...  5.86 us
    pallas_call x1, Pallas kernels, network(): pl.pallas_call(functools.partial(network_kernel, plan=plan), grid=(per_de...  3.54 us
    pallas_call x1, Pallas kernels, col_partial(): pl.pallas_call(col_kernel, in_specs=[whole] * 3 + [beyond] * 3, out_specs...  3.08 us
  transfers between devices with their start and end apart: 3, of which 2 were waited for; matrix products, arithmetic and copies ran while one was open for 0% of the time, Pallas kernels for 12%

profile of v13, /device:TPU:0, one launch (start us, length us, event | category | flops | bytes accessed | tf_op | source)
XLA Modules:
  0.0 65.4 jit_solution(6537703908886735256)
XLA Ops:
  1.3 3.5 %network.1 = f32[32,1,16,128]{3,2,1,0:T(8,128)} custom-call(s32[1,1,256]{2,1,0:T(1,128)} %bitcast.14, s32[1,32,256]{2,1,0:T(8,128)} %ids_ref.1, f32[1,32,256]{2,1,0:T(8,128)} %switch_ref.1, f32[1,64,256]{2,1,0:T(8,128)} %bitcast.13, f32[1,1,256]{2,1,0:T(1,128)} %bitcast.15, f32[1,1,1]{2,1,0:T(1,128)} %bitcast.8.target_ref, f32[4,64]{1,0:T(4,128)} %embed_ref.1, ...), custom_call_target="tpu_custom_call" | custom-call | tf_op jit(solution)/shard_map/network/pallas_call | solution.py:118
  4.8 7.3 %all-to-all-start = ((f32[32,1,16,128]{3,2,1,0:T(8,128)}), f32[32,1,16,128]{3,2,1,0:T(8,128)S(1)}, u32[]{:S(2)}, u32[]{:S(2)}) async-start(f32[32,1,16,128]{3,2,1,0:T(8,128)} %network.1), calls=%async_computation | async-start | bytes 524288 | tf_op jit(solution)/shard_map/all_to_all | solution.py:482
  12.1 6.2 %stage.1 = (bf16[384,2048]{1,0:T(8,128)(2,1)}, bf16[384,2048]{1,0:T(8,128)(2,1)}, bf16[384,2048]{1,0:T(8,128)(2,1)S(1)}, bf16[384,2048]{1,0:T(8,128)(2,1)S(1)}) custom-call(f32[1024,2048]{1,0:T(8,128)} %cov_ref.7), custom_call_target="tpu_custom_call" | custom-call | tf_op jit(solution)/shard_map/stage/pallas_call | solution.py:175
  18.3 0.0 copy-start
  18.3 1.2 %copy-done = bf16[384,2048]{1,0:T(8,128)(2,1)} copy-done((bf16[384,2048]{1,0:T(8,128)(2,1)}, bf16[384,2048]{1,0:T(8,128)(2,1)S(1)}, u32[]{:S(2)}) %copy-start) | copy-done | bytes 1572888
  19.4 2.9 %all-to-all-done = f32[32,1,16,128]{3,2,1,0:T(8,128)S(1)} async-done(((f32[32,1,16,128]{3,2,1,0:T(8,128)}), f32[32,1,16,128]{3,2,1,0:T(8,128)S(1)}, u32[]{:S(2)}, u32[]{:S(2)}) %all-to-all-start) | async-done | bytes 262176 | tf_op jit(solution)/shard_map/all_to_all | solution.py:482
  22.3 0.0 copy-start.1
  22.3 1.4 %copy-done.1 = bf16[384,2048]{1,0:T(8,128)(2,1)S(1)} copy-done((bf16[384,2048]{1,0:T(8,128)(2,1)S(1)}, bf16[384,2048]{1,0:T(8,128)(2,1)}, u32[]{:S(2)}) %copy-start.1) | copy-done | bytes 1572888
  23.7 3.1 %col_cross.1._ = f32[8,32,256]{2,1,0:T(8,128)S(1)} custom-call(f32[32,16,128]{2,1,0:T(8,128)S(1)} %bitcast.11, bf16[384,2048]{1,0:T(8,128)(2,1)S(1)} %get-tuple-element.11.hi_head_ref, bf16[384,2048]{1,0:T(8,128)(2,1)S(1)} %copy-done.1, bf16[384,2048]{1,0:T(8,128)(2,1)} %get-tuple-element.13.hi_ref, bf16[384,2048]{1,0:T(8,128)(2,1)} %get-tuple-element.14.lo_ref, ...), custom_call_target="tpu_custom_call" | custom-call | tf_op jit(solution)/shard_map/col_cross/pallas_call | solution.py:253
  26.8 9.3 %all_to_all.15.pieces_ref = f32[8,32,256]{2,1,0:T(8,128)S(1)} all-to-all(f32[8,32,256]{2,1,0:T(8,128)S(1)} %col_cross.1._), channel_id=1, replica_groups=mesh['row'=8,'col'=4] {'row'}, dimensions={0} | all-to-all | bytes 524288 | tf_op jit(solution)/shard_map/all_to_all | solution.py:482
  36.2 0.3 slab.1
  36.4 0.7 %collective-permute-start = (f32[32,256]{1,0:T(8,128)S(1)}, f32[32,256]{1,0:T(8,128)S(1)}, u32[]{:S(2)}, u32[]{:S(2)}) collective-permute-start(f32[32,256]{1,0:T(8,128)S(1)} %get-tuple-element.15), channel_id=1, source_target_pairs={{0,0},{1,8},{2,16},{3,24},{4,1},{5,9},{6,17},{7,25},{8,2},{9,10},{... | collective-permute-start | bytes 98312 | tf_op jit(solution)/shard_map/ppermute | solution.py:541
  37.1 11.6 %all-gather = f32[576,128]{1,0:T(8,128)S(1)} all-gather(f32[72,128]{1,0:T(8,128)S(1)} %get-tuple-element.16), channel_id=2, replica_groups=mesh['row'=8,'col'=4] {'row'}, dimensions={0}, use_global_device_ids=true | all-gather | bytes 331776 | tf_op jit(solution)/shard_map/all_gather | solution.py:542
  48.7 0.0 collective-permute-done.own_ref
  48.7 0.7 %term.1 = f32[4,72,128]{2,1,0:T(8,128)} custom-call(f32[32,256]{1,0:T(8,128)S(1)} %collective-permute-done.own_ref, f32[8,72,128]{2,1,0:T(8,128)S(1)} %bitcast.9), custom_call_target="tpu_custom_call" | custom-call | tf_op jit(solution)/shard_map/term/pallas_call | solution.py:331
  49.4 3.3 %all-to-all-start.2 = ((f32[4,72,128]{2,1,0:T(8,128)}), f32[4,72,128]{2,1,0:T(8,128)S(1)}, u32[]{:S(2)}, u32[]{:S(2)}) async-start(f32[4,72,128]{2,1,0:T(8,128)} %term.1), calls=%async_computation.2 | async-start | bytes 294912 | tf_op jit(solution)/shard_map/all_to_all | solution.py:482
  52.7 0.0 copy-start.2
  52.7 1.6 %head.1.head_ref = f32[256,2048]{1,0:T(8,128)S(1)} custom-call(f32[1024,2048]{1,0:T(8,128)} %cov_ref.7, f32[8,32,256]{2,1,0:T(8,128)S(1)} %col_cross.1._), custom_call_target="tpu_custom_call" | custom-call | tf_op jit(solution)/shard_map/head/pallas_call | solution.py:364
  54.3 5.2 %all-to-all-done.2.rows_ref = f32[4,72,128]{2,1,0:T(8,128)S(1)} async-done(((f32[4,72,128]{2,1,0:T(8,128)}), f32[4,72,128]{2,1,0:T(8,128)S(1)}, u32[]{:S(2)}, u32[]{:S(2)}) %all-to-all-start.2) | async-done | bytes 147488 | tf_op jit(solution)/shard_map/all_to_all | solution.py:482
  59.5 0.0 copy-done.2
  59.5 5.9 %update.1 = (f32[2,128]{1,0:T(2,128)}, f32[1024,2048]{1,0:T(8,128)}) custom-call(f32[4,72,128]{2,1,0:T(8,128)S(1)} %all-to-all-done.2.rows_ref, f32[8,72,128]{2,1,0:T(8,128)S(1)} %bitcast.10, f32[32,128]{1,0:T(8,128)S(1)} %get-tuple-element.17.error_ref, f32[64,128]{1,0:T(8,128)S(1)} %copy-done.2, f32[256,2048]{1,0:T(8,128)S(1)} %head.1.head_ref, ...), custom_call_target="tpu_custom_call" | custom-call | tf_op jit(solution)/shard_map/update/pallas_call | solution.py:441
Async XLA Ops:
  4.8 17.5 %all-to-all-start = ((f32[32,1,16,128]{3,2,1,0:T(8,128)}), f32[32,1,16,128]{3,2,1,0:T(8,128)S(1)}, u32[]{:S(2)}, u32[]{:S(2)}) async-start(f32[32,1,16,128]{3,2,1,0:T(8,128)} %network.1), calls=%async_computation | async-start | bytes 524288 | tf_op jit(solution)/shard_map/all_to_all | solution.py:482
  18.3 1.2 %copy-start = (bf16[384,2048]{1,0:T(8,128)(2,1)}, bf16[384,2048]{1,0:T(8,128)(2,1)S(1)}, u32[]{:S(2)}) copy-start(bf16[384,2048]{1,0:T(8,128)(2,1)S(1)} %get-tuple-element.12.lo_head_ref) | copy-start | bytes 4718596
  22.3 1.4 %copy-start.1 = (bf16[384,2048]{1,0:T(8,128)(2,1)S(1)}, bf16[384,2048]{1,0:T(8,128)(2,1)}, u32[]{:S(2)}) copy-start(bf16[384,2048]{1,0:T(8,128)(2,1)} %copy-done) | copy-start | bytes 4718596
  36.4 12.3 %collective-permute-start = (f32[32,256]{1,0:T(8,128)S(1)}, f32[32,256]{1,0:T(8,128)S(1)}, u32[]{:S(2)}, u32[]{:S(2)}) collective-permute-start(f32[32,256]{1,0:T(8,128)S(1)} %get-tuple-element.15), channel_id=1, source_target_pairs={{0,0},{1,8},{2,16},{3,24},{4,1},{5,9},{6,17},{7,25},{8,2},{9,10},{... | collective-permute-start | bytes 98312 | tf_op jit(solution)/shard_map/ppermute | solution.py:541
  49.4 10.1 %all-to-all-start.2 = ((f32[4,72,128]{2,1,0:T(8,128)}), f32[4,72,128]{2,1,0:T(8,128)S(1)}, u32[]{:S(2)}, u32[]{:S(2)}) async-start(f32[4,72,128]{2,1,0:T(8,128)} %term.1), calls=%async_computation.2 | async-start | bytes 294912 | tf_op jit(solution)/shard_map/all_to_all | solution.py:482
  52.7 6.8 %copy-start.2 = (f32[64,128]{1,0:T(8,128)S(1)}, f32[64,128]{1,0:T(8,128)}, u32[]{:S(2)}) copy-start(f32[64,128]{1,0:T(8,128)} %weight_ref.3) | copy-start | bytes 98308

commit v14 on v13

--- a/solution.py
+++ b/solution.py
@@ -532,7 +532,7 @@
     plan = [[(r * row_size, row_size), ((c * rows_n + r) * slab_size, slab_size)] for r, c in devices]
     jac = exchange(run_network(plan), ("row", "col"))
     jac = jac.reshape(-1, *jac.shape[2:])
-    hi, lo, hi_head, lo_head = stage(covariance, tile_rows // 8 * 3, tile_rows // 4)
+    hi, lo, hi_head, lo_head = stage(covariance, tile_rows // 4, tile_rows // 4)
     col_part = col_partial(jac, hi_head, lo_head, hi, lo, covariance, slab)
     pieces = exchange(col_part, "row")
     head = read_head(covariance, col_part)

time: 65.9 us -> 64.8 us (0.983)
  local copies, waits for them, and re-layouts: 2.57 us -> 0.01 us
  waiting for transfers between devices: 8.03 us -> 8.91 us
  Pallas kernels: 21.2 us -> 21.9 us
    unnamed x6 -> x2, local copies, waits for them, and re-layouts: 2.57 us -> 0.01 us
    all_to_all x2, waiting for transfers between devices: 8.03 us -> 8.91 us  [exchange(): return lax.all_to_all(x, axes, split_axis=0, concat_axis=0, tiled=True)]
  transfers between devices with their start and end apart: 3 -> 3, of which waited for: 2 -> 2; matrix products, arithmetic and copies ran while one was open for 0% -> 0% of each run, Pallas kernels for 12% -> 13%
where the time goes in v14:
time: 64.8 us; the launch traced here: 64.2 us
  Pallas kernels  21.9 us (34%)
  blocking collectives  20.8 us (32%)
  starting transfers between devices  11.3 us (17%)
  waiting for transfers between devices  8.91 us (14%)
  between operations  1.33 us (2%)
    all_gather x1, blocking collectives, on_device(): col_slabs = lax.all_gather(with_term, 'row', axis=0, tiled=False)  11.5 us
    all_to_all x2, starting transfers between devices, exchange(): return lax.all_to_all(x, axes, split_axis=0, concat_axis=0, tiled=True)  10.6 us
    all_to_all x1, blocking collectives, exchange(): return lax.all_to_all(x, axes, split_axis=0, concat_axis=0, tiled=True)  9.35 us
    all_to_all x2, waiting for transfers between devices, exchange(): return lax.all_to_all(x, axes, split_axis=0, concat_axis=0, tiled=True)  8.91 us
    pallas_call x1, Pallas kernels, stage(): pl.pallas_call(functools.partial(stage_kernel, head_steps=head_steps), gr...  6.44 us
    pallas_call x1, Pallas kernels, update(): pl.pallas_call(update_kernel, in_specs=[whole] * 5 + [beyond], out_specs=...  5.86 us
    pallas_call x1, Pallas kernels, network(): pl.pallas_call(functools.partial(network_kernel, plan=plan), grid=(per_de...  3.54 us
    pallas_call x1, Pallas kernels, col_partial(): pl.pallas_call(col_kernel, in_specs=[whole] * 3 + [beyond] * 3, out_specs...  3.48 us
  transfers between devices with their start and end apart: 3, of which 2 were waited for; matrix products, arithmetic and copies ran while one was open for 0% of the time, Pallas kernels for 13%

profile of v14, /device:TPU:0, one launch (start us, length us, event | category | flops | bytes accessed | tf_op | source)
XLA Modules:
  0.0 64.2 jit_solution(17930830757495405239)
XLA Ops:
  1.3 3.5 %network.1 = f32[32,1,16,128]{3,2,1,0:T(8,128)} custom-call(s32[1,1,256]{2,1,0:T(1,128)} %bitcast.14, s32[1,32,256]{2,1,0:T(8,128)} %ids_ref.1, f32[1,32,256]{2,1,0:T(8,128)} %switch_ref.1, f32[1,64,256]{2,1,0:T(8,128)} %bitcast.13, f32[1,1,256]{2,1,0:T(1,128)} %bitcast.15, f32[1,1,1]{2,1,0:T(1,128)} %bitcast.8.target_ref, f32[4,64]{1,0:T(4,128)} %embed_ref.1, ...), custom_call_target="tpu_custom_call" | custom-call | tf_op jit(solution)/shard_map/network/pallas_call | solution.py:118
  4.8 7.3 %all-to-all-start = ((f32[32,1,16,128]{3,2,1,0:T(8,128)}), f32[32,1,16,128]{3,2,1,0:T(8,128)S(1)}, u32[]{:S(2)}, u32[]{:S(2)}) async-start(f32[32,1,16,128]{3,2,1,0:T(8,128)} %network.1), calls=%async_computation | async-start | bytes 524288 | tf_op jit(solution)/shard_map/all_to_all | solution.py:482
  12.1 6.4 %stage.1 = (bf16[512,2048]{1,0:T(8,128)(2,1)}, bf16[512,2048]{1,0:T(8,128)(2,1)}, bf16[256,2048]{1,0:T(8,128)(2,1)S(1)}, bf16[256,2048]{1,0:T(8,128)(2,1)S(1)}) custom-call(f32[1024,2048]{1,0:T(8,128)} %cov_ref.7), custom_call_target="tpu_custom_call" | custom-call | tf_op jit(solution)/shard_map/stage/pallas_call | solution.py:175
  18.6 3.8 %all-to-all-done = f32[32,1,16,128]{3,2,1,0:T(8,128)S(1)} async-done(((f32[32,1,16,128]{3,2,1,0:T(8,128)}), f32[32,1,16,128]{3,2,1,0:T(8,128)S(1)}, u32[]{:S(2)}, u32[]{:S(2)}) %all-to-all-start) | async-done | bytes 262176 | tf_op jit(solution)/shard_map/all_to_all | solution.py:482
  22.3 3.5 %col_cross.1._ = f32[8,32,256]{2,1,0:T(8,128)S(1)} custom-call(f32[32,16,128]{2,1,0:T(8,128)S(1)} %bitcast.11, bf16[256,2048]{1,0:T(8,128)(2,1)S(1)} %get-tuple-element.11.hi_head_ref, bf16[256,2048]{1,0:T(8,128)(2,1)S(1)} %get-tuple-element.12.lo_head_ref, bf16[512,2048]{1,0:T(8,128)(2,1)} %get-tuple-element.13.hi_ref, ...), custom_call_target="tpu_custom_call" | custom-call | tf_op jit(solution)/shard_map/col_cross/pallas_call | solution.py:253
  25.8 9.3 %all_to_all.15.pieces_ref = f32[8,32,256]{2,1,0:T(8,128)S(1)} all-to-all(f32[8,32,256]{2,1,0:T(8,128)S(1)} %col_cross.1._), channel_id=1, replica_groups=mesh['row'=8,'col'=4] {'row'}, dimensions={0} | all-to-all | bytes 524288 | tf_op jit(solution)/shard_map/all_to_all | solution.py:482
  35.2 0.3 slab.1
  35.4 0.7 %collective-permute-start = (f32[32,256]{1,0:T(8,128)S(1)}, f32[32,256]{1,0:T(8,128)S(1)}, u32[]{:S(2)}, u32[]{:S(2)}) collective-permute-start(f32[32,256]{1,0:T(8,128)S(1)} %get-tuple-element.15), channel_id=1, source_target_pairs={{0,0},{1,8},{2,16},{3,24},{4,1},{5,9},{6,17},{7,25},{8,2},{9,10},{... | collective-permute-start | bytes 98312 | tf_op jit(solution)/shard_map/ppermute | solution.py:541
  36.1 11.5 %all-gather = f32[576,128]{1,0:T(8,128)S(1)} all-gather(f32[72,128]{1,0:T(8,128)S(1)} %get-tuple-element.16), channel_id=2, replica_groups=mesh['row'=8,'col'=4] {'row'}, dimensions={0}, use_global_device_ids=true | all-gather | bytes 331776 | tf_op jit(solution)/shard_map/all_gather | solution.py:542
  47.5 0.0 collective-permute-done.own_ref
  47.5 0.7 %term.1 = f32[4,72,128]{2,1,0:T(8,128)} custom-call(f32[32,256]{1,0:T(8,128)S(1)} %collective-permute-done.own_ref, f32[8,72,128]{2,1,0:T(8,128)S(1)} %bitcast.9), custom_call_target="tpu_custom_call" | custom-call | tf_op jit(solution)/shard_map/term/pallas_call | solution.py:331
  48.2 3.3 %all-to-all-start.2 = ((f32[4,72,128]{2,1,0:T(8,128)}), f32[4,72,128]{2,1,0:T(8,128)S(1)}, u32[]{:S(2)}, u32[]{:S(2)}) async-start(f32[4,72,128]{2,1,0:T(8,128)} %term.1), calls=%async_computation.2 | async-start | bytes 294912 | tf_op jit(solution)/shard_map/all_to_all | solution.py:482
  51.6 0.0 copy-start
  51.6 1.6 %head.1.head_ref = f32[256,2048]{1,0:T(8,128)S(1)} custom-call(f32[1024,2048]{1,0:T(8,128)} %cov_ref.7, f32[8,32,256]{2,1,0:T(8,128)S(1)} %col_cross.1._), custom_call_target="tpu_custom_call" | custom-call | tf_op jit(solution)/shard_map/head/pallas_call | solution.py:364
  53.2 5.2 %all-to-all-done.2.rows_ref = f32[4,72,128]{2,1,0:T(8,128)S(1)} async-done(((f32[4,72,128]{2,1,0:T(8,128)}), f32[4,72,128]{2,1,0:T(8,128)S(1)}, u32[]{:S(2)}, u32[]{:S(2)}) %all-to-all-start.2) | async-done | bytes 147488 | tf_op jit(solution)/shard_map/all_to_all | solution.py:482
  58.3 0.0 copy-done
  58.3 5.9 %update.1 = (f32[2,128]{1,0:T(2,128)}, f32[1024,2048]{1,0:T(8,128)}) custom-call(f32[4,72,128]{2,1,0:T(8,128)S(1)} %all-to-all-done.2.rows_ref, f32[8,72,128]{2,1,0:T(8,128)S(1)} %bitcast.10, f32[32,128]{1,0:T(8,128)S(1)} %get-tuple-element.17.error_ref, f32[64,128]{1,0:T(8,128)S(1)} %copy-done, f32[256,2048]{1,0:T(8,128)S(1)} %head.1.head_ref, ...), custom_call_target="tpu_custom_call" | custom-call | tf_op jit(solution)/shard_map/update/pallas_call | solution.py:441
Async XLA Ops:
  4.8 17.5 %all-to-all-start = ((f32[32,1,16,128]{3,2,1,0:T(8,128)}), f32[32,1,16,128]{3,2,1,0:T(8,128)S(1)}, u32[]{:S(2)}, u32[]{:S(2)}) async-start(f32[32,1,16,128]{3,2,1,0:T(8,128)} %network.1), calls=%async_computation | async-start | bytes 524288 | tf_op jit(solution)/shard_map/all_to_all | solution.py:482
  35.4 12.1 %collective-permute-start = (f32[32,256]{1,0:T(8,128)S(1)}, f32[32,256]{1,0:T(8,128)S(1)}, u32[]{:S(2)}, u32[]{:S(2)}) collective-permute-start(f32[32,256]{1,0:T(8,128)S(1)} %get-tuple-element.15), channel_id=1, source_target_pairs={{0,0},{1,8},{2,16},{3,24},{4,1},{5,9},{6,17},{7,25},{8,2},{9,10},{... | collective-permute-start | bytes 98312 | tf_op jit(solution)/shard_map/ppermute | solution.py:541
  48.2 10.1 %all-to-all-start.2 = ((f32[4,72,128]{2,1,0:T(8,128)}), f32[4,72,128]{2,1,0:T(8,128)S(1)}, u32[]{:S(2)}, u32[]{:S(2)}) async-start(f32[4,72,128]{2,1,0:T(8,128)} %term.1), calls=%async_computation.2 | async-start | bytes 294912 | tf_op jit(solution)/shard_map/all_to_all | solution.py:482
  51.6 6.8 %copy-start = (f32[64,128]{1,0:T(8,128)S(1)}, f32[64,128]{1,0:T(8,128)}, u32[]{:S(2)}) copy-start(f32[64,128]{1,0:T(8,128)} %weight_ref.3) | copy-start | bytes 98308

commit v15 on v14

--- a/solution.py
+++ b/solution.py
@@ -92,13 +92,13 @@
     parts = jnp.concatenate(split3(hidden * force), axis=0)
     jacobian = five_products(parts, *split2(slopes), ((1,), (0,))) * scale
     error = target_ref[...] - predicted
-    for block, pieces in enumerate(plan):
-        at = 0
+    at = 0
+    for pieces in plan:
         for start, size in pieces:
-            payload_ref[block, at : at + size, :] = jacobian[start : start + size, :]
+            payload_ref[at : at + size, :] = jacobian[start : start + size, :]
             at += size
-        rest = payload_ref.shape[1] - at
-        payload_ref[block, at:, :] = jnp.broadcast_to(error, (rest, jacobian.shape[1]))
+        payload_ref[at : at + 1, :] = jnp.broadcast_to(error, (1, jacobian.shape[1]))
+        at += 1
 
 
 def network(
@@ -106,8 +106,7 @@
 ):
     per_dev, neighbours, atoms = neighbor_ids.shape
     hin, width = layer_weight.shape
-    blocks = len(plan)
-    rows = pl.cdiv(sum(size for _, size in plan[0]) + 1, SUBLANES) * SUBLANES
+    rows = sum(1 + sum(size for _, size in pieces) for pieces in plan)
 
     def per_stream(*shape):
         return pl.BlockSpec((None,) + shape, lambda s: (s,) + (0,) * len(shape))
@@ -129,8 +128,8 @@
             shared(layer_weight.shape),
             shared((1, width)),
         ],
-        out_specs=pl.BlockSpec((blocks, None, rows, width), lambda s: (0, s, 0, 0)),
-        out_shape=jax.ShapeDtypeStruct((blocks, per_dev, rows, width), f32),
+        out_specs=per_stream(rows, width),
+        out_shape=jax.ShapeDtypeStruct((per_dev, rows, width), f32),
         scratch_shapes=[pltpu.VMEM((atoms, atoms), f32)],
         name="network",
     )(
@@ -207,9 +206,9 @@
     sems,
     tail_sem,
 ):
-    streams, rows, lanes = jac_ref.shape
     head, tile_cols = hi_head_ref.shape
-    slabs, _, slab = out_ref.shape
+    slabs, streams, slab = out_ref.shape
+    rows, lanes = jac_ref.shape[0] // streams, jac_ref.shape[1]
     chunks = sems.shape[0]
     copies = []
     for n in range(chunks):
@@ -225,8 +224,7 @@
     tail = tail_ref.shape[0]
     last = pltpu.make_async_copy(cov_ref.at[pl.ds(cov_ref.shape[0] - tail, tail)], tail_ref, tail_sem)
     last.start()
-    flat = jac_ref.reshape(streams * rows, lanes)
-    stacked_parts(flat, 0, parts_ref.shape[1] // lanes, streams, rows, parts_ref)
+    stacked_parts(jac_ref, 0, parts_ref.shape[1] // lanes, streams, rows, parts_ref)
     sums_ref[...] = five_products(parts_ref[:, 0:head], hi_head_ref[...], lo_head_ref[...], ((1,), (0,)))
     for n in range(chunks):
         for copy in copies[n]:
@@ -243,8 +241,7 @@
         out_ref[n] = sums_ref[:, n * slab : (n + 1) * slab]
 
 
-def col_partial(jac, hi_head, lo_head, hi, lo, covariance, slab):
-    streams = jac.shape[0]
+def col_partial(jac, streams, hi_head, lo_head, hi, lo, covariance, slab):
     rest, tile_cols = hi.shape
     head = hi_head.shape[0]
     tail = covariance.shape[0] - head - rest
@@ -283,21 +280,20 @@
 
 
 def slab_kernel(pieces_ref, jac_ref, own_ref, out_ref, error_ref, *, first):
-    streams, rows, lanes = jac_ref.shape
-    slab = own_ref.shape[1]
+    streams, slab = own_ref.shape
+    rows, lanes = jac_ref.shape[0] // streams, jac_ref.shape[1]
     total = pieces_ref[0]
     for n in range(1, pieces_ref.shape[0]):
         total = total + pieces_ref[n]
     own_ref[...] = total
-    flat = jac_ref.reshape(streams * rows, lanes)
     term = jnp.zeros((streams, streams), f32)
     for i in range(slab // lanes):
-        own = flat[pl.ds(first + i, streams, stride=rows), :]
+        own = jac_ref[pl.ds(first + i, streams, stride=rows), :]
         here = total[:, i * lanes : (i + 1) * lanes]
         term = term + dot(own, here, ((1,), (1,)), highest)
         out_ref[i * streams : (i + 1) * streams, :] = here
     out_ref[slab // lanes * streams :, :] = packed(term)
-    error_ref[...] = flat[pl.ds(first + slab // lanes, streams, stride=rows), :]
+    error_ref[...] = jac_ref[pl.ds(first + slab // lanes, streams, stride=rows), :]
 
 
 def slab_sum(pieces, jac, first):
@@ -524,16 +520,16 @@
         and streams * streams % (SUBLANES * LANES) == 0
     )
     if not kernels:
-        payload = run_network([[(0, hin)]])[0]
+        payload = run_network([[(0, hin)]])
         jac_all = lax.all_gather(payload, ("row", "col"), axis=0, tiled=True)
         return plain_steps(at, jac_all[:, 0:hin], jac_all[:, hin, 0], layer_weight, covariance, slab, cols_n)
     row_size, slab_size = tile_rows // LANES, slab // LANES
     devices = [(r, c) for r in range(rows_n) for c in range(cols_n)]
     plan = [[(r * row_size, row_size), ((c * rows_n + r) * slab_size, slab_size)] for r, c in devices]
-    jac = exchange(run_network(plan), ("row", "col"))
-    jac = jac.reshape(-1, *jac.shape[2:])
+    payload = run_network(plan).reshape(streams, 1, -1)
+    jac = exchange(payload, ("row", "col")).reshape(-1, width)
     hi, lo, hi_head, lo_head = stage(covariance, tile_rows // 4, tile_rows // 4)
-    col_part = col_partial(jac, hi_head, lo_head, hi, lo, covariance, slab)
+    col_part = col_partial(jac, streams, hi_head, lo_head, hi, lo, covariance, slab)
     pieces = exchange(col_part, "row")
     head = read_head(covariance, col_part)
     col_own, with_term, errors = slab_sum(pieces, jac, row_size)

time: 64.8 us -> 64.2 us (level)
  waiting for transfers between devices: 8.91 us -> 7.82 us
    all_to_all x2, waiting for transfers between devices: 8.91 us -> 7.81 us  [exchange(): return lax.all_to_all(x, axes, split_axis=0, concat_axis=0, tiled=True)]
where the time goes in v15:
time: 64.2 us; the launch traced here: 63.7 us
  Pallas kernels  22.1 us (34%)
  blocking collectives  21.2 us (33%)
  starting transfers between devices  11.3 us (18%)
  waiting for transfers between devices  7.82 us (12%)
  between operations  1.33 us (2%)
    all_gather x1, blocking collectives, on_device(): col_slabs = lax.all_gather(with_term, 'row', axis=0, tiled=False)  11.8 us
    all_to_all x2, starting transfers between devices, exchange(): return lax.all_to_all(x, axes, split_axis=0, concat_axis=0, tiled=True)  10.6 us
    all_to_all x1, blocking collectives, exchange(): return lax.all_to_all(x, axes, split_axis=0, concat_axis=0, tiled=True)  9.35 us
    all_to_all x2, waiting for transfers between devices, exchange(): return lax.all_to_all(x, axes, split_axis=0, concat_axis=0, tiled=True)  7.81 us
    pallas_call x1, Pallas kernels, stage(): pl.pallas_call(functools.partial(stage_kernel, head_steps=head_steps), gr...  6.44 us
    pallas_call x1, Pallas kernels, update(): pl.pallas_call(update_kernel, in_specs=[whole] * 5 + [beyond], out_specs=...  5.86 us
    pallas_call x1, Pallas kernels, col_partial(): pl.pallas_call(col_kernel, in_specs=[whole] * 3 + [beyond] * 3, out_specs...  3.76 us
    pallas_call x1, Pallas kernels, network(): pl.pallas_call(functools.partial(network_kernel, plan=plan), grid=(per_de...  3.51 us
  transfers between devices with their start and end apart: 3, of which 2 were waited for; matrix products, arithmetic and copies ran while one was open for 0% of the time, Pallas kernels for 13%

profile of v15, /device:TPU:0, one launch (start us, length us, event | category | flops | bytes accessed | tf_op | source)
XLA Modules:
  0.0 63.7 jit_solution(11380883453273871808)
XLA Ops:
  1.3 3.5 %network.1 = f32[1,352,128]{2,1,0:T(8,128)} custom-call(s32[1,1,256]{2,1,0:T(1,128)} %bitcast.16, s32[1,32,256]{2,1,0:T(8,128)} %ids_ref.1, f32[1,32,256]{2,1,0:T(8,128)} %switch_ref.1, f32[1,64,256]{2,1,0:T(8,128)} %bitcast.15, f32[1,1,256]{2,1,0:T(1,128)} %bitcast.17, f32[1,1,1]{2,1,0:T(1,128)} %bitcast.9.target_ref, f32[4,64]{1,0:T(4,128)} %embed_ref.1, ...), custom_call_target="tpu_custom_call" | custom-call | tf_op jit(solution)/shard_map/network/pallas_call | solution.py:117
  4.8 7.3 %all-to-all-start = ((f32[32,1,1408]{2,1,0:T(1,128)}), f32[32,1,1408]{2,1,0:T(1,128)S(1)}, u32[]{:S(2)}, u32[]{:S(2)}) async-start(f32[32,1,1408]{2,1,0:T(1,128)} %bitcast.14), calls=%async_computation | async-start | bytes 360448 | tf_op jit(solution)/shard_map/all_to_all | solution.py:478
  12.1 6.4 %stage.1 = (bf16[512,2048]{1,0:T(8,128)(2,1)}, bf16[512,2048]{1,0:T(8,128)(2,1)}, bf16[256,2048]{1,0:T(8,128)(2,1)S(1)}, bf16[256,2048]{1,0:T(8,128)(2,1)S(1)}) custom-call(f32[1024,2048]{1,0:T(8,128)} %cov_ref.7), custom_call_target="tpu_custom_call" | custom-call | tf_op jit(solution)/shard_map/stage/pallas_call | solution.py:174
  18.5 2.7 %all-to-all-done = f32[32,1,1408]{2,1,0:T(1,128)S(1)} async-done(((f32[32,1,1408]{2,1,0:T(1,128)}), f32[32,1,1408]{2,1,0:T(1,128)S(1)}, u32[]{:S(2)}, u32[]{:S(2)}) %all-to-all-start) | async-done | bytes 180256 | tf_op jit(solution)/shard_map/all_to_all | solution.py:478
  21.2 3.8 %col_cross.1._ = f32[8,32,256]{2,1,0:T(8,128)S(1)} custom-call(f32[352,128]{1,0:T(8,128)S(1)} %bitcast.12, bf16[256,2048]{1,0:T(8,128)(2,1)S(1)} %get-tuple-element.11.hi_head_ref, bf16[256,2048]{1,0:T(8,128)(2,1)S(1)} %get-tuple-element.12.lo_head_ref, bf16[512,2048]{1,0:T(8,128)(2,1)} %get-tuple-element.13.hi_ref, ...), custom_call_target="tpu_custom_call" | custom-call | tf_op jit(solution)/shard_map/col_cross/pallas_call | solution.py:250
  25.0 9.3 %all_to_all.15.pieces_ref = f32[8,32,256]{2,1,0:T(8,128)S(1)} all-to-all(f32[8,32,256]{2,1,0:T(8,128)S(1)} %col_cross.1._), channel_id=1, replica_groups=mesh['row'=8,'col'=4] {'row'}, dimensions={0} | all-to-all | bytes 524288 | tf_op jit(solution)/shard_map/all_to_all | solution.py:478
  34.3 0.2 slab.1
  34.5 0.7 %collective-permute-start = (f32[32,256]{1,0:T(8,128)S(1)}, f32[32,256]{1,0:T(8,128)S(1)}, u32[]{:S(2)}, u32[]{:S(2)}) collective-permute-start(f32[32,256]{1,0:T(8,128)S(1)} %get-tuple-element.15), channel_id=1, source_target_pairs={{0,0},{1,8},{2,16},{3,24},{4,1},{5,9},{6,17},{7,25},{8,2},{9,10},{... | collective-permute-start | bytes 98312 | tf_op jit(solution)/shard_map/ppermute | solution.py:537
  35.2 11.8 %all-gather = f32[576,128]{1,0:T(8,128)S(1)} all-gather(f32[72,128]{1,0:T(8,128)S(1)} %get-tuple-element.16), channel_id=2, replica_groups=mesh['row'=8,'col'=4] {'row'}, dimensions={0}, use_global_device_ids=true | all-gather | bytes 331776 | tf_op jit(solution)/shard_map/all_gather | solution.py:538
  47.0 0.0 collective-permute-done.own_ref
  47.0 0.7 %term.1 = f32[4,72,128]{2,1,0:T(8,128)} custom-call(f32[32,256]{1,0:T(8,128)S(1)} %collective-permute-done.own_ref, f32[8,72,128]{2,1,0:T(8,128)S(1)} %bitcast.10), custom_call_target="tpu_custom_call" | custom-call | tf_op jit(solution)/shard_map/term/pallas_call | solution.py:327
  47.7 3.3 %all-to-all-start.2 = ((f32[4,72,128]{2,1,0:T(8,128)}), f32[4,72,128]{2,1,0:T(8,128)S(1)}, u32[]{:S(2)}, u32[]{:S(2)}) async-start(f32[4,72,128]{2,1,0:T(8,128)} %term.1), calls=%async_computation.2 | async-start | bytes 294912 | tf_op jit(solution)/shard_map/all_to_all | solution.py:478
  51.1 0.0 copy-start
  51.1 1.6 %head.1.head_ref = f32[256,2048]{1,0:T(8,128)S(1)} custom-call(f32[1024,2048]{1,0:T(8,128)} %cov_ref.7, f32[8,32,256]{2,1,0:T(8,128)S(1)} %col_cross.1._), custom_call_target="tpu_custom_call" | custom-call | tf_op jit(solution)/shard_map/head/pallas_call | solution.py:360
  52.7 5.2 %all-to-all-done.2.rows_ref = f32[4,72,128]{2,1,0:T(8,128)S(1)} async-done(((f32[4,72,128]{2,1,0:T(8,128)}), f32[4,72,128]{2,1,0:T(8,128)S(1)}, u32[]{:S(2)}, u32[]{:S(2)}) %all-to-all-start.2) | async-done | bytes 147488 | tf_op jit(solution)/shard_map/all_to_all | solution.py:478
  57.8 0.0 copy-done
  57.8 5.9 %update.1 = (f32[2,128]{1,0:T(2,128)}, f32[1024,2048]{1,0:T(8,128)}) custom-call(f32[4,72,128]{2,1,0:T(8,128)S(1)} %all-to-all-done.2.rows_ref, f32[8,72,128]{2,1,0:T(8,128)S(1)} %bitcast.11, f32[32,128]{1,0:T(8,128)S(1)} %get-tuple-element.17.error_ref, f32[64,128]{1,0:T(8,128)S(1)} %copy-done, f32[256,2048]{1,0:T(8,128)S(1)} %head.1.head_ref, ...), custom_call_target="tpu_custom_call" | custom-call | tf_op jit(solution)/shard_map/update/pallas_call | solution.py:437
Async XLA Ops:
  4.8 16.4 %all-to-all-start = ((f32[32,1,1408]{2,1,0:T(1,128)}), f32[32,1,1408]{2,1,0:T(1,128)S(1)}, u32[]{:S(2)}, u32[]{:S(2)}) async-start(f32[32,1,1408]{2,1,0:T(1,128)} %bitcast.14), calls=%async_computation | async-start | bytes 360448 | tf_op jit(solution)/shard_map/all_to_all | solution.py:478
  34.5 12.5 %collective-permute-start = (f32[32,256]{1,0:T(8,128)S(1)}, f32[32,256]{1,0:T(8,128)S(1)}, u32[]{:S(2)}, u32[]{:S(2)}) collective-permute-start(f32[32,256]{1,0:T(8,128)S(1)} %get-tuple-element.15), channel_id=1, source_target_pairs={{0,0},{1,8},{2,16},{3,24},{4,1},{5,9},{6,17},{7,25},{8,2},{9,10},{... | collective-permute-start | bytes 98312 | tf_op jit(solution)/shard_map/ppermute | solution.py:537
  47.7 10.1 %all-to-all-start.2 = ((f32[4,72,128]{2,1,0:T(8,128)}), f32[4,72,128]{2,1,0:T(8,128)S(1)}, u32[]{:S(2)}, u32[]{:S(2)}) async-start(f32[4,72,128]{2,1,0:T(8,128)} %term.1), calls=%async_computation.2 | async-start | bytes 294912 | tf_op jit(solution)/shard_map/all_to_all | solution.py:478
  51.1 6.8 %copy-start = (f32[64,128]{1,0:T(8,128)S(1)}, f32[64,128]{1,0:T(8,128)}, u32[]{:S(2)}) copy-start(f32[64,128]{1,0:T(8,128)} %weight_ref.3) | copy-start | bytes 98308

commit v16 on v15

--- a/solution.py
+++ b/solution.py
@@ -204,7 +204,7 @@
     tail_ref,
     sums_ref,
     sems,
-    tail_sem,
+    tail_sems,
 ):
     head, tile_cols = hi_head_ref.shape
     slabs, streams, slab = out_ref.shape
@@ -222,8 +222,12 @@
         for copy in copies[-1]:
             copy.start()
     tail = tail_ref.shape[0]
-    last = pltpu.make_async_copy(cov_ref.at[pl.ds(cov_ref.shape[0] - tail, tail)], tail_ref, tail_sem)
-    last.start()
+    first = cov_ref.shape[0] - tail
+    last = []
+    for n in range(tail // head):
+        source, target = pl.ds(first + n * head, head), pl.ds(n * head, head)
+        last.append(pltpu.make_async_copy(cov_ref.at[source], tail_ref.at[target], tail_sems.at[n]))
+        last[-1].start()
     stacked_parts(jac_ref, 0, parts_ref.shape[1] // lanes, streams, rows, parts_ref)
     sums_ref[...] = five_products(parts_ref[:, 0:head], hi_head_ref[...], lo_head_ref[...], ((1,), (0,)))
     for n in range(chunks):
@@ -233,10 +237,11 @@
         sums_ref[...] += five_products(
             parts_ref[:, (n + 1) * head : (n + 2) * head], hi_rest_ref[here, :], lo_rest_ref[here, :], ((1,), (0,))
         )
-    last.wait()
-    sums_ref[...] += five_products(
-        parts_ref[:, parts_ref.shape[1] - tail :], *split2(tail_ref[...]), ((1,), (0,))
-    )
+    for n in range(tail // head):
+        last[n].wait()
+        hi, lo = split2(tail_ref[n * head : (n + 1) * head, :])
+        parts = parts_ref[:, first + n * head : first + (n + 1) * head]
+        sums_ref[...] += five_products(parts, hi, lo, ((1,), (0,)))
     for n in range(slabs):
         out_ref[n] = sums_ref[:, n * slab : (n + 1) * slab]
 
@@ -259,9 +264,9 @@
             pltpu.VMEM((tail, tile_cols), f32),
             pltpu.VMEM((streams, tile_cols), f32),
             pltpu.SemaphoreType.DMA((rest // head, 2)),
-            pltpu.SemaphoreType.DMA,
+            pltpu.SemaphoreType.DMA((tail // head,)),
         ],
-        compiler_params=limit(16),
+        compiler_params=limit(20),
         name="col_cross",
     )(jac, in_vmem(hi_head), in_vmem(lo_head), in_hbm(hi), in_hbm(lo), in_hbm(covariance))
 
@@ -528,7 +533,7 @@
     plan = [[(r * row_size, row_size), ((c * rows_n + r) * slab_size, slab_size)] for r, c in devices]
     payload = run_network(plan).reshape(streams, 1, -1)
     jac = exchange(payload, ("row", "col")).reshape(-1, width)
-    hi, lo, hi_head, lo_head = stage(covariance, tile_rows // 4, tile_rows // 4)
+    hi, lo, hi_head, lo_head = stage(covariance, tile_rows // 4, tile_rows // 2)
     col_part = col_partial(jac, streams, hi_head, lo_head, hi, lo, covariance, slab)
     pieces = exchange(col_part, "row")
     head = read_head(covariance, col_part)

time: 64.2 us -> 63.7 us (level)
  Pallas kernels: 22.1 us -> 19.6 us
  waiting for transfers between devices: 7.82 us -> 10 us
    all_to_all x2, waiting for transfers between devices: 7.81 us -> 10 us  [exchange(): return lax.all_to_all(x, axes, split_axis=0, concat_axis=0, tiled=True)]
    pallas_call x1, Pallas kernels: 6.44 us -> 4.26 us  [stage(): pl.pallas_call(functools.partial(stage_kernel, head_steps=head_steps), gr...]
  transfers between devices with their start and end apart: 3 -> 3, of which waited for: 2 -> 2; matrix products, arithmetic and copies ran while one was open for 0% -> 0% of each run, Pallas kernels for 13% -> 9%
where the time goes in v16:
time: 63.7 us; the launch traced here: 63.1 us
  blocking collectives  20.9 us (33%)
  Pallas kernels  19.6 us (31%)
  starting transfers between devices  11.3 us (18%)
  waiting for transfers between devices  10 us (16%)
  between operations  1.33 us (2%)
    all_gather x1, blocking collectives, on_device(): col_slabs = lax.all_gather(with_term, 'row', axis=0, tiled=False)  11.5 us
    all_to_all x2, starting transfers between devices, exchange(): return lax.all_to_all(x, axes, split_axis=0, concat_axis=0, tiled=True)  10.6 us
    all_to_all x2, waiting for transfers between devices, exchange(): return lax.all_to_all(x, axes, split_axis=0, concat_axis=0, tiled=True)  10 us
    all_to_all x1, blocking collectives, exchange(): return lax.all_to_all(x, axes, split_axis=0, concat_axis=0, tiled=True)  9.35 us
    pallas_call x1, Pallas kernels, update(): pl.pallas_call(update_kernel, in_specs=[whole] * 5 + [beyond], out_specs=...  5.86 us
    pallas_call x1, Pallas kernels, stage(): pl.pallas_call(functools.partial(stage_kernel, head_steps=head_steps), gr...  4.26 us
    pallas_call x1, Pallas kernels, network(): pl.pallas_call(functools.partial(network_kernel, plan=plan), grid=(per_de...  3.5 us
    pallas_call x1, Pallas kernels, col_partial(): pl.pallas_call(col_kernel, in_specs=[whole] * 3 + [beyond] * 3, out_specs...  3.49 us
  transfers between devices with their start and end apart: 3, of which 2 were waited for; matrix products, arithmetic and copies ran while one was open for 0% of the time, Pallas kernels for 9%

profile of v16, /device:TPU:0, one launch (start us, length us, event | category | flops | bytes accessed | tf_op | source)
XLA Modules:
  0.0 63.1 jit_solution(7206880048709351951)
XLA Ops:
  1.3 3.5 %network.1 = f32[1,352,128]{2,1,0:T(8,128)} custom-call(s32[1,1,256]{2,1,0:T(1,128)} %bitcast.16, s32[1,32,256]{2,1,0:T(8,128)} %ids_ref.1, f32[1,32,256]{2,1,0:T(8,128)} %switch_ref.1, f32[1,64,256]{2,1,0:T(8,128)} %bitcast.15, f32[1,1,256]{2,1,0:T(1,128)} %bitcast.17, f32[1,1,1]{2,1,0:T(1,128)} %bitcast.9.target_ref, f32[4,64]{1,0:T(4,128)} %embed_ref.1, ...), custom_call_target="tpu_custom_call" | custom-call | tf_op jit(solution)/shard_map/network/pallas_call | solution.py:117
  4.8 7.3 %all-to-all-start = ((f32[32,1,1408]{2,1,0:T(1,128)}), f32[32,1,1408]{2,1,0:T(1,128)S(1)}, u32[]{:S(2)}, u32[]{:S(2)}) async-start(f32[32,1,1408]{2,1,0:T(1,128)} %bitcast.14), calls=%async_computation | async-start | bytes 360448 | tf_op jit(solution)/shard_map/all_to_all | solution.py:483
  12.1 4.3 %stage.1 = (bf16[256,2048]{1,0:T(8,128)(2,1)}, bf16[256,2048]{1,0:T(8,128)(2,1)}, bf16[256,2048]{1,0:T(8,128)(2,1)S(1)}, bf16[256,2048]{1,0:T(8,128)(2,1)S(1)}) custom-call(f32[1024,2048]{1,0:T(8,128)} %cov_ref.7), custom_call_target="tpu_custom_call" | custom-call | tf_op jit(solution)/shard_map/stage/pallas_call | solution.py:174
  16.3 4.8 %all-to-all-done = f32[32,1,1408]{2,1,0:T(1,128)S(1)} async-done(((f32[32,1,1408]{2,1,0:T(1,128)}), f32[32,1,1408]{2,1,0:T(1,128)S(1)}, u32[]{:S(2)}, u32[]{:S(2)}) %all-to-all-start) | async-done | bytes 180256 | tf_op jit(solution)/shard_map/all_to_all | solution.py:483
  21.2 3.5 %col_cross.1._ = f32[8,32,256]{2,1,0:T(8,128)S(1)} custom-call(f32[352,128]{1,0:T(8,128)S(1)} %bitcast.12, bf16[256,2048]{1,0:T(8,128)(2,1)S(1)} %get-tuple-element.11.hi_head_ref, bf16[256,2048]{1,0:T(8,128)(2,1)S(1)} %get-tuple-element.12.lo_head_ref, bf16[256,2048]{1,0:T(8,128)(2,1)} %get-tuple-element.13.hi_ref, ...), custom_call_target="tpu_custom_call" | custom-call | tf_op jit(solution)/shard_map/col_cross/pallas_call | solution.py:255
  24.7 0.0 copy-start
  24.7 9.3 %all_to_all.15.pieces_ref = f32[8,32,256]{2,1,0:T(8,128)S(1)} all-to-all(f32[8,32,256]{2,1,0:T(8,128)S(1)} %col_cross.1._), channel_id=1, replica_groups=mesh['row'=8,'col'=4] {'row'}, dimensions={0} | all-to-all | bytes 524288 | tf_op jit(solution)/shard_map/all_to_all | solution.py:483
  34.0 0.2 slab.1
  34.3 0.7 %collective-permute-start = (f32[32,256]{1,0:T(8,128)S(1)}, f32[32,256]{1,0:T(8,128)S(1)}, u32[]{:S(2)}, u32[]{:S(2)}) collective-permute-start(f32[32,256]{1,0:T(8,128)S(1)} %get-tuple-element.15), channel_id=1, source_target_pairs={{0,0},{1,8},{2,16},{3,24},{4,1},{5,9},{6,17},{7,25},{8,2},{9,10},{... | collective-permute-start | bytes 98312 | tf_op jit(solution)/shard_map/ppermute | solution.py:542
  35.0 11.5 %all-gather = f32[576,128]{1,0:T(8,128)S(1)} all-gather(f32[72,128]{1,0:T(8,128)S(1)} %get-tuple-element.16), channel_id=2, replica_groups=mesh['row'=8,'col'=4] {'row'}, dimensions={0}, use_global_device_ids=true | all-gather | bytes 331776 | tf_op jit(solution)/shard_map/all_gather | solution.py:543
  46.5 0.0 collective-permute-done.own_ref
  46.5 0.7 %term.1 = f32[4,72,128]{2,1,0:T(8,128)} custom-call(f32[32,256]{1,0:T(8,128)S(1)} %collective-permute-done.own_ref, f32[8,72,128]{2,1,0:T(8,128)S(1)} %bitcast.10), custom_call_target="tpu_custom_call" | custom-call | tf_op jit(solution)/shard_map/term/pallas_call | solution.py:332
  47.1 3.3 %all-to-all-start.2 = ((f32[4,72,128]{2,1,0:T(8,128)}), f32[4,72,128]{2,1,0:T(8,128)S(1)}, u32[]{:S(2)}, u32[]{:S(2)}) async-start(f32[4,72,128]{2,1,0:T(8,128)} %term.1), calls=%async_computation.2 | async-start | bytes 294912 | tf_op jit(solution)/shard_map/all_to_all | solution.py:483
  50.5 1.6 %head.1.head_ref = f32[256,2048]{1,0:T(8,128)S(1)} custom-call(f32[1024,2048]{1,0:T(8,128)} %cov_ref.7, f32[8,32,256]{2,1,0:T(8,128)S(1)} %col_cross.1._), custom_call_target="tpu_custom_call" | custom-call | tf_op jit(solution)/shard_map/head/pallas_call | solution.py:365
  52.1 5.2 %all-to-all-done.2.rows_ref = f32[4,72,128]{2,1,0:T(8,128)S(1)} async-done(((f32[4,72,128]{2,1,0:T(8,128)}), f32[4,72,128]{2,1,0:T(8,128)S(1)}, u32[]{:S(2)}, u32[]{:S(2)}) %all-to-all-start.2) | async-done | bytes 147488 | tf_op jit(solution)/shard_map/all_to_all | solution.py:483
  57.3 0.0 copy-done
  57.3 5.9 %update.1 = (f32[2,128]{1,0:T(2,128)}, f32[1024,2048]{1,0:T(8,128)}) custom-call(f32[4,72,128]{2,1,0:T(8,128)S(1)} %all-to-all-done.2.rows_ref, f32[8,72,128]{2,1,0:T(8,128)S(1)} %bitcast.11, f32[32,128]{1,0:T(8,128)S(1)} %get-tuple-element.17.error_ref, f32[64,128]{1,0:T(8,128)S(1)} %copy-done, f32[256,2048]{1,0:T(8,128)S(1)} %head.1.head_ref, ...), custom_call_target="tpu_custom_call" | custom-call | tf_op jit(solution)/shard_map/update/pallas_call | solution.py:442
Async XLA Ops:
  4.8 16.4 %all-to-all-start = ((f32[32,1,1408]{2,1,0:T(1,128)}), f32[32,1,1408]{2,1,0:T(1,128)S(1)}, u32[]{:S(2)}, u32[]{:S(2)}) async-start(f32[32,1,1408]{2,1,0:T(1,128)} %bitcast.14), calls=%async_computation | async-start | bytes 360448 | tf_op jit(solution)/shard_map/all_to_all | solution.py:483
  24.7 32.6 %copy-start = (f32[64,128]{1,0:T(8,128)S(1)}, f32[64,128]{1,0:T(8,128)}, u32[]{:S(2)}) copy-start(f32[64,128]{1,0:T(8,128)} %weight_ref.3) | copy-start | bytes 98308
  34.3 12.2 %collective-permute-start = (f32[32,256]{1,0:T(8,128)S(1)}, f32[32,256]{1,0:T(8,128)S(1)}, u32[]{:S(2)}, u32[]{:S(2)}) collective-permute-start(f32[32,256]{1,0:T(8,128)S(1)} %get-tuple-element.15), channel_id=1, source_target_pairs={{0,0},{1,8},{2,16},{3,24},{4,1},{5,9},{6,17},{7,25},{8,2},{9,10},{... | collective-permute-start | bytes 98312 | tf_op jit(solution)/shard_map/ppermute | solution.py:542
  47.1 10.1 %all-to-all-start.2 = ((f32[4,72,128]{2,1,0:T(8,128)}), f32[4,72,128]{2,1,0:T(8,128)S(1)}, u32[]{:S(2)}, u32[]{:S(2)}) async-start(f32[4,72,128]{2,1,0:T(8,128)} %term.1), calls=%async_computation.2 | async-start | bytes 294912 | tf_op jit(solution)/shard_map/all_to_all | solution.py:483

commit v17 on v16

--- a/solution.py
+++ b/solution.py
@@ -82,7 +82,11 @@
     parts = jnp.concatenate(split3(mixed), axis=0)
     descriptor = five_products(parts, *split2(mix), ((1,), (0,))) * (1.0 / math.sqrt(neighbours))
     hidden = jnp.tanh(descriptor)
-    activity = jnp.tanh(dot(hidden, weight_ref[...], ((0,), (0,)), highest))
+    hidden_hi, hidden_lo = split2(hidden)
+    weight_hi, weight_lo = split2(weight_ref[...])
+    left = jnp.concatenate([hidden_hi, hidden_hi, hidden_lo, hidden_lo], axis=0)
+    right = jnp.concatenate([weight_hi, weight_lo, weight_hi, weight_lo], axis=0)
+    activity = jnp.tanh(dot(left, right, ((0,), (0,))))
     out_weight = out_weight_ref[...]
     scale = 1.0 / math.sqrt(atoms)
     force = force_ref[...]
@@ -284,7 +288,7 @@
     )
 
 
-def slab_kernel(pieces_ref, jac_ref, own_ref, out_ref, error_ref, *, first):
+def slab_kernel(pieces_ref, jac_ref, _, own_ref, out_ref, error_ref, *, first):
     streams, slab = own_ref.shape
     rows, lanes = jac_ref.shape[0] // streams, jac_ref.shape[1]
     total = pieces_ref[0]
@@ -301,10 +305,11 @@
     error_ref[...] = jac_ref[pl.ds(first + slab // lanes, streams, stride=rows), :]
 
 
-def slab_sum(pieces, jac, first):
+def slab_sum(pieces, jac, after, first):
     _, streams, slab = pieces.shape
     return pl.pallas_call(
         functools.partial(slab_kernel, first=first),
+        in_specs=[pl.BlockSpec(memory_space=pltpu.VMEM)] * 2 + [pl.BlockSpec(memory_space=pl.ANY)],
         out_shape=[
             jax.ShapeDtypeStruct((streams, slab), f32),
             jax.ShapeDtypeStruct((streams * (slab + streams) // LANES, LANES), f32),
@@ -312,7 +317,7 @@
         ],
         compiler_params=limit(8),
         name="slab",
-    )(pieces, jac)
+    )(pieces, jac, in_vmem(after))
 
 
 def term_kernel(own_ref, cols_ref, out_ref):
@@ -537,7 +542,7 @@
     col_part = col_partial(jac, streams, hi_head, lo_head, hi, lo, covariance, slab)
     pieces = exchange(col_part, "row")
     head = read_head(covariance, col_part)
-    col_own, with_term, errors = slab_sum(pieces, jac, row_size)
+    col_own, with_term, errors = slab_sum(pieces, jac, head, row_size)
     to_row = [(r * cols_n + c, c * rows_n + r) for r, c in devices]
     row_own = lax.ppermute(col_own, ("row", "col"), to_row)
     col_slabs = lax.all_gather(with_term, "row", axis=0, tiled=False)

time: 63.7 us -> 64 us (level)
    pallas_call x1, Pallas kernels: 3.49 us -> 4.23 us  [col_partial(): pl.pallas_call(col_kernel, in_specs=[whole] * 3 + [beyond] * 3, out_specs...]
    pallas_call x1, Pallas kernels: 0.68 us -> 0.01 us  [with_terms(): pl.pallas_call(term_kernel, out_shape=jax.ShapeDtypeStruct((copies,) + co...]
where the time goes in v17:
time: 64 us; the launch traced here: 63.5 us
  blocking collectives  21.1 us (33%)
  Pallas kernels  19.5 us (30%)
  starting transfers between devices  11.4 us (18%)
  waiting for transfers between devices  10.1 us (16%)
  between operations  1.33 us (2%)
    all_gather x1, blocking collectives, on_device(): col_slabs = lax.all_gather(with_term, 'row', axis=0, tiled=False)  11.6 us
    all_to_all x2, starting transfers between devices, exchange(): return lax.all_to_all(x, axes, split_axis=0, concat_axis=0, tiled=True)  10.7 us
    all_to_all x2, waiting for transfers between devices, exchange(): return lax.all_to_all(x, axes, split_axis=0, concat_axis=0, tiled=True)  10.1 us
    all_to_all x1, blocking collectives, exchange(): return lax.all_to_all(x, axes, split_axis=0, concat_axis=0, tiled=True)  9.58 us
    pallas_call x1, Pallas kernels, update(): pl.pallas_call(update_kernel, in_specs=[whole] * 5 + [beyond], out_specs=...  5.86 us
    pallas_call x1, Pallas kernels, stage(): pl.pallas_call(functools.partial(stage_kernel, head_steps=head_steps), gr...  4.26 us
    pallas_call x1, Pallas kernels, col_partial(): pl.pallas_call(col_kernel, in_specs=[whole] * 3 + [beyond] * 3, out_specs...  4.23 us
    pallas_call x1, Pallas kernels, network(): pl.pallas_call(functools.partial(network_kernel, plan=plan), grid=(per_de...  3.33 us
  transfers between devices with their start and end apart: 3, of which 2 were waited for; matrix products, arithmetic and copies ran while one was open for 0% of the time, Pallas kernels for 9%

profile of v17, /device:TPU:0, one launch (start us, length us, event | category | flops | bytes accessed | tf_op | source)
XLA Modules:
  0.0 63.5 jit_solution(324407728472247242)
XLA Ops:
  1.3 3.3 %network.1 = f32[1,352,128]{2,1,0:T(8,128)} custom-call(s32[1,1,256]{2,1,0:T(1,128)} %bitcast.16, s32[1,32,256]{2,1,0:T(8,128)} %ids_ref.1, f32[1,32,256]{2,1,0:T(8,128)} %switch_ref.1, f32[1,64,256]{2,1,0:T(8,128)} %bitcast.15, f32[1,1,256]{2,1,0:T(1,128)} %bitcast.17, f32[1,1,1]{2,1,0:T(1,128)} %bitcast.9.target_ref, f32[4,64]{1,0:T(4,128)} %embed_ref.1, ...), custom_call_target="tpu_custom_call" | custom-call | tf_op jit(solution)/shard_map/network/pallas_call | solution.py:121
  4.6 7.3 %all-to-all-start = ((f32[32,1,1408]{2,1,0:T(1,128)}), f32[32,1,1408]{2,1,0:T(1,128)S(1)}, u32[]{:S(2)}, u32[]{:S(2)}) async-start(f32[32,1,1408]{2,1,0:T(1,128)} %bitcast.14), calls=%async_computation | async-start | bytes 360448 | tf_op jit(solution)/shard_map/all_to_all | solution.py:488
  11.9 4.3 %stage.1 = (bf16[256,2048]{1,0:T(8,128)(2,1)}, bf16[256,2048]{1,0:T(8,128)(2,1)}, bf16[256,2048]{1,0:T(8,128)(2,1)S(1)}, bf16[256,2048]{1,0:T(8,128)(2,1)S(1)}) custom-call(f32[1024,2048]{1,0:T(8,128)} %cov_ref.7), custom_call_target="tpu_custom_call" | custom-call | tf_op jit(solution)/shard_map/stage/pallas_call | solution.py:178
  16.2 4.8 %all-to-all-done = f32[32,1,1408]{2,1,0:T(1,128)S(1)} async-done(((f32[32,1,1408]{2,1,0:T(1,128)}), f32[32,1,1408]{2,1,0:T(1,128)S(1)}, u32[]{:S(2)}, u32[]{:S(2)}) %all-to-all-start) | async-done | bytes 180256 | tf_op jit(solution)/shard_map/all_to_all | solution.py:488
  21.0 4.2 %col_cross.1._ = f32[8,32,256]{2,1,0:T(8,128)} custom-call(f32[352,128]{1,0:T(8,128)S(1)} %bitcast.12, bf16[256,2048]{1,0:T(8,128)(2,1)S(1)} %get-tuple-element.11.hi_head_ref, bf16[256,2048]{1,0:T(8,128)(2,1)S(1)} %get-tuple-element.12.lo_head_ref, bf16[256,2048]{1,0:T(8,128)(2,1)} %get-tuple-element.13.hi_ref, bf16[256,2048]{1,0:T(8,128)(2,1)} %get-tuple-element.14.lo_ref, ...), custom_call_target="tpu_custom_call" | custom-call | tf_op jit(solution)/shard_map/col_cross/pallas_call | solution.py:259
  25.3 0.0 copy-start
  25.3 3.4 %all-to-all-start.1 = ((f32[8,32,256]{2,1,0:T(8,128)}), f32[8,32,256]{2,1,0:T(8,128)S(1)}, u32[]{:S(2)}, u32[]{:S(2)}) async-start(f32[8,32,256]{2,1,0:T(8,128)} %col_cross.1._), calls=%async_computation.1 | async-start | bytes 524288 | tf_op jit(solution)/shard_map/all_to_all | solution.py:488
  28.7 1.6 %head.1._.head_ref = f32[256,2048]{1,0:T(8,128)S(1)} custom-call(f32[1024,2048]{1,0:T(8,128)} %cov_ref.7, f32[8,32,256]{2,1,0:T(8,128)} %col_cross.1._), custom_call_target="tpu_custom_call" | custom-call | tf_op jit(solution)/shard_map/head/pallas_call | solution.py:370
  30.3 5.3 %all-to-all-done.1.pieces_ref = f32[8,32,256]{2,1,0:T(8,128)S(1)} async-done(((f32[8,32,256]{2,1,0:T(8,128)}), f32[8,32,256]{2,1,0:T(8,128)S(1)}, u32[]{:S(2)}, u32[]{:S(2)}) %all-to-all-start.1) | async-done | bytes 262176 | tf_op jit(solution)/shard_map/all_to_all | solution.py:488
  35.6 0.2 slab.1
  35.8 0.7 %collective-permute-start = (f32[32,256]{1,0:T(8,128)S(1)}, f32[32,256]{1,0:T(8,128)S(1)}, u32[]{:S(2)}, u32[]{:S(2)}) collective-permute-start(f32[32,256]{1,0:T(8,128)S(1)} %get-tuple-element.15), channel_id=1, source_target_pairs={{0,0},{1,8},{2,16},{3,24},{4,1},{5,9},{6,17},{7,25},{8,2},{9,10},{... | collective-permute-start | bytes 98312 | tf_op jit(solution)/shard_map/ppermute | solution.py:547
  36.5 11.6 %all-gather = f32[576,128]{1,0:T(8,128)S(1)} all-gather(f32[72,128]{1,0:T(8,128)S(1)} %get-tuple-element.16), channel_id=2, replica_groups=mesh['row'=8,'col'=4] {'row'}, dimensions={0}, use_global_device_ids=true | all-gather | bytes 331776 | tf_op jit(solution)/shard_map/all_gather | solution.py:548
  48.0 0.0 collective-permute-done.own_ref
  48.0 9.6 %all_to_all.15.rows_ref = f32[4,72,128]{2,1,0:T(8,128)S(1)} all-to-all(f32[4,72,128]{2,1,0:T(8,128)S(1)} %term.1), channel_id=1, replica_groups=mesh['row'=8,'col'=4] {'col'}, dimensions={0} | all-to-all | bytes 294912 | tf_op jit(solution)/shard_map/all_to_all | solution.py:488
  57.6 0.0 copy-done
  57.6 5.9 %update.1 = (f32[2,128]{1,0:T(2,128)}, f32[1024,2048]{1,0:T(8,128)}) custom-call(f32[4,72,128]{2,1,0:T(8,128)S(1)} %all_to_all.15.rows_ref, f32[8,72,128]{2,1,0:T(8,128)S(1)} %bitcast.11, f32[32,128]{1,0:T(8,128)S(1)} %get-tuple-element.17.error_ref, f32[64,128]{1,0:T(8,128)S(1)} %copy-done, f32[256,2048]{1,0:T(8,128)S(1)} %head.1._.head_ref, ...), custom_call_target="tpu_custom_call" | custom-call | tf_op jit(solution)/shard_map/update/pallas_call | solution.py:447
  (1 shorter events, 0.0 us)
Async XLA Ops:
  4.6 16.4 %all-to-all-start = ((f32[32,1,1408]{2,1,0:T(1,128)}), f32[32,1,1408]{2,1,0:T(1,128)S(1)}, u32[]{:S(2)}, u32[]{:S(2)}) async-start(f32[32,1,1408]{2,1,0:T(1,128)} %bitcast.14), calls=%async_computation | async-start | bytes 360448 | tf_op jit(solution)/shard_map/all_to_all | solution.py:488
  25.3 32.4 %copy-start = (f32[64,128]{1,0:T(8,128)S(1)}, f32[64,128]{1,0:T(8,128)}, u32[]{:S(2)}) copy-start(f32[64,128]{1,0:T(8,128)} %weight_ref.3) | copy-start | bytes 98308
  25.3 10.3 %all-to-all-start.1 = ((f32[8,32,256]{2,1,0:T(8,128)}), f32[8,32,256]{2,1,0:T(8,128)S(1)}, u32[]{:S(2)}, u32[]{:S(2)}) async-start(f32[8,32,256]{2,1,0:T(8,128)} %col_cross.1._), calls=%async_computation.1 | async-start | bytes 524288 | tf_op jit(solution)/shard_map/all_to_all | solution.py:488
  35.8 12.2 %collective-permute-start = (f32[32,256]{1,0:T(8,128)S(1)}, f32[32,256]{1,0:T(8,128)S(1)}, u32[]{:S(2)}, u32[]{:S(2)}) collective-permute-start(f32[32,256]{1,0:T(8,128)S(1)} %get-tuple-element.15), channel_id=1, source_target_pairs={{0,0},{1,8},{2,16},{3,24},{4,1},{5,9},{6,17},{7,25},{8,2},{9,10},{... | collective-permute-start | bytes 98312 | tf_op jit(solution)/shard_map/ppermute | solution.py:547

commit v18 on v16

--- a/solution.py
+++ b/solution.py
@@ -82,7 +82,11 @@
     parts = jnp.concatenate(split3(mixed), axis=0)
     descriptor = five_products(parts, *split2(mix), ((1,), (0,))) * (1.0 / math.sqrt(neighbours))
     hidden = jnp.tanh(descriptor)
-    activity = jnp.tanh(dot(hidden, weight_ref[...], ((0,), (0,)), highest))
+    hidden_hi, hidden_lo = split2(hidden)
+    weight_hi, weight_lo = split2(weight_ref[...])
+    left = jnp.concatenate([hidden_hi, hidden_hi, hidden_lo, hidden_lo], axis=0)
+    right = jnp.concatenate([weight_hi, weight_lo, weight_hi, weight_lo], axis=0)
+    activity = jnp.tanh(dot(left, right, ((0,), (0,))))
     out_weight = out_weight_ref[...]
     scale = 1.0 / math.sqrt(atoms)
     force = force_ref[...]

time: 63.7 us -> 63.6 us (level)
  no operation moved by 1% of the time
where the time goes in v18:
time: 63.6 us; the launch traced here: 63 us
  blocking collectives  20.9 us (33%)
  Pallas kernels  19.5 us (31%)
  starting transfers between devices  11.3 us (18%)
  waiting for transfers between devices  10 us (16%)
  between operations  1.33 us (2%)
    all_gather x1, blocking collectives, on_device(): col_slabs = lax.all_gather(with_term, 'row', axis=0, tiled=False)  11.6 us
    all_to_all x2, starting transfers between devices, exchange(): return lax.all_to_all(x, axes, split_axis=0, concat_axis=0, tiled=True)  10.6 us
    all_to_all x2, waiting for transfers between devices, exchange(): return lax.all_to_all(x, axes, split_axis=0, concat_axis=0, tiled=True)  10 us
    all_to_all x1, blocking collectives, exchange(): return lax.all_to_all(x, axes, split_axis=0, concat_axis=0, tiled=True)  9.35 us
    pallas_call x1, Pallas kernels, update(): pl.pallas_call(update_kernel, in_specs=[whole] * 5 + [beyond], out_specs=...  5.86 us
    pallas_call x1, Pallas kernels, stage(): pl.pallas_call(functools.partial(stage_kernel, head_steps=head_steps), gr...  4.26 us
    pallas_call x1, Pallas kernels, col_partial(): pl.pallas_call(col_kernel, in_specs=[whole] * 3 + [beyond] * 3, out_specs...  3.49 us
    pallas_call x1, Pallas kernels, network(): pl.pallas_call(functools.partial(network_kernel, plan=plan), grid=(per_de...  3.33 us
  transfers between devices with their start and end apart: 3, of which 2 were waited for; matrix products, arithmetic and copies ran while one was open for 0% of the time, Pallas kernels for 9%

profile of v18, /device:TPU:0, one launch (start us, length us, event | category | flops | bytes accessed | tf_op | source)
XLA Modules:
  0.0 63.0 jit_solution(13546742862884446462)
XLA Ops:
  1.3 3.3 %network.1 = f32[1,352,128]{2,1,0:T(8,128)} custom-call(s32[1,1,256]{2,1,0:T(1,128)} %bitcast.16, s32[1,32,256]{2,1,0:T(8,128)} %ids_ref.1, f32[1,32,256]{2,1,0:T(8,128)} %switch_ref.1, f32[1,64,256]{2,1,0:T(8,128)} %bitcast.15, f32[1,1,256]{2,1,0:T(1,128)} %bitcast.17, f32[1,1,1]{2,1,0:T(1,128)} %bitcast.9.target_ref, f32[4,64]{1,0:T(4,128)} %embed_ref.1, ...), custom_call_target="tpu_custom_call" | custom-call | tf_op jit(solution)/shard_map/network/pallas_call | solution.py:121
  4.6 7.3 %all-to-all-start = ((f32[32,1,1408]{2,1,0:T(1,128)}), f32[32,1,1408]{2,1,0:T(1,128)S(1)}, u32[]{:S(2)}, u32[]{:S(2)}) async-start(f32[32,1,1408]{2,1,0:T(1,128)} %bitcast.14), calls=%async_computation | async-start | bytes 360448 | tf_op jit(solution)/shard_map/all_to_all | solution.py:487
  11.9 4.3 %stage.1 = (bf16[256,2048]{1,0:T(8,128)(2,1)}, bf16[256,2048]{1,0:T(8,128)(2,1)}, bf16[256,2048]{1,0:T(8,128)(2,1)S(1)}, bf16[256,2048]{1,0:T(8,128)(2,1)S(1)}) custom-call(f32[1024,2048]{1,0:T(8,128)} %cov_ref.7), custom_call_target="tpu_custom_call" | custom-call | tf_op jit(solution)/shard_map/stage/pallas_call | solution.py:178
  16.2 4.8 %all-to-all-done = f32[32,1,1408]{2,1,0:T(1,128)S(1)} async-done(((f32[32,1,1408]{2,1,0:T(1,128)}), f32[32,1,1408]{2,1,0:T(1,128)S(1)}, u32[]{:S(2)}, u32[]{:S(2)}) %all-to-all-start) | async-done | bytes 180256 | tf_op jit(solution)/shard_map/all_to_all | solution.py:487
  21.0 3.5 %col_cross.1._ = f32[8,32,256]{2,1,0:T(8,128)S(1)} custom-call(f32[352,128]{1,0:T(8,128)S(1)} %bitcast.12, bf16[256,2048]{1,0:T(8,128)(2,1)S(1)} %get-tuple-element.11.hi_head_ref, bf16[256,2048]{1,0:T(8,128)(2,1)S(1)} %get-tuple-element.12.lo_head_ref, bf16[256,2048]{1,0:T(8,128)(2,1)} %get-tuple-element.13.hi_ref, ...), custom_call_target="tpu_custom_call" | custom-call | tf_op jit(solution)/shard_map/col_cross/pallas_call | solution.py:259
  24.5 0.0 copy-start
  24.5 9.3 %all_to_all.15.pieces_ref = f32[8,32,256]{2,1,0:T(8,128)S(1)} all-to-all(f32[8,32,256]{2,1,0:T(8,128)S(1)} %col_cross.1._), channel_id=1, replica_groups=mesh['row'=8,'col'=4] {'row'}, dimensions={0} | all-to-all | bytes 524288 | tf_op jit(solution)/shard_map/all_to_all | solution.py:487
  33.9 0.2 slab.1
  34.1 0.7 %collective-permute-start = (f32[32,256]{1,0:T(8,128)S(1)}, f32[32,256]{1,0:T(8,128)S(1)}, u32[]{:S(2)}, u32[]{:S(2)}) collective-permute-start(f32[32,256]{1,0:T(8,128)S(1)} %get-tuple-element.15), channel_id=1, source_target_pairs={{0,0},{1,8},{2,16},{3,24},{4,1},{5,9},{6,17},{7,25},{8,2},{9,10},{... | collective-permute-start | bytes 98312 | tf_op jit(solution)/shard_map/ppermute | solution.py:546
  34.8 11.6 %all-gather = f32[576,128]{1,0:T(8,128)S(1)} all-gather(f32[72,128]{1,0:T(8,128)S(1)} %get-tuple-element.16), channel_id=2, replica_groups=mesh['row'=8,'col'=4] {'row'}, dimensions={0}, use_global_device_ids=true | all-gather | bytes 331776 | tf_op jit(solution)/shard_map/all_gather | solution.py:547
  46.3 0.0 collective-permute-done.own_ref
  46.3 0.7 %term.1 = f32[4,72,128]{2,1,0:T(8,128)} custom-call(f32[32,256]{1,0:T(8,128)S(1)} %collective-permute-done.own_ref, f32[8,72,128]{2,1,0:T(8,128)S(1)} %bitcast.10), custom_call_target="tpu_custom_call" | custom-call | tf_op jit(solution)/shard_map/term/pallas_call | solution.py:336
  47.0 3.3 %all-to-all-start.2 = ((f32[4,72,128]{2,1,0:T(8,128)}), f32[4,72,128]{2,1,0:T(8,128)S(1)}, u32[]{:S(2)}, u32[]{:S(2)}) async-start(f32[4,72,128]{2,1,0:T(8,128)} %term.1), calls=%async_computation.2 | async-start | bytes 294912 | tf_op jit(solution)/shard_map/all_to_all | solution.py:487
  50.4 1.6 %head.1.head_ref = f32[256,2048]{1,0:T(8,128)S(1)} custom-call(f32[1024,2048]{1,0:T(8,128)} %cov_ref.7, f32[8,32,256]{2,1,0:T(8,128)S(1)} %col_cross.1._), custom_call_target="tpu_custom_call" | custom-call | tf_op jit(solution)/shard_map/head/pallas_call | solution.py:369
  52.0 5.2 %all-to-all-done.2.rows_ref = f32[4,72,128]{2,1,0:T(8,128)S(1)} async-done(((f32[4,72,128]{2,1,0:T(8,128)}), f32[4,72,128]{2,1,0:T(8,128)S(1)}, u32[]{:S(2)}, u32[]{:S(2)}) %all-to-all-start.2) | async-done | bytes 147488 | tf_op jit(solution)/shard_map/all_to_all | solution.py:487
  57.1 0.0 copy-done
  57.2 5.9 %update.1 = (f32[2,128]{1,0:T(2,128)}, f32[1024,2048]{1,0:T(8,128)}) custom-call(f32[4,72,128]{2,1,0:T(8,128)S(1)} %all-to-all-done.2.rows_ref, f32[8,72,128]{2,1,0:T(8,128)S(1)} %bitcast.11, f32[32,128]{1,0:T(8,128)S(1)} %get-tuple-element.17.error_ref, f32[64,128]{1,0:T(8,128)S(1)} %copy-done, f32[256,2048]{1,0:T(8,128)S(1)} %head.1.head_ref, ...), custom_call_target="tpu_custom_call" | custom-call | tf_op jit(solution)/shard_map/update/pallas_call | solution.py:446
Async XLA Ops:
  4.6 16.4 %all-to-all-start = ((f32[32,1,1408]{2,1,0:T(1,128)}), f32[32,1,1408]{2,1,0:T(1,128)S(1)}, u32[]{:S(2)}, u32[]{:S(2)}) async-start(f32[32,1,1408]{2,1,0:T(1,128)} %bitcast.14), calls=%async_computation | async-start | bytes 360448 | tf_op jit(solution)/shard_map/all_to_all | solution.py:487
  24.5 32.6 %copy-start = (f32[64,128]{1,0:T(8,128)S(1)}, f32[64,128]{1,0:T(8,128)}, u32[]{:S(2)}) copy-start(f32[64,128]{1,0:T(8,128)} %weight_ref.3) | copy-start | bytes 98308
  34.1 12.2 %collective-permute-start = (f32[32,256]{1,0:T(8,128)S(1)}, f32[32,256]{1,0:T(8,128)S(1)}, u32[]{:S(2)}, u32[]{:S(2)}) collective-permute-start(f32[32,256]{1,0:T(8,128)S(1)} %get-tuple-element.15), channel_id=1, source_target_pairs={{0,0},{1,8},{2,16},{3,24},{4,1},{5,9},{6,17},{7,25},{8,2},{9,10},{... | collective-permute-start | bytes 98312 | tf_op jit(solution)/shard_map/ppermute | solution.py:546
  47.0 10.1 %all-to-all-start.2 = ((f32[4,72,128]{2,1,0:T(8,128)}), f32[4,72,128]{2,1,0:T(8,128)S(1)}, u32[]{:S(2)}, u32[]{:S(2)}) async-start(f32[4,72,128]{2,1,0:T(8,128)} %term.1), calls=%async_computation.2 | async-start | bytes 294912 | tf_op jit(solution)/shard_map/all_to_all | solution.py:487
